TPU v7x, 32 devices: a whole 2x2x4 slice. The times are simulated.
32 devices in a mesh: lon: 16 (over z, x, core), lat: 2 (over y).
Axes of the slice: x: 2, y: 2, z: 4, core: 2. Of those that a mesh axis runs over, the one named last changes fastest.
Arguments:
- cotangent: bfloat16 [128, 32, 512], P('lon', 'lat'), may hold values from -6 to 6
- states: bfloat16 [3, 128, 32, 512], P(None, 'lon', 'lat'), may hold values from -6 to 6
- w_up: bfloat16 [512, 1024], replicated, may hold values from -0.25 to 0.25
- w_down: bfloat16 [512, 1024], replicated, may hold values from -0.1875 to 0.1875
- norm_gain: float32 [512], replicated, may hold values from 0.5 to 1.5
- kernel: float32 [3, 3, 512], replicated, may hold values from -0.6 to 0.6
- bilinear: float32 [3, 4, 128, 32], P(None, None, 'lon', 'lat'), may hold values from 0.05 to 0.5
- lon_move: int32 [3, 4], replicated, may hold values from 0 to 63, as said below
- lat_move: int32 [3, 4], replicated, may hold values from 0 to 31
Outputs:
- grad_state: bfloat16 [128, 32, 512], P('lon', 'lat')
- grad_up: float32 [512, 1024], P('lon', 'lat')
- grad_down: float32 [512, 1024], P('lon', 'lat')
- grad_kernel: float32 [3, 3, 512], replicated
- grad_gain: float32 [512], replicated
Inputs may be any that keep to these rules, and one draw needn't show every extreme that they name: `lon_move`: a whole number of longitude tiles below 8, times 8, plus an offset below 8.
All inputs are finite; a program needn't handle non-finite values.
Results may differ from a plain program's by a relative error of at most 0.02.
Values may be sent and summed in bfloat16 or wider, within the bound.
No kernel may reach another device: no remote copies, remote signals or barrier semaphores. Data moves between devices by JAX's collectives and lax.ppermute only.
A program may use at most 64 MiB of HBM per device.

v0:
```python
import jax
import jax.numpy as jnp
from jax import lax
from jax.sharding import PartitionSpec as P

GROUP = 128
GROUPS = 4
STEPS = 3
REACH = 8


EPSILON = 1e-06


def with_halo(block, sides, width, periodic):
    for axis, dim in sides:
        count = lax.axis_size(axis)
        forward = [(i, i + 1) for i in range(count - 1)]
        if periodic:
            forward.append((count - 1, 0))
        backward = [(target, source) for source, target in forward]
        low = lax.ppermute(
            lax.slice_in_dim(block, block.shape[dim] - width, None, axis=dim), axis, forward
        )
        high = lax.ppermute(lax.slice_in_dim(block, 0, width, axis=dim), axis, backward)
        block = jnp.concatenate([low, block, high], axis=dim)
    return block


def shifted(value, axis, steps):
    count = lax.axis_size(axis)
    first, last = (max(0, -steps), min(count, count - steps))
    return lax.ppermute(value, axis, [(source, source + steps) for source in range(first, last)])


def as_sent(array):
    return jax.tree.map(lambda a: a.astype(jnp.bfloat16) if a.dtype == jnp.float32 else a, array)


def passed_along(value, axis, steps):
    count = lax.axis_size(axis)
    pairs = [(source, (source + steps) % count) for source in range(count)]
    return lax.ppermute(value, axis, pairs)


def tapped(padded, kernel, rows_out, cols_out, mirror):
    running = jnp.zeros((rows_out, cols_out, padded.shape[2]), jnp.float32)
    for row_tap in range(3):
        for col_tap in range(3):
            start_row = 2 - row_tap if mirror else row_tap
            start_col = 2 - col_tap if mirror else col_tap
            window = padded[
                start_row : start_row + rows_out, start_col : start_col + cols_out
            ].astype(jnp.float32)
            running = running + kernel[row_tap, col_tap] * window
    return running


def local(cotangent, states, w_up, w_down, norm_gain, kernel, bilinear, lon_move, lat_move):
    upstream = cotangent
    acc_up = jnp.zeros(w_up.shape, jnp.float32)
    acc_down = jnp.zeros(w_down.shape, jnp.float32)
    acc_kernel = jnp.zeros(kernel.shape, jnp.float32)
    acc_gain = jnp.zeros(norm_gain.shape, jnp.float32)
    levels = REACH.bit_length() - 1
    lead_contract = (((0,), (0,)), ((), ()))
    for index_step in reversed(range(STEPS)):
        state_now = states[index_step]
        rows_out, cols_out, channels = state_now.shape
        state_cycle = with_halo(state_now, (("lon", 0),), 1, True)
        padded_state = with_halo(state_cycle, (("lat", 1),), 1, False)
        mixed_field = state_now.astype(jnp.float32) + tapped(
            padded_state, kernel, rows_out, cols_out, False
        )
        inv_root = lax.rsqrt(jnp.mean(mixed_field * mixed_field, axis=-1, keepdims=True) + EPSILON)
        normed = mixed_field * inv_root
        normed_rows = (normed * norm_gain).astype(jnp.bfloat16).reshape(-1, channels)
        hidden_pre = jnp.dot(normed_rows, w_up, preferred_element_type=jnp.float32)
        hidden = jax.nn.silu(hidden_pre).astype(jnp.bfloat16)
        weights_now = bilinear[index_step]
        upstream_f = upstream.astype(jnp.float32)
        weighted = [weights_now[corner][:, :, None] * upstream_f for corner in range(4)]
        lat_edges = (
            shifted(weighted[2][:, :1].astype(jnp.bfloat16), "lat", -1).astype(jnp.float32),
            shifted(weighted[3][:, :1].astype(jnp.bfloat16), "lat", -1).astype(jnp.float32),
        )
        third_term = jnp.concatenate([weighted[2], lat_edges[0]], axis=1)
        fourth_term = jnp.concatenate([weighted[3], lat_edges[1]], axis=1)
        lon_edges = (
            passed_along(weighted[1][:1].astype(jnp.bfloat16), "lon", -1).astype(jnp.float32),
            passed_along(as_sent(fourth_term[:1]), "lon", -1),
        )
        spread = (
            weighted[0]
            + jnp.concatenate([weighted[1][1:], lon_edges[0]], axis=0)
            + third_term[:, 1:]
        )
        spread = spread + jnp.concatenate([fourth_term[1:], lon_edges[1]], axis=0)[:, 1:]
        spread = spread.astype(jnp.bfloat16)
        grouped = spread.reshape(rows_out, cols_out, GROUPS, GROUP)
        far_tiles = lon_move[index_step] // rows_out
        near_cells = lon_move[index_step] % rows_out
        for bit_level in range(levels):
            arrived = passed_along(grouped, "lon", -(1 << bit_level))
            chosen = far_tiles >> bit_level & 1 == 1
            grouped = jnp.where(chosen[None, None, :, None], arrived, grouped)
        following = passed_along(grouped, "lon", -1)
        joined = jnp.concatenate([grouped, following], axis=0)
        moved_lon = jnp.stack(
            [
                lax.dynamic_slice_in_dim(
                    joined[:, :, group_index], near_cells[group_index], rows_out, 0
                )
                for group_index in range(GROUPS)
            ],
            axis=2,
        )
        blocks = [moved_lon]
        for distance_lat in (1, 2):
            blocks.append(shifted(moved_lon, "lat", -distance_lat))
        stacked_lat = jnp.concatenate(blocks, axis=1)
        lat_now = lat_move[index_step]
        moved_back = jnp.stack(
            [
                lax.dynamic_slice_in_dim(
                    stacked_lat[:, :, group_index], lat_now[group_index], cols_out, 1
                )
                for group_index in range(GROUPS)
            ],
            axis=2,
        )
        moved_back = moved_back.reshape(rows_out, cols_out, channels)
        moved_rows = moved_back.reshape(-1, channels)
        grad_hidden = jnp.dot(moved_rows, w_down, preferred_element_type=jnp.float32)
        sigmoid_pre = jax.nn.sigmoid(hidden_pre)
        grad_pre = (grad_hidden * sigmoid_pre * (1.0 + hidden_pre * (1.0 - sigmoid_pre))).astype(
            jnp.bfloat16
        )
        grad_normed = lax.dot_general(
            grad_pre, w_up, (((1,), (1,)), ((), ())), preferred_element_type=jnp.float32
        )
        grad_normed = grad_normed.reshape(rows_out, cols_out, channels)
        acc_up = acc_up + lax.dot_general(
            normed_rows, grad_pre, lead_contract, preferred_element_type=jnp.float32
        )
        acc_down = acc_down + lax.dot_general(
            moved_rows, hidden, lead_contract, preferred_element_type=jnp.float32
        )
        acc_gain = acc_gain + jnp.sum(grad_normed * normed, axis=(0, 1))
        scaled = grad_normed * norm_gain
        grad_mixed = inv_root * (
            scaled - normed * jnp.mean(scaled * normed, axis=-1, keepdims=True)
        )
        grad_field = (moved_back.astype(jnp.float32) + grad_mixed).astype(jnp.bfloat16)
        grad_cycle = with_halo(grad_field, (("lon", 0),), 1, True)
        padded_grad = with_halo(grad_cycle, (("lat", 1),), 1, False)
        result = grad_field.astype(jnp.float32) + tapped(
            padded_grad, kernel, rows_out, cols_out, True
        )
        grad_f = grad_field.astype(jnp.float32)
        term_kernel = jnp.stack(
            [
                jnp.stack(
                    [
                        jnp.sum(
                            padded_state[
                                row_tap : row_tap + rows_out, col_tap : col_tap + cols_out
                            ].astype(jnp.float32)
                            * grad_f,
                            axis=(0, 1),
                        )
                        for col_tap in range(3)
                    ]
                )
                for row_tap in range(3)
            ]
        )
        acc_kernel = acc_kernel + term_kernel
        upstream = result.astype(jnp.bfloat16)
    rows_up, rows_down = (
        lax.psum_scatter(
            acc_up.astype(jnp.bfloat16), "lon", scatter_dimension=0, tiled=True
        ).astype(jnp.float32),
        lax.psum_scatter(
            acc_down.astype(jnp.bfloat16), "lon", scatter_dimension=0, tiled=True
        ).astype(jnp.float32),
    )
    share_up, share_down = (
        lax.psum_scatter(
            rows_up.astype(jnp.bfloat16), "lat", scatter_dimension=1, tiled=True
        ).astype(jnp.float32),
        lax.psum_scatter(
            rows_down.astype(jnp.bfloat16), "lat", scatter_dimension=1, tiled=True
        ).astype(jnp.float32),
    )
    total_kernel, total_gain = lax.psum((acc_kernel, acc_gain), ("lon", "lat"))
    return (upstream, share_up, share_down, total_kernel, total_gain)


def solution(mesh):
    placed = (
        P("lon", "lat", None),
        P(None, "lon", "lat", None),
        P(),
        P(),
        P(),
        P(),
        P(None, None, "lon", "lat"),
        P(),
        P(),
    )
    return jax.shard_map(
        local,
        mesh=mesh,
        in_specs=placed,
        out_specs=(P("lon", "lat", None), P("lon", "lat"), P("lon", "lat"), P(), P()),
        check_vma=False,
    )
```

profile of v0, /device:TPU:0, one launch (start us, length us, event | category | flops | bytes accessed | tf_op | source)
XLA Modules:
  0.0 411.2 jit_solution(1183063236653693942)
XLA Ops:
  8.6 5.0 %collective-permute-start.29 = (bf16[1,16,512]{2,1,0:T(8,128)(2,1)S(1)}, bf16[1,16,512]{2,1,0:T(8,128)(2,1)S(1)}, u32[]{:S(2)}, u32[]{:S(2)}) collective-permute-start(bf16[1,16,512]{2,1,0:T(8,128)(2,1)S(1)} %get-tuple-element.89), channel_id=1, source_target_pairs={{2,0},{4,2},{6,4},{8,6},{10,8},{12,10},{14,12},{16,14},{18,16},{20... | collective-permute-start | bytes 49160 | tf_op jit(solution)/shard_map/ppermute | solution.py:25
  13.7 4.4 %collective-permute-start.11 = (bf16[1,16,512]{2,1,0:T(8,128)(2,1)S(1)}, bf16[1,16,512]{2,1,0:T(8,128)(2,1)S(1)}, u32[]{:S(2)}, u32[]{:S(2)}) collective-permute-start(bf16[1,16,512]{2,1,0:T(8,128)(2,1)S(1)} %get-tuple-element.91), channel_id=1, source_target_pairs={{2,0},{4,2},{6,4},{8,6},{10,8},{12,10},{14,12},{16,14},{18,16},{20... | collective-permute-start | bytes 49160 | tf_op jit(solution)/shard_map/ppermute | solution.py:25
  44.7 4.3 %collective-permute-done.1 = bf16[8,1,512]{2,1,0:T(2,128)(2,1)S(1)} collective-permute-done((bf16[8,1,512]{2,1,0:T(2,128)(2,1)S(1)}, bf16[8,1,512]{2,1,0:T(2,128)(2,1)S(1)}, u32[]{:S(2)}, u32[]{:S(2)}) %collective-permute-start.1) | collective-permute-done | bytes 8224 | tf_op jit(solution)/shard_map/ppermute | solution.py:33
  49.6 3.9 collective-permute-start
  60.5 4.5 %collective-permute-start.48 = (bf16[10,1,512]{2,1,0:T(2,128)(2,1)}, bf16[10,1,512]{2,1,0:T(2,128)(2,1)S(1)}, u32[]{:S(2)}, u32[]{:S(2)}) collective-permute-start(bf16[10,1,512]{2,1,0:T(2,128)(2,1)} %get-tuple-element.124), channel_id=1, source_target_pairs={{0,1},{2,3},{4,5},{6,7},{8,9},{10,11},{12,13},{14,15},{16,17},{18,... | collective-permute-start | bytes 30728 | tf_op jit(solution)/shard_map/ppermute | solution.py:22
  69.5 3.5 collective-permute-done.31
  74.6 4.4 %collective-permute-done.5 = bf16[8,16,4,128]{3,2,1,0:T(4,128)(2,1)S(1)} collective-permute-done((bf16[8,16,4,128]{3,2,1,0:T(4,128)(2,1)S(1)}, bf16[8,16,4,128]{3,2,1,0:T(4,128)(2,1)S(1)}, u32[]{:S(2)}, u32[]{:S(2)}) %collective-permute-start.5) | collective-permute-done | bytes 131104 | tf_op jit(solution)/shard_map/ppermute | solution.py:43
  79.7 4.6 %collective-permute-done.6 = bf16[8,16,4,128]{3,2,1,0:T(4,128)(2,1)S(1)} collective-permute-done((bf16[8,16,4,128]{3,2,1,0:T(4,128)(2,1)S(1)}, bf16[8,16,4,128]{3,2,1,0:T(4,128)(2,1)S(1)}, u32[]{:S(2)}, u32[]{:S(2)}) %collective-permute-start.6) | collective-permute-done | bytes 131104 | tf_op jit(solution)/shard_map/ppermute | solution.py:43
  84.4 5.9 %collective-permute-start.7 = (bf16[8,16,4,128]{3,2,1,0:T(4,128)(2,1)S(1)}, bf16[8,16,4,128]{3,2,1,0:T(4,128)(2,1)S(1)}, u32[]{:S(2)}, u32[]{:S(2)}) collective-permute-start(bf16[8,16,4,128]{3,2,1,0:T(4,128)(2,1)S(1)} %broadcast_select_fusion.2), channel_id=1, source_target_pairs={{0,30},{2,0},{4,2},{6,4},{8,6},{10,8},{12,10},{14,12},{16,14},{18,... | collective-permute-start | bytes 393224 | tf_op jit(solution)/shard_map/ppermute | solution.py:43
  96.0 5.5 %collective-permute-done.8 = bf16[8,16,4,128]{3,2,1,0:T(4,128)(2,1)S(1)} collective-permute-done((bf16[8,16,4,128]{3,2,1,0:T(4,128)(2,1)S(1)}, bf16[8,16,4,128]{3,2,1,0:T(4,128)(2,1)S(1)}, u32[]{:S(2)}, u32[]{:S(2)}) %collective-permute-start.8) | collective-permute-done | bytes 131104 | tf_op jit(solution)/shard_map/ppermute | solution.py:33
  107.7 4.4 %collective-permute-start.15 = (bf16[1,16,512]{2,1,0:T(8,128)(2,1)S(1)}, bf16[1,16,512]{2,1,0:T(8,128)(2,1)S(1)}, u32[]{:S(2)}, u32[]{:S(2)}) collective-permute-start(bf16[1,16,512]{2,1,0:T(8,128)(2,1)S(1)} %get-tuple-element.146), channel_id=1, source_target_pairs={{2,0},{4,2},{6,4},{8,6},{10,8},{12,10},{14,12},{16,14},{18,16},{20... | collective-permute-start | bytes 49160 | tf_op jit(solution)/shard_map/ppermute | solution.py:25
  114.9 4.5 %collective-permute-start.17 = (bf16[10,1,512]{2,1,0:T(2,128)(2,1)S(1)}, bf16[10,1,512]{2,1,0:T(2,128)(2,1)S(1)}, u32[]{:S(2)}, u32[]{:S(2)}) collective-permute-start(bf16[10,1,512]{2,1,0:T(2,128)(2,1)S(1)} %get-tuple-element.116), channel_id=1, source_target_pairs={{0,1},{2,3},{4,5},{6,7},{8,9},{10,11},{12,13},{14,15},{16,17},{18,... | collective-permute-start | bytes 30728 | tf_op jit(solution)/shard_map/ppermute | solution.py:22
  122.8 3.3 collective-permute-start.18
  132.1 3.5 collective-permute-start.22
  138.3 5.0 %collective-permute-done.23 = bf16[8,16,4,128]{3,2,1,0:T(4,128)(2,1)S(1)} collective-permute-done((bf16[8,16,4,128]{3,2,1,0:T(4,128)(2,1)S(1)}, bf16[8,16,4,128]{3,2,1,0:T(4,128)(2,1)S(1)}, u32[]{:S(2)}, u32[]{:S(2)}) %collective-permute-start.23) | collective-permute-done | bytes 131104 | tf_op jit(solution)/shard_map/ppermute | solution.py:43
  143.5 5.7 %collective-permute-done.24 = bf16[8,16,4,128]{3,2,1,0:T(4,128)(2,1)S(1)} collective-permute-done((bf16[8,16,4,128]{3,2,1,0:T(4,128)(2,1)S(1)}, bf16[8,16,4,128]{3,2,1,0:T(4,128)(2,1)S(1)}, u32[]{:S(2)}, u32[]{:S(2)}) %collective-permute-start.24) | collective-permute-done | bytes 131104 | tf_op jit(solution)/shard_map/ppermute | solution.py:43
  149.3 6.5 %collective-permute-start.25 = (bf16[8,16,4,128]{3,2,1,0:T(4,128)(2,1)S(1)}, bf16[8,16,4,128]{3,2,1,0:T(4,128)(2,1)S(1)}, u32[]{:S(2)}, u32[]{:S(2)}) collective-permute-start(bf16[8,16,4,128]{3,2,1,0:T(4,128)(2,1)S(1)} %broadcast_select_fusion.5), channel_id=1, source_target_pairs={{0,30},{2,0},{4,2},{6,4},{8,6},{10,8},{12,10},{14,12},{16,14},{18,... | collective-permute-start | bytes 393224 | tf_op jit(solution)/shard_map/ppermute | solution.py:43
  175.4 5.2 %collective-permute-done.26 = bf16[8,16,4,128]{3,2,1,0:T(4,128)(2,1)S(1)} collective-permute-done((bf16[8,16,4,128]{3,2,1,0:T(4,128)(2,1)S(1)}, bf16[8,16,4,128]{3,2,1,0:T(4,128)(2,1)S(1)}, u32[]{:S(2)}, u32[]{:S(2)}) %collective-permute-start.26) | collective-permute-done | bytes 131104 | tf_op jit(solution)/shard_map/ppermute | solution.py:33
  186.7 4.4 %collective-permute-start.33 = (bf16[1,16,512]{2,1,0:T(8,128)(2,1)S(1)}, bf16[1,16,512]{2,1,0:T(8,128)(2,1)S(1)}, u32[]{:S(2)}, u32[]{:S(2)}) collective-permute-start(bf16[1,16,512]{2,1,0:T(8,128)(2,1)S(1)} %get-tuple-element.136), channel_id=1, source_target_pairs={{2,0},{4,2},{6,4},{8,6},{10,8},{12,10},{14,12},{16,14},{18,16},{20... | collective-permute-start | bytes 49160 | tf_op jit(solution)/shard_map/ppermute | solution.py:25
  194.0 4.5 %collective-permute-start.35 = (bf16[10,1,512]{2,1,0:T(2,128)(2,1)S(1)}, bf16[10,1,512]{2,1,0:T(2,128)(2,1)S(1)}, u32[]{:S(2)}, u32[]{:S(2)}) collective-permute-start(bf16[10,1,512]{2,1,0:T(2,128)(2,1)S(1)} %get-tuple-element.108), channel_id=1, source_target_pairs={{0,1},{2,3},{4,5},{6,7},{8,9},{10,11},{12,13},{14,15},{16,17},{18,... | collective-permute-start | bytes 30728 | tf_op jit(solution)/shard_map/ppermute | solution.py:22
  221.9 4.2 %collective-permute-done.37 = bf16[8,1,512]{2,1,0:T(2,128)(2,1)S(1)} collective-permute-done((bf16[8,1,512]{2,1,0:T(2,128)(2,1)S(1)}, bf16[8,1,512]{2,1,0:T(2,128)(2,1)S(1)}, u32[]{:S(2)}, u32[]{:S(2)}) %collective-permute-start.37) | collective-permute-done | bytes 8224 | tf_op jit(solution)/shard_map/ppermute | solution.py:33
  232.3 3.5 collective-permute-done.41
  236.4 5.4 %collective-permute-done.42 = bf16[8,16,4,128]{3,2,1,0:T(4,128)(2,1)S(1)} collective-permute-done((bf16[8,16,4,128]{3,2,1,0:T(4,128)(2,1)S(1)}, bf16[8,16,4,128]{3,2,1,0:T(4,128)(2,1)S(1)}, u32[]{:S(2)}, u32[]{:S(2)}) %collective-permute-start.42) | collective-permute-done | bytes 131104 | tf_op jit(solution)/shard_map/ppermute | solution.py:43
  241.9 6.3 %collective-permute-start.43 = (bf16[8,16,4,128]{3,2,1,0:T(4,128)(2,1)S(1)}, bf16[8,16,4,128]{3,2,1,0:T(4,128)(2,1)S(1)}, u32[]{:S(2)}, u32[]{:S(2)}) collective-permute-start(bf16[8,16,4,128]{3,2,1,0:T(4,128)(2,1)S(1)} %broadcast_select_fusion.8), channel_id=1, source_target_pairs={{0,30},{2,0},{4,2},{6,4},{8,6},{10,8},{12,10},{14,12},{16,14},{18,... | collective-permute-start | bytes 393224 | tf_op jit(solution)/shard_map/ppermute | solution.py:43
  255.9 3.6 collective-permute-done.44
  272.0 4.4 %collective-permute-start.51 = (bf16[1,16,512]{2,1,0:T(8,128)(2,1)}, bf16[1,16,512]{2,1,0:T(8,128)(2,1)}, u32[]{:S(2)}, u32[]{:S(2)}) collective-permute-start(bf16[1,16,512]{2,1,0:T(8,128)(2,1)} %get-tuple-element.126), channel_id=1, source_target_pairs={{2,0},{4,2},{6,4},{8,6},{10,8},{12,10},{14,12},{16,14},{18,16},{20... | collective-permute-start | bytes 49160 | tf_op jit(solution)/shard_map/ppermute | solution.py:25
  282.8 4.5 %collective-permute-start.53 = (bf16[10,1,512]{2,1,0:T(2,128)(2,1)S(1)}, bf16[10,1,512]{2,1,0:T(2,128)(2,1)S(1)}, u32[]{:S(2)}, u32[]{:S(2)}) collective-permute-start(bf16[10,1,512]{2,1,0:T(2,128)(2,1)S(1)} %get-tuple-element.104), channel_id=1, source_target_pairs={{0,1},{2,3},{4,5},{6,7},{8,9},{10,11},{12,13},{14,15},{16,17},{18,... | collective-permute-start | bytes 30728 | tf_op jit(solution)/shard_map/ppermute | solution.py:22
  287.3 32.3 %reduce-scatter.9.cloned.1.call-done = bf16[32,1024]{1,0:T(8,128)(2,1)} async-done(((bf16[512,1024]{1,0:T(8,128)(2,1)}), bf16[32,1024]{1,0:T(8,128)(2,1)}) %reduce-scatter.9.cloned.1.call-update) | async-done | bytes 65552 | tf_op jit(solution)/shard_map/reduce_scatter | solution.py:184
  319.8 40.8 %all-reduce = (f32[3,3,512]{2,1,0:T(4,128)}, f32[512]{0:T(512)}) all-reduce(f32[3,3,512]{2,1,0:T(4,128)S(1)} %fusion.113, f32[512]{0:T(512)S(1)} %add_add_fusion), channel_id=1, replica_groups=mesh['lon'=16,'lat'=2] {'lon','lat'}, use_global_device_ids=true, to_apply=%region_37.38 | all-reduce | flops 5120 | bytes 40960 | tf_op jit(solution)/shard_map/psum | solution.py:196
  361.5 18.7 %reduce-scatter.5.cloned.1.call-done = bf16[32,1024]{1,0:T(8,128)(2,1)} async-done(((bf16[512,1024]{1,0:T(8,128)(2,1)}), bf16[32,1024]{1,0:T(8,128)(2,1)}) %reduce-scatter.5.cloned.1.call-update) | async-done | bytes 65552 | tf_op jit(solution)/shard_map/reduce_scatter | solution.py:181
  381.9 9.4 %reduce-scatter.11.cloned.1.call-done = bf16[32,512]{1,0:T(8,128)(2,1)} async-done(((bf16[32,1024]{1,0:T(8,128)(2,1)}), bf16[32,512]{1,0:T(8,128)(2,1)}) %reduce-scatter.11.cloned.1.call-update) | async-done | bytes 32784 | tf_op jit(solution)/shard_map/reduce_scatter | solution.py:192
  392.7 10.6 %reduce-scatter.7.cloned.1.call-done = bf16[32,512]{1,0:T(8,128)(2,1)} async-done(((bf16[32,1024]{1,0:T(8,128)(2,1)}), bf16[32,512]{1,0:T(8,128)(2,1)}) %reduce-scatter.7.cloned.1.call-update) | async-done | bytes 32784 | tf_op jit(solution)/shard_map/reduce_scatter | solution.py:189
  (432 shorter events, 112.6 us)
Async XLA Ops:
  7.2 312.5 %reduce-scatter.9.cloned.1.call-start = ((), (), s32[]{:S(2)}) async-start(), calls=%async_computation.6 | async-start | bytes 1114112 | tf_op jit(solution)/shard_map/reduce_scatter | solution.py:184
  8.1 40.9 %collective-permute-start.10 = (bf16[1,16,512]{2,1,0:T(8,128)(2,1)S(1)}, bf16[1,16,512]{2,1,0:T(8,128)(2,1)S(1)}, u32[]{:S(2)}, u32[]{:S(2)}) collective-permute-start(bf16[1,16,512]{2,1,0:T(8,128)(2,1)S(1)} %get-tuple-element.88), channel_id=1, source_target_pairs={{0,2},{2,4},{4,6},{6,8},{8,10},{10,12},{12,14},{14,16},{16,18},{18... | collective-permute-start | bytes 49160 | tf_op jit(solution)/shard_map/ppermute | solution.py:22
  8.6 48.6 %collective-permute-start.29 = (bf16[1,16,512]{2,1,0:T(8,128)(2,1)S(1)}, bf16[1,16,512]{2,1,0:T(8,128)(2,1)S(1)}, u32[]{:S(2)}, u32[]{:S(2)}) collective-permute-start(bf16[1,16,512]{2,1,0:T(8,128)(2,1)S(1)} %get-tuple-element.89), channel_id=1, source_target_pairs={{2,0},{4,2},{6,4},{8,6},{10,8},{12,10},{14,12},{16,14},{18,16},{20... | collective-permute-start | bytes 49160 | tf_op jit(solution)/shard_map/ppermute | solution.py:25
  13.7 44.9 %collective-permute-start.28 = (bf16[1,16,512]{2,1,0:T(8,128)(2,1)S(1)}, bf16[1,16,512]{2,1,0:T(8,128)(2,1)S(1)}, u32[]{:S(2)}, u32[]{:S(2)}) collective-permute-start(bf16[1,16,512]{2,1,0:T(8,128)(2,1)S(1)} %get-tuple-element.90), channel_id=1, source_target_pairs={{0,2},{2,4},{4,6},{6,8},{8,10},{10,12},{12,14},{14,16},{16,18},{18... | collective-permute-start | bytes 49160 | tf_op jit(solution)/shard_map/ppermute | solution.py:22
  13.7 35.9 %collective-permute-start.11 = (bf16[1,16,512]{2,1,0:T(8,128)(2,1)S(1)}, bf16[1,16,512]{2,1,0:T(8,128)(2,1)S(1)}, u32[]{:S(2)}, u32[]{:S(2)}) collective-permute-start(bf16[1,16,512]{2,1,0:T(8,128)(2,1)S(1)} %get-tuple-element.91), channel_id=1, source_target_pairs={{2,0},{4,2},{6,4},{8,6},{10,8},{12,10},{14,12},{16,14},{18,16},{20... | collective-permute-start | bytes 49160 | tf_op jit(solution)/shard_map/ppermute | solution.py:25
  20.7 22.7 %collective-permute-start.2 = (bf16[8,1,512]{2,1,0:T(2,128)(2,1)S(1)}, bf16[8,1,512]{2,1,0:T(2,128)(2,1)S(1)}, u32[]{:S(2)}, u32[]{:S(2)}) collective-permute-start(bf16[8,1,512]{2,1,0:T(2,128)(2,1)S(1)} %slice.1129), channel_id=1, source_target_pairs={{1,0},{3,2},{5,4},{7,6},{9,8},{11,10},{13,12},{15,14},{17,16},{19,... | collective-permute-start | bytes 24584 | tf_op jit(solution)/shard_map/ppermute | solution.py:33
  49.6 10.9 %collective-permute-start = (bf16[1,16,512]{2,1,0:T(8,128)(2,1)S(1)}, bf16[1,16,512]{2,1,0:T(8,128)(2,1)S(1)}, u32[]{:S(2)}, u32[]{:S(2)}) collective-permute-start(bf16[1,16,512]{2,1,0:T(8,128)(2,1)S(1)} %slice.1124), channel_id=1, source_target_pairs={{0,30},{2,0},{4,2},{6,4},{8,6},{10,8},{12,10},{14,12},{16,14},{18,... | collective-permute-start | bytes 49160 | tf_op jit(solution)/shard_map/ppermute | solution.py:43
  53.6 11.4 %collective-permute-start.3 = (bf16[1,17,512]{2,1,0:T(8,128)(2,1)S(1)}, bf16[1,17,512]{2,1,0:T(8,128)(2,1)S(1)}, u32[]{:S(2)}, u32[]{:S(2)}) collective-permute-start(bf16[1,17,512]{2,1,0:T(8,128)(2,1)S(1)} %fusion.112), channel_id=1, source_target_pairs={{0,30},{2,0},{4,2},{6,4},{8,6},{10,8},{12,10},{14,12},{16,14},{18,... | collective-permute-start | bytes 52232 | tf_op jit(solution)/shard_map/ppermute | solution.py:43
  54.9 12.2 %collective-permute-start.12 = (bf16[10,1,512]{2,1,0:T(2,128)(2,1)S(1)}, bf16[10,1,512]{2,1,0:T(2,128)(2,1)S(1)}, u32[]{:S(2)}, u32[]{:S(2)}) collective-permute-start(bf16[10,1,512]{2,1,0:T(2,128)(2,1)S(1)} %get-tuple-element.119), channel_id=1, source_target_pairs={{0,1},{2,3},{4,5},{6,7},{8,9},{10,11},{12,13},{14,15},{16,17},{18,... | collective-permute-start | bytes 30728 | tf_op jit(solution)/shard_map/ppermute | solution.py:22
  57.2 11.2 %collective-permute-start.13 = (bf16[10,1,512]{2,1,0:T(2,128)(2,1)S(1)}, bf16[10,1,512]{2,1,0:T(2,128)(2,1)S(1)}, u32[]{:S(2)}, u32[]{:S(2)}) collective-permute-start(bf16[10,1,512]{2,1,0:T(2,128)(2,1)S(1)} %get-tuple-element.120), channel_id=1, source_target_pairs={{1,0},{3,2},{5,4},{7,6},{9,8},{11,10},{13,12},{15,14},{17,16},{19,... | collective-permute-start | bytes 30728 | tf_op jit(solution)/shard_map/ppermute | solution.py:25
  58.5 16.0 %collective-permute-start.49 = (bf16[10,1,512]{2,1,0:T(2,128)(2,1)}, bf16[10,1,512]{2,1,0:T(2,128)(2,1)S(1)}, u32[]{:S(2)}, u32[]{:S(2)}) collective-permute-start(bf16[10,1,512]{2,1,0:T(2,128)(2,1)} %get-tuple-element.123), channel_id=1, source_target_pairs={{1,0},{3,2},{5,4},{7,6},{9,8},{11,10},{13,12},{15,14},{17,16},{19,... | collective-permute-start | bytes 30728 | tf_op jit(solution)/shard_map/ppermute | solution.py:25
  60.5 14.0 %collective-permute-start.48 = (bf16[10,1,512]{2,1,0:T(2,128)(2,1)}, bf16[10,1,512]{2,1,0:T(2,128)(2,1)S(1)}, u32[]{:S(2)}, u32[]{:S(2)}) collective-permute-start(bf16[10,1,512]{2,1,0:T(2,128)(2,1)} %get-tuple-element.124), channel_id=1, source_target_pairs={{0,1},{2,3},{4,5},{6,7},{8,9},{10,11},{12,13},{14,15},{16,17},{18,... | collective-permute-start | bytes 30728 | tf_op jit(solution)/shard_map/ppermute | solution.py:22
  84.4 8.4 %collective-permute-start.7 = (bf16[8,16,4,128]{3,2,1,0:T(4,128)(2,1)S(1)}, bf16[8,16,4,128]{3,2,1,0:T(4,128)(2,1)S(1)}, u32[]{:S(2)}, u32[]{:S(2)}) collective-permute-start(bf16[8,16,4,128]{3,2,1,0:T(4,128)(2,1)S(1)} %broadcast_select_fusion.2), channel_id=1, source_target_pairs={{0,30},{2,0},{4,2},{6,4},{8,6},{10,8},{12,10},{14,12},{16,14},{18,... | collective-permute-start | bytes 393224 | tf_op jit(solution)/shard_map/ppermute | solution.py:43
  94.6 6.9 %collective-permute-start.8 = (bf16[8,16,4,128]{3,2,1,0:T(4,128)(2,1)S(1)}, bf16[8,16,4,128]{3,2,1,0:T(4,128)(2,1)S(1)}, u32[]{:S(2)}, u32[]{:S(2)}) collective-permute-start(bf16[8,16,4,128]{3,2,1,0:T(4,128)(2,1)S(1)} %pad_maximum_fusion.27), channel_id=1, source_target_pairs={{1,0},{3,2},{5,4},{7,6},{9,8},{11,10},{13,12},{15,14},{17,16},{19,... | collective-permute-start | bytes 393224 | tf_op jit(solution)/shard_map/ppermute | solution.py:33
  114.9 6.0 %collective-permute-start.17 = (bf16[10,1,512]{2,1,0:T(2,128)(2,1)S(1)}, bf16[10,1,512]{2,1,0:T(2,128)(2,1)S(1)}, u32[]{:S(2)}, u32[]{:S(2)}) collective-permute-start(bf16[10,1,512]{2,1,0:T(2,128)(2,1)S(1)} %get-tuple-element.116), channel_id=1, source_target_pairs={{0,1},{2,3},{4,5},{6,7},{8,9},{10,11},{12,13},{14,15},{16,17},{18,... | collective-permute-start | bytes 30728 | tf_op jit(solution)/shard_map/ppermute | solution.py:22
  121.5 6.0 %collective-permute-start.20 = (bf16[8,1,512]{2,1,0:T(2,128)(2,1)S(1)}, bf16[8,1,512]{2,1,0:T(2,128)(2,1)S(1)}, u32[]{:S(2)}, u32[]{:S(2)}) collective-permute-start(bf16[8,1,512]{2,1,0:T(2,128)(2,1)S(1)} %slice.1127), channel_id=1, source_target_pairs={{1,0},{3,2},{5,4},{7,6},{9,8},{11,10},{13,12},{15,14},{17,16},{19,... | collective-permute-start | bytes 24584 | tf_op jit(solution)/shard_map/ppermute | solution.py:33
  122.8 9.0 %collective-permute-start.18 = (bf16[1,16,512]{2,1,0:T(8,128)(2,1)S(1)}, bf16[1,16,512]{2,1,0:T(8,128)(2,1)S(1)}, u32[]{:S(2)}, u32[]{:S(2)}) collective-permute-start(bf16[1,16,512]{2,1,0:T(8,128)(2,1)S(1)} %slice.1123), channel_id=1, source_target_pairs={{0,30},{2,0},{4,2},{6,4},{8,6},{10,8},{12,10},{14,12},{16,14},{18,... | collective-permute-start | bytes 49160 | tf_op jit(solution)/shard_map/ppermute | solution.py:43
  132.1 6.0 %collective-permute-start.22 = (bf16[8,16,4,128]{3,2,1,0:T(4,128)(2,1)S(1)}, bf16[8,16,4,128]{3,2,1,0:T(4,128)(2,1)S(1)}, u32[]{:S(2)}, u32[]{:S(2)}) collective-permute-start(bf16[8,16,4,128]{3,2,1,0:T(4,128)(2,1)S(1)} %reshape.365), channel_id=1, source_target_pairs={{0,30},{2,0},{4,2},{6,4},{8,6},{10,8},{12,10},{14,12},{16,14},{18,... | collective-permute-start | bytes 393224 | tf_op jit(solution)/shard_map/ppermute | solution.py:43
  149.3 22.6 %collective-permute-start.25 = (bf16[8,16,4,128]{3,2,1,0:T(4,128)(2,1)S(1)}, bf16[8,16,4,128]{3,2,1,0:T(4,128)(2,1)S(1)}, u32[]{:S(2)}, u32[]{:S(2)}) collective-permute-start(bf16[8,16,4,128]{3,2,1,0:T(4,128)(2,1)S(1)} %broadcast_select_fusion.5), channel_id=1, source_target_pairs={{0,30},{2,0},{4,2},{6,4},{8,6},{10,8},{12,10},{14,12},{16,14},{18,... | collective-permute-start | bytes 393224 | tf_op jit(solution)/shard_map/ppermute | solution.py:43
  173.8 6.9 %collective-permute-start.26 = (bf16[8,16,4,128]{3,2,1,0:T(4,128)(2,1)S(1)}, bf16[8,16,4,128]{3,2,1,0:T(4,128)(2,1)S(1)}, u32[]{:S(2)}, u32[]{:S(2)}) collective-permute-start(bf16[8,16,4,128]{3,2,1,0:T(4,128)(2,1)S(1)} %pad_maximum_fusion.29), channel_id=1, source_target_pairs={{1,0},{3,2},{5,4},{7,6},{9,8},{11,10},{13,12},{15,14},{17,16},{19,... | collective-permute-start | bytes 393224 | tf_op jit(solution)/shard_map/ppermute | solution.py:33
  194.0 6.0 %collective-permute-start.35 = (bf16[10,1,512]{2,1,0:T(2,128)(2,1)S(1)}, bf16[10,1,512]{2,1,0:T(2,128)(2,1)S(1)}, u32[]{:S(2)}, u32[]{:S(2)}) collective-permute-start(bf16[10,1,512]{2,1,0:T(2,128)(2,1)S(1)} %get-tuple-element.108), channel_id=1, source_target_pairs={{0,1},{2,3},{4,5},{6,7},{8,9},{10,11},{12,13},{14,15},{16,17},{18,... | collective-permute-start | bytes 30728 | tf_op jit(solution)/shard_map/ppermute | solution.py:22
  200.6 21.2 %collective-permute-start.38 = (bf16[8,1,512]{2,1,0:T(2,128)(2,1)S(1)}, bf16[8,1,512]{2,1,0:T(2,128)(2,1)S(1)}, u32[]{:S(2)}, u32[]{:S(2)}) collective-permute-start(bf16[8,1,512]{2,1,0:T(2,128)(2,1)S(1)} %slice.1125), channel_id=1, source_target_pairs={{1,0},{3,2},{5,4},{7,6},{9,8},{11,10},{13,12},{15,14},{17,16},{19,... | collective-permute-start | bytes 24584 | tf_op jit(solution)/shard_map/ppermute | solution.py:33
  217.1 9.0 %collective-permute-start.36 = (bf16[1,16,512]{2,1,0:T(8,128)(2,1)S(1)}, bf16[1,16,512]{2,1,0:T(8,128)(2,1)S(1)}, u32[]{:S(2)}, u32[]{:S(2)}) collective-permute-start(bf16[1,16,512]{2,1,0:T(8,128)(2,1)S(1)} %slice.1122), channel_id=1, source_target_pairs={{0,30},{2,0},{4,2},{6,4},{8,6},{10,8},{12,10},{14,12},{16,14},{18,... | collective-permute-start | bytes 49160 | tf_op jit(solution)/shard_map/ppermute | solution.py:43
  241.9 8.8 %collective-permute-start.43 = (bf16[8,16,4,128]{3,2,1,0:T(4,128)(2,1)S(1)}, bf16[8,16,4,128]{3,2,1,0:T(4,128)(2,1)S(1)}, u32[]{:S(2)}, u32[]{:S(2)}) collective-permute-start(bf16[8,16,4,128]{3,2,1,0:T(4,128)(2,1)S(1)} %broadcast_select_fusion.8), channel_id=1, source_target_pairs={{0,30},{2,0},{4,2},{6,4},{8,6},{10,8},{12,10},{14,12},{16,14},{18,... | collective-permute-start | bytes 393224 | tf_op jit(solution)/shard_map/ppermute | solution.py:43
  252.6 6.9 %collective-permute-start.44 = (bf16[8,16,4,128]{3,2,1,0:T(4,128)(2,1)S(1)}, bf16[8,16,4,128]{3,2,1,0:T(4,128)(2,1)S(1)}, u32[]{:S(2)}, u32[]{:S(2)}) collective-permute-start(bf16[8,16,4,128]{3,2,1,0:T(4,128)(2,1)S(1)} %pad_maximum_fusion.31), channel_id=1, source_target_pairs={{1,0},{3,2},{5,4},{7,6},{9,8},{11,10},{13,12},{15,14},{17,16},{19,... | collective-permute-start | bytes 393224 | tf_op jit(solution)/shard_map/ppermute | solution.py:33
  262.7 117.5 %reduce-scatter.5.cloned.1.call-start = ((), (), s32[]{:S(2)}) async-start(), calls=%async_computation.4 | async-start | bytes 1114112 | tf_op jit(solution)/shard_map/reduce_scatter | solution.py:181
  272.0 8.7 %collective-permute-start.50 = (bf16[1,16,512]{2,1,0:T(8,128)(2,1)}, bf16[1,16,512]{2,1,0:T(8,128)(2,1)}, u32[]{:S(2)}, u32[]{:S(2)}) collective-permute-start(bf16[1,16,512]{2,1,0:T(8,128)(2,1)} %get-tuple-element.125), channel_id=1, source_target_pairs={{0,2},{2,4},{4,6},{6,8},{8,10},{10,12},{12,14},{14,16},{16,18},{18... | collective-permute-start | bytes 49160 | tf_op jit(solution)/shard_map/ppermute | solution.py:22
  272.0 8.7 %collective-permute-start.51 = (bf16[1,16,512]{2,1,0:T(8,128)(2,1)}, bf16[1,16,512]{2,1,0:T(8,128)(2,1)}, u32[]{:S(2)}, u32[]{:S(2)}) collective-permute-start(bf16[1,16,512]{2,1,0:T(8,128)(2,1)} %get-tuple-element.126), channel_id=1, source_target_pairs={{2,0},{4,2},{6,4},{8,6},{10,8},{12,10},{14,12},{16,14},{18,16},{20... | collective-permute-start | bytes 49160 | tf_op jit(solution)/shard_map/ppermute | solution.py:25
  278.1 113.2 %reduce-scatter.11.cloned.1.call-start = ((), (), s32[]{:S(2)}) async-start(), calls=%async_computation.7 | async-start | bytes 98304 | tf_op jit(solution)/shard_map/reduce_scatter | solution.py:192
  281.5 79.1 %collective-permute-start.52 = (bf16[10,1,512]{2,1,0:T(2,128)(2,1)S(1)}, bf16[10,1,512]{2,1,0:T(2,128)(2,1)S(1)}, u32[]{:S(2)}, u32[]{:S(2)}) collective-permute-start(bf16[10,1,512]{2,1,0:T(2,128)(2,1)S(1)} %get-tuple-element.103), channel_id=1, source_target_pairs={{1,0},{3,2},{5,4},{7,6},{9,8},{11,10},{13,12},{15,14},{17,16},{19,... | collective-permute-start | bytes 30728 | tf_op jit(solution)/shard_map/ppermute | solution.py:25
  282.8 77.8 %collective-permute-start.53 = (bf16[10,1,512]{2,1,0:T(2,128)(2,1)S(1)}, bf16[10,1,512]{2,1,0:T(2,128)(2,1)S(1)}, u32[]{:S(2)}, u32[]{:S(2)}) collective-permute-start(bf16[10,1,512]{2,1,0:T(2,128)(2,1)S(1)} %get-tuple-element.104), channel_id=1, source_target_pairs={{0,1},{2,3},{4,5},{6,7},{8,9},{10,11},{12,13},{14,15},{16,17},{18,... | collective-permute-start | bytes 30728 | tf_op jit(solution)/shard_map/ppermute | solution.py:22
  319.7 83.6 %reduce-scatter.7.cloned.1.call-start = ((), (), s32[]{:S(2)}) async-start(), calls=%async_computation.5 | async-start | bytes 98304 | tf_op jit(solution)/shard_map/reduce_scatter | solution.py:189
  (113 other events, 3529.2 us)
Sparse Core Ops, SparseCore 0:
  262.8 56.8 reduce-scatter.8
  323.7 56.4 reduce-scatter.4
  382.4 8.9 reduce-scatter.10
  393.4 9.8 reduce-scatter.6
where the time goes:
time: 413 us; the launch traced here: 411 us
  waiting for transfers between devices  142 us (34%)
  starting transfers between devices  105 us (25%)
  between operations  61.7 us (15%)
  blocking collectives  40.8 us (10%)
  other arithmetic  30.9 us (7%)
  matrix products  16.1 us (4%)
  local copies, waits for them, and re-layouts  14.8 us (4%)
    psum x1, blocking collectives, local(): total_kernel, total_gain = lax.psum((acc_kernel, acc_gain), ('lon', 'lat'))  40.8 us
    ppermute x18, starting transfers between devices, passed_along(): return lax.ppermute(value, axis, pairs)  38 us
    ppermute x18, waiting for transfers between devices, passed_along(): return lax.ppermute(value, axis, pairs)  36.4 us
    reduce_scatter x1, waiting for transfers between devices, local(): lax.psum_scatter(acc_down.astype(jnp.bfloat16), 'lon', scatter_dimension=...  32.3 us
    ppermute x12, starting transfers between devices, with_halo(): lax.ppermute(lax.slice_in_dim(block, 0, width, axis=dim), axis, backward)  30.5 us
    ppermute x12, waiting for transfers between devices, shifted(): lax.ppermute(value, axis, [(source, source + steps) for source in range(f...  25.2 us
    ppermute x12, starting transfers between devices, with_halo(): lax.ppermute(lax.slice_in_dim(block, block.shape[dim] - width, None, axis...  22.8 us
    reduce_scatter x1, waiting for transfers between devices, local(): lax.psum_scatter(acc_up.astype(jnp.bfloat16), 'lon', scatter_dimension=0,...  18.7 us
  transfers between devices with their start and end apart: 58, of which 26 were waited for; matrix products, arithmetic and copies ran while one was open for 9% of the time, Pallas kernels for 0%

commit v1 on v0

v1 whole, which is shorter than its diff:
```python
import functools

import jax
import jax.numpy as jnp
from jax import lax
from jax.experimental import pallas as pl
from jax.experimental.pallas import tpu as pltpu
from jax.sharding import PartitionSpec as P

EPSILON = 1e-06
AXES = ("lon", "lat")
ROWS = 16
LAT_REACH = 2
VMEM_LIMIT = 40 * 1024 * 1024


def with_halo(block, sides, width, periodic):
    for axis, dim in sides:
        count = lax.axis_size(axis)
        forward = [(i, i + 1) for i in range(count - 1)]
        if periodic:
            forward.append((count - 1, 0))
        backward = [(target, source) for source, target in forward]
        low = lax.ppermute(
            lax.slice_in_dim(block, block.shape[dim] - width, None, axis=dim), axis, forward
        )
        high = lax.ppermute(lax.slice_in_dim(block, 0, width, axis=dim), axis, backward)
        block = jnp.concatenate([low, block, high], axis=dim)
    return block


def pieces_of(value, count):
    parts = []
    for _ in range(count):
        part = lax.reduce_precision(value, 8, 7)
        parts.append(part.astype(jnp.bfloat16))
        value = value - part
    return parts


def exchanged(blocks):
    return lax.all_to_all(blocks, AXES, split_axis=0, concat_axis=0, tiled=True)


def call(kernel, out_shape, *operands, scratch=(), scalars=0, flops=0, moved=0):
    space = [pltpu.SMEM] * scalars + [pltpu.VMEM] * (len(operands) - scalars)
    return pl.pallas_call(
        kernel,
        out_shape=out_shape,
        in_specs=[pl.BlockSpec(memory_space=kind) for kind in space],
        out_specs=jax.tree.map(lambda _: pl.BlockSpec(memory_space=pltpu.VMEM), out_shape),
        scratch_shapes=scratch,
        compiler_params=pltpu.CompilerParams(vmem_limit_bytes=VMEM_LIMIT),
        cost_estimate=pl.CostEstimate(flops=flops, bytes_accessed=moved, transcendentals=0),
    )(*operands)


def forward_kernel(padded_ref, kernel_ref, gain_ref, up_ref, n_ref, normed_ref, inv_ref, hid_ref, slope_ref):
    rows_out, cols_out = padded_ref.shape[1] - 2, padded_ref.shape[2] - 2
    channels = padded_ref.shape[3]
    padded = padded_ref[0].astype(jnp.float32)
    mixed = padded[1 : 1 + rows_out, 1 : 1 + cols_out]
    running = jnp.zeros_like(mixed)
    for col_tap in range(3):
        shifted_cols = padded[:, col_tap : col_tap + cols_out]
        for row_tap in range(3):
            tap = kernel_ref[3 * row_tap + col_tap : 3 * row_tap + col_tap + 1]
            running = running + tap[None] * shifted_cols[row_tap : row_tap + rows_out]
    mixed = (mixed + running).reshape(rows_out * cols_out, channels).T
    inv_root = lax.rsqrt(jnp.mean(mixed * mixed, axis=0, keepdims=True) + EPSILON)
    normed = mixed * inv_root
    narrow = (normed * gain_ref[...]).astype(jnp.bfloat16)
    pre = jnp.dot(up_ref[...], narrow, preferred_element_type=jnp.float32)
    sigmoid = jax.nn.sigmoid(pre)
    n_ref[0] = narrow
    normed_ref[0] = normed
    inv_ref[0] = inv_root
    hid_ref[0] = (pre * sigmoid).astype(jnp.bfloat16)
    slope_ref[0] = sigmoid * (1.0 + pre * (1.0 - sigmoid))


def forward_parts(padded, kernel, gain, w_up_t):
    steps, rows_in, cols_in, channels = padded.shape
    hid = w_up_t.shape[0]
    count = (rows_in - 2) * (cols_in - 2)
    whole = lambda *shape: pl.BlockSpec(shape, lambda s: (0,) * len(shape))
    one = lambda *shape: pl.BlockSpec((1, *shape), lambda s: (steps - 1 - s, *([0] * len(shape))))
    sds = jax.ShapeDtypeStruct
    return pl.pallas_call(
        forward_kernel,
        grid=(steps,),
        in_specs=[one(rows_in, cols_in, channels), whole(9, channels), whole(channels, 1), whole(hid, channels)],
        out_specs=[one(channels, count), one(channels, count), one(1, count), one(hid, count), one(hid, count)],
        out_shape=[
            sds((steps, channels, count), jnp.bfloat16),
            sds((steps, channels, count), jnp.float32),
            sds((steps, 1, count), jnp.float32),
            sds((steps, hid, count), jnp.bfloat16),
            sds((steps, hid, count), jnp.float32),
        ],
        compiler_params=pltpu.CompilerParams(vmem_limit_bytes=VMEM_LIMIT),
        cost_estimate=pl.CostEstimate(
            flops=2 * steps * count * hid * channels, bytes_accessed=6 * 2**20, transcendentals=0
        ),
    )(padded, kernel.reshape(9, channels), gain, w_up_t)


def network_kernel(moved_ref, down_ref, up_ref, slope_ref, normed_ref, inv_ref, gain_ref, field_ref, grad_ref, term_ref):
    moved = moved_ref[...]
    grad_hidden = jnp.dot(down_ref[...], moved, preferred_element_type=jnp.float32)
    grad_pre = (grad_hidden * slope_ref[...]).astype(jnp.bfloat16)
    grad_ref[...] = grad_pre
    grad_n = jnp.dot(up_ref[...], grad_pre, preferred_element_type=jnp.float32)
    normed = normed_ref[...]
    term = grad_n * normed
    term_ref[...] = term
    gain = gain_ref[...]
    mean = jnp.mean(term * gain, axis=0, keepdims=True)
    field = moved.astype(jnp.float32) + inv_ref[...] * (grad_n * gain - normed * mean)
    field_ref[...] = field.astype(jnp.bfloat16)


def network_back(moved, w_down_t, w_up, slope, normed, inv_root, gain):
    channels, count = moved.shape
    hid = w_down_t.shape[0]
    sds = jax.ShapeDtypeStruct
    return call(
        network_kernel,
        [
            sds((channels, count), jnp.bfloat16),
            sds((hid, count), jnp.bfloat16),
            sds((channels, count), jnp.float32),
        ],
        moved,
        w_down_t,
        w_up,
        slope,
        normed,
        inv_root,
        gain,
        flops=4 * count * hid * channels,
        moved=4 * 2**20,
    )


def spatial_kernel(mode, near_lon, near_lat, *refs):
    refs = list(refs)
    take = lambda: refs.pop(0)
    with_move, with_stencil = mode != "last", mode != "first"
    move_ref = take() if with_move else None
    in_ref = take()
    state_ref, kern_ref = (take(), take()) if with_stencil else (None, None)
    weight_ref = take() if with_move else None
    out_ref = take()
    term_ref = take() if with_stencil else None
    high_ref, own_ref, low_ref, spread_ref = take(), take(), take(), take()
    tiles_lon, tiles_lat, rows, lanes = in_ref.shape
    lane = lax.broadcasted_iota(jnp.int32, (rows, lanes), 1)
    col = lax.rem(lane, near_lat)
    unroll = 16 if tiles_lon * tiles_lat <= 32 else 1
    zero = jnp.zeros((rows, lanes), jnp.float32)

    def turn(value, steps):
        return pltpu.roll(value, steps % lanes, 1) if isinstance(steps, int) else pltpu.roll(value, steps, 1)

    def lat_after(tiles):
        following = tiles[1:] + [None]
        return [
            jnp.where(col < near_lat - 1, turn(here, -1), 0.0 if after is None else turn(after, near_lat - 1))
            for here, after in zip(tiles, following)
        ]

    def lat_before(tiles):
        preceding = [None] + tiles[:-1]
        return [
            jnp.where(col > 0, turn(here, 1), 0.0 if before is None else turn(before, 1 - near_lat))
            for here, before in zip(tiles, preceding)
        ]

    def lon_after(here, after):
        return turn(jnp.where(lane < near_lat, after, here), -near_lat)

    def lon_before(here, before):
        return turn(jnp.where(lane >= lanes - near_lat, before, here), near_lat)

    def next_tile(a):
        return lax.rem(a + 1, tiles_lon)

    def last_tile(a):
        return lax.rem(a + tiles_lon - 1, tiles_lon)

    def read(ref, a):
        return [ref[a, b].astype(jnp.float32) for b in range(tiles_lat)]

    def loop(body, init=None):
        return lax.fori_loop(0, tiles_lon, body, init, unroll=unroll)

    if with_stencil:
        taps = [[kern_ref[3 * a + b] for b in range(3)] for a in range(3)]

        def mix(a, sums):
            here = read(in_ref, a)
            by_col = [lat_after(here), here, lat_before(here)]
            state, state_next, state_last = (read(state_ref, k) for k in (a, next_tile(a), last_tile(a)))
            sums = list(sums)
            for b in range(tiles_lat):
                by_row = [
                    lon_before(state[b], state_last[b]),
                    state[b],
                    lon_after(state[b], state_next[b]),
                ]
                mixes = []
                for row in range(3):
                    mixed = None
                    for c in range(3):
                        shifted = by_col[c][b]
                        sums[3 * row + c] = sums[3 * row + c] + by_row[row] * shifted
                        term = taps[row][c] * shifted
                        mixed = term if mixed is None else mixed + term
                    mixes.append(mixed)
                high_ref[a, b] = mixes[0]
                own_ref[a, b] = here[b] + mixes[1]
                low_ref[a, b] = mixes[2]
            return tuple(sums)

        sums = loop(mix, tuple(zero for _ in range(9)))
        for k in range(9):
            term_ref[k] = sums[k]

    def gather(a):
        if not with_stencil:
            return read(in_ref, a)
        result = []
        for b in range(tiles_lat):
            value = own_ref[a, b] + lon_after(high_ref[a, b], high_ref[next_tile(a), b])
            value = value + lon_before(low_ref[a, b], low_ref[last_tile(a), b])
            result.append(value)
        return result

    if not with_move:

        def finish(a, carry):
            for b, value in enumerate(gather(a)):
                out_ref[a, b] = value.astype(jnp.bfloat16)
            return carry

        loop(finish)
        return

    own2_ref, lon2_ref = refs

    def weigh(a, carry):
        here = [value.astype(jnp.bfloat16).astype(jnp.float32) for value in gather(a)]
        weights = [
            [weight_ref[a, b, k : k + 1].astype(jnp.float32) + weight_ref[a, b, 4 + k : 5 + k].astype(jnp.float32) for k in range(4)]
            for b in range(tiles_lat)
        ]
        own = lat_after([weights[b][2] * here[b] for b in range(tiles_lat)])
        lon = lat_after([weights[b][3] * here[b] for b in range(tiles_lat)])
        for b in range(tiles_lat):
            own2_ref[a, b] = weights[b][0] * here[b] + own[b]
            lon2_ref[a, b] = weights[b][1] * here[b] + lon[b]
        return carry

    loop(weigh)

    def spread(a, carry):
        for b in range(tiles_lat):
            value = own2_ref[a, b] + lon_after(lon2_ref[a, b], lon2_ref[next_tile(a), b])
            spread_ref[a, b] = value.astype(jnp.bfloat16).astype(jnp.float32)
        for b in range(LAT_REACH):
            spread_ref[a, tiles_lat + b] = zero
        return carry

    loop(spread)

    lon_move, lat_move = move_ref[0], move_ref[1]
    far_lon, off_lon = lon_move // near_lon, lax.rem(lon_move, near_lon)
    far_lat, off_lat = lat_move // near_lat, lax.rem(lat_move, near_lat)
    shift = off_lon * near_lat + off_lat
    turn_here = lax.rem(2 * lanes - shift, lanes)
    turn_next = lax.rem(2 * lanes - shift + near_lat, lanes)
    same_lon = lane >= off_lon * near_lat
    same_lat = col + off_lat < near_lat

    def move(a, carry):
        source = lax.rem(a + far_lon, tiles_lon)
        source_next = next_tile(source)
        for b in range(tiles_lat):
            here, after = (
                jnp.where(same_lon, spread_ref[source, far_lat + k], spread_ref[source_next, far_lat + k])
                for k in (b, b + 1)
            )
            value = jnp.where(same_lat, turn(here, turn_here), turn(after, turn_next))
            out_ref[a, b] = value.astype(jnp.bfloat16)
        return carry

    loop(move)


def spatial(mode, tile, field, state, kern, weights, moves):
    shape = field.shape
    tiles_lon, tiles_lat, rows, lanes = shape
    with_move, with_stencil = mode != "last", mode != "first"
    operands = ([moves] if with_move else []) + [field]
    operands += [state, kern] if with_stencil else []
    operands += [weights] if with_move else []
    sds = jax.ShapeDtypeStruct
    out = [sds(shape, jnp.bfloat16)]
    if with_stencil:
        out.append(sds((9, rows, lanes), jnp.float32))
    grid = pltpu.VMEM(shape, jnp.float32)
    scratch = [grid, grid, grid, pltpu.VMEM((tiles_lon, tiles_lat + LAT_REACH, rows, lanes), jnp.float32)]
    if with_move:
        scratch += [grid, grid]
    return call(
        functools.partial(spatial_kernel, mode, *tile),
        out,
        *operands,
        scratch=scratch,
        scalars=1 if with_move else 0,
        flops=2**22,
        moved=2**20,
    )


def halved(value, axis, bit, dim):
    count = lax.axis_size(axis)
    mine = lax.axis_index(axis) >> bit & 1
    kept = lax.dynamic_index_in_dim(value, mine, dim, keepdims=False)
    sent = lax.dynamic_index_in_dim(value, 1 - mine, dim, keepdims=False).astype(jnp.bfloat16)
    arrived = lax.ppermute(sent, axis, [(i, i ^ (1 << bit)) for i in range(count)])
    return kept + arrived.astype(jnp.float32)


def scattered(value, lat_first):
    channels, hid = value.shape
    lon_bits = lax.axis_size("lon").bit_length() - 1
    lat_bits = lax.axis_size("lat").bit_length() - 1
    rows = channels >> lon_bits
    value = value.reshape(*([2] * lon_bits), rows, *([2] * lat_bits), hid >> lat_bits)

    def over_lon(value, bit, left):
        return halved(value, "lon", bit, left.index(bit)), [k for k in left if k != bit]

    left_lon = list(range(lon_bits))[::-1]
    left_lat = list(range(lat_bits))[::-1]
    order = [("lon", 0), ("lon", 1)] + [("lat", k) for k in range(lat_bits)]
    if lat_first:
        order = [("lon", 0)] + [("lat", k) for k in range(lat_bits)] + [("lon", 1)]
    order += [("lon", k) for k in range(2, lon_bits)]
    for axis, bit in order:
        if axis == "lon":
            value, left_lon = over_lon(value, bit, left_lon)
        else:
            value = halved(value, "lat", bit, len(left_lon) + 1 + left_lat.index(bit))
            left_lat.remove(bit)
    return value


def local(cotangent, states, w_up, w_down, norm_gain, kernel, bilinear, lon_move, lat_move):
    steps, rows_out, cols_out, channels = states.shape
    tiles_lon, tiles_lat = lax.axis_size("lon"), lax.axis_size("lat")
    devices = tiles_lon * tiles_lat
    count = rows_out * cols_out
    tile = (rows_out, cols_out)
    share = channels // devices
    padded_share = -(-share // ROWS) * ROWS
    group_size = channels // lon_move.shape[1]
    me = lax.axis_index("lon") * tiles_lat + lax.axis_index("lat")

    def as_blocks(value):
        value = value.reshape(devices, share, count)
        if padded_share != share:
            value = jnp.pad(value, ((0, 0), (0, padded_share - share), (0, 0)))
        return value

    def as_rows(blocks):
        return blocks[:, :share].reshape(channels, count)

    def as_grid(blocks):
        return blocks.reshape(tiles_lon, tiles_lat, *blocks.shape[1:])

    weight_rows = pieces_of(bilinear.reshape(steps, 4, count), 2)
    weight_rows = jnp.concatenate(weight_rows, axis=1)

    def to_all(value):
        padding = -value.shape[0] % ROWS
        value = jnp.pad(value, ((0, padding), (0, 0)))
        return jnp.broadcast_to(value[None], (devices, *value.shape))

    blocks = as_blocks(cotangent.reshape(count, channels).T)
    arrived = exchanged(jnp.concatenate([blocks, to_all(weight_rows[steps - 1])], axis=1))
    grid_now = as_grid(arrived[:, :padded_share])
    weights = {steps - 1: as_grid(arrived[:, padded_share:])}

    state_blocks = [as_blocks(states[s].reshape(count, channels).T) for s in range(steps)]
    rest = [to_all(weight_rows[s]) for s in range(steps - 1)]
    arrived = exchanged(jnp.concatenate(state_blocks + rest, axis=1))
    grid_states = [as_grid(arrived[:, padded_share * s : padded_share * (s + 1)]) for s in range(steps)]
    for s in range(steps - 1):
        start = padded_share * steps + ROWS * s
        weights[s] = as_grid(arrived[:, start : start + ROWS])

    kern = lax.dynamic_slice_in_dim(kernel.reshape(9, channels), me * share, share, 1)
    kern = jnp.pad(kern, ((0, 0), (0, padded_share - share)))
    kern = jnp.broadcast_to(kern[:, :, None], (9, padded_share, count))
    group = me * share // group_size
    moves = jnp.stack([lon_move[:, group], lat_move[:, group]], axis=1)

    padded = with_halo(with_halo(states, (("lon", 1),), 1, True), (("lat", 2),), 1, False)
    gain = norm_gain[:, None]
    narrow, normed, inv_root, hidden, slope = forward_parts(padded, kernel, gain, w_up.T)
    w_down_t = w_down.T

    (grid_now,) = spatial("first", tile, grid_now, None, None, weights[steps - 1], moves[steps - 1])
    lanes_both = (((1,), (1,)), ((), ()))
    acc_up = acc_down = 0.0
    acc_gain = 0.0
    acc_kernel = 0.0
    for s in reversed(range(steps)):
        moved = as_rows(exchanged(grid_now.reshape(devices, padded_share, count)))
        field, grad_pre, term = network_back(moved, w_down_t, w_up, slope[s], normed[s], inv_root[s], gain)
        acc_up = acc_up + lax.dot_general(narrow[s], grad_pre, lanes_both, preferred_element_type=jnp.float32)
        acc_down = acc_down + lax.dot_general(moved, hidden[s], lanes_both, preferred_element_type=jnp.float32)
        acc_gain = acc_gain + term
        blocks = as_blocks(field)
        if s > 0:
            arrived = exchanged(blocks)
            grid_now, term = spatial(
                "mid", tile, as_grid(arrived), grid_states[s], kern, weights[s - 1], moves[s - 1]
            )
        else:
            sums = pieces_of(jnp.sum(acc_gain, axis=1, keepdims=True), 3)
            sums = jnp.pad(jnp.concatenate(sums, axis=1), ((0, 0), (0, count - 3)))
            arrived = exchanged(jnp.concatenate([blocks, as_blocks(sums)], axis=1))
            grid_now, term = spatial(
                "last", tile, as_grid(arrived[:, :padded_share]), grid_states[s], kern, None, None
            )
            total_gain = jnp.sum(arrived[:, padded_share:, :3].astype(jnp.float32), axis=(0, 2))
        acc_kernel = acc_kernel + term

    sums = jnp.concatenate([jnp.sum(acc_kernel, axis=2), total_gain[None]], axis=0)
    sums = jnp.concatenate(pieces_of(sums, 3), axis=0).T
    sums = jnp.pad(sums, ((0, 0), (0, count - sums.shape[1])))
    sums = jnp.broadcast_to(sums[None], (devices, padded_share, count))
    blocks = grid_now.reshape(devices, padded_share, count)
    arrived = exchanged(jnp.concatenate([blocks, sums], axis=1))
    grad_state = as_rows(arrived[:, :padded_share]).T.reshape(rows_out, cols_out, channels)
    sums = as_rows(arrived[:, padded_share:])[:, :30].astype(jnp.float32)
    sums = (sums[:, :10] + sums[:, 10:20] + sums[:, 20:30]).T
    grad_kernel = sums[:9].reshape(kernel.shape)
    return (grad_state, scattered(acc_up, False), scattered(acc_down, True), grad_kernel, sums[9])


def solution(mesh):
    placed = (
        P("lon", "lat", None),
        P(None, "lon", "lat", None),
        P(),
        P(),
        P(),
        P(),
        P(None, None, "lon", "lat"),
        P(),
        P(),
    )
    return jax.shard_map(
        local,
        mesh=mesh,
        in_specs=placed,
        out_specs=(P("lon", "lat", None), P("lon", "lat"), P("lon", "lat"), P(), P()),
        check_vma=False,
    )
```

time: 413 us -> 189 us (0.46)
  waiting for transfers between devices: 142 us -> 42 us
  between operations: 61.7 us -> 1.44 us
  starting transfers between devices: 105 us -> 62.3 us
  blocking collectives: 40.8 us -> 0 us
  local copies, waits for them, and re-layouts: 14.8 us -> 42.5 us
  other arithmetic: 30.9 us -> 7.24 us
  Pallas kernels: 0 us -> 15.2 us
    reduce_scatter x4 -> x0, waiting for transfers between devices: 71 us -> none  [the longest x1 32.3 us: local(): lax.psum_scatter(acc_down.astype(jnp.bfloat16), 'lon', scatter_dimension=...]
    ppermute x30 -> x10, waiting for transfers between devices: 61.6 us -> 11.7 us  [halved(): lax.ppermute(sent, axis, [(i, i ^ 1 << bit) for i in range(count)])]
    psum x1 -> x0, blocking collectives: 40.8 us -> none  [local(): total_kernel, total_gain = lax.psum((acc_kernel, acc_gain), ('lon', 'lat'))]
    ppermute x30 -> x10, starting transfers between devices: 51.8 us -> 13.2 us  [halved(): lax.ppermute(sent, axis, [(i, i ^ 1 << bit) for i in range(count)])]
    all_to_all x0 -> x9, starting transfers between devices: none -> 37.7 us  [exchanged(): return lax.all_to_all(blocks, AXES, split_axis=0, concat_axis=0, tiled=True)]
    all_to_all x0 -> x9, waiting for transfers between devices: none -> 29.7 us  [exchanged(): return lax.all_to_all(blocks, AXES, split_axis=0, concat_axis=0, tiled=True)]
    ppermute x12 -> x2, starting transfers between devices: 30.5 us -> 5.47 us  [with_halo(): lax.ppermute(lax.slice_in_dim(block, 0, width, axis=dim), axis, backward)]
    ppermute x12 -> x2, starting transfers between devices: 22.8 us -> 6.05 us  [with_halo(): lax.ppermute(lax.slice_in_dim(block, block.shape[dim] - width, None, axis...]
  transfers between devices with their start and end apart: 58 -> 23, of which waited for: 26 -> 10; matrix products, arithmetic and copies ran while one was open for 9% -> 28% of each run, Pallas kernels for 0% -> 3%
where the time goes in v1:
time: 189 us; the launch traced here: 188 us
  starting transfers between devices  62.3 us (33%)
  local copies, waits for them, and re-layouts  42.5 us (22%)
  waiting for transfers between devices  42 us (22%)
  matrix products  17.5 us (9%)
  Pallas kernels  15.2 us (8%)
  other arithmetic  7.24 us (4%)
    all_to_all x9, starting transfers between devices, exchanged(): return lax.all_to_all(blocks, AXES, split_axis=0, concat_axis=0, tiled=True)  37.7 us
    all_to_all x9, waiting for transfers between devices, exchanged(): return lax.all_to_all(blocks, AXES, split_axis=0, concat_axis=0, tiled=True)  29.7 us
    unnamed x93, local copies, waits for them, and re-layouts  16.9 us
    ppermute x10, starting transfers between devices, halved(): lax.ppermute(sent, axis, [(i, i ^ 1 << bit) for i in range(count)])  13.2 us
    pallas_call x7, Pallas kernels, call(): pl.pallas_call(kernel, out_shape=out_shape, in_specs=[pl.BlockSpec(memory...  12.4 us
    ppermute x10, waiting for transfers between devices, halved(): lax.ppermute(sent, axis, [(i, i ^ 1 << bit) for i in range(count)])  11.7 us
    dot_general x3, matrix products, local(): lax.dot_general(narrow[s], grad_pre, lanes_both, preferred_element_type=j...  9.28 us
    dot_general x3, matrix products, local(): lax.dot_general(moved, hidden[s], lanes_both, preferred_element_type=jnp....  8.2 us
  transfers between devices with their start and end apart: 23, of which 10 were waited for; matrix products, arithmetic and copies ran while one was open for 28% of the time, Pallas kernels for 3%

profile of v1, /device:TPU:0, one launch (start us, length us, event | category | flops | bytes accessed | tf_op | source)
XLA Modules:
  0.0 188.2 jit_solution(13712701411983820655)
XLA Ops:
  3.4 7.3 %all-to-all-start = ((bf16[32,32,128]{2,1,0:T(8,128)(2,1)}), bf16[32,32,128]{2,1,0:T(8,128)(2,1)S(1)}, u32[]{:S(2)}, u32[]{:S(2)}) async-start(bf16[32,32,128]{2,1,0:T(8,128)(2,1)} %pad_maximum_fusion.1), calls=%async_computation | async-start | bytes 524288 | tf_op jit(solution)/shard_map/all_to_all | solution.py:42
  11.9 4.2 %collective-permute-start.1 = (bf16[3,1,16,512]{3,2,1,0:T(8,128)(2,1)S(1)}, bf16[3,1,16,512]{3,2,1,0:T(8,128)(2,1)S(1)}, u32[]{:S(2)}, u32[]{:S(2)}) collective-permute-start(bf16[3,1,16,512]{3,2,1,0:T(8,128)(2,1)S(1)} %get-tuple-element.61), channel_id=1, source_target_pairs={{2,0},{4,2},{6,4},{8,6},{10,8},{12,10},{14,12},{16,14},{18,16},{20... | collective-permute-start | bytes 147464 | tf_op jit(solution)/shard_map/ppermute | solution.py:27
  23.5 3.1 %all-to-all-start.1 = ((bf16[32,16,128]{2,1,0:T(8,128)(2,1)}), bf16[32,16,128]{2,1,0:T(8,128)(2,1)S(1)}, u32[]{:S(2)}, u32[]{:S(2)}) async-start(bf16[32,16,128]{2,1,0:T(8,128)(2,1)} %bitcast.9), calls=%async_computation.1 | async-start | bytes 262144 | tf_op jit(solution)/shard_map/all_to_all | solution.py:42
  26.8 8.5 %all-to-all-done.1 = bf16[32,16,128]{2,1,0:T(8,128)(2,1)S(1)} async-done(((bf16[32,16,128]{2,1,0:T(8,128)(2,1)}), bf16[32,16,128]{2,1,0:T(8,128)(2,1)S(1)}, u32[]{:S(2)}, u32[]{:S(2)}) %all-to-all-start.1) | async-done | bytes 131104 | tf_op jit(solution)/shard_map/all_to_all | solution.py:42
  35.3 3.3 %all-to-all-start.3 = ((bf16[32,80,128]{2,1,0:T(8,128)(2,1)}), bf16[32,80,128]{2,1,0:T(8,128)(2,1)}, u32[]{:S(2)}, u32[]{:S(2)}) async-start(bf16[32,80,128]{2,1,0:T(8,128)(2,1)} %broadcast_dynamic-update-slice_fusion), calls=%async_computation.3 | async-start | bytes 1310720 | tf_op jit(solution)/shard_map/all_to_all | solution.py:42
  40.6 5.8 %collective-permute-start.2 = (bf16[3,10,1,512]{3,2,1,0:T(2,128)(2,1)}, bf16[3,10,1,512]{3,2,1,0:T(2,128)(2,1)}, u32[]{:S(2)}, u32[]{:S(2)}) collective-permute-start(bf16[3,10,1,512]{3,2,1,0:T(2,128)(2,1)} %get-tuple-element.56), channel_id=1, source_target_pairs={{0,1},{2,3},{4,5},{6,7},{8,9},{10,11},{12,13},{14,15},{16,17},{18,... | collective-permute-start | bytes 92168 | tf_op jit(solution)/shard_map/ppermute | solution.py:24
  50.6 2.8 %shard_map.129 = (bf16[3,512,128]{2,1,0:T(8,128)(2,1)S(1)}, f32[3,512,128]{2,1,0:T(8,128)S(1)}, f32[3,1,128]{2,1,0:T(1,128)S(1)}, bf16[3,1024,128]{2,1,0:T(8,128)(2,1)S(1)}, f32[3,1024,128]{2,1,0:T(8,128)S(1)}) custom-call(bf16[3,10,18,512]{3,2,1,0:T(8,128)(2,1)S(1)} %pad_maximum_fusion.padded_ref, f32[9,512]{1,0:T(8,128)S(1)} %copy-done.19, ...), custom_call_target="tpu_custom_call" | custom-call | flops 402653184 | bytes 6291456 | tf_op jit(solution)/shard_map/pallas_call | solution.py:89
  58.2 6.7 %all-to-all-start.2 = ((bf16[32,16,128]{2,1,0:T(8,128)(2,1)}), bf16[32,16,128]{2,1,0:T(8,128)(2,1)}, u32[]{:S(2)}, u32[]{:S(2)}) async-start(bf16[32,16,128]{2,1,0:T(8,128)(2,1)} %bitcast.170), calls=%async_computation.2 | async-start | bytes 262144 | tf_op jit(solution)/shard_map/all_to_all | solution.py:42
  65.0 2.7 %fusion.7 = f32[512,1024]{1,0:T(8,128)} fusion(bf16[512,128]{1,0:T(8,128)(2,1)S(1)} %bitcast.157, bf16[3,1024,128]{2,1,0:T(8,128)(2,1)} %copy-done.5), kind=kOutput, calls=%fused_computation.25 | convolution fusion | flops 134217728 | bytes 2490368 | tf_op jit(solution)/shard_map/dot_general | solution.py:425
  67.7 2.0 %fusion.38 = (bf16[32,16,128]{2,1,0:T(8,128)(2,1)}, bf16[32,16,128]{2,1,0:T(8,128)(2,1)}, bf16[32,16,128]{2,1,0:T(8,128)(2,1)}, bf16[32,16,128]{2,1,0:T(8,128)(2,1)S(1)}, bf16[32,16,128]{2,1,0:T(8,128)(2,1)}) fusion(bf16[32,80,128]{2,1,0:T(8,128)(2,1)} %all-to-all-done.3), kind=kLoop, calls=%fused_computation.115 | loop fusion | bytes 1310720 | tf_op jit(solution)/shard_map/slice | solution.py:400
  69.6 3.9 %all-to-all-done.2 = bf16[32,16,128]{2,1,0:T(8,128)(2,1)} async-done(((bf16[32,16,128]{2,1,0:T(8,128)(2,1)}), bf16[32,16,128]{2,1,0:T(8,128)(2,1)}, u32[]{:S(2)}, u32[]{:S(2)}) %all-to-all-start.2) | async-done | bytes 131104 | tf_op jit(solution)/shard_map/all_to_all | solution.py:42
  74.6 2.9 %shard_map.131 = (bf16[16,2,16,128]{3,2,1,0:T(8,128)(2,1)S(1)}, f32[9,16,128]{2,1,0:T(8,128)S(1)}) custom-call(s32[2]{0:T(128)S(1)} %get-tuple-element.79.refs_0_, bf16[16,2,16,128]{3,2,1,0:T(8,128)(2,1)} %bitcast.18.refs_1_, bf16[16,2,16,128]{3,2,1,0:T(8,128)(2,1)S(1)} %bitcast.165, f32[9,16,128]{2,1,0:T(8,128)S(1)} %broadcast_in_dim.18.refs_3_.refs_2_, ...), custom_call_target="tpu_custom_call" | custom-call | flops 4194304 | bytes 1048576 | tf_op jit(solution)/shard_map/pallas_call | solution.py:47
  79.4 2.6 %all-to-all-start.4 = ((bf16[32,16,128]{2,1,0:T(8,128)(2,1)}), bf16[32,16,128]{2,1,0:T(8,128)(2,1)S(1)}, u32[]{:S(2)}, u32[]{:S(2)}) async-start(bf16[32,16,128]{2,1,0:T(8,128)(2,1)} %bitcast.171), calls=%async_computation.4 | async-start | bytes 262144 | tf_op jit(solution)/shard_map/all_to_all | solution.py:42
  82.0 2.8 %fusion.17 = f32[512,1024]{1,0:T(8,128)} fusion(bf16[1024,128]{1,0:T(8,128)(2,1)} %copy-done.15, bf16[3,512,128]{2,1,0:T(8,128)(2,1)} %copy-done.10), kind=kOutput, calls=%fused_computation.45 | convolution fusion | flops 134217728 | bytes 2490368 | tf_op jit(solution)/shard_map/dot_general | solution.py:424
  84.8 5.8 %all-to-all-done.4 = bf16[32,16,128]{2,1,0:T(8,128)(2,1)S(1)} async-done(((bf16[32,16,128]{2,1,0:T(8,128)(2,1)}), bf16[32,16,128]{2,1,0:T(8,128)(2,1)S(1)}, u32[]{:S(2)}, u32[]{:S(2)}) %all-to-all-start.4) | async-done | bytes 131104 | tf_op jit(solution)/shard_map/all_to_all | solution.py:42
  94.9 3.4 %all-to-all-start.5 = ((bf16[32,16,128]{2,1,0:T(8,128)(2,1)}), bf16[32,16,128]{2,1,0:T(8,128)(2,1)}, u32[]{:S(2)}, u32[]{:S(2)}) async-start(bf16[32,16,128]{2,1,0:T(8,128)(2,1)} %bitcast.172), calls=%async_computation.5 | async-start | bytes 262144 | tf_op jit(solution)/shard_map/all_to_all | solution.py:42
  98.3 2.7 %fusion.5 = f32[512,1024]{1,0:T(8,128)} fusion(bf16[512,128]{1,0:T(8,128)(2,1)S(1)} %bitcast.161, bf16[3,1024,128]{2,1,0:T(8,128)(2,1)} %copy-done.5), kind=kOutput, calls=%fused_computation.23 | convolution fusion | flops 134217728 | bytes 2490368 | tf_op jit(solution)/shard_map/dot_general | solution.py:425
  101.1 5.9 %all-to-all-done.5 = bf16[32,16,128]{2,1,0:T(8,128)(2,1)} async-done(((bf16[32,16,128]{2,1,0:T(8,128)(2,1)}), bf16[32,16,128]{2,1,0:T(8,128)(2,1)}, u32[]{:S(2)}, u32[]{:S(2)}) %all-to-all-start.5) | async-done | bytes 131104 | tf_op jit(solution)/shard_map/all_to_all | solution.py:42
  107.8 3.6 %shard_map.133 = (bf16[16,2,16,128]{3,2,1,0:T(8,128)(2,1)}, f32[9,16,128]{2,1,0:T(8,128)S(1)}) custom-call(s32[2]{0:T(128)S(1)} %copy-done.25, bf16[16,2,16,128]{3,2,1,0:T(8,128)(2,1)} %bitcast.38.refs_1_, bf16[16,2,16,128]{3,2,1,0:T(8,128)(2,1)S(1)} %bitcast.163, f32[9,16,128]{2,1,0:T(8,128)S(1)} %copy-done.2, bf16[16,2,16,128]{3,2,1,0:T(8,128)(2,1)S(1)} %bitcast.162), custom_call_target="tpu_custom_call" | custom-call | flops 4194304 | bytes 1048576 | tf_op jit(solution)/shard_map/pallas_call | solution.py:47
  111.4 2.8 %all-to-all-start.6 = ((bf16[32,16,128]{2,1,0:T(8,128)(2,1)}), bf16[32,16,128]{2,1,0:T(8,128)(2,1)S(1)}, u32[]{:S(2)}, u32[]{:S(2)}) async-start(bf16[32,16,128]{2,1,0:T(8,128)(2,1)} %bitcast.41), calls=%async_computation.6 | async-start | bytes 262144 | tf_op jit(solution)/shard_map/all_to_all | solution.py:42
  114.2 2.9 %fusion.15 = f32[512,1024]{1,0:T(8,128)} fusion(bf16[1024,128]{1,0:T(8,128)(2,1)} %copy-done.17, bf16[3,512,128]{2,1,0:T(8,128)(2,1)} %copy-done.10), kind=kOutput, calls=%fused_computation.43 | convolution fusion | flops 134217728 | bytes 2490368 | tf_op jit(solution)/shard_map/dot_general | solution.py:424
  117.0 5.6 %all-to-all-done.6 = bf16[32,16,128]{2,1,0:T(8,128)(2,1)S(1)} async-done(((bf16[32,16,128]{2,1,0:T(8,128)(2,1)}), bf16[32,16,128]{2,1,0:T(8,128)(2,1)S(1)}, u32[]{:S(2)}, u32[]{:S(2)}) %all-to-all-start.6) | async-done | bytes 131104 | tf_op jit(solution)/shard_map/all_to_all | solution.py:42
  126.3 2.6 %all-to-all-start.7 = ((bf16[32,32,128]{2,1,0:T(8,128)(2,1)}), bf16[32,32,128]{2,1,0:T(8,128)(2,1)S(1)}, u32[]{:S(2)}, u32[]{:S(2)}) async-start(bf16[32,32,128]{2,1,0:T(8,128)(2,1)} %pad_maximum_fusion.2), calls=%async_computation.7 | async-start | bytes 524288 | tf_op jit(solution)/shard_map/all_to_all | solution.py:42
  128.9 3.6 %add_add_fusion.1 = f32[512,1024]{1,0:T(8,128)} fusion(f32[512,1024]{1,0:T(8,128)S(1)} %copy-done.28, f32[512,1024]{1,0:T(8,128)} %fusion.15, bf16[1024,128]{1,0:T(8,128)(2,1)} %copy-done.16, bf16[3,512,128]{2,1,0:T(8,128)(2,1)} %copy-done.10), kind=kOutput, calls=%fused_computation.1 | convolution fusion | flops 135266304 | bytes 6684672 | tf_op jit(solution)/shard_map/dot_general | solution.py:424
  132.5 4.1 %reshape.202 = f32[2,2,2,2,32,2,512]{6,5,4,3,2,1,0:T(2,128)} reshape(f32[512,1024]{1,0:T(8,128)} %add_add_fusion.1) | data formatting | bytes 4194304 | tf_op jit(solution)/shard_map/reshape | solution.py:341
  139.4 2.8 %add_add_fusion = f32[512,1024]{1,0:T(8,128)} fusion(f32[512,1024]{1,0:T(8,128)S(1)} %copy-done.27, f32[512,1024]{1,0:T(8,128)S(1)} %copy-done.29, bf16[512,128]{1,0:T(8,128)(2,1)S(1)} %bitcast.159, bf16[3,1024,128]{2,1,0:T(8,128)(2,1)} %copy-done.5), kind=kOutput, calls=%fused_computation | convolution fusion | flops 135266304 | bytes 6684672 | tf_op jit(solution)/shard_map/dot_general | solution.py:425
  142.2 4.0 %reshape.203 = f32[2,2,2,2,32,2,512]{6,5,4,3,2,1,0:T(2,128)} reshape(f32[512,1024]{1,0:T(8,128)} %add_add_fusion) | data formatting | bytes 4194304 | tf_op jit(solution)/shard_map/reshape | solution.py:341
  152.6 5.8 %all-to-all-start.8 = ((bf16[32,32,128]{2,1,0:T(8,128)(2,1)}), bf16[32,32,128]{2,1,0:T(8,128)(2,1)S(1)}, u32[]{:S(2)}, u32[]{:S(2)}) async-start(bf16[32,32,128]{2,1,0:T(8,128)(2,1)} %pad_maximum_fusion.3), calls=%async_computation.8 | async-start | bytes 524288 | tf_op jit(solution)/shard_map/all_to_all | solution.py:42
  159.8 1.8 collective-permute-start.5
  163.4 6.8 %collective-permute-done.5 = bf16[2,2,32,2,512]{4,2,0,1,3:T(8,128)(2,1)S(1)} collective-permute-done((bf16[2,2,32,2,512]{4,2,0,1,3:T(8,128)(2,1)S(1)}, bf16[2,2,32,2,512]{4,2,0,1,3:T(8,128)(2,1)S(1)}, u32[]{:S(2)}, u32[]{:S(2)}) %collective-permute-start.5) | collective-permute-done | bytes 262176 | tf_op jit(solution)/shard_map/ppermute | solution.py:332
  173.0 2.6 %collective-permute-done.6 = bf16[2,2,32,512]{3,2,0,1:T(8,128)(2,1)S(1)} collective-permute-done((bf16[2,2,32,512]{3,2,0,1:T(8,128)(2,1)S(1)}, bf16[2,2,32,512]{3,2,0,1:T(8,128)(2,1)S(1)}, u32[]{:S(2)}, u32[]{:S(2)}) %collective-permute-start.6) | collective-permute-done | bytes 131104 | tf_op jit(solution)/shard_map/ppermute | solution.py:332
  180.0 2.2 %collective-permute-start.8 = (bf16[32,512]{1,0:T(8,128)(2,1)S(1)}, bf16[32,512]{1,0:T(8,128)(2,1)S(1)}, u32[]{:S(2)}, u32[]{:S(2)}) collective-permute-start(bf16[32,512]{1,0:T(8,128)(2,1)S(1)} %fusion.24), channel_id=1, source_target_pairs={{0,16},{2,18},{4,20},{6,22},{8,24},{10,26},{12,28},{14,30},{16,0},... | collective-permute-start | bytes 98312 | tf_op jit(solution)/shard_map/ppermute | solution.py:332
  (194 shorter events, 59.1 us)
Async XLA Ops:
  0.6 16.5 %copy-start.38 = (s32[3,4]{1,0:T(4,128)S(1)}, s32[3,4]{1,0:T(4,128)}, u32[]{:S(2)}) copy-start(s32[3,4]{1,0:T(4,128)} %param.17) | copy-start | bytes 148
  0.6 16.5 %copy-start.39 = (s32[3,4]{1,0:T(4,128)S(1)}, s32[3,4]{1,0:T(4,128)}, u32[]{:S(2)}) copy-start(s32[3,4]{1,0:T(4,128)} %param.16) | copy-start | bytes 148
  0.7 19.7 %copy-start.36 = (f32[3,3,512]{2,1,0:T(4,128)S(1)}, f32[3,3,512]{2,1,0:T(4,128)}, u32[]{:S(2)}) copy-start(f32[3,3,512]{2,1,0:T(4,128)} %param.14) | copy-start | bytes 55300
  3.4 18.4 %all-to-all-start = ((bf16[32,32,128]{2,1,0:T(8,128)(2,1)}), bf16[32,32,128]{2,1,0:T(8,128)(2,1)S(1)}, u32[]{:S(2)}, u32[]{:S(2)}) async-start(bf16[32,32,128]{2,1,0:T(8,128)(2,1)} %pad_maximum_fusion.1), calls=%async_computation | async-start | bytes 524288 | tf_op jit(solution)/shard_map/all_to_all | solution.py:42
  11.6 15.0 %collective-permute-start = (bf16[3,1,16,512]{3,2,1,0:T(8,128)(2,1)S(1)}, bf16[3,1,16,512]{3,2,1,0:T(8,128)(2,1)S(1)}, u32[]{:S(2)}, u32[]{:S(2)}) collective-permute-start(bf16[3,1,16,512]{3,2,1,0:T(8,128)(2,1)S(1)} %get-tuple-element.62), channel_id=1, source_target_pairs={{0,2},{2,4},{4,6},{6,8},{8,10},{10,12},{12,14},{14,16},{16,18},{18... | collective-permute-start | bytes 147464 | tf_op jit(solution)/shard_map/ppermute | solution.py:24
  11.9 14.8 %collective-permute-start.1 = (bf16[3,1,16,512]{3,2,1,0:T(8,128)(2,1)S(1)}, bf16[3,1,16,512]{3,2,1,0:T(8,128)(2,1)S(1)}, u32[]{:S(2)}, u32[]{:S(2)}) collective-permute-start(bf16[3,1,16,512]{3,2,1,0:T(8,128)(2,1)S(1)} %get-tuple-element.61), channel_id=1, source_target_pairs={{2,0},{4,2},{6,4},{8,6},{10,8},{12,10},{14,12},{16,14},{18,16},{20... | collective-permute-start | bytes 147464 | tf_op jit(solution)/shard_map/ppermute | solution.py:27
  20.4 26.1 %copy-start.34 = (bf16[512,1024]{1,0:T(8,128)(2,1)S(1)}, bf16[512,1024]{1,0:T(8,128)(2,1)}, u32[]{:S(2)}) copy-start(bf16[512,1024]{1,0:T(8,128)(2,1)} %param.12) | copy-start | bytes 3145732
  20.4 26.1 %copy-start.18 = (f32[9,512]{1,0:T(8,128)}, f32[9,512]{1,0:T(8,128)S(1)}, u32[]{:S(2)}) copy-start(f32[9,512]{1,0:T(8,128)S(1)} %reshape.179.kernel_ref) | copy-start | bytes 55300
  23.5 11.7 %all-to-all-start.1 = ((bf16[32,16,128]{2,1,0:T(8,128)(2,1)}), bf16[32,16,128]{2,1,0:T(8,128)(2,1)S(1)}, u32[]{:S(2)}, u32[]{:S(2)}) async-start(bf16[32,16,128]{2,1,0:T(8,128)(2,1)} %bitcast.9), calls=%async_computation.1 | async-start | bytes 262144 | tf_op jit(solution)/shard_map/all_to_all | solution.py:42
  26.7 20.3 %copy-start.37 = (f32[512]{0:T(512)S(1)}, f32[512]{0:T(512)}, u32[]{:S(2)}) copy-start(f32[512]{0:T(512)} %param.13) | copy-start | bytes 6148
  26.7 20.5 %copy-start = (bf16[512,1024]{1,0:T(8,128)(2,1)S(1)}, bf16[512,1024]{1,0:T(8,128)(2,1)}, u32[]{:S(2)}) copy-start(bf16[512,1024]{1,0:T(8,128)(2,1)} %up_ref.5) | copy-start | bytes 3145732
  26.8 19.7 %copy-start.35 = (bf16[3,10,16,512]{3,2,1,0:T(8,128)(2,1)}, bf16[3,10,16,512]{3,2,1,0:T(8,128)(2,1)S(1)}, u32[]{:S(2)}) copy-start(bf16[3,10,16,512]{3,2,1,0:T(8,128)(2,1)S(1)} %constant_dynamic-update-slice_fusion) | copy-start | bytes 1474564
  35.3 23.0 %all-to-all-start.3 = ((bf16[32,80,128]{2,1,0:T(8,128)(2,1)}), bf16[32,80,128]{2,1,0:T(8,128)(2,1)}, u32[]{:S(2)}, u32[]{:S(2)}) async-start(bf16[32,80,128]{2,1,0:T(8,128)(2,1)} %broadcast_dynamic-update-slice_fusion), calls=%async_computation.3 | async-start | bytes 1310720 | tf_op jit(solution)/shard_map/all_to_all | solution.py:42
  39.3 8.4 %collective-permute-start.3 = (bf16[3,10,1,512]{3,2,1,0:T(2,128)(2,1)}, bf16[3,10,1,512]{3,2,1,0:T(2,128)(2,1)}, u32[]{:S(2)}, u32[]{:S(2)}) collective-permute-start(bf16[3,10,1,512]{3,2,1,0:T(2,128)(2,1)} %get-tuple-element.57), channel_id=1, source_target_pairs={{1,0},{3,2},{5,4},{7,6},{9,8},{11,10},{13,12},{15,14},{17,16},{19,... | collective-permute-start | bytes 92168 | tf_op jit(solution)/shard_map/ppermute | solution.py:27
  40.6 7.7 %collective-permute-start.2 = (bf16[3,10,1,512]{3,2,1,0:T(2,128)(2,1)}, bf16[3,10,1,512]{3,2,1,0:T(2,128)(2,1)}, u32[]{:S(2)}, u32[]{:S(2)}) collective-permute-start(bf16[3,10,1,512]{3,2,1,0:T(2,128)(2,1)} %get-tuple-element.56), channel_id=1, source_target_pairs={{0,1},{2,3},{4,5},{6,7},{8,9},{10,11},{12,13},{14,15},{16,17},{18,... | collective-permute-start | bytes 92168 | tf_op jit(solution)/shard_map/ppermute | solution.py:24
  58.2 15.4 %all-to-all-start.2 = ((bf16[32,16,128]{2,1,0:T(8,128)(2,1)}), bf16[32,16,128]{2,1,0:T(8,128)(2,1)}, u32[]{:S(2)}, u32[]{:S(2)}) async-start(bf16[32,16,128]{2,1,0:T(8,128)(2,1)} %bitcast.170), calls=%async_computation.2 | async-start | bytes 262144 | tf_op jit(solution)/shard_map/all_to_all | solution.py:42
  79.4 11.2 %all-to-all-start.4 = ((bf16[32,16,128]{2,1,0:T(8,128)(2,1)}), bf16[32,16,128]{2,1,0:T(8,128)(2,1)S(1)}, u32[]{:S(2)}, u32[]{:S(2)}) async-start(bf16[32,16,128]{2,1,0:T(8,128)(2,1)} %bitcast.171), calls=%async_computation.4 | async-start | bytes 262144 | tf_op jit(solution)/shard_map/all_to_all | solution.py:42
  94.9 12.0 %all-to-all-start.5 = ((bf16[32,16,128]{2,1,0:T(8,128)(2,1)}), bf16[32,16,128]{2,1,0:T(8,128)(2,1)}, u32[]{:S(2)}, u32[]{:S(2)}) async-start(bf16[32,16,128]{2,1,0:T(8,128)(2,1)} %bitcast.172), calls=%async_computation.5 | async-start | bytes 262144 | tf_op jit(solution)/shard_map/all_to_all | solution.py:42
  101.1 21.6 %copy-start.3 = (f32[512,128]{1,0:T(8,128)S(1)}, f32[512,128]{1,0:T(8,128)}, u32[]{:S(2)}) copy-start(f32[512,128]{1,0:T(8,128)} %get-tuple-element.48.normed_ref) | copy-start | bytes 786436
  111.4 11.2 %all-to-all-start.6 = ((bf16[32,16,128]{2,1,0:T(8,128)(2,1)}), bf16[32,16,128]{2,1,0:T(8,128)(2,1)S(1)}, u32[]{:S(2)}, u32[]{:S(2)}) async-start(bf16[32,16,128]{2,1,0:T(8,128)(2,1)} %bitcast.41), calls=%async_computation.6 | async-start | bytes 262144 | tf_op jit(solution)/shard_map/all_to_all | solution.py:42
  126.3 24.6 %all-to-all-start.7 = ((bf16[32,32,128]{2,1,0:T(8,128)(2,1)}), bf16[32,32,128]{2,1,0:T(8,128)(2,1)S(1)}, u32[]{:S(2)}, u32[]{:S(2)}) async-start(bf16[32,32,128]{2,1,0:T(8,128)(2,1)} %pad_maximum_fusion.2), calls=%async_computation.7 | async-start | bytes 524288 | tf_op jit(solution)/shard_map/all_to_all | solution.py:42
  139.3 19.1 %collective-permute-start.4 = (bf16[2,2,2,32,2,512]{5,3,0,1,4,2:T(8,128)(2,1)}, bf16[2,2,2,32,2,512]{5,3,0,1,4,2:T(8,128)(2,1)}, u32[]{:S(2)}, u32[]{:S(2)}) collective-permute-start(bf16[2,2,2,32,2,512]{5,3,0,1,4,2:T(8,128)(2,1)} %bitcast.148), channel_id=1, source_target_pairs={{0,2},{2,0},{4,6},{6,4},{8,10},{10,8},{12,14},{14,12},{16,18},{18,... | collective-permute-start | bytes 1572872 | tf_op jit(solution)/shard_map/ppermute | solution.py:332
  148.8 12.8 %collective-permute-start.9 = (bf16[2,2,2,32,2,512]{5,3,0,1,2,4:T(8,128)(2,1)}, bf16[2,2,2,32,2,512]{5,3,0,1,2,4:T(8,128)(2,1)S(1)}, u32[]{:S(2)}, u32[]{:S(2)}) collective-permute-start(bf16[2,2,2,32,2,512]{5,3,0,1,2,4:T(8,128)(2,1)} %bitcast.149), channel_id=1, source_target_pairs={{0,2},{2,0},{4,6},{6,4},{8,10},{10,8},{12,14},{14,12},{16,18},{18,... | collective-permute-start | bytes 1572872 | tf_op jit(solution)/shard_map/ppermute | solution.py:332
  152.6 31.3 %all-to-all-start.8 = ((bf16[32,32,128]{2,1,0:T(8,128)(2,1)}), bf16[32,32,128]{2,1,0:T(8,128)(2,1)S(1)}, u32[]{:S(2)}, u32[]{:S(2)}) async-start(bf16[32,32,128]{2,1,0:T(8,128)(2,1)} %pad_maximum_fusion.3), calls=%async_computation.8 | async-start | bytes 524288 | tf_op jit(solution)/shard_map/all_to_all | solution.py:42
  159.8 10.5 %collective-permute-start.5 = (bf16[2,2,32,2,512]{4,2,0,1,3:T(8,128)(2,1)S(1)}, bf16[2,2,32,2,512]{4,2,0,1,3:T(8,128)(2,1)S(1)}, u32[]{:S(2)}, u32[]{:S(2)}) collective-permute-start(bf16[2,2,32,2,512]{4,2,0,1,3:T(8,128)(2,1)S(1)} %fusion.2), channel_id=1, source_target_pairs={{0,4},{2,6},{4,0},{6,2},{8,12},{10,14},{12,8},{14,10},{16,20},{18,... | collective-permute-start | bytes 786440 | tf_op jit(solution)/shard_map/ppermute | solution.py:332
  161.9 10.0 %collective-permute-start.10 = (bf16[2,2,2,32,512]{4,3,0,1,2:T(8,128)(2,1)S(1)}, bf16[2,2,2,32,512]{4,3,0,1,2:T(8,128)(2,1)S(1)}, u32[]{:S(2)}, u32[]{:S(2)}) collective-permute-start(bf16[2,2,2,32,512]{4,3,0,1,2:T(8,128)(2,1)S(1)} %fusion.3), channel_id=1, source_target_pairs={{0,1},{1,0},{2,3},{3,2},{4,5},{5,4},{6,7},{7,6},{8,9},{9,8},{10,11... | collective-permute-start | bytes 786440 | tf_op jit(solution)/shard_map/ppermute | solution.py:332
  170.3 5.2 %collective-permute-start.6 = (bf16[2,2,32,512]{3,2,0,1:T(8,128)(2,1)S(1)}, bf16[2,2,32,512]{3,2,0,1:T(8,128)(2,1)S(1)}, u32[]{:S(2)}, u32[]{:S(2)}) collective-permute-start(bf16[2,2,32,512]{3,2,0,1:T(8,128)(2,1)S(1)} %fusion.12), channel_id=1, source_target_pairs={{0,1},{1,0},{2,3},{3,2},{4,5},{5,4},{6,7},{7,6},{8,9},{9,8},{10,11... | collective-permute-start | bytes 393224 | tf_op jit(solution)/shard_map/ppermute | solution.py:332
  172.0 5.2 %collective-permute-start.11 = (bf16[2,2,32,512]{3,2,0,1:T(8,128)(2,1)S(1)}, bf16[2,2,32,512]{3,2,0,1:T(8,128)(2,1)S(1)}, u32[]{:S(2)}, u32[]{:S(2)}) collective-permute-start(bf16[2,2,32,512]{3,2,0,1:T(8,128)(2,1)S(1)} %fusion.13), channel_id=1, source_target_pairs={{0,4},{2,6},{4,0},{6,2},{8,12},{10,14},{12,8},{14,10},{16,20},{18,... | collective-permute-start | bytes 393224 | tf_op jit(solution)/shard_map/ppermute | solution.py:332
  175.6 4.3 %collective-permute-start.7 = (bf16[2,32,512]{2,1,0:T(8,128)(2,1)S(1)}, bf16[2,32,512]{2,1,0:T(8,128)(2,1)S(1)}, u32[]{:S(2)}, u32[]{:S(2)}) collective-permute-start(bf16[2,32,512]{2,1,0:T(8,128)(2,1)S(1)} %fusion.22), channel_id=1, source_target_pairs={{0,8},{2,10},{4,12},{6,14},{8,0},{10,2},{12,4},{14,6},{16,24},{18,... | collective-permute-start | bytes 196616 | tf_op jit(solution)/shard_map/ppermute | solution.py:332
  177.2 5.0 %collective-permute-start.12 = (bf16[2,32,512]{2,1,0:T(8,128)(2,1)S(1)}, bf16[2,32,512]{2,1,0:T(8,128)(2,1)S(1)}, u32[]{:S(2)}, u32[]{:S(2)}) collective-permute-start(bf16[2,32,512]{2,1,0:T(8,128)(2,1)S(1)} %fusion.23), channel_id=1, source_target_pairs={{0,8},{2,10},{4,12},{6,14},{8,0},{10,2},{12,4},{14,6},{16,24},{18,... | collective-permute-start | bytes 196616 | tf_op jit(solution)/shard_map/ppermute | solution.py:332
  180.0 5.0 %collective-permute-start.8 = (bf16[32,512]{1,0:T(8,128)(2,1)S(1)}, bf16[32,512]{1,0:T(8,128)(2,1)S(1)}, u32[]{:S(2)}, u32[]{:S(2)}) collective-permute-start(bf16[32,512]{1,0:T(8,128)(2,1)S(1)} %fusion.24), channel_id=1, source_target_pairs={{0,16},{2,18},{4,20},{6,22},{8,24},{10,26},{12,28},{14,30},{16,0},... | collective-permute-start | bytes 98312 | tf_op jit(solution)/shard_map/ppermute | solution.py:332
  182.3 5.3 %collective-permute-start.13 = (bf16[32,512]{1,0:T(8,128)(2,1)S(1)}, bf16[32,512]{1,0:T(8,128)(2,1)S(1)}, u32[]{:S(2)}, u32[]{:S(2)}) collective-permute-start(bf16[32,512]{1,0:T(8,128)(2,1)S(1)} %fusion.25), channel_id=1, source_target_pairs={{0,16},{2,18},{4,20},{6,22},{8,24},{10,26},{12,28},{14,30},{16,0},... | collective-permute-start | bytes 98312 | tf_op jit(solution)/shard_map/ppermute | solution.py:332
  (31 other events, 104.3 us)

commit v2 on v1

v2 whole, which is shorter than its diff:
```python
import functools

import jax
import jax.numpy as jnp
from jax import lax
from jax.experimental import pallas as pl
from jax.experimental.pallas import tpu as pltpu
from jax.sharding import PartitionSpec as P

EPSILON = 1e-06
AXES = ("lon", "lat")
ROWS = 16
LAT_REACH = 2
MIB = 1024 * 1024


def with_halo(block, sides, width, periodic):
    for axis, dim in sides:
        count = lax.axis_size(axis)
        forward = [(i, i + 1) for i in range(count - 1)]
        if periodic:
            forward.append((count - 1, 0))
        backward = [(target, source) for source, target in forward]
        low = lax.ppermute(
            lax.slice_in_dim(block, block.shape[dim] - width, None, axis=dim), axis, forward
        )
        high = lax.ppermute(lax.slice_in_dim(block, 0, width, axis=dim), axis, backward)
        block = jnp.concatenate([low, block, high], axis=dim)
    return block


def exchanged(blocks):
    return lax.all_to_all(blocks, AXES, split_axis=0, concat_axis=0, tiled=True)


def call(kernel, out_shape, *operands, scratch=(), scalars=0, flops=0, moved=0, limit=8):
    space = [pltpu.SMEM] * scalars + [pltpu.VMEM] * (len(operands) - scalars)
    return pl.pallas_call(
        kernel,
        out_shape=out_shape,
        in_specs=[pl.BlockSpec(memory_space=kind) for kind in space],
        out_specs=jax.tree.map(lambda _: pl.BlockSpec(memory_space=pltpu.VMEM), out_shape),
        scratch_shapes=scratch,
        compiler_params=pltpu.CompilerParams(vmem_limit_bytes=limit * MIB),
        cost_estimate=pl.CostEstimate(flops=flops, bytes_accessed=moved, transcendentals=0),
    )(*operands)


def split_three(value, lane, width):
    value = jnp.where(lane < width, value, 0.0)
    result = jnp.zeros_like(value)
    for k in range(3):
        piece = value.astype(jnp.bfloat16).astype(jnp.float32)
        result = result + (pltpu.roll(piece, k * width, 1) if k else piece)
        value = value - piece
    return result.astype(jnp.bfloat16)


def join_three(value, width):
    lanes = value.shape[1]
    return value + pltpu.roll(value, lanes - width, 1) + pltpu.roll(value, lanes - 2 * width, 1)


def pack_kernel(cotangent_ref, weight_ref, out_ref):
    channels = cotangent_ref.shape[1]
    devices, _, count = out_ref.shape
    share = channels // devices
    turned = cotangent_ref[...].astype(jnp.float32).T.astype(jnp.bfloat16)
    out_ref[:, :share] = turned.reshape(devices, share, count)
    rows = weight_ref.shape[0]
    weights = jnp.concatenate([weight_ref[:, i] for i in range(weight_ref.shape[1])], axis=1)
    weights = jnp.concatenate([weights, jnp.zeros((ROWS - rows, count), jnp.float32)], axis=0)
    weights = weights.astype(jnp.bfloat16)
    out_ref[:, share:] = jnp.broadcast_to(weights[None], (devices, ROWS, count))


def packed(cotangent, bilinear, devices):
    rows_out, cols_out, channels = cotangent.shape
    steps, corners = bilinear.shape[:2]
    count = rows_out * cols_out
    share = channels // devices
    if share % ROWS:
        blocks = cotangent.reshape(count, channels).T.reshape(devices, share, count)
        blocks = jnp.pad(blocks, ((0, 0), (0, -share % ROWS), (0, 0)))
        weights = bilinear.reshape(steps * corners, count).astype(jnp.bfloat16)
        weights = jnp.pad(weights, ((0, ROWS - steps * corners), (0, 0)))
        return jnp.concatenate([blocks, jnp.broadcast_to(weights[None], (devices, ROWS, count))], axis=1)
    return call(
        pack_kernel,
        jax.ShapeDtypeStruct((devices, share + ROWS, count), jnp.bfloat16),
        cotangent.reshape(count, channels),
        bilinear.reshape(steps * corners, rows_out, cols_out),
        moved=2**19,
    )


def forward_kernel(step, padded_ref, kernel_ref, gain_ref, up_ref, n_ref, normed_ref, inv_ref, hid_ref, slope_ref):
    rows_out, cols_out = padded_ref.shape[1] - 2, padded_ref.shape[2] - 2
    channels = padded_ref.shape[3]
    padded = padded_ref[step].astype(jnp.float32)
    mixed = padded[1 : 1 + rows_out, 1 : 1 + cols_out]
    running = jnp.zeros_like(mixed)
    for col_tap in range(3):
        shifted_cols = padded[:, col_tap : col_tap + cols_out]
        for row_tap in range(3):
            tap = kernel_ref[3 * row_tap + col_tap : 3 * row_tap + col_tap + 1]
            running = running + tap[None] * shifted_cols[row_tap : row_tap + rows_out]
    mixed = (mixed + running).reshape(rows_out * cols_out, channels).T
    inv_root = lax.rsqrt(jnp.mean(mixed * mixed, axis=0, keepdims=True) + EPSILON)
    normed = mixed * inv_root
    narrow = (normed * gain_ref[...]).astype(jnp.bfloat16)
    pre = jnp.dot(up_ref[...], narrow, preferred_element_type=jnp.float32)
    sigmoid = jax.nn.sigmoid(pre)
    n_ref[...] = narrow
    normed_ref[...] = normed
    inv_ref[...] = inv_root
    hid_ref[...] = (pre * sigmoid).astype(jnp.bfloat16)
    slope_ref[...] = sigmoid * (1.0 + pre * (1.0 - sigmoid))


def forward_parts(step, padded, taps, gain, w_up_t):
    _, rows_in, cols_in, channels = padded.shape
    hid = w_up_t.shape[0]
    count = (rows_in - 2) * (cols_in - 2)
    sds = jax.ShapeDtypeStruct
    return call(
        functools.partial(forward_kernel, step),
        [
            sds((channels, count), jnp.bfloat16),
            sds((channels, count), jnp.float32),
            sds((1, count), jnp.float32),
            sds((hid, count), jnp.bfloat16),
            sds((hid, count), jnp.float32),
        ],
        padded,
        taps,
        gain,
        w_up_t,
        flops=2 * count * hid * channels,
        moved=2**21,
        limit=12,
    )


def stencil_sums(step, padded_ref, field):
    rows_out, cols_out = padded_ref.shape[1] - 2, padded_ref.shape[2] - 2
    channels = padded_ref.shape[3]
    field = field.astype(jnp.float32).T.reshape(rows_out, cols_out, channels)
    padded = padded_ref[step].astype(jnp.float32)
    result = [None] * 9
    for col_tap in range(3):
        shifted_cols = padded[:, col_tap : col_tap + cols_out]
        for row_tap in range(3):
            products = jnp.sum(shifted_cols[row_tap : row_tap + rows_out] * field, axis=0)
            result[3 * row_tap + col_tap] = jnp.sum(products, axis=0, keepdims=True)
    return result


def stencil_kernel(steps, *refs):
    padded_ref, *field_refs, out_ref = refs
    total = None
    for step, ref in zip(steps, field_refs):
        rows = stencil_sums(step, padded_ref, ref[...])
        total = rows if total is None else [a + b for a, b in zip(total, rows)]
    out_ref[...] = jnp.zeros_like(out_ref)
    for k, row in enumerate(total):
        out_ref[k : k + 1] = row


def stencil_terms(steps, padded, fields):
    return call(
        functools.partial(stencil_kernel, steps),
        jax.ShapeDtypeStruct((ROWS, padded.shape[3]), jnp.float32),
        padded,
        *fields,
        moved=2**20,
        limit=12,
    )


def network_kernel(step, *refs):
    refs = list(refs)
    moved_ref, down_ref, up_ref, slope_ref, normed_ref, inv_ref, gain_ref = refs[:7]
    refs = refs[7:]
    before_ref = refs.pop(0) if step is not None or len(refs) > 3 else None
    moved = moved_ref[...]
    grad_hidden = jnp.dot(down_ref[...], moved, preferred_element_type=jnp.float32)
    grad_pre = (grad_hidden * slope_ref[...]).astype(jnp.bfloat16)
    grad_n = jnp.dot(up_ref[...], grad_pre, preferred_element_type=jnp.float32)
    normed = normed_ref[...]
    term = grad_n * normed
    gain = gain_ref[...]
    mean = jnp.mean(term * gain, axis=0, keepdims=True)
    field = moved.astype(jnp.float32) + inv_ref[...] * (grad_n * gain - normed * mean)
    field = field.astype(jnp.bfloat16)
    if before_ref is not None:
        term = before_ref[...] + term
    if step is None:
        field_ref, grad_ref, term_ref = refs
        field_ref[...] = field
        grad_ref[...] = grad_pre
        term_ref[...] = term
        return
    padded_ref, sums_ref, out_ref, grad_ref = refs
    grad_ref[...] = grad_pre
    devices, _, count = out_ref.shape
    channels = moved.shape[0]
    share = channels // devices
    rows = stencil_sums(step, padded_ref, field)
    rows = jnp.concatenate(rows + [jnp.zeros((count - 9, channels), jnp.float32)], axis=0)
    before = jnp.concatenate([sums_ref[...], jnp.zeros((count - ROWS, channels), jnp.float32)], axis=0)
    sums = (rows + before).T
    lane = lax.broadcasted_iota(jnp.int32, sums.shape, 1)
    sums = jnp.where(lane == 9, jnp.sum(term, axis=1, keepdims=True), sums)
    out_ref[:, :share] = field.reshape(devices, share, count)
    out_ref[:, share:] = split_three(sums, lane, ROWS).reshape(devices, share, count)


def network_back(step, devices, moved, w_down_t, w_up, slope, normed, inv_root, gain, before, padded=None, sums=None):
    channels, count = moved.shape
    hid = w_down_t.shape[0]
    sds = jax.ShapeDtypeStruct
    operands = [moved, w_down_t, w_up, slope, normed, inv_root, gain]
    operands += [] if before is None else [before]
    if padded is None:
        out = [
            sds((channels, count), jnp.bfloat16),
            sds((hid, count), jnp.bfloat16),
            sds((channels, count), jnp.float32),
        ]
    else:
        operands += [padded, sums]
        out = [
            sds((devices, 2 * channels // devices, count), jnp.bfloat16),
            sds((hid, count), jnp.bfloat16),
        ]
    return call(
        functools.partial(network_kernel, step if padded is not None else None),
        out,
        *operands,
        flops=4 * count * hid * channels,
        moved=4 * 2**20,
        limit=12,
    )


def final_kernel(arrived_ref, state_ref, sums_ref):
    devices, rows, count = arrived_ref.shape
    share = rows // 2
    channels = devices * share
    state = arrived_ref[:, :share].reshape(channels, count).astype(jnp.float32)
    state_ref[...] = state.T.astype(jnp.bfloat16)
    sums = arrived_ref[:, share:].reshape(channels, count).astype(jnp.float32)
    sums_ref[...] = join_three(sums, ROWS).T[:ROWS]


def final_parts(arrived, channels):
    devices, rows, count = arrived.shape
    sds = jax.ShapeDtypeStruct
    return call(
        final_kernel,
        [sds((count, channels), jnp.bfloat16), sds((ROWS, channels), jnp.float32)],
        arrived,
        moved=2**19,
    )


def spatial_kernel(mode, step, near_lon, near_lat, *refs):
    refs = list(refs)
    take = lambda: refs.pop(0)
    with_move, with_stencil = mode != "last", mode != "first"
    move_ref = take() if with_move else None
    in_ref = take()
    kern_ref = take() if with_stencil else None
    weight_ref = take() if with_move else None
    out_ref = take()
    high_ref, own_ref, low_ref, spread_ref = take(), take(), take(), take()
    tiles_lon, tiles_lat, _, lanes = in_ref.shape
    rows = high_ref.shape[2]
    lane = lax.broadcasted_iota(jnp.int32, (rows, lanes), 1)
    col = lax.rem(lane, near_lat)
    unroll = 16 if tiles_lon * tiles_lat <= 32 else 1
    zero = jnp.zeros((rows, lanes), jnp.float32)

    def turn(value, steps):
        return pltpu.roll(value, steps % lanes, 1) if isinstance(steps, int) else pltpu.roll(value, steps, 1)

    def lat_after(tiles):
        following = tiles[1:] + [None]
        return [
            jnp.where(col < near_lat - 1, turn(here, -1), 0.0 if after is None else turn(after, near_lat - 1))
            for here, after in zip(tiles, following)
        ]

    def lat_before(tiles):
        preceding = [None] + tiles[:-1]
        return [
            jnp.where(col > 0, turn(here, 1), 0.0 if before is None else turn(before, 1 - near_lat))
            for here, before in zip(tiles, preceding)
        ]

    def lon_after(here, after):
        return turn(jnp.where(lane < near_lat, after, here), -near_lat)

    def lon_before(here, before):
        return turn(jnp.where(lane >= lanes - near_lat, before, here), near_lat)

    def next_tile(a):
        return lax.rem(a + 1, tiles_lon)

    def last_tile(a):
        return lax.rem(a + tiles_lon - 1, tiles_lon)

    def read(ref, a):
        return [ref[a, b, :rows].astype(jnp.float32) for b in range(tiles_lat)]

    def loop(body, init=None):
        return lax.fori_loop(0, tiles_lon, body, init, unroll=unroll)

    if with_stencil:
        taps = [[kern_ref[3 * a + b] for b in range(3)] for a in range(3)]

        def mix(a, carry):
            here = read(in_ref, a)
            by_col = [lat_after(here), here, lat_before(here)]
            for b in range(tiles_lat):
                mixes = []
                for row in range(3):
                    mixed = None
                    for c in range(3):
                        shifted = by_col[c][b]
                        term = taps[row][c] * shifted
                        mixed = term if mixed is None else mixed + term
                    mixes.append(mixed)
                high_ref[a, b] = mixes[0]
                own_ref[a, b] = here[b] + mixes[1]
                low_ref[a, b] = mixes[2]
            return carry

        loop(mix)

    def gather(a):
        if not with_stencil:
            return read(in_ref, a)
        result = []
        for b in range(tiles_lat):
            value = own_ref[a, b] + lon_after(high_ref[a, b], high_ref[next_tile(a), b])
            value = value + lon_before(low_ref[a, b], low_ref[last_tile(a), b])
            result.append(value)
        return result

    if not with_move:

        def finish(a, carry):
            for b, value in enumerate(gather(a)):
                out_ref[a, b, :rows] = value.astype(jnp.bfloat16)
            return carry

        loop(finish)
        sums = jnp.sum(in_ref[:, :, rows:].astype(jnp.float32), axis=(0, 1))
        sums = split_three(join_three(sums, ROWS), lane, ROWS)
        out_ref[:, :, rows:] = jnp.broadcast_to(sums[None, None], (tiles_lon, tiles_lat, rows, lanes))
        return

    own2_ref, lon2_ref = refs
    weight_row = weight_ref.shape[2] - ROWS + 4 * step

    def weigh(a, carry):
        here = [value.astype(jnp.bfloat16).astype(jnp.float32) for value in gather(a)]
        weights = [
            [weight_ref[a, b, weight_row + k : weight_row + k + 1].astype(jnp.float32) for k in range(4)]
            for b in range(tiles_lat)
        ]
        own = lat_after([weights[b][2] * here[b] for b in range(tiles_lat)])
        lon = lat_after([weights[b][3] * here[b] for b in range(tiles_lat)])
        for b in range(tiles_lat):
            own2_ref[a, b] = weights[b][0] * here[b] + own[b]
            lon2_ref[a, b] = weights[b][1] * here[b] + lon[b]
        return carry

    loop(weigh)

    def spread(a, carry):
        for b in range(tiles_lat):
            value = own2_ref[a, b] + lon_after(lon2_ref[a, b], lon2_ref[next_tile(a), b])
            spread_ref[a, b] = value.astype(jnp.bfloat16).astype(jnp.float32)
        for b in range(LAT_REACH):
            spread_ref[a, tiles_lat + b] = zero
        return carry

    loop(spread)

    lon_move, lat_move = move_ref[0], move_ref[1]
    far_lon, off_lon = lon_move // near_lon, lax.rem(lon_move, near_lon)
    far_lat, off_lat = lat_move // near_lat, lax.rem(lat_move, near_lat)
    shift = off_lon * near_lat + off_lat
    turn_here = lax.rem(2 * lanes - shift, lanes)
    turn_next = lax.rem(2 * lanes - shift + near_lat, lanes)
    same_lon = lane >= off_lon * near_lat
    same_lat = col + off_lat < near_lat

    def move(a, carry):
        source = lax.rem(a + far_lon, tiles_lon)
        source_next = next_tile(source)
        for b in range(tiles_lat):
            here, after = (
                jnp.where(same_lon, spread_ref[source, far_lat + k], spread_ref[source_next, far_lat + k])
                for k in (b, b + 1)
            )
            value = jnp.where(same_lat, turn(here, turn_here), turn(after, turn_next))
            out_ref[a, b] = value.astype(jnp.bfloat16)
        return carry

    loop(move)


def spatial(mode, step, tile, rows, field, kern, weights, moves):
    tiles_lon, tiles_lat, _, lanes = field.shape
    with_move, with_stencil = mode != "last", mode != "first"
    operands = ([moves] if with_move else []) + [field]
    operands += [kern] if with_stencil else []
    operands += [weights] if with_move else []
    out_rows = rows if with_move else 2 * rows
    grid = pltpu.VMEM((tiles_lon, tiles_lat, rows, lanes), jnp.float32)
    scratch = [grid, grid, grid, pltpu.VMEM((tiles_lon, tiles_lat + LAT_REACH, rows, lanes), jnp.float32)]
    if with_move:
        scratch += [grid, grid]
    return call(
        functools.partial(spatial_kernel, mode, step, *tile),
        jax.ShapeDtypeStruct((tiles_lon, tiles_lat, out_rows, lanes), jnp.bfloat16),
        *operands,
        scratch=scratch,
        scalars=1 if with_move else 0,
        flops=2**22,
        moved=2**20,
        limit=max(8, 10 * tiles_lon * tiles_lat * rows * lanes * 4 // MIB),
    )


def halved(value, axis, bit, dim):
    count = lax.axis_size(axis)
    mine = lax.axis_index(axis) >> bit & 1
    kept = lax.dynamic_index_in_dim(value, mine, dim, keepdims=False)
    sent = lax.dynamic_index_in_dim(value, 1 - mine, dim, keepdims=False).astype(jnp.bfloat16)
    arrived = lax.ppermute(sent, axis, [(i, i ^ (1 << bit)) for i in range(count)])
    return kept + arrived.astype(jnp.float32)


def scattered(value, lat_first):
    channels, hid = value.shape
    lon_bits = lax.axis_size("lon").bit_length() - 1
    lat_bits = lax.axis_size("lat").bit_length() - 1
    rows = channels >> lon_bits
    value = value.reshape(*([2] * lon_bits), rows, *([2] * lat_bits), hid >> lat_bits)

    def over_lon(value, bit, left):
        return halved(value, "lon", bit, left.index(bit)), [k for k in left if k != bit]

    left_lon = list(range(lon_bits))[::-1]
    left_lat = list(range(lat_bits))[::-1]
    order = [("lon", 0), ("lon", 1)] + [("lat", k) for k in range(lat_bits)]
    if lat_first:
        order = [("lon", 0)] + [("lat", k) for k in range(lat_bits)] + [("lon", 1)]
    order += [("lon", k) for k in range(2, lon_bits)]
    for axis, bit in order:
        if axis == "lon":
            value, left_lon = over_lon(value, bit, left_lon)
        else:
            value = halved(value, "lat", bit, len(left_lon) + 1 + left_lat.index(bit))
            left_lat.remove(bit)
    return value


def gradient_kernel(row_groups, bit_ref, *refs):
    *inputs, send_ref, keep_ref = refs
    steps = len(inputs) // 4
    for k in range(2):
        left = inputs[2 * k * steps : (2 * k + 1) * steps]
        right = inputs[(2 * k + 1) * steps : (2 * k + 2) * steps]
        right = jnp.concatenate([ref[...] for ref in right], axis=1)
        channels = left[0].shape[0]
        chunk = channels // (2 * row_groups)
        for which, out_ref in ((1 - bit_ref[0], send_ref), (bit_ref[0], keep_ref)):
            rows = []
            for p in range(row_groups):
                start = pl.multiple_of((2 * p + which) * chunk, chunk)
                rows.append(jnp.concatenate([ref[pl.ds(start, chunk)] for ref in left], axis=1))
            rows = jnp.concatenate(rows, axis=0)
            value = lax.dot_general(rows, right, (((1,), (1,)), ((), ())), preferred_element_type=jnp.float32)
            out_ref[k] = value.astype(out_ref.dtype)


def halves_kernel(plan, together, bit_ref, *refs):
    refs = list(refs)
    count = len(plan)
    joint_in = len(refs) == 2 + (2 if together else 2 * count)
    if joint_in:
        kept, arrived = refs[0], refs[1]
        kept, arrived = [kept.at[k] for k in range(count)], [arrived.at[k] for k in range(count)]
        refs = refs[2:]
    else:
        kept, arrived = refs[:count], refs[count : 2 * count]
        refs = refs[2 * count :]
    if together:
        sends, keeps = [refs[0].at[k] for k in range(count)], [refs[1].at[k] for k in range(count)]
    else:
        sends, keeps = refs[:count], refs[count:]
    for k, (dim, groups, bit_at) in enumerate(plan):
        bit = bit_ref[bit_at]
        size = kept[k].shape[dim] // (2 * groups)
        for which, out_ref in ((1 - bit, sends[k]), (bit, keeps[k])):
            for p in range(groups):
                start = pl.multiple_of((2 * p + which) * size, size)
                place = (pl.ds(start, size),) if dim == 0 else (slice(None), pl.ds(start, size))
                goal = (pl.ds(p * size, size),) if dim == 0 else (slice(None), pl.ds(p * size, size))
                value = kept[k][place] + arrived[k][place].astype(jnp.float32)
                out_ref[goal] = value.astype(out_ref.dtype)


def halves(plan, together, bits, kept, arrived):
    shapes = []
    arrays = [kept[k] for k in range(len(plan))] if isinstance(kept, (list, tuple)) else kept
    for k, (dim, _, _) in enumerate(plan):
        shape = list(arrays[k].shape if isinstance(arrays, list) else arrays.shape[1:])
        shape[dim] //= 2
        shapes.append(tuple(shape))
    sds = jax.ShapeDtypeStruct
    if together:
        shape = (len(plan), *shapes[0])
        out = [sds(shape, jnp.bfloat16), sds(shape, jnp.float32)]
    else:
        out = [sds(shape, jnp.bfloat16) for shape in shapes] + [sds(shape, jnp.float32) for shape in shapes]
    operands = [*kept, *arrived] if isinstance(kept, (list, tuple)) else [kept, arrived]
    return call(
        functools.partial(halves_kernel, plan, together), out, bits, *operands, scalars=1, moved=2**20, limit=12
    )


def last_sum_kernel(kept_ref, arrived_ref, up_ref, down_ref):
    up_ref[...] = kept_ref[0] + arrived_ref[0].astype(jnp.float32)
    down_ref[...] = kept_ref[1] + arrived_ref[1].astype(jnp.float32)


def swapped(value, axis, bit):
    count = lax.axis_size(axis)
    return lax.ppermute(value, axis, [(i, i ^ (1 << bit)) for i in range(count)])


def projection_sums(narrow, grads, moved, hidden):
    channels, hid = narrow[0].shape[0], grads[0].shape[0]
    lon, lat = lax.axis_size("lon"), lax.axis_size("lat")
    if lat != 2 or lon != 16:
        lanes_both = (((1,), (1,)), ((), ()))
        dots = lambda left, right: sum(
            lax.dot_general(a, b, lanes_both, preferred_element_type=jnp.float32) for a, b in zip(left, right)
        )
        return scattered(dots(narrow, grads), False), scattered(dots(moved, hidden), True)
    here = lax.axis_index("lon")
    bits = jnp.stack([here >> k & 1 for k in range(4)] + [lax.axis_index("lat")]).astype(jnp.int32)
    sds = jax.ShapeDtypeStruct
    groups = lon // 2
    shape = (2, channels // 2, hid)
    send, keep = call(
        functools.partial(gradient_kernel, groups),
        [sds(shape, jnp.bfloat16), sds(shape, jnp.float32)],
        bits,
        *narrow,
        *grads,
        *moved,
        *hidden,
        scalars=1,
        flops=12 * 2**28,
        moved=6 * 2**20,
        limit=16,
    )
    arrived = swapped(send, "lon", 0)
    send_up, send_down, *keep = halves(((0, groups // 2, 1), (1, 1, 4)), False, bits, keep, arrived)
    arrived = [swapped(send_up, "lon", 1), swapped(send_down, "lat", 0)]
    send_up, send_down, *keep = halves(((1, 1, 4), (0, groups // 2, 1)), False, bits, keep, arrived)
    arrived = [swapped(send_up, "lat", 0), swapped(send_down, "lon", 1)]
    send, keep = halves(((0, groups // 4, 2), (0, groups // 4, 2)), True, bits, keep, arrived)
    arrived = swapped(send, "lon", 2)
    send, keep = halves(((0, groups // 8, 3), (0, groups // 8, 3)), True, bits, keep, arrived)
    arrived = swapped(send, "lon", 3)
    out = sds((channels // lon, hid // lat), jnp.float32)
    return call(last_sum_kernel, [out, out], keep, arrived, moved=2**18)


def local(cotangent, states, w_up, w_down, norm_gain, kernel, bilinear, lon_move, lat_move):
    steps, rows_out, cols_out, channels = states.shape
    tiles_lon, tiles_lat = lax.axis_size("lon"), lax.axis_size("lat")
    devices = tiles_lon * tiles_lat
    count = rows_out * cols_out
    tile = (rows_out, cols_out)
    share = channels // devices
    padded_share = -(-share // ROWS) * ROWS
    whole_share = share == padded_share
    group_size = channels // lon_move.shape[1]
    me = lax.axis_index("lon") * tiles_lat + lax.axis_index("lat")

    def as_blocks(value):
        value = value.reshape(devices, share, count)
        return value if whole_share else jnp.pad(value, ((0, 0), (0, padded_share - share), (0, 0)))

    def as_rows(blocks):
        return blocks[:, :share].reshape(channels, count)

    def as_grid(blocks):
        return blocks.reshape(tiles_lon, tiles_lat, *blocks.shape[1:])

    def as_pairs(blocks):
        if whole_share:
            return blocks
        parts = [blocks[:, :share], blocks[:, share:]]
        parts = [jnp.pad(part, ((0, 0), (0, padded_share - share), (0, 0))) for part in parts]
        return jnp.concatenate(parts, axis=1)

    def from_pairs(blocks):
        if whole_share:
            return blocks
        return jnp.concatenate([blocks[:, :share], blocks[:, padded_share : padded_share + share]], axis=1)

    arrived = as_grid(exchanged(packed(cotangent, bilinear, devices)))
    weights = arrived
    group = me * share // group_size
    moves = jnp.stack([lon_move[:, group], lat_move[:, group]], axis=1)
    grid_now = spatial("first", steps - 1, tile, padded_share, arrived, None, weights, moves[steps - 1])

    kern = lax.dynamic_slice_in_dim(kernel.reshape(9, channels), me * share, share, 1)
    kern = jnp.pad(kern, ((0, 0), (0, padded_share - share)))
    kern = jnp.broadcast_to(kern[:, :, None], (9, padded_share, count))

    padded = with_halo(with_halo(states, (("lon", 1),), 1, True), (("lat", 2),), 1, False)
    gain = norm_gain[:, None]
    taps = kernel.reshape(9, channels)
    w_up_t, w_down_t = w_up.T, w_down.T
    forward = {s: forward_parts(s, padded, taps, gain, w_up_t) for s in reversed(range(steps))}

    moved, grads, fields = {}, {}, {}
    term = None
    for s in reversed(range(steps)):
        moved[s] = as_rows(exchanged(grid_now.reshape(devices, padded_share, count)))
        narrow, normed, inv_root, hidden, slope = forward[s]
        common = (s, devices, moved[s], w_down_t, w_up, slope, normed, inv_root, gain, term)
        if s > 0:
            fields[s], grads[s], term = network_back(*common)
            arrived = as_grid(exchanged(as_blocks(fields[s])))
            grid_now = spatial("mid", s - 1, tile, padded_share, arrived, kern, weights, moves[s - 1])
        else:
            later = list(fields)
            sums = stencil_terms(later, padded, [fields[k] for k in later])
            blocks, grads[s] = network_back(*common, padded, sums)
            arrived = as_grid(exchanged(as_pairs(blocks)))
            grid_now = spatial("last", None, tile, padded_share, arrived, kern, None, None)

    arrived = exchanged(grid_now.reshape(devices, 2 * padded_share, count))
    grad_state, sums = final_parts(from_pairs(arrived), channels)
    order = list(reversed(range(steps)))
    grad_up, grad_down = projection_sums(
        [forward[s][0] for s in order],
        [grads[s] for s in order],
        [moved[s] for s in order],
        [forward[s][3] for s in order],
    )
    grad_kernel = sums[:9].reshape(kernel.shape)
    return (grad_state.reshape(cotangent.shape), grad_up, grad_down, grad_kernel, sums[9])


def solution(mesh):
    placed = (
        P("lon", "lat", None),
        P(None, "lon", "lat", None),
        P(),
        P(),
        P(),
        P(),
        P(None, None, "lon", "lat"),
        P(),
        P(),
    )
    return jax.shard_map(
        local,
        mesh=mesh,
        in_specs=placed,
        out_specs=(P("lon", "lat", None), P("lon", "lat"), P("lon", "lat"), P(), P()),
        check_vma=False,
    )
```

time: 189 us -> 157 us (0.83)
  matrix products: 17.5 us -> 0 us
  Pallas kernels: 15.2 us -> 27.7 us
  local copies, waits for them, and re-layouts: 42.5 us -> 30.7 us
  starting transfers between devices: 62.3 us -> 51.3 us
  blocking collectives: 0 us -> 10.6 us
  waiting for transfers between devices: 42 us -> 32.6 us
  other arithmetic: 7.24 us -> 1.64 us
    dot_general x6 -> x0, matrix products: 17.5 us -> none  [the longest x3 9.28 us: local(): lax.dot_general(narrow[s], grad_pre, lanes_both, preferred_element_type=j...]
    pallas_call x7 -> x19, Pallas kernels: 12.4 us -> 27.7 us  [call(): pl.pallas_call(kernel, out_shape=out_shape, in_specs=[pl.BlockSpec(memory...]
    all_to_all x0 -> x1, blocking collectives: none -> 10.6 us  [exchanged(): return lax.all_to_all(blocks, AXES, split_axis=0, concat_axis=0, tiled=True)]
    all_to_all x9 -> x7, waiting for transfers between devices: 29.7 us -> 19.7 us  [exchanged(): return lax.all_to_all(blocks, AXES, split_axis=0, concat_axis=0, tiled=True)]
    unnamed x93 -> x106, local copies, waits for them, and re-layouts: 16.9 us -> 26.7 us
    reshape x5 -> x1, local copies, waits for them, and re-layouts: 9.82 us -> 0.01 us  [local(): taps = kernel.reshape(9, channels)]
    all_to_all x9 -> x7, starting transfers between devices: 37.7 us -> 28.7 us  [exchanged(): return lax.all_to_all(blocks, AXES, split_axis=0, concat_axis=0, tiled=True)]
    dynamic_slice x4 -> x0, local copies, waits for them, and re-layouts: 5.17 us -> none  [the longest x2 3.47 us: halved(): lax.dynamic_index_in_dim(value, 1 - mine, dim, keepdims=False)]
  transfers between devices with their start and end apart: 23 -> 18, of which waited for: 10 -> 10; matrix products, arithmetic and copies ran while one was open for 28% -> 5% of each run, Pallas kernels for 3% -> 6%
where the time goes in v2:
time: 157 us; the launch traced here: 156 us
  starting transfers between devices  51.3 us (33%)
  waiting for transfers between devices  32.6 us (21%)
  local copies, waits for them, and re-layouts  30.7 us (20%)
  Pallas kernels  27.7 us (18%)
  blocking collectives  10.6 us (7%)
  other arithmetic  1.64 us (1%)
    all_to_all x7, starting transfers between devices, exchanged(): return lax.all_to_all(blocks, AXES, split_axis=0, concat_axis=0, tiled=True)  28.7 us
    pallas_call x19, Pallas kernels, call(): pl.pallas_call(kernel, out_shape=out_shape, in_specs=[pl.BlockSpec(memory...  27.7 us
    unnamed x106, local copies, waits for them, and re-layouts  26.7 us
    all_to_all x7, waiting for transfers between devices, exchanged(): return lax.all_to_all(blocks, AXES, split_axis=0, concat_axis=0, tiled=True)  19.7 us
    ppermute x7, starting transfers between devices, swapped(): return lax.ppermute(value, axis, [(i, i ^ 1 << bit) for i in range(count)])  11.1 us
    all_to_all x1, blocking collectives, exchanged(): return lax.all_to_all(blocks, AXES, split_axis=0, concat_axis=0, tiled=True)  10.6 us
    ppermute x7, waiting for transfers between devices, swapped(): return lax.ppermute(value, axis, [(i, i ^ 1 << bit) for i in range(count)])  8.67 us
    ppermute x2, starting transfers between devices, with_halo(): lax.ppermute(lax.slice_in_dim(block, block.shape[dim] - width, None, axis...  6.05 us
  transfers between devices with their start and end apart: 18, of which 10 were waited for; matrix products, arithmetic and copies ran while one was open for 5% of the time, Pallas kernels for 6%

profile of v2, /device:TPU:0, one launch (start us, length us, event | category | flops | bytes accessed | tf_op | source)
XLA Modules:
  0.0 155.7 jit_solution(5385935876360981207)
XLA Ops:
  3.2 7.3 %all-to-all-start = ((bf16[32,32,128]{2,1,0:T(8,128)(2,1)}), bf16[32,32,128]{2,1,0:T(8,128)(2,1)S(1)}, u32[]{:S(2)}, u32[]{:S(2)}) async-start(bf16[32,32,128]{2,1,0:T(8,128)(2,1)} %shard_map.128), calls=%async_computation | async-start | bytes 524288 | tf_op jit(solution)/shard_map/all_to_all | solution.py:33
  11.6 4.2 %collective-permute-start.1 = (bf16[3,1,16,512]{3,2,1,0:T(8,128)(2,1)S(1)}, bf16[3,1,16,512]{3,2,1,0:T(8,128)(2,1)S(1)}, u32[]{:S(2)}, u32[]{:S(2)}) collective-permute-start(bf16[3,1,16,512]{3,2,1,0:T(8,128)(2,1)S(1)} %get-tuple-element.89), channel_id=1, source_target_pairs={{2,0},{4,2},{6,4},{8,6},{10,8},{12,10},{14,12},{16,14},{18,16},{20... | collective-permute-start | bytes 147464 | tf_op jit(solution)/shard_map/ppermute | solution.py:27
  16.7 4.2 %collective-permute-done = bf16[3,1,16,512]{3,2,1,0:T(8,128)(2,1)S(1)} collective-permute-done((bf16[3,1,16,512]{3,2,1,0:T(8,128)(2,1)S(1)}, bf16[3,1,16,512]{3,2,1,0:T(8,128)(2,1)S(1)}, u32[]{:S(2)}, u32[]{:S(2)}) %collective-permute-start) | collective-permute-done | bytes 49184 | tf_op jit(solution)/shard_map/ppermute | solution.py:24
  21.6 1.7 %shard_map.129 = bf16[16,2,16,128]{3,2,1,0:T(8,128)(2,1)} custom-call(s32[2]{0:T(128)S(1)} %get-tuple-element.91.refs_0_, bf16[16,2,32,128]{3,2,1,0:T(8,128)(2,1)S(1)} %bitcast.38, bf16[16,2,32,128]{3,2,1,0:T(8,128)(2,1)S(1)} %bitcast.39), custom_call_target="tpu_custom_call" | custom-call | flops 4194304 | bytes 1048576 | tf_op jit(solution)/shard_map/pallas_call | solution.py:38
  23.3 3.4 %all-to-all-start.1 = ((bf16[32,16,128]{2,1,0:T(8,128)(2,1)}), bf16[32,16,128]{2,1,0:T(8,128)(2,1)}, u32[]{:S(2)}, u32[]{:S(2)}) async-start(bf16[32,16,128]{2,1,0:T(8,128)(2,1)} %bitcast.6), calls=%async_computation.1 | async-start | bytes 262144 | tf_op jit(solution)/shard_map/all_to_all | solution.py:33
  28.7 5.8 %collective-permute-start.2 = (bf16[3,10,1,512]{3,2,1,0:T(2,128)(2,1)S(1)}, bf16[3,10,1,512]{3,2,1,0:T(2,128)(2,1)}, u32[]{:S(2)}, u32[]{:S(2)}) collective-permute-start(bf16[3,10,1,512]{3,2,1,0:T(2,128)(2,1)S(1)} %get-tuple-element.87), channel_id=1, source_target_pairs={{0,1},{2,3},{4,5},{6,7},{8,9},{10,11},{12,13},{14,15},{16,17},{18,... | collective-permute-start | bytes 92168 | tf_op jit(solution)/shard_map/ppermute | solution.py:24
  36.6 1.6 %pad_maximum_fusion.padded_ref.refs_0_.refs_8_ = bf16[3,10,18,512]{3,2,1,0:T(8,128)(2,1)S(1)} fusion(bf16[3,10,1,512]{3,2,1,0:T(2,128)(2,1)} %collective-permute-done.3, bf16[3,10,16,512]{3,2,1,0:T(8,128)(2,1)} %copy-done.47, bf16[3,10,1,512]{3,2,1,0:T(2,128)(2,1)} %collective-permute-done.2), kind=kLoop, calls=%fused_computation | loop fusion | flops 1658880 | bytes 1105920 | tf_op jit(solution)/shard_map/concatenate | solution.py:28
  44.0 2.1 %shard_map.131 = (bf16[512,128]{1,0:T(8,128)(2,1)S(1)}, bf16[1024,128]{1,0:T(8,128)(2,1)S(1)}, f32[512,128]{1,0:T(8,128)S(1)}) custom-call(bf16[512,128]{1,0:T(8,128)(2,1)} %bitcast.7.refs_0_.refs_6_, bf16[1024,512]{1,0:T(8,128)(2,1)S(1)} %bitcast.32, bf16[512,1024]{1,0:T(8,128)(2,1)S(1)} %copy-done, f32[1024,128]{1,0:T(8,128)S(1)} %copy-done.11, ...), custom_call_target="tpu_custom_call" | custom-call | flops 268435456 | bytes 4194304 | tf_op jit(solution)/shard_map/pallas_call | solution.py:38
  48.2 5.9 %all-to-all-start.2 = ((bf16[32,16,128]{2,1,0:T(8,128)(2,1)}), bf16[32,16,128]{2,1,0:T(8,128)(2,1)}, u32[]{:S(2)}, u32[]{:S(2)}) async-start(bf16[32,16,128]{2,1,0:T(8,128)(2,1)} %bitcast.48), calls=%async_computation.2 | async-start | bytes 262144 | tf_op jit(solution)/shard_map/all_to_all | solution.py:33
  54.2 8.5 %all-to-all-done.2 = bf16[32,16,128]{2,1,0:T(8,128)(2,1)} async-done(((bf16[32,16,128]{2,1,0:T(8,128)(2,1)}), bf16[32,16,128]{2,1,0:T(8,128)(2,1)}, u32[]{:S(2)}, u32[]{:S(2)}) %all-to-all-start.2) | async-done | bytes 131104 | tf_op jit(solution)/shard_map/all_to_all | solution.py:33
  62.8 2.7 %shard_map.132 = bf16[16,2,16,128]{3,2,1,0:T(8,128)(2,1)S(1)} custom-call(s32[2]{0:T(128)S(1)} %get-tuple-element.92.refs_0_, bf16[16,2,16,128]{3,2,1,0:T(8,128)(2,1)} %bitcast.12.refs_1_, f32[9,16,128]{2,1,0:T(8,128)S(1)} %broadcast_in_dim.10.refs_2_.refs_1_, bf16[16,2,32,128]{3,2,1,0:T(8,128)(2,1)S(1)} %bitcast.40), custom_call_target="tpu_custom_call" | custom-call | flops 4194304 | bytes 1048576 | tf_op jit(solution)/shard_map/pallas_call | solution.py:38
  66.2 3.3 %all-to-all-start.3 = ((bf16[32,16,128]{2,1,0:T(8,128)(2,1)}), bf16[32,16,128]{2,1,0:T(8,128)(2,1)}, u32[]{:S(2)}, u32[]{:S(2)}) async-start(bf16[32,16,128]{2,1,0:T(8,128)(2,1)} %bitcast.46), calls=%async_computation.3 | async-start | bytes 262144 | tf_op jit(solution)/shard_map/all_to_all | solution.py:33
  74.5 3.6 %all-to-all-done.3 = bf16[32,16,128]{2,1,0:T(8,128)(2,1)} async-done(((bf16[32,16,128]{2,1,0:T(8,128)(2,1)}), bf16[32,16,128]{2,1,0:T(8,128)(2,1)}, u32[]{:S(2)}, u32[]{:S(2)}) %all-to-all-start.3) | async-done | bytes 131104 | tf_op jit(solution)/shard_map/all_to_all | solution.py:33
  81.1 2.1 %shard_map.134 = (bf16[512,128]{1,0:T(8,128)(2,1)S(1)}, bf16[1024,128]{1,0:T(8,128)(2,1)S(1)}, f32[512,128]{1,0:T(8,128)S(1)}) custom-call(bf16[512,128]{1,0:T(8,128)(2,1)} %bitcast.14.refs_0_.refs_7_, bf16[1024,512]{1,0:T(8,128)(2,1)S(1)} %bitcast.33, bf16[512,1024]{1,0:T(8,128)(2,1)S(1)} %copy-done, f32[1024,128]{1,0:T(8,128)S(1)} %copy-done.17, ...), custom_call_target="tpu_custom_call" | custom-call | flops 268435456 | bytes 4194304 | tf_op jit(solution)/shard_map/pallas_call | solution.py:38
  83.3 10.6 %all_to_all.40 = bf16[32,16,128]{2,1,0:T(8,128)(2,1)S(1)} all-to-all(bf16[32,16,128]{2,1,0:T(8,128)(2,1)S(1)} %bitcast.49), channel_id=1, replica_groups=mesh['lon'=16,'lat'=2] {'lon','lat'}, dimensions={0} | all-to-all | bytes 262144 | tf_op jit(solution)/shard_map/all_to_all | solution.py:33
  93.9 2.4 %shard_map.135 = bf16[16,2,16,128]{3,2,1,0:T(8,128)(2,1)S(1)} custom-call(s32[2]{0:T(128)S(1)} %get-tuple-element.93.refs_0_, bf16[16,2,16,128]{3,2,1,0:T(8,128)(2,1)S(1)} %bitcast.47, f32[9,16,128]{2,1,0:T(8,128)S(1)} %broadcast_in_dim.10.refs_2_.refs_1_, bf16[16,2,32,128]{3,2,1,0:T(8,128)(2,1)S(1)} %bitcast.41), custom_call_target="tpu_custom_call" | custom-call | flops 4194304 | bytes 1048576 | tf_op jit(solution)/shard_map/pallas_call | solution.py:38
  96.9 2.9 %all-to-all-start.5 = ((bf16[32,16,128]{2,1,0:T(8,128)(2,1)}), bf16[32,16,128]{2,1,0:T(8,128)(2,1)S(1)}, u32[]{:S(2)}, u32[]{:S(2)}) async-start(bf16[32,16,128]{2,1,0:T(8,128)(2,1)} %bitcast.45), calls=%async_computation.5 | async-start | bytes 262144 | tf_op jit(solution)/shard_map/all_to_all | solution.py:33
  105.7 2.5 %all-to-all-done.5 = bf16[32,16,128]{2,1,0:T(8,128)(2,1)S(1)} async-done(((bf16[32,16,128]{2,1,0:T(8,128)(2,1)}), bf16[32,16,128]{2,1,0:T(8,128)(2,1)S(1)}, u32[]{:S(2)}, u32[]{:S(2)}) %all-to-all-start.5) | async-done | bytes 131104 | tf_op jit(solution)/shard_map/all_to_all | solution.py:33
  111.2 2.6 %shard_map.138 = (bf16[32,32,128]{2,1,0:T(8,128)(2,1)}, bf16[1024,128]{1,0:T(8,128)(2,1)S(1)}) custom-call(bf16[512,128]{1,0:T(8,128)(2,1)S(1)} %bitcast.43, bf16[1024,512]{1,0:T(8,128)(2,1)S(1)} %bitcast.34, bf16[512,1024]{1,0:T(8,128)(2,1)S(1)} %copy-done, f32[1024,128]{1,0:T(8,128)S(1)} %copy-done.5, f32[512,128]{1,0:T(8,128)S(1)} %copy-done.21, ...), custom_call_target="tpu_custom_call" | custom-call | flops 268435456 | bytes 4194304 | tf_op jit(solution)/shard_map/pallas_call | solution.py:38
  113.9 3.0 %shard_map.141 = (bf16[2,256,1024]{2,1,0:T(8,128)(2,1)}, f32[2,256,1024]{2,1,0:T(8,128)S(1)}) custom-call(s32[5]{0:T(128)S(1)} %stack.27.bit_ref, bf16[512,128]{1,0:T(8,128)(2,1)S(1)} %copy-done.41, bf16[512,128]{1,0:T(8,128)(2,1)S(1)} %copy-done.43, bf16[512,128]{1,0:T(8,128)(2,1)S(1)} %copy-done.45, bf16[1024,128]{1,0:T(8,128)(2,1)S(1)} %copy-done.33, ...), custom_call_target="tpu_custom_call" | custom-call | flops 3221225472 | bytes 6291456 | tf_op jit(solution)/shard_map/pallas_call | solution.py:38
  116.9 3.3 %all-to-all-start.6 = ((bf16[32,32,128]{2,1,0:T(8,128)(2,1)}), bf16[32,32,128]{2,1,0:T(8,128)(2,1)S(1)}, u32[]{:S(2)}, u32[]{:S(2)}) async-start(bf16[32,32,128]{2,1,0:T(8,128)(2,1)} %get-tuple-element.59), calls=%async_computation.6 | async-start | bytes 524288 | tf_op jit(solution)/shard_map/all_to_all | solution.py:33
  120.2 2.2 %shard_map.142 = (bf16[128,1024]{1,0:T(8,128)(2,1)}, bf16[256,512]{1,0:T(8,128)(2,1)}, f32[128,1024]{1,0:T(8,128)S(1)}, f32[256,512]{1,0:T(8,128)S(1)}) custom-call(s32[5]{0:T(128)S(1)} %stack.27.bit_ref, f32[2,256,1024]{2,1,0:T(8,128)S(1)} %get-tuple-element.70.refs_0_, bf16[2,256,1024]{2,1,0:T(8,128)(2,1)} %collective-permute-done.4.refs_1_), custom_call_target="tpu_custom_call" | custom-call | bytes 1048576 | tf_op jit(solution)/shard_map/pallas_call | solution.py:38
  123.2 1.8 %collective-permute-start.5 = (bf16[128,1024]{1,0:T(8,128)(2,1)}, bf16[128,1024]{1,0:T(8,128)(2,1)S(1)}, u32[]{:S(2)}, u32[]{:S(2)}) collective-permute-start(bf16[128,1024]{1,0:T(8,128)(2,1)} %get-tuple-element.74), channel_id=1, source_target_pairs={{0,4},{2,6},{4,0},{6,2},{8,12},{10,14},{12,8},{14,10},{16,20},{18,... | collective-permute-start | bytes 786440 | tf_op jit(solution)/shard_map/ppermute | solution.py:546
  125.0 1.5 collective-permute-start.6
  126.4 4.4 %all-to-all-done.6 = bf16[32,32,128]{2,1,0:T(8,128)(2,1)S(1)} async-done(((bf16[32,32,128]{2,1,0:T(8,128)(2,1)}), bf16[32,32,128]{2,1,0:T(8,128)(2,1)S(1)}, u32[]{:S(2)}, u32[]{:S(2)}) %all-to-all-start.6) | async-done | bytes 262176 | tf_op jit(solution)/shard_map/all_to_all | solution.py:33
  132.0 2.6 %all-to-all-start.7 = ((bf16[32,32,128]{2,1,0:T(8,128)(2,1)}), bf16[32,32,128]{2,1,0:T(8,128)(2,1)S(1)}, u32[]{:S(2)}, u32[]{:S(2)}) async-start(bf16[32,32,128]{2,1,0:T(8,128)(2,1)} %bitcast.20), calls=%async_computation.7 | async-start | bytes 524288 | tf_op jit(solution)/shard_map/all_to_all | solution.py:33
  135.2 1.7 %collective-permute-start.7 = (bf16[128,512]{1,0:T(8,128)(2,1)S(1)}, bf16[128,512]{1,0:T(8,128)(2,1)S(1)}, u32[]{:S(2)}, u32[]{:S(2)}) collective-permute-start(bf16[128,512]{1,0:T(8,128)(2,1)S(1)} %get-tuple-element.78), channel_id=1, source_target_pairs={{0,1},{1,0},{2,3},{3,2},{4,5},{5,4},{6,7},{7,6},{8,9},{9,8},{10,11... | collective-permute-start | bytes 393224 | tf_op jit(solution)/shard_map/ppermute | solution.py:546
  136.9 1.5 collective-permute-start.8
  138.4 4.2 %collective-permute-done.7.refs_2_ = bf16[128,512]{1,0:T(8,128)(2,1)S(1)} collective-permute-done((bf16[128,512]{1,0:T(8,128)(2,1)S(1)}, bf16[128,512]{1,0:T(8,128)(2,1)S(1)}, u32[]{:S(2)}, u32[]{:S(2)}) %collective-permute-start.7) | collective-permute-done | bytes 131104 | tf_op jit(solution)/shard_map/ppermute | solution.py:546
  144.0 1.8 %collective-permute-start.9 = (bf16[2,64,512]{2,1,0:T(8,128)(2,1)S(1)}, bf16[2,64,512]{2,1,0:T(8,128)(2,1)S(1)}, u32[]{:S(2)}, u32[]{:S(2)}) collective-permute-start(bf16[2,64,512]{2,1,0:T(8,128)(2,1)S(1)} %get-tuple-element.81), channel_id=1, source_target_pairs={{0,8},{2,10},{4,12},{6,14},{8,0},{10,2},{12,4},{14,6},{16,24},{18,... | collective-permute-start | bytes 393224 | tf_op jit(solution)/shard_map/ppermute | solution.py:546
  145.8 3.2 %collective-permute-done.9.refs_1_ = bf16[2,64,512]{2,1,0:T(8,128)(2,1)S(1)} collective-permute-done((bf16[2,64,512]{2,1,0:T(8,128)(2,1)S(1)}, bf16[2,64,512]{2,1,0:T(8,128)(2,1)S(1)}, u32[]{:S(2)}, u32[]{:S(2)}) %collective-permute-start.9) | collective-permute-done | bytes 131104 | tf_op jit(solution)/shard_map/ppermute | solution.py:546
  149.6 2.9 %collective-permute-start.10 = (bf16[2,32,512]{2,1,0:T(8,128)(2,1)S(1)}, bf16[2,32,512]{2,1,0:T(8,128)(2,1)S(1)}, u32[]{:S(2)}, u32[]{:S(2)}) collective-permute-start(bf16[2,32,512]{2,1,0:T(8,128)(2,1)S(1)} %get-tuple-element.83), channel_id=1, source_target_pairs={{0,16},{2,18},{4,20},{6,22},{8,24},{10,26},{12,28},{14,30},{16,0},... | collective-permute-start | bytes 196616 | tf_op jit(solution)/shard_map/ppermute | solution.py:546
  (144 shorter events, 43.0 us)
Async XLA Ops:
  2.3 18.5 %copy-start.48 = (bf16[3,8,16,512]{3,2,1,0:T(8,128)(2,1)S(1)}, bf16[3,8,16,512]{3,2,1,0:T(8,128)(2,1)}, u32[]{:S(2)}) copy-start(bf16[3,8,16,512]{3,2,1,0:T(8,128)(2,1)} %param.10) | copy-start | bytes 1179652
  3.2 31.3 %copy-start.46 = (bf16[512,1024]{1,0:T(8,128)(2,1)S(1)}, bf16[512,1024]{1,0:T(8,128)(2,1)}, u32[]{:S(2)}) copy-start(bf16[512,1024]{1,0:T(8,128)(2,1)} %param.12) | copy-start | bytes 3145732
  3.2 18.4 %all-to-all-start = ((bf16[32,32,128]{2,1,0:T(8,128)(2,1)}), bf16[32,32,128]{2,1,0:T(8,128)(2,1)S(1)}, u32[]{:S(2)}, u32[]{:S(2)}) async-start(bf16[32,32,128]{2,1,0:T(8,128)(2,1)} %shard_map.128), calls=%async_computation | async-start | bytes 524288 | tf_op jit(solution)/shard_map/all_to_all | solution.py:33
  11.3 9.5 %collective-permute-start = (bf16[3,1,16,512]{3,2,1,0:T(8,128)(2,1)S(1)}, bf16[3,1,16,512]{3,2,1,0:T(8,128)(2,1)S(1)}, u32[]{:S(2)}, u32[]{:S(2)}) collective-permute-start(bf16[3,1,16,512]{3,2,1,0:T(8,128)(2,1)S(1)} %get-tuple-element.90), channel_id=1, source_target_pairs={{0,2},{2,4},{4,6},{6,8},{8,10},{10,12},{12,14},{14,16},{16,18},{18... | collective-permute-start | bytes 147464 | tf_op jit(solution)/shard_map/ppermute | solution.py:24
  11.6 9.3 %collective-permute-start.1 = (bf16[3,1,16,512]{3,2,1,0:T(8,128)(2,1)S(1)}, bf16[3,1,16,512]{3,2,1,0:T(8,128)(2,1)S(1)}, u32[]{:S(2)}, u32[]{:S(2)}) collective-permute-start(bf16[3,1,16,512]{3,2,1,0:T(8,128)(2,1)S(1)} %get-tuple-element.89), channel_id=1, source_target_pairs={{2,0},{4,2},{6,4},{8,6},{10,8},{12,10},{14,12},{16,14},{18,16},{20... | collective-permute-start | bytes 147464 | tf_op jit(solution)/shard_map/ppermute | solution.py:27
  20.9 7.8 %copy-start.47 = (bf16[3,10,16,512]{3,2,1,0:T(8,128)(2,1)}, bf16[3,10,16,512]{3,2,1,0:T(8,128)(2,1)S(1)}, u32[]{:S(2)}) copy-start(bf16[3,10,16,512]{3,2,1,0:T(8,128)(2,1)S(1)} %constant_dynamic-update-slice_fusion) | copy-start | bytes 1474564
  21.6 13.5 %copy-start.49 = (f32[3,3,512]{2,1,0:T(4,128)S(1)}, f32[3,3,512]{2,1,0:T(4,128)}, u32[]{:S(2)}) copy-start(f32[3,3,512]{2,1,0:T(4,128)} %param.14) | copy-start | bytes 55300
  23.3 11.8 %copy-start.50 = (f32[512]{0:T(512)S(1)}, f32[512]{0:T(512)}, u32[]{:S(2)}) copy-start(f32[512]{0:T(512)} %param.13) | copy-start | bytes 6148
  23.3 12.0 %copy-start = (bf16[512,1024]{1,0:T(8,128)(2,1)S(1)}, bf16[512,1024]{1,0:T(8,128)(2,1)}, u32[]{:S(2)}) copy-start(bf16[512,1024]{1,0:T(8,128)(2,1)} %refs_2_.5) | copy-start | bytes 3145732
  23.3 18.7 %all-to-all-start.1 = ((bf16[32,16,128]{2,1,0:T(8,128)(2,1)}), bf16[32,16,128]{2,1,0:T(8,128)(2,1)}, u32[]{:S(2)}, u32[]{:S(2)}) async-start(bf16[32,16,128]{2,1,0:T(8,128)(2,1)} %bitcast.6), calls=%async_computation.1 | async-start | bytes 262144 | tf_op jit(solution)/shard_map/all_to_all | solution.py:33
  27.4 9.1 %collective-permute-start.3 = (bf16[3,10,1,512]{3,2,1,0:T(2,128)(2,1)}, bf16[3,10,1,512]{3,2,1,0:T(2,128)(2,1)}, u32[]{:S(2)}, u32[]{:S(2)}) collective-permute-start(bf16[3,10,1,512]{3,2,1,0:T(2,128)(2,1)} %get-tuple-element.88), channel_id=1, source_target_pairs={{1,0},{3,2},{5,4},{7,6},{9,8},{11,10},{13,12},{15,14},{17,16},{19,... | collective-permute-start | bytes 92168 | tf_op jit(solution)/shard_map/ppermute | solution.py:27
  28.7 7.8 %collective-permute-start.2 = (bf16[3,10,1,512]{3,2,1,0:T(2,128)(2,1)S(1)}, bf16[3,10,1,512]{3,2,1,0:T(2,128)(2,1)}, u32[]{:S(2)}, u32[]{:S(2)}) collective-permute-start(bf16[3,10,1,512]{3,2,1,0:T(2,128)(2,1)S(1)} %get-tuple-element.87), channel_id=1, source_target_pairs={{0,1},{2,3},{4,5},{6,7},{8,9},{10,11},{12,13},{14,15},{16,17},{18,... | collective-permute-start | bytes 92168 | tf_op jit(solution)/shard_map/ppermute | solution.py:24
  48.2 14.5 %all-to-all-start.2 = ((bf16[32,16,128]{2,1,0:T(8,128)(2,1)}), bf16[32,16,128]{2,1,0:T(8,128)(2,1)}, u32[]{:S(2)}, u32[]{:S(2)}) async-start(bf16[32,16,128]{2,1,0:T(8,128)(2,1)} %bitcast.48), calls=%async_computation.2 | async-start | bytes 262144 | tf_op jit(solution)/shard_map/all_to_all | solution.py:33
  66.2 11.9 %all-to-all-start.3 = ((bf16[32,16,128]{2,1,0:T(8,128)(2,1)}), bf16[32,16,128]{2,1,0:T(8,128)(2,1)}, u32[]{:S(2)}, u32[]{:S(2)}) async-start(bf16[32,16,128]{2,1,0:T(8,128)(2,1)} %bitcast.46), calls=%async_computation.3 | async-start | bytes 262144 | tf_op jit(solution)/shard_map/all_to_all | solution.py:33
  83.2 13.0 %copy-start.14 = (bf16[512,128]{1,0:T(8,128)(2,1)}, bf16[512,128]{1,0:T(8,128)(2,1)S(1)}, u32[]{:S(2)}) copy-start(bf16[512,128]{1,0:T(8,128)(2,1)S(1)} %get-tuple-element.54.refs_2_) | copy-start | bytes 393220
  83.2 13.0 %copy-start.18 = (f32[512,128]{1,0:T(8,128)}, f32[512,128]{1,0:T(8,128)S(1)}, u32[]{:S(2)}) copy-start(f32[512,128]{1,0:T(8,128)S(1)} %get-tuple-element.58.refs_7_) | copy-start | bytes 786436
  83.2 13.0 %copy-start.36 = (bf16[1024,128]{1,0:T(8,128)(2,1)}, bf16[1024,128]{1,0:T(8,128)(2,1)S(1)}, u32[]{:S(2)}) copy-start(bf16[1024,128]{1,0:T(8,128)(2,1)S(1)} %get-tuple-element.65.refs_4_) | copy-start | bytes 786436
  96.9 8.0 %copy-start.13 = (bf16[512,128]{1,0:T(8,128)(2,1)S(1)}, bf16[512,128]{1,0:T(8,128)(2,1)}, u32[]{:S(2)}) copy-start(bf16[512,128]{1,0:T(8,128)(2,1)} %copy-done.12) | copy-start | bytes 393220
  96.9 11.3 %all-to-all-start.5 = ((bf16[32,16,128]{2,1,0:T(8,128)(2,1)}), bf16[32,16,128]{2,1,0:T(8,128)(2,1)S(1)}, u32[]{:S(2)}, u32[]{:S(2)}) async-start(bf16[32,16,128]{2,1,0:T(8,128)(2,1)} %bitcast.45), calls=%async_computation.5 | async-start | bytes 262144 | tf_op jit(solution)/shard_map/all_to_all | solution.py:33
  101.1 3.8 %copy-start.15 = (bf16[512,128]{1,0:T(8,128)(2,1)S(1)}, bf16[512,128]{1,0:T(8,128)(2,1)}, u32[]{:S(2)}) copy-start(bf16[512,128]{1,0:T(8,128)(2,1)} %copy-done.14) | copy-start | bytes 393220
  111.2 2.7 %copy-start.39 = (bf16[1024,128]{1,0:T(8,128)(2,1)S(1)}, bf16[1024,128]{1,0:T(8,128)(2,1)}, u32[]{:S(2)}) copy-start(bf16[1024,128]{1,0:T(8,128)(2,1)} %copy-done.38) | copy-start | bytes 786436
  111.2 2.7 %copy-start.41 = (bf16[512,128]{1,0:T(8,128)(2,1)S(1)}, bf16[512,128]{1,0:T(8,128)(2,1)}, u32[]{:S(2)}) copy-start(bf16[512,128]{1,0:T(8,128)(2,1)} %copy-done.40) | copy-start | bytes 393220
  116.9 3.3 %collective-permute-start.4 = (bf16[2,256,1024]{2,1,0:T(8,128)(2,1)}, bf16[2,256,1024]{2,1,0:T(8,128)(2,1)}, u32[]{:S(2)}, u32[]{:S(2)}) collective-permute-start(bf16[2,256,1024]{2,1,0:T(8,128)(2,1)} %get-tuple-element.71), channel_id=1, source_target_pairs={{0,2},{2,0},{4,6},{6,4},{8,10},{10,8},{12,14},{14,12},{16,18},{18,... | collective-permute-start | bytes 3145736 | tf_op jit(solution)/shard_map/ppermute | solution.py:546
  116.9 14.0 %all-to-all-start.6 = ((bf16[32,32,128]{2,1,0:T(8,128)(2,1)}), bf16[32,32,128]{2,1,0:T(8,128)(2,1)S(1)}, u32[]{:S(2)}, u32[]{:S(2)}) async-start(bf16[32,32,128]{2,1,0:T(8,128)(2,1)} %get-tuple-element.59), calls=%async_computation.6 | async-start | bytes 524288 | tf_op jit(solution)/shard_map/all_to_all | solution.py:33
  123.2 11.4 %copy-start.7 = (f32[256,512]{1,0:T(8,128)S(1)}, f32[256,512]{1,0:T(8,128)}, u32[]{:S(2)}) copy-start(f32[256,512]{1,0:T(8,128)} %copy-done.6) | copy-start | bytes 1572868
  123.2 11.4 %collective-permute-start.5 = (bf16[128,1024]{1,0:T(8,128)(2,1)}, bf16[128,1024]{1,0:T(8,128)(2,1)S(1)}, u32[]{:S(2)}, u32[]{:S(2)}) collective-permute-start(bf16[128,1024]{1,0:T(8,128)(2,1)} %get-tuple-element.74), channel_id=1, source_target_pairs={{0,4},{2,6},{4,0},{6,2},{8,12},{10,14},{12,8},{14,10},{16,20},{18,... | collective-permute-start | bytes 786440 | tf_op jit(solution)/shard_map/ppermute | solution.py:546
  125.0 9.6 %collective-permute-start.6 = (bf16[256,512]{1,0:T(8,128)(2,1)}, bf16[256,512]{1,0:T(8,128)(2,1)S(1)}, u32[]{:S(2)}, u32[]{:S(2)}) collective-permute-start(bf16[256,512]{1,0:T(8,128)(2,1)} %get-tuple-element.75), channel_id=1, source_target_pairs={{0,1},{1,0},{2,3},{3,2},{4,5},{5,4},{6,7},{7,6},{8,9},{9,8},{10,11... | collective-permute-start | bytes 786440 | tf_op jit(solution)/shard_map/ppermute | solution.py:546
  132.0 20.5 %all-to-all-start.7 = ((bf16[32,32,128]{2,1,0:T(8,128)(2,1)}), bf16[32,32,128]{2,1,0:T(8,128)(2,1)S(1)}, u32[]{:S(2)}, u32[]{:S(2)}) async-start(bf16[32,32,128]{2,1,0:T(8,128)(2,1)} %bitcast.20), calls=%async_computation.7 | async-start | bytes 524288 | tf_op jit(solution)/shard_map/all_to_all | solution.py:33
  135.2 7.4 %collective-permute-start.7 = (bf16[128,512]{1,0:T(8,128)(2,1)S(1)}, bf16[128,512]{1,0:T(8,128)(2,1)S(1)}, u32[]{:S(2)}, u32[]{:S(2)}) collective-permute-start(bf16[128,512]{1,0:T(8,128)(2,1)S(1)} %get-tuple-element.78), channel_id=1, source_target_pairs={{0,1},{1,0},{2,3},{3,2},{4,5},{5,4},{6,7},{7,6},{8,9},{9,8},{10,11... | collective-permute-start | bytes 393224 | tf_op jit(solution)/shard_map/ppermute | solution.py:546
  136.9 6.5 %collective-permute-start.8 = (bf16[128,512]{1,0:T(8,128)(2,1)S(1)}, bf16[128,512]{1,0:T(8,128)(2,1)S(1)}, u32[]{:S(2)}, u32[]{:S(2)}) collective-permute-start(bf16[128,512]{1,0:T(8,128)(2,1)S(1)} %get-tuple-element.79), channel_id=1, source_target_pairs={{0,4},{2,6},{4,0},{6,2},{8,12},{10,14},{12,8},{14,10},{16,20},{18,... | collective-permute-start | bytes 393224 | tf_op jit(solution)/shard_map/ppermute | solution.py:546
  144.0 5.0 %collective-permute-start.9 = (bf16[2,64,512]{2,1,0:T(8,128)(2,1)S(1)}, bf16[2,64,512]{2,1,0:T(8,128)(2,1)S(1)}, u32[]{:S(2)}, u32[]{:S(2)}) collective-permute-start(bf16[2,64,512]{2,1,0:T(8,128)(2,1)S(1)} %get-tuple-element.81), channel_id=1, source_target_pairs={{0,8},{2,10},{4,12},{6,14},{8,0},{10,2},{12,4},{14,6},{16,24},{18,... | collective-permute-start | bytes 393224 | tf_op jit(solution)/shard_map/ppermute | solution.py:546
  149.6 5.3 %collective-permute-start.10 = (bf16[2,32,512]{2,1,0:T(8,128)(2,1)S(1)}, bf16[2,32,512]{2,1,0:T(8,128)(2,1)S(1)}, u32[]{:S(2)}, u32[]{:S(2)}) collective-permute-start(bf16[2,32,512]{2,1,0:T(8,128)(2,1)S(1)} %get-tuple-element.83), channel_id=1, source_target_pairs={{0,16},{2,18},{4,20},{6,22},{8,24},{10,26},{12,28},{14,30},{16,0},... | collective-permute-start | bytes 196616 | tf_op jit(solution)/shard_map/ppermute | solution.py:546
  (37 other events, 42.3 us)

commit v3 on v2

--- a/solution.py
+++ b/solution.py
@@ -14,36 +14,35 @@
 MIB = 1024 * 1024
 
 
-def with_halo(block, sides, width, periodic):
-    for axis, dim in sides:
-        count = lax.axis_size(axis)
-        forward = [(i, i + 1) for i in range(count - 1)]
-        if periodic:
-            forward.append((count - 1, 0))
-        backward = [(target, source) for source, target in forward]
-        low = lax.ppermute(
-            lax.slice_in_dim(block, block.shape[dim] - width, None, axis=dim), axis, forward
-        )
-        high = lax.ppermute(lax.slice_in_dim(block, 0, width, axis=dim), axis, backward)
-        block = jnp.concatenate([low, block, high], axis=dim)
-    return block
-
-
 def exchanged(blocks):
     return lax.all_to_all(blocks, AXES, split_axis=0, concat_axis=0, tiled=True)
 
 
-def call(kernel, out_shape, *operands, scratch=(), scalars=0, flops=0, moved=0, limit=8):
-    space = [pltpu.SMEM] * scalars + [pltpu.VMEM] * (len(operands) - scalars)
+SPACES = {"s": pltpu.SMEM, "v": pltpu.VMEM, "h": pltpu.HBM}
+
+
+def call(kernel, out_shape, operands, ins, outs, scratch=(), flops=0, moved=0, limit=8):
     return pl.pallas_call(
         kernel,
         out_shape=out_shape,
-        in_specs=[pl.BlockSpec(memory_space=kind) for kind in space],
-        out_specs=jax.tree.map(lambda _: pl.BlockSpec(memory_space=pltpu.VMEM), out_shape),
+        in_specs=[pl.BlockSpec(memory_space=SPACES[kind]) for kind in ins],
+        out_specs=[pl.BlockSpec(memory_space=SPACES[kind]) for kind in outs],
         scratch_shapes=scratch,
         compiler_params=pltpu.CompilerParams(vmem_limit_bytes=limit * MIB),
         cost_estimate=pl.CostEstimate(flops=flops, bytes_accessed=moved, transcendentals=0),
     )(*operands)
+
+
+def copies(sems, first, pairs):
+    started = [pltpu.make_async_copy(src, dst, sems.at[first + k]) for k, (src, dst) in enumerate(pairs)]
+    for copy in started:
+        copy.start()
+    return started
+
+
+def finish(started):
+    for copy in started:
+        copy.wait()
 
 
 def split_three(value, lane, width):
@@ -61,17 +60,21 @@
     return value + pltpu.roll(value, lanes - width, 1) + pltpu.roll(value, lanes - 2 * width, 1)
 
 
-def pack_kernel(cotangent_ref, weight_ref, out_ref):
+def pack_kernel(cotangent_hbm, weight_hbm, out_hbm, cotangent_ref, weight_ref, out_ref, sems):
+    started = copies(sems, 0, [(cotangent_hbm, cotangent_ref), (weight_hbm, weight_ref)])
     channels = cotangent_ref.shape[1]
     devices, _, count = out_ref.shape
     share = channels // devices
-    turned = cotangent_ref[...].astype(jnp.float32).T.astype(jnp.bfloat16)
-    out_ref[:, :share] = turned.reshape(devices, share, count)
+    started[1].wait()
     rows = weight_ref.shape[0]
     weights = jnp.concatenate([weight_ref[:, i] for i in range(weight_ref.shape[1])], axis=1)
     weights = jnp.concatenate([weights, jnp.zeros((ROWS - rows, count), jnp.float32)], axis=0)
     weights = weights.astype(jnp.bfloat16)
     out_ref[:, share:] = jnp.broadcast_to(weights[None], (devices, ROWS, count))
+    started[0].wait()
+    turned = cotangent_ref[...].astype(jnp.float32).T.astype(jnp.bfloat16)
+    out_ref[:, :share] = turned.reshape(devices, share, count)
+    finish(copies(sems, 2, [(out_ref, out_hbm)]))
 
 
 def packed(cotangent, bilinear, devices):
@@ -85,128 +88,210 @@
         weights = bilinear.reshape(steps * corners, count).astype(jnp.bfloat16)
         weights = jnp.pad(weights, ((0, ROWS - steps * corners), (0, 0)))
         return jnp.concatenate([blocks, jnp.broadcast_to(weights[None], (devices, ROWS, count))], axis=1)
+    shape = (devices, share + ROWS, count)
     return call(
         pack_kernel,
-        jax.ShapeDtypeStruct((devices, share + ROWS, count), jnp.bfloat16),
-        cotangent.reshape(count, channels),
-        bilinear.reshape(steps * corners, rows_out, cols_out),
+        [jax.ShapeDtypeStruct(shape, jnp.bfloat16)],
+        [cotangent.reshape(count, channels), bilinear.reshape(steps * corners, rows_out, cols_out)],
+        "hh",
+        "h",
+        scratch=[
+            pltpu.VMEM((count, channels), jnp.bfloat16),
+            pltpu.VMEM((steps * corners, rows_out, cols_out), jnp.float32),
+            pltpu.VMEM(shape, jnp.bfloat16),
+            pltpu.SemaphoreType.DMA((3,)),
+        ],
         moved=2**19,
+    )[0]
+
+
+def edges(states):
+    lon, lat = lax.axis_size("lon"), lax.axis_size("lat")
+    lat_at = lax.axis_index("lat")
+    ahead = lambda value: lax.ppermute(value, "lon", [(i, (i + 1) % lon) for i in range(lon)])
+    behind = lambda value: lax.ppermute(value, "lon", [(i, (i - 1) % lon) for i in range(lon)])
+    low, high = ahead(states[:, -1:]), behind(states[:, :1])
+
+    def sent(value, lon_by, pairs):
+        both = [
+            (i * lat + a, (i + lon_by) % lon * lat + b) for i in range(lon) for a, b in pairs
+        ]
+        return lax.ppermute(value, AXES, both)
+
+    def column(edge, pairs):
+        parts = [sent(edge[:, -1:], 1, pairs), sent(edge, 0, pairs), sent(edge[:, :1], -1, pairs)]
+        return jnp.concatenate(parts, axis=1)
+
+    first, last = states[:, :, :1], states[:, :, -1:]
+    if lat == 2:
+        arrived = column(jnp.where(lat_at == 0, last, first), [(0, 1), (1, 0)])
+        before, after = jnp.where(lat_at == 0, 0, arrived), jnp.where(lat_at == 0, arrived, 0)
+    else:
+        before = column(last, [(i, i + 1) for i in range(lat - 1)])
+        after = column(first, [(i + 1, i) for i in range(lat - 1)])
+    return low, high, before, after
+
+
+MARGIN = 8
+
+
+def forward_kernel(
+    states_hbm, low_ref, high_ref, before_ref, after_ref, kernel_ref, gain_ref, up_ref,
+    n_hbm, aux_hbm, hid_hbm, slope_hbm, pad_hbm,
+    states_ref, n_ref, aux_ref, hid_ref, slope_ref, pad_ref, sems,
+):
+    steps, rows_out, cols_out, channels = states_ref.shape
+    count = rows_out * cols_out
+    order = list(reversed(range(steps)))
+    arriving = copies(sems, 0, [(states_hbm.at[s], states_ref.at[s]) for s in order])
+    gain = jnp.broadcast_to(gain_ref[...], (count, channels)).T
+    leaving = []
+    for turn, s in enumerate(order):
+        arriving[turn].wait()
+        pad_ref[s, 1 : 1 + rows_out, MARGIN : MARGIN + cols_out] = states_ref[s].astype(jnp.float32)
+        pad_ref[s, :1, MARGIN : MARGIN + cols_out] = low_ref[s].astype(jnp.float32)
+        pad_ref[s, 1 + rows_out :, MARGIN : MARGIN + cols_out] = high_ref[s].astype(jnp.float32)
+        pad_ref[s, :, MARGIN - 1 : MARGIN] = before_ref[s].astype(jnp.float32)
+        pad_ref[s, :, MARGIN + cols_out : MARGIN + cols_out + 1] = after_ref[s].astype(jnp.float32)
+        mixed = pad_ref[s, 1 : 1 + rows_out, MARGIN : MARGIN + cols_out]
+        for col_tap in range(3):
+            place = MARGIN - 1 + col_tap
+            shifted_cols = pad_ref[s, :, place : place + cols_out]
+            for row_tap in range(3):
+                tap = kernel_ref[row_tap, col_tap : col_tap + 1]
+                mixed = mixed + tap[None] * shifted_cols[row_tap : row_tap + rows_out]
+        mixed = mixed.reshape(count, channels).T
+        inv_root = lax.rsqrt(jnp.mean(mixed * mixed, axis=0, keepdims=True) + EPSILON)
+        normed = mixed * inv_root
+        narrow = (normed * gain).astype(jnp.bfloat16)
+        pre = jnp.dot(up_ref[...], narrow, preferred_element_type=jnp.float32)
+        sigmoid = jax.nn.sigmoid(pre)
+        n_ref[s] = narrow
+        aux_ref[s, :channels] = normed
+        aux_ref[s, channels : 2 * channels] = gain
+        aux_ref[s, 2 * channels :] = jnp.broadcast_to(inv_root, (8, count))
+        hid_ref[s] = (pre * sigmoid).astype(jnp.bfloat16)
+        slope_ref[s] = sigmoid * (1.0 + pre * (1.0 - sigmoid))
+        pairs = [(slope_ref, slope_hbm), (aux_ref, aux_hbm), (n_ref, n_hbm), (hid_ref, hid_hbm), (pad_ref, pad_hbm)]
+        leaving += copies(sems, steps + 5 * turn, [(src.at[s], dst.at[s]) for src, dst in pairs])
+    finish(leaving)
+
+
+def forward_parts(states, around, kernel, norm_gain, w_up_t):
+    steps, rows_out, cols_out, channels = states.shape
+    hid = w_up_t.shape[0]
+    count = rows_out * cols_out
+    shapes = [
+        ((steps, channels, count), jnp.bfloat16),
+        ((steps, 2 * channels + 8, count), jnp.float32),
+        ((steps, hid, count), jnp.bfloat16),
+        ((steps, hid, count), jnp.float32),
+        ((steps, rows_out + 2, cols_out + 2 * MARGIN, channels), jnp.float32),
+    ]
+    return call(
+        forward_kernel,
+        [jax.ShapeDtypeStruct(*shape) for shape in shapes],
+        [states, *around, kernel, norm_gain.reshape(1, channels), w_up_t],
+        "hvvvvvvv",
+        "hhhhh",
+        scratch=[pltpu.VMEM(states.shape, jnp.bfloat16)]
+        + [pltpu.VMEM(*shape) for shape in shapes]
+        + [pltpu.SemaphoreType.DMA((6 * steps,))],
+        flops=2 * steps * count * hid * channels,
+        moved=2**23,
+        limit=20,
     )
 
 
-def forward_kernel(step, padded_ref, kernel_ref, gain_ref, up_ref, n_ref, normed_ref, inv_ref, hid_ref, slope_ref):
-    rows_out, cols_out = padded_ref.shape[1] - 2, padded_ref.shape[2] - 2
-    channels = padded_ref.shape[3]
-    padded = padded_ref[step].astype(jnp.float32)
-    mixed = padded[1 : 1 + rows_out, 1 : 1 + cols_out]
-    running = jnp.zeros_like(mixed)
-    for col_tap in range(3):
-        shifted_cols = padded[:, col_tap : col_tap + cols_out]
-        for row_tap in range(3):
-            tap = kernel_ref[3 * row_tap + col_tap : 3 * row_tap + col_tap + 1]
-            running = running + tap[None] * shifted_cols[row_tap : row_tap + rows_out]
-    mixed = (mixed + running).reshape(rows_out * cols_out, channels).T
-    inv_root = lax.rsqrt(jnp.mean(mixed * mixed, axis=0, keepdims=True) + EPSILON)
-    normed = mixed * inv_root
-    narrow = (normed * gain_ref[...]).astype(jnp.bfloat16)
-    pre = jnp.dot(up_ref[...], narrow, preferred_element_type=jnp.float32)
-    sigmoid = jax.nn.sigmoid(pre)
-    n_ref[...] = narrow
-    normed_ref[...] = normed
-    inv_ref[...] = inv_root
-    hid_ref[...] = (pre * sigmoid).astype(jnp.bfloat16)
-    slope_ref[...] = sigmoid * (1.0 + pre * (1.0 - sigmoid))
-
-
-def forward_parts(step, padded, taps, gain, w_up_t):
-    _, rows_in, cols_in, channels = padded.shape
-    hid = w_up_t.shape[0]
-    count = (rows_in - 2) * (cols_in - 2)
-    sds = jax.ShapeDtypeStruct
-    return call(
-        functools.partial(forward_kernel, step),
-        [
-            sds((channels, count), jnp.bfloat16),
-            sds((channels, count), jnp.float32),
-            sds((1, count), jnp.float32),
-            sds((hid, count), jnp.bfloat16),
-            sds((hid, count), jnp.float32),
-        ],
-        padded,
-        taps,
-        gain,
-        w_up_t,
-        flops=2 * count * hid * channels,
-        moved=2**21,
-        limit=12,
-    )
-
-
-def stencil_sums(step, padded_ref, field):
-    rows_out, cols_out = padded_ref.shape[1] - 2, padded_ref.shape[2] - 2
-    channels = padded_ref.shape[3]
+def stencil_sums(pad_ref, field, tile):
+    rows_out, cols_out = tile
+    channels = pad_ref.shape[-1]
     field = field.astype(jnp.float32).T.reshape(rows_out, cols_out, channels)
-    padded = padded_ref[step].astype(jnp.float32)
     result = [None] * 9
     for col_tap in range(3):
-        shifted_cols = padded[:, col_tap : col_tap + cols_out]
+        place = MARGIN - 1 + col_tap
+        shifted_cols = pad_ref[:, place : place + cols_out]
         for row_tap in range(3):
             products = jnp.sum(shifted_cols[row_tap : row_tap + rows_out] * field, axis=0)
             result[3 * row_tap + col_tap] = jnp.sum(products, axis=0, keepdims=True)
     return result
 
 
-def stencil_kernel(steps, *refs):
-    padded_ref, *field_refs, out_ref = refs
+def stencil_kernel(steps, tile, *refs):
+    pad_hbm, *field_hbm, out_ref, pad_ref, field_ref, sems = refs
+    arriving = copies(sems, 0, [(pad_hbm.at[s], pad_ref.at[k]) for k, s in enumerate(steps)])
+    arriving += copies(sems, len(steps), [(ref, field_ref.at[k]) for k, ref in enumerate(field_hbm)])
     total = None
-    for step, ref in zip(steps, field_refs):
-        rows = stencil_sums(step, padded_ref, ref[...])
+    for k in range(len(steps)):
+        arriving[k].wait()
+        arriving[len(steps) + k].wait()
+        rows = stencil_sums(pad_ref.at[k], field_ref[k], tile)
         total = rows if total is None else [a + b for a, b in zip(total, rows)]
     out_ref[...] = jnp.zeros_like(out_ref)
     for k, row in enumerate(total):
         out_ref[k : k + 1] = row
 
 
-def stencil_terms(steps, padded, fields):
+def stencil_terms(steps, tile, pad, fields):
+    channels, count = fields[0].shape
     return call(
-        functools.partial(stencil_kernel, steps),
-        jax.ShapeDtypeStruct((ROWS, padded.shape[3]), jnp.float32),
-        padded,
-        *fields,
-        moved=2**20,
+        functools.partial(stencil_kernel, steps, tile),
+        [jax.ShapeDtypeStruct((ROWS, channels), jnp.float32)],
+        [pad, *fields],
+        "h" * (1 + len(fields)),
+        "v",
+        scratch=[
+            pltpu.VMEM((len(steps), *pad.shape[1:]), jnp.float32),
+            pltpu.VMEM((len(steps), channels, count), jnp.bfloat16),
+            pltpu.SemaphoreType.DMA((2 * len(steps),)),
+        ],
+        moved=2**21,
         limit=12,
-    )
-
-
-def network_kernel(step, *refs):
+    )[0]
+
+
+def network_kernel(step, tile, with_before, with_sums, *refs):
     refs = list(refs)
-    moved_ref, down_ref, up_ref, slope_ref, normed_ref, inv_ref, gain_ref = refs[:7]
-    refs = refs[7:]
-    before_ref = refs.pop(0) if step is not None or len(refs) > 3 else None
+    take = lambda: refs.pop(0)
+    moved_ref, down_ref, up_ref, slope_hbm, aux_hbm = (take() for _ in range(5))
+    before_hbm = take() if with_before else None
+    pad_hbm, sums_ref = (take(), take()) if with_sums else (None, None)
+    out_hbm, grad_hbm, saved_hbm = take(), take(), take()
+    term_hbm = None if with_sums else take()
+    slope_ref, aux_ref, before_ref, out_ref, grad_ref, pad_ref, sems = refs
+    pairs = [(slope_hbm.at[step], slope_ref), (aux_hbm.at[step], aux_ref)]
+    if with_before:
+        pairs.append((before_hbm, before_ref))
+    if with_sums:
+        pairs.append((pad_hbm.at[step], pad_ref))
+    arriving = copies(sems, 0, pairs)
+    leaving = copies(sems, 4, [(moved_ref, saved_hbm)])
     moved = moved_ref[...]
+    channels, count = moved.shape
     grad_hidden = jnp.dot(down_ref[...], moved, preferred_element_type=jnp.float32)
+    arriving[0].wait()
     grad_pre = (grad_hidden * slope_ref[...]).astype(jnp.bfloat16)
+    grad_ref[...] = grad_pre
+    leaving += copies(sems, 5, [(grad_ref, grad_hbm)])
     grad_n = jnp.dot(up_ref[...], grad_pre, preferred_element_type=jnp.float32)
-    normed = normed_ref[...]
+    finish(arriving[1:])
+    normed, gain = aux_ref[:channels], aux_ref[channels : 2 * channels]
     term = grad_n * normed
-    gain = gain_ref[...]
     mean = jnp.mean(term * gain, axis=0, keepdims=True)
-    field = moved.astype(jnp.float32) + inv_ref[...] * (grad_n * gain - normed * mean)
+    field = moved.astype(jnp.float32) + aux_ref[2 * channels : 2 * channels + 1] * (grad_n * gain - normed * mean)
     field = field.astype(jnp.bfloat16)
-    if before_ref is not None:
+    if with_before:
         term = before_ref[...] + term
-    if step is None:
-        field_ref, grad_ref, term_ref = refs
-        field_ref[...] = field
-        grad_ref[...] = grad_pre
-        term_ref[...] = term
+    if not with_sums:
+        out_ref[...] = field
+        leaving += copies(sems, 6, [(out_ref, out_hbm)])
+        before_ref[...] = term
+        leaving += copies(sems, 7, [(before_ref, term_hbm)])
+        finish(leaving)
         return
-    padded_ref, sums_ref, out_ref, grad_ref = refs
-    grad_ref[...] = grad_pre
     devices, _, count = out_ref.shape
-    channels = moved.shape[0]
     share = channels // devices
-    rows = stencil_sums(step, padded_ref, field)
+    rows = stencil_sums(pad_ref, field, tile)
     rows = jnp.concatenate(rows + [jnp.zeros((count - 9, channels), jnp.float32)], axis=0)
     before = jnp.concatenate([sums_ref[...], jnp.zeros((count - ROWS, channels), jnp.float32)], axis=0)
     sums = (rows + before).T
@@ -214,44 +299,54 @@
     sums = jnp.where(lane == 9, jnp.sum(term, axis=1, keepdims=True), sums)
     out_ref[:, :share] = field.reshape(devices, share, count)
     out_ref[:, share:] = split_three(sums, lane, ROWS).reshape(devices, share, count)
-
-
-def network_back(step, devices, moved, w_down_t, w_up, slope, normed, inv_root, gain, before, padded=None, sums=None):
+    finish(leaving + copies(sems, 6, [(out_ref, out_hbm)]))
+
+
+def network_back(step, tile, devices, moved, w_down_t, w_up, slope, aux, before, pad=None, sums=None):
     channels, count = moved.shape
     hid = w_down_t.shape[0]
+    with_before, with_sums = before is not None, pad is not None
+    out_shape = (devices, 2 * channels // devices, count) if with_sums else (channels, count)
     sds = jax.ShapeDtypeStruct
-    operands = [moved, w_down_t, w_up, slope, normed, inv_root, gain]
-    operands += [] if before is None else [before]
-    if padded is None:
-        out = [
-            sds((channels, count), jnp.bfloat16),
-            sds((hid, count), jnp.bfloat16),
-            sds((channels, count), jnp.float32),
-        ]
-    else:
-        operands += [padded, sums]
-        out = [
-            sds((devices, 2 * channels // devices, count), jnp.bfloat16),
-            sds((hid, count), jnp.bfloat16),
-        ]
+    out = [sds(out_shape, jnp.bfloat16), sds((hid, count), jnp.bfloat16), sds((channels, count), jnp.bfloat16)]
+    out += [] if with_sums else [sds((channels, count), jnp.float32)]
+    operands = [moved, w_down_t, w_up, slope, aux]
+    operands += [before] if with_before else []
+    operands += [pad, sums] if with_sums else []
     return call(
-        functools.partial(network_kernel, step if padded is not None else None),
+        functools.partial(network_kernel, step, tile, with_before, with_sums),
         out,
-        *operands,
+        operands,
+        "vvvhh" + "h" * with_before + "hv" * with_sums,
+        "h" * len(out),
+        scratch=[
+            pltpu.VMEM((hid, count), jnp.float32),
+            pltpu.VMEM(aux.shape[1:], jnp.float32),
+            pltpu.VMEM((channels, count), jnp.float32),
+            pltpu.VMEM(out_shape, jnp.bfloat16),
+            pltpu.VMEM((hid, count), jnp.bfloat16),
+            pltpu.VMEM(pad.shape[1:] if with_sums else (8, count), jnp.float32),
+            pltpu.SemaphoreType.DMA((8,)),
+        ],
         flops=4 * count * hid * channels,
         moved=4 * 2**20,
         limit=12,
     )
 
 
-def final_kernel(arrived_ref, state_ref, sums_ref):
+def final_kernel(arrived_ref, state_hbm, taps_ref, gain_ref, state_ref, sems):
     devices, rows, count = arrived_ref.shape
     share = rows // 2
     channels = devices * share
     state = arrived_ref[:, :share].reshape(channels, count).astype(jnp.float32)
     state_ref[...] = state.T.astype(jnp.bfloat16)
+    leaving = copies(sems, 0, [(state_ref, state_hbm)])
     sums = arrived_ref[:, share:].reshape(channels, count).astype(jnp.float32)
-    sums_ref[...] = join_three(sums, ROWS).T[:ROWS]
+    sums = join_three(sums, ROWS).T
+    for k in range(9):
+        taps_ref[k // 3, k % 3 : k % 3 + 1] = sums[k : k + 1]
+    gain_ref[...] = sums[9:10]
+    finish(leaving)
 
 
 def final_parts(arrived, channels):
@@ -259,8 +354,11 @@
     sds = jax.ShapeDtypeStruct
     return call(
         final_kernel,
-        [sds((count, channels), jnp.bfloat16), sds((ROWS, channels), jnp.float32)],
-        arrived,
+        [sds((count, channels), jnp.bfloat16), sds((3, 3, channels), jnp.float32), sds((1, channels), jnp.float32)],
+        [arrived],
+        "v",
+        "hvv",
+        scratch=[pltpu.VMEM((count, channels), jnp.bfloat16), pltpu.SemaphoreType.DMA((1,))],
         moved=2**19,
     )
 
@@ -272,15 +370,24 @@
     move_ref = take() if with_move else None
     in_ref = take()
     kern_ref = take() if with_stencil else None
-    weight_ref = take() if with_move else None
-    out_ref = take()
-    high_ref, own_ref, low_ref, spread_ref = take(), take(), take(), take()
+    weight_hbm = take() if mode == "mid" else None
+    out_hbm = take()
+    saved_hbm = take() if mode == "first" else None
+    high_ref, own_ref, low_ref, spread_ref, out_ref, sems = (take() for _ in range(6))
     tiles_lon, tiles_lat, _, lanes = in_ref.shape
     rows = high_ref.shape[2]
     lane = lax.broadcasted_iota(jnp.int32, (rows, lanes), 1)
     col = lax.rem(lane, near_lat)
     unroll = 16 if tiles_lon * tiles_lat <= 32 else 1
     zero = jnp.zeros((rows, lanes), jnp.float32)
+    started = []
+    if with_move:
+        own2_ref, lon2_ref, weight_ref = refs
+        if mode == "mid":
+            arriving = copies(sems, 0, [(weight_hbm, weight_ref)])
+        else:
+            weight_ref[...] = in_ref[:, :, rows:]
+            started += copies(sems, 0, [(weight_ref, saved_hbm)])
 
     def turn(value, steps):
         return pltpu.roll(value, steps % lanes, 1) if isinstance(steps, int) else pltpu.roll(value, steps, 1)
@@ -318,7 +425,9 @@
         return lax.fori_loop(0, tiles_lon, body, init, unroll=unroll)
 
     if with_stencil:
-        taps = [[kern_ref[3 * a + b] for b in range(3)] for a in range(3)]
+        taps = [
+            [jnp.broadcast_to(kern_ref[:, 3 * a + b : 3 * a + b + 1], (rows, lanes)) for b in range(3)] for a in range(3)
+        ]
 
         def mix(a, carry):
             here = read(in_ref, a)
@@ -351,19 +460,21 @@
 
     if not with_move:
 
-        def finish(a, carry):
+        def complete(a, carry):
             for b, value in enumerate(gather(a)):
                 out_ref[a, b, :rows] = value.astype(jnp.bfloat16)
             return carry
 
-        loop(finish)
+        loop(complete)
         sums = jnp.sum(in_ref[:, :, rows:].astype(jnp.float32), axis=(0, 1))
         sums = split_three(join_three(sums, ROWS), lane, ROWS)
         out_ref[:, :, rows:] = jnp.broadcast_to(sums[None, None], (tiles_lon, tiles_lat, rows, lanes))
+        finish(copies(sems, 1, [(out_ref, out_hbm)]))
         return
 
-    own2_ref, lon2_ref = refs
-    weight_row = weight_ref.shape[2] - ROWS + 4 * step
+    weight_row = 4 * step
+    if mode == "mid":
+        finish(arriving)
 
     def weigh(a, carry):
         here = [value.astype(jnp.bfloat16).astype(jnp.float32) for value in gather(a)]
@@ -411,7 +522,12 @@
             out_ref[a, b] = value.astype(jnp.bfloat16)
         return carry
 
-    loop(move)
+    half = tiles_lon // 2
+    for k in range(2):
+        lax.fori_loop(k * half, (k + 1) * half, move, None, unroll=unroll if unroll == 1 else half)
+        part = pl.ds(k * half, half)
+        started += copies(sems, 1 + k, [(out_ref.at[part], out_hbm.at[part])])
+    finish(started)
 
 
 def spatial(mode, step, tile, rows, field, kern, weights, moves):
@@ -419,21 +535,26 @@
     with_move, with_stencil = mode != "last", mode != "first"
     operands = ([moves] if with_move else []) + [field]
     operands += [kern] if with_stencil else []
-    operands += [weights] if with_move else []
-    out_rows = rows if with_move else 2 * rows
+    operands += [weights] if mode == "mid" else []
+    out_shape = (tiles_lon, tiles_lat, rows if with_move else 2 * rows, lanes)
+    weight_shape = (tiles_lon, tiles_lat, ROWS, lanes)
+    sds = jax.ShapeDtypeStruct
+    out = [sds(out_shape, jnp.bfloat16)] + ([sds(weight_shape, jnp.bfloat16)] if mode == "first" else [])
     grid = pltpu.VMEM((tiles_lon, tiles_lat, rows, lanes), jnp.float32)
     scratch = [grid, grid, grid, pltpu.VMEM((tiles_lon, tiles_lat + LAT_REACH, rows, lanes), jnp.float32)]
+    scratch += [pltpu.VMEM(out_shape, jnp.bfloat16), pltpu.SemaphoreType.DMA((3,))]
     if with_move:
-        scratch += [grid, grid]
+        scratch += [grid, grid, pltpu.VMEM(weight_shape, jnp.bfloat16)]
     return call(
         functools.partial(spatial_kernel, mode, step, *tile),
-        jax.ShapeDtypeStruct((tiles_lon, tiles_lat, out_rows, lanes), jnp.bfloat16),
-        *operands,
+        out,
+        operands,
+        "s" * with_move + "v" + "v" * with_stencil + "h" * (mode == "mid"),
+        "h" * len(out),
         scratch=scratch,
-        scalars=1 if with_move else 0,
         flops=2**22,
         moved=2**20,
-        limit=max(8, 10 * tiles_lon * tiles_lat * rows * lanes * 4 // MIB),
+        limit=max(8, 12 * tiles_lon * tiles_lat * rows * lanes * 4 // MIB),
     )
 
 
@@ -472,19 +593,29 @@
 
 
 def gradient_kernel(row_groups, bit_ref, *refs):
-    *inputs, send_ref, keep_ref = refs
-    steps = len(inputs) // 4
+    *inputs, send_ref, keep_ref, left_ref, right_ref, sems = refs
+    steps = len(inputs) // 2 - 1
+    narrow_hbm, hidden_hbm = inputs[:2]
+    grads_hbm, moved_hbm = inputs[2 : 2 + steps], inputs[2 + steps :]
+    channels, hid = left_ref.shape[1], right_ref.shape[1]
+    count = narrow_hbm.shape[2]
+    arriving = []
     for k in range(2):
-        left = inputs[2 * k * steps : (2 * k + 1) * steps]
-        right = inputs[(2 * k + 1) * steps : (2 * k + 2) * steps]
-        right = jnp.concatenate([ref[...] for ref in right], axis=1)
-        channels = left[0].shape[0]
-        chunk = channels // (2 * row_groups)
+        for s in range(steps):
+            lanes = pl.ds(s * count, count)
+            left = narrow_hbm.at[s] if k == 0 else moved_hbm[s]
+            right = grads_hbm[s] if k == 0 else hidden_hbm.at[s]
+            pairs = [(left, left_ref.at[k, :, lanes]), (right, right_ref.at[k, :, lanes])]
+            arriving += copies(sems, 2 * (k * steps + s), pairs)
+    chunk = channels // (2 * row_groups)
+    for k in range(2):
+        finish(arriving[2 * k * steps : 2 * (k + 1) * steps])
+        right = right_ref[k]
         for which, out_ref in ((1 - bit_ref[0], send_ref), (bit_ref[0], keep_ref)):
             rows = []
             for p in range(row_groups):
                 start = pl.multiple_of((2 * p + which) * chunk, chunk)
-                rows.append(jnp.concatenate([ref[pl.ds(start, chunk)] for ref in left], axis=1))
+                rows.append(left_ref[k, pl.ds(start, chunk)])
             rows = jnp.concatenate(rows, axis=0)
             value = lax.dot_general(rows, right, (((1,), (1,)), ((), ())), preferred_element_type=jnp.float32)
             out_ref[k] = value.astype(out_ref.dtype)
@@ -513,7 +644,7 @@
                 start = pl.multiple_of((2 * p + which) * size, size)
                 place = (pl.ds(start, size),) if dim == 0 else (slice(None), pl.ds(start, size))
                 goal = (pl.ds(p * size, size),) if dim == 0 else (slice(None), pl.ds(p * size, size))
-                value = kept[k][place] + arrived[k][place].astype(jnp.float32)
+                value = kept[k][place].astype(jnp.float32) + arrived[k][place].astype(jnp.float32)
                 out_ref[goal] = value.astype(out_ref.dtype)
 
 
@@ -532,7 +663,13 @@
         out = [sds(shape, jnp.bfloat16) for shape in shapes] + [sds(shape, jnp.float32) for shape in shapes]
     operands = [*kept, *arrived] if isinstance(kept, (list, tuple)) else [kept, arrived]
     return call(
-        functools.partial(halves_kernel, plan, together), out, bits, *operands, scalars=1, moved=2**20, limit=12
+        functools.partial(halves_kernel, plan, together),
+        out,
+        [bits, *operands],
+        "s" + "v" * len(operands),
+        "v" * len(out),
+        moved=2**20,
+        limit=12,
     )
 
 
@@ -546,13 +683,14 @@
     return lax.ppermute(value, axis, [(i, i ^ (1 << bit)) for i in range(count)])
 
 
-def projection_sums(narrow, grads, moved, hidden):
-    channels, hid = narrow[0].shape[0], grads[0].shape[0]
+def projection_sums(narrow, hidden, grads, moved):
+    steps, channels, count = narrow.shape
+    hid = hidden.shape[1]
     lon, lat = lax.axis_size("lon"), lax.axis_size("lat")
     if lat != 2 or lon != 16:
         lanes_both = (((1,), (1,)), ((), ()))
         dots = lambda left, right: sum(
-            lax.dot_general(a, b, lanes_both, preferred_element_type=jnp.float32) for a, b in zip(left, right)
+            lax.dot_general(left[s], right[s], lanes_both, preferred_element_type=jnp.float32) for s in range(steps)
         )
         return scattered(dots(narrow, grads), False), scattered(dots(moved, hidden), True)
     here = lax.axis_index("lon")
@@ -562,13 +700,15 @@
     shape = (2, channels // 2, hid)
     send, keep = call(
         functools.partial(gradient_kernel, groups),
-        [sds(shape, jnp.bfloat16), sds(shape, jnp.float32)],
-        bits,
-        *narrow,
-        *grads,
-        *moved,
-        *hidden,
-        scalars=1,
+        [sds(shape, jnp.bfloat16), sds(shape, jnp.bfloat16)],
+        [bits, narrow, hidden, *grads, *moved],
+        "shh" + "h" * 2 * steps,
+        "vv",
+        scratch=[
+            pltpu.VMEM((2, channels, steps * count), jnp.bfloat16),
+            pltpu.VMEM((2, hid, steps * count), jnp.bfloat16),
+            pltpu.SemaphoreType.DMA((4 * steps,)),
+        ],
         flops=12 * 2**28,
         moved=6 * 2**20,
         limit=16,
@@ -583,7 +723,7 @@
     send, keep = halves(((0, groups // 8, 3), (0, groups // 8, 3)), True, bits, keep, arrived)
     arrived = swapped(send, "lon", 3)
     out = sds((channels // lon, hid // lat), jnp.float32)
-    return call(last_sum_kernel, [out, out], keep, arrived, moved=2**18)
+    return call(last_sum_kernel, [out, out], [keep, arrived], "vv", "vv", moved=2**18)
 
 
 def local(cotangent, states, w_up, w_down, norm_gain, kernel, bilinear, lon_move, lat_move):
@@ -621,49 +761,39 @@
         return jnp.concatenate([blocks[:, :share], blocks[:, padded_share : padded_share + share]], axis=1)
 
     arrived = as_grid(exchanged(packed(cotangent, bilinear, devices)))
-    weights = arrived
     group = me * share // group_size
     moves = jnp.stack([lon_move[:, group], lat_move[:, group]], axis=1)
-    grid_now = spatial("first", steps - 1, tile, padded_share, arrived, None, weights, moves[steps - 1])
-
-    kern = lax.dynamic_slice_in_dim(kernel.reshape(9, channels), me * share, share, 1)
-    kern = jnp.pad(kern, ((0, 0), (0, padded_share - share)))
-    kern = jnp.broadcast_to(kern[:, :, None], (9, padded_share, count))
-
-    padded = with_halo(with_halo(states, (("lon", 1),), 1, True), (("lat", 2),), 1, False)
-    gain = norm_gain[:, None]
-    taps = kernel.reshape(9, channels)
+    grid_now, weights = spatial("first", steps - 1, tile, padded_share, arrived, None, None, moves[steps - 1])
+
+    taps = lax.dynamic_slice_in_dim(kernel.reshape(9, channels), me * share, share, 1).T
+    taps = jnp.pad(taps, ((0, padded_share - share), (0, count - 9)))
+
+    around = edges(states)
     w_up_t, w_down_t = w_up.T, w_down.T
-    forward = {s: forward_parts(s, padded, taps, gain, w_up_t) for s in reversed(range(steps))}
+    grid_now, around = lax.optimization_barrier((grid_now, around))
+    narrow, aux, hidden, slope, pad = forward_parts(states, around, kernel, norm_gain, w_up_t)
 
     moved, grads, fields = {}, {}, {}
     term = None
     for s in reversed(range(steps)):
-        moved[s] = as_rows(exchanged(grid_now.reshape(devices, padded_share, count)))
-        narrow, normed, inv_root, hidden, slope = forward[s]
-        common = (s, devices, moved[s], w_down_t, w_up, slope, normed, inv_root, gain, term)
+        here = as_rows(exchanged(grid_now.reshape(devices, padded_share, count)))
+        common = (s, tile, devices, here, w_down_t, w_up, slope, aux, term)
         if s > 0:
-            fields[s], grads[s], term = network_back(*common)
+            fields[s], grads[s], moved[s], term = network_back(*common)
             arrived = as_grid(exchanged(as_blocks(fields[s])))
-            grid_now = spatial("mid", s - 1, tile, padded_share, arrived, kern, weights, moves[s - 1])
+            (grid_now,) = spatial("mid", s - 1, tile, padded_share, arrived, taps, weights, moves[s - 1])
         else:
             later = list(fields)
-            sums = stencil_terms(later, padded, [fields[k] for k in later])
-            blocks, grads[s] = network_back(*common, padded, sums)
+            sums = stencil_terms(later, tile, pad, [fields[k] for k in later])
+            blocks, grads[s], moved[s] = network_back(*common, pad, sums)
             arrived = as_grid(exchanged(as_pairs(blocks)))
-            grid_now = spatial("last", None, tile, padded_share, arrived, kern, None, None)
+            (grid_now,) = spatial("last", None, tile, padded_share, arrived, taps, None, None)
 
     arrived = exchanged(grid_now.reshape(devices, 2 * padded_share, count))
-    grad_state, sums = final_parts(from_pairs(arrived), channels)
-    order = list(reversed(range(steps)))
-    grad_up, grad_down = projection_sums(
-        [forward[s][0] for s in order],
-        [grads[s] for s in order],
-        [moved[s] for s in order],
-        [forward[s][3] for s in order],
-    )
-    grad_kernel = sums[:9].reshape(kernel.shape)
-    return (grad_state.reshape(cotangent.shape), grad_up, grad_down, grad_kernel, sums[9])
+    grad_state, grad_kernel, grad_gain = final_parts(from_pairs(arrived), channels)
+    by_step = lambda values: [values[s] for s in range(steps)]
+    grad_up, grad_down = projection_sums(narrow, hidden, by_step(grads), by_step(moved))
+    return (grad_state.reshape(cotangent.shape), grad_up, grad_down, grad_kernel, grad_gain.reshape(channels))
 
 
 def solution(mesh):

time: 157 us -> 171 us (1.089)
  blocking collectives: 10.6 us -> 20.7 us
  Pallas kernels: 27.7 us -> 35.1 us
  starting transfers between devices: 51.3 us -> 45 us
  waiting for transfers between devices: 32.6 us -> 37.1 us
  local copies, waits for them, and re-layouts: 30.7 us -> 28.3 us
    all_to_all x1 -> x2, blocking collectives: 10.6 us -> 20.7 us  [exchanged(): return lax.all_to_all(blocks, AXES, split_axis=0, concat_axis=0, tiled=True)]
    all_to_all x7 -> x6, waiting for transfers between devices: 19.7 us -> 27.9 us  [exchanged(): return lax.all_to_all(blocks, AXES, split_axis=0, concat_axis=0, tiled=True)]
    pallas_call x19 -> x17, Pallas kernels: 27.7 us -> 35.1 us  [call(): pl.pallas_call(kernel, out_shape=out_shape, in_specs=[pl.BlockSpec(memory...]
    all_to_all x7 -> x6, starting transfers between devices: 28.7 us -> 21.8 us  [exchanged(): return lax.all_to_all(blocks, AXES, split_axis=0, concat_axis=0, tiled=True)]
    ppermute x4 -> x5, waiting for transfers between devices: 4.21 us -> 0.01 us  [the longest x3 0.01 us: sent(): return lax.ppermute(value, AXES, both)]
    select_n x0 -> x2, other arithmetic: none -> 1.86 us  [the longest x1 1.11 us: edges(): arrived = column(jnp.where(lat_at == 0, last, first), [(0, 1), (1, 0)])]
    ppermute x4 -> x5, starting transfers between devices: 11.5 us -> 12.2 us  [the longest x3 6.72 us: sent(): return lax.ppermute(value, AXES, both)]
    unnamed x106 -> x83, local copies, waits for them, and re-layouts: 26.7 us -> 26.4 us
  transfers between devices with their start and end apart: 18 -> 18, of which waited for: 10 -> 8; matrix products, arithmetic and copies ran while one was open for 5% -> 2% of each run, Pallas kernels for 6% -> 10%
where the time goes in v3:
time: 171 us; the launch traced here: 169 us
  starting transfers between devices  45 us (26%)
  waiting for transfers between devices  37.1 us (22%)
  Pallas kernels  35.1 us (21%)
  local copies, waits for them, and re-layouts  28.3 us (17%)
  blocking collectives  20.7 us (12%)
  other arithmetic  1.94 us (1%)
    pallas_call x17, Pallas kernels, call(): pl.pallas_call(kernel, out_shape=out_shape, in_specs=[pl.BlockSpec(memory...  35.1 us
    all_to_all x6, waiting for transfers between devices, exchanged(): return lax.all_to_all(blocks, AXES, split_axis=0, concat_axis=0, tiled=True)  27.9 us
    unnamed x83, local copies, waits for them, and re-layouts  26.4 us
    all_to_all x6, starting transfers between devices, exchanged(): return lax.all_to_all(blocks, AXES, split_axis=0, concat_axis=0, tiled=True)  21.8 us
    all_to_all x2, blocking collectives, exchanged(): return lax.all_to_all(blocks, AXES, split_axis=0, concat_axis=0, tiled=True)  20.7 us
    ppermute x7, starting transfers between devices, swapped(): return lax.ppermute(value, axis, [(i, i ^ 1 << bit) for i in range(count)])  11 us
    ppermute x7, waiting for transfers between devices, swapped(): return lax.ppermute(value, axis, [(i, i ^ 1 << bit) for i in range(count)])  9.28 us
    ppermute x3, starting transfers between devices, sent(): return lax.ppermute(value, AXES, both)  6.72 us
  transfers between devices with their start and end apart: 18, of which 8 were waited for; matrix products, arithmetic and copies ran while one was open for 2% of the time, Pallas kernels for 10%

profile of v3, /device:TPU:0, one launch (start us, length us, event | category | flops | bytes accessed | tf_op | source)
XLA Modules:
  0.0 169.3 jit_solution(16110925980153064711)
XLA Ops:
  1.7 3.0 %collective-permute-start.3 = (bf16[3,8,1,512]{3,2,1,0:T(2,128)(2,1)S(1)}, bf16[3,8,1,512]{3,2,1,0:T(2,128)(2,1)S(1)}, u32[]{:S(2)}, u32[]{:S(2)}) collective-permute-start(bf16[3,8,1,512]{3,2,1,0:T(2,128)(2,1)S(1)} %broadcast_select_fusion.2), channel_id=1, source_target_pairs={{0,1},{1,0},{2,3},{3,2},{4,5},{5,4},{6,7},{7,6},{8,9},{9,8},{10,11... | collective-permute-start | bytes 73736 | tf_op jit(solution)/shard_map/ppermute | solution.py:119
  4.8 3.7 %collective-permute-start.4 = (bf16[3,1,1,512]{3,2,1,0:T(2,128)(2,1)S(1)}, bf16[3,1,1,512]{3,2,1,0:T(2,128)(2,1)S(1)}, u32[]{:S(2)}, u32[]{:S(2)}) collective-permute-start(bf16[3,1,1,512]{3,2,1,0:T(2,128)(2,1)S(1)} %get-tuple-element.93), channel_id=1, source_target_pairs={{0,31},{1,30},{2,1},{3,0},{4,3},{5,2},{6,5},{7,4},{8,7},{9,6},{10,... | collective-permute-start | bytes 9224 | tf_op jit(solution)/shard_map/ppermute | solution.py:119
  9.3 5.4 %collective-permute-start.1 = (bf16[3,1,16,512]{3,2,1,0:T(8,128)(2,1)S(1)}, bf16[3,1,16,512]{3,2,1,0:T(8,128)(2,1)S(1)}, u32[]{:S(2)}, u32[]{:S(2)}) collective-permute-start(bf16[3,1,16,512]{3,2,1,0:T(8,128)(2,1)S(1)} %get-tuple-element.89), channel_id=1, source_target_pairs={{0,30},{2,0},{4,2},{6,4},{8,6},{10,8},{12,10},{14,12},{16,14},{18,... | collective-permute-start | bytes 147464 | tf_op jit(solution)/shard_map/ppermute | solution.py:112
  17.6 4.8 %all-to-all-start = ((bf16[32,32,128]{2,1,0:T(8,128)(2,1)}), bf16[32,32,128]{2,1,0:T(8,128)(2,1)S(1)}, u32[]{:S(2)}, u32[]{:S(2)}) async-start(bf16[32,32,128]{2,1,0:T(8,128)(2,1)} %shard_map.128), calls=%async_computation | async-start | bytes 524288 | tf_op jit(solution)/shard_map/all_to_all | solution.py:18
  24.3 8.8 %all-to-all-done = bf16[32,32,128]{2,1,0:T(8,128)(2,1)S(1)} async-done(((bf16[32,32,128]{2,1,0:T(8,128)(2,1)}), bf16[32,32,128]{2,1,0:T(8,128)(2,1)S(1)}, u32[]{:S(2)}, u32[]{:S(2)}) %all-to-all-start) | async-done | bytes 262176 | tf_op jit(solution)/shard_map/all_to_all | solution.py:18
  33.1 1.9 %shard_map.129 = (bf16[16,2,16,128]{3,2,1,0:T(8,128)(2,1)}, bf16[16,2,16,128]{3,2,1,0:T(8,128)(2,1)S(1)}) custom-call(s32[2]{0:T(128)S(1)} %get-tuple-element.95.refs_0_, bf16[16,2,32,128]{3,2,1,0:T(8,128)(2,1)S(1)} %bitcast.36), custom_call_target="tpu_custom_call" | custom-call | flops 4194304 | bytes 1048576 | tf_op jit(solution)/shard_map/pallas_call | solution.py:25
  36.3 3.3 %all-to-all-start.1 = ((bf16[32,16,128]{2,1,0:T(8,128)(2,1)}), bf16[32,16,128]{2,1,0:T(8,128)(2,1)}, u32[]{:S(2)}, u32[]{:S(2)}) async-start(bf16[32,16,128]{2,1,0:T(8,128)(2,1)} %bitcast.6), calls=%async_computation.1 | async-start | bytes 262144 | tf_op jit(solution)/shard_map/all_to_all | solution.py:18
  44.8 5.7 %shard_map.130 = (bf16[3,512,128]{2,1,0:T(8,128)(2,1)S(1)}, f32[3,1032,128]{2,1,0:T(8,128)S(1)}, bf16[3,1024,128]{2,1,0:T(8,128)(2,1)S(1)}, f32[3,1024,128]{2,1,0:T(8,128)S(1)}, f32[3,10,32,512]{3,2,1,0:T(8,128)S(1)}) custom-call(bf16[3,8,16,512]{3,2,1,0:T(8,128)(2,1)S(1)} %copy-done.12, bf16[3,1,16,512]{3,2,1,0:T(8,128)(2,1)S(1)} %copy-done.23, ...), custom_call_target="tpu_custom_call" | custom-call | flops 402653184 | bytes 8388608 | tf_op jit(solution)/shard_map/pallas_call | solution.py:25
  58.6 3.5 %shard_map.131 = (bf16[512,128]{1,0:T(8,128)(2,1)}, bf16[1024,128]{1,0:T(8,128)(2,1)S(1)}, bf16[512,128]{1,0:T(8,128)(2,1)S(1)}, f32[512,128]{1,0:T(8,128)S(1)}) custom-call(bf16[512,128]{1,0:T(8,128)(2,1)} %bitcast.7.refs_0_, bf16[1024,512]{1,0:T(8,128)(2,1)S(1)} %bitcast.32, bf16[512,1024]{1,0:T(8,128)(2,1)S(1)} %copy-done, f32[3,1024,128]{2,1,0:T(8,128)S(1)} %copy-done.6, ...), custom_call_target="tpu_custom_call" | custom-call | flops 268435456 | bytes 4194304 | tf_op jit(solution)/shard_map/pallas_call | solution.py:25
  63.4 5.8 %all-to-all-start.2 = ((bf16[32,16,128]{2,1,0:T(8,128)(2,1)}), bf16[32,16,128]{2,1,0:T(8,128)(2,1)S(1)}, u32[]{:S(2)}, u32[]{:S(2)}) async-start(bf16[32,16,128]{2,1,0:T(8,128)(2,1)} %bitcast.11), calls=%async_computation.2 | async-start | bytes 262144 | tf_op jit(solution)/shard_map/all_to_all | solution.py:18
  69.4 8.4 %all-to-all-done.2 = bf16[32,16,128]{2,1,0:T(8,128)(2,1)S(1)} async-done(((bf16[32,16,128]{2,1,0:T(8,128)(2,1)}), bf16[32,16,128]{2,1,0:T(8,128)(2,1)S(1)}, u32[]{:S(2)}, u32[]{:S(2)}) %all-to-all-start.2) | async-done | bytes 131104 | tf_op jit(solution)/shard_map/all_to_all | solution.py:18
  77.8 2.7 %shard_map.132 = bf16[16,2,16,128]{3,2,1,0:T(8,128)(2,1)S(1)} custom-call(s32[2]{0:T(128)S(1)} %get-tuple-element.96.refs_0_, bf16[16,2,16,128]{3,2,1,0:T(8,128)(2,1)S(1)} %bitcast.41, f32[16,128]{1,0:T(8,128)S(1)} %pad.4.refs_2_.refs_1_, bf16[16,2,16,128]{3,2,1,0:T(8,128)(2,1)S(1)} %copy-done.14), custom_call_target="tpu_custom_call" | custom-call | flops 4194304 | bytes 1048576 | tf_op jit(solution)/shard_map/pallas_call | solution.py:25
  80.6 10.3 %all_to_all.40 = bf16[32,16,128]{2,1,0:T(8,128)(2,1)S(1)} all-to-all(bf16[32,16,128]{2,1,0:T(8,128)(2,1)S(1)} %bitcast.43), channel_id=1, replica_groups=mesh['lon'=16,'lat'=2] {'lon','lat'}, dimensions={0} | all-to-all | bytes 262144 | tf_op jit(solution)/shard_map/all_to_all | solution.py:18
  93.7 2.1 %shard_map.133 = (bf16[512,128]{1,0:T(8,128)(2,1)S(1)}, bf16[1024,128]{1,0:T(8,128)(2,1)S(1)}, bf16[512,128]{1,0:T(8,128)(2,1)S(1)}, f32[512,128]{1,0:T(8,128)S(1)}) custom-call(bf16[512,128]{1,0:T(8,128)(2,1)S(1)} %bitcast.40, bf16[1024,512]{1,0:T(8,128)(2,1)S(1)} %bitcast.33, bf16[512,1024]{1,0:T(8,128)(2,1)S(1)} %copy-done, ...), custom_call_target="tpu_custom_call" | custom-call | flops 268435456 | bytes 4194304 | tf_op jit(solution)/shard_map/pallas_call | solution.py:25
  95.9 10.3 %all_to_all.41 = bf16[32,16,128]{2,1,0:T(8,128)(2,1)S(1)} all-to-all(bf16[32,16,128]{2,1,0:T(8,128)(2,1)S(1)} %bitcast.39), channel_id=1, replica_groups=mesh['lon'=16,'lat'=2] {'lon','lat'}, dimensions={0} | all-to-all | bytes 262144 | tf_op jit(solution)/shard_map/all_to_all | solution.py:18
  106.2 3.1 %shard_map.134 = bf16[16,2,16,128]{3,2,1,0:T(8,128)(2,1)} custom-call(s32[2]{0:T(128)S(1)} %get-tuple-element.97.refs_0_, bf16[16,2,16,128]{3,2,1,0:T(8,128)(2,1)S(1)} %bitcast.42, f32[16,128]{1,0:T(8,128)S(1)} %pad.4.refs_2_.refs_1_, bf16[16,2,16,128]{3,2,1,0:T(8,128)(2,1)S(1)} %copy-done.14), custom_call_target="tpu_custom_call" | custom-call | flops 4194304 | bytes 1048576 | tf_op jit(solution)/shard_map/pallas_call | solution.py:25
  109.3 2.8 %all-to-all-start.5 = ((bf16[32,16,128]{2,1,0:T(8,128)(2,1)}), bf16[32,16,128]{2,1,0:T(8,128)(2,1)S(1)}, u32[]{:S(2)}, u32[]{:S(2)}) async-start(bf16[32,16,128]{2,1,0:T(8,128)(2,1)} %bitcast.18), calls=%async_computation.5 | async-start | bytes 262144 | tf_op jit(solution)/shard_map/all_to_all | solution.py:18
  112.2 1.5 copy-done.10
  113.8 2.2 %shard_map.135.refs_7_ = f32[16,512]{1,0:T(8,128)S(1)} custom-call(f32[3,10,32,512]{3,2,1,0:T(8,128)S(1)} %copy-done.10, bf16[512,128]{1,0:T(8,128)(2,1)} %get-tuple-element.55.refs_1_, bf16[512,128]{1,0:T(8,128)(2,1)S(1)} %get-tuple-element.58.refs_2_), custom_call_target="tpu_custom_call" | custom-call | bytes 2097152 | tf_op jit(solution)/shard_map/pallas_call | solution.py:25
  116.0 4.5 %all-to-all-done.5 = bf16[32,16,128]{2,1,0:T(8,128)(2,1)S(1)} async-done(((bf16[32,16,128]{2,1,0:T(8,128)(2,1)}), bf16[32,16,128]{2,1,0:T(8,128)(2,1)S(1)}, u32[]{:S(2)}, u32[]{:S(2)}) %all-to-all-start.5) | async-done | bytes 131104 | tf_op jit(solution)/shard_map/all_to_all | solution.py:18
  123.4 1.5 copy-done.11
  125.0 3.5 %shard_map.136 = (bf16[32,32,128]{2,1,0:T(8,128)(2,1)}, bf16[1024,128]{1,0:T(8,128)(2,1)S(1)}, bf16[512,128]{1,0:T(8,128)(2,1)S(1)}) custom-call(bf16[512,128]{1,0:T(8,128)(2,1)S(1)} %bitcast.38, bf16[1024,512]{1,0:T(8,128)(2,1)S(1)} %bitcast.34, bf16[512,1024]{1,0:T(8,128)(2,1)S(1)} %copy-done, f32[3,1024,128]{2,1,0:T(8,128)S(1)} %copy-done.8, ...), custom_call_target="tpu_custom_call" | custom-call | flops 268435456 | bytes 4194304 | tf_op jit(solution)/shard_map/pallas_call | solution.py:25
  128.5 2.6 %shard_map.139 = (bf16[2,256,1024]{2,1,0:T(8,128)(2,1)S(1)}, bf16[2,256,1024]{2,1,0:T(8,128)(2,1)S(1)}) custom-call(s32[5]{0:T(128)S(1)} %stack.27.bit_ref, bf16[3,512,128]{2,1,0:T(8,128)(2,1)S(1)} %copy-done.29, bf16[3,1024,128]{2,1,0:T(8,128)(2,1)S(1)} %copy-done.27, bf16[1024,128]{1,0:T(8,128)(2,1)S(1)} %get-tuple-element.65.refs_2_, ...), custom_call_target="tpu_custom_call" | custom-call | flops 3221225472 | bytes 6291456 | tf_op jit(solution)/shard_map/pallas_call | solution.py:25
  131.1 2.6 %all-to-all-start.6 = ((bf16[32,32,128]{2,1,0:T(8,128)(2,1)}), bf16[32,32,128]{2,1,0:T(8,128)(2,1)S(1)}, u32[]{:S(2)}, u32[]{:S(2)}) async-start(bf16[32,32,128]{2,1,0:T(8,128)(2,1)} %get-tuple-element.61), calls=%async_computation.6 | async-start | bytes 524288 | tf_op jit(solution)/shard_map/all_to_all | solution.py:18
  135.3 1.6 collective-permute-start.6
  138.4 6.0 %all-to-all-done.6 = bf16[32,32,128]{2,1,0:T(8,128)(2,1)S(1)} async-done(((bf16[32,32,128]{2,1,0:T(8,128)(2,1)}), bf16[32,32,128]{2,1,0:T(8,128)(2,1)S(1)}, u32[]{:S(2)}, u32[]{:S(2)}) %all-to-all-start.6) | async-done | bytes 262176 | tf_op jit(solution)/shard_map/all_to_all | solution.py:18
  145.6 2.6 %all-to-all-start.7 = ((bf16[32,32,128]{2,1,0:T(8,128)(2,1)}), bf16[32,32,128]{2,1,0:T(8,128)(2,1)S(1)}, u32[]{:S(2)}, u32[]{:S(2)}) async-start(bf16[32,32,128]{2,1,0:T(8,128)(2,1)} %bitcast.21), calls=%async_computation.7 | async-start | bytes 524288 | tf_op jit(solution)/shard_map/all_to_all | solution.py:18
  148.9 1.7 %collective-permute-start.8 = (bf16[128,512]{1,0:T(8,128)(2,1)S(1)}, bf16[128,512]{1,0:T(8,128)(2,1)S(1)}, u32[]{:S(2)}, u32[]{:S(2)}) collective-permute-start(bf16[128,512]{1,0:T(8,128)(2,1)S(1)} %get-tuple-element.79), channel_id=1, source_target_pairs={{0,1},{1,0},{2,3},{3,2},{4,5},{5,4},{6,7},{7,6},{8,9},{9,8},{10,11... | collective-permute-start | bytes 393224 | tf_op jit(solution)/shard_map/ppermute | solution.py:683
  152.1 4.3 %collective-permute-done.8.refs_2_ = bf16[128,512]{1,0:T(8,128)(2,1)S(1)} collective-permute-done((bf16[128,512]{1,0:T(8,128)(2,1)S(1)}, bf16[128,512]{1,0:T(8,128)(2,1)S(1)}, u32[]{:S(2)}, u32[]{:S(2)}) %collective-permute-start.8) | collective-permute-done | bytes 131104 | tf_op jit(solution)/shard_map/ppermute | solution.py:683
  157.7 1.8 %collective-permute-start.10 = (bf16[2,64,512]{2,1,0:T(8,128)(2,1)S(1)}, bf16[2,64,512]{2,1,0:T(8,128)(2,1)S(1)}, u32[]{:S(2)}, u32[]{:S(2)}) collective-permute-start(bf16[2,64,512]{2,1,0:T(8,128)(2,1)S(1)} %get-tuple-element.82), channel_id=1, source_target_pairs={{0,8},{2,10},{4,12},{6,14},{8,0},{10,2},{12,4},{14,6},{16,24},{18,... | collective-permute-start | bytes 393224 | tf_op jit(solution)/shard_map/ppermute | solution.py:683
  159.5 3.2 %collective-permute-done.10.refs_1_ = bf16[2,64,512]{2,1,0:T(8,128)(2,1)S(1)} collective-permute-done((bf16[2,64,512]{2,1,0:T(8,128)(2,1)S(1)}, bf16[2,64,512]{2,1,0:T(8,128)(2,1)S(1)}, u32[]{:S(2)}, u32[]{:S(2)}) %collective-permute-start.10) | collective-permute-done | bytes 131104 | tf_op jit(solution)/shard_map/ppermute | solution.py:683
  163.3 2.9 %collective-permute-start.11 = (bf16[2,32,512]{2,1,0:T(8,128)(2,1)S(1)}, bf16[2,32,512]{2,1,0:T(8,128)(2,1)S(1)}, u32[]{:S(2)}, u32[]{:S(2)}) collective-permute-start(bf16[2,32,512]{2,1,0:T(8,128)(2,1)S(1)} %get-tuple-element.84), channel_id=1, source_target_pairs={{0,16},{2,18},{4,20},{6,22},{8,24},{10,26},{12,28},{14,30},{16,0},... | collective-permute-start | bytes 196616 | tf_op jit(solution)/shard_map/ppermute | solution.py:683
  (118 shorter events, 39.8 us)
Async XLA Ops:
  1.7 21.7 %collective-permute-start.3 = (bf16[3,8,1,512]{3,2,1,0:T(2,128)(2,1)S(1)}, bf16[3,8,1,512]{3,2,1,0:T(2,128)(2,1)S(1)}, u32[]{:S(2)}, u32[]{:S(2)}) collective-permute-start(bf16[3,8,1,512]{3,2,1,0:T(2,128)(2,1)S(1)} %broadcast_select_fusion.2), channel_id=1, source_target_pairs={{0,1},{1,0},{2,3},{3,2},{4,5},{5,4},{6,7},{7,6},{8,9},{9,8},{10,11... | collective-permute-start | bytes 73736 | tf_op jit(solution)/shard_map/ppermute | solution.py:119
  4.8 18.7 %collective-permute-start.4 = (bf16[3,1,1,512]{3,2,1,0:T(2,128)(2,1)S(1)}, bf16[3,1,1,512]{3,2,1,0:T(2,128)(2,1)S(1)}, u32[]{:S(2)}, u32[]{:S(2)}) collective-permute-start(bf16[3,1,1,512]{3,2,1,0:T(2,128)(2,1)S(1)} %get-tuple-element.93), channel_id=1, source_target_pairs={{0,31},{1,30},{2,1},{3,0},{4,3},{5,2},{6,5},{7,4},{8,7},{9,6},{10,... | collective-permute-start | bytes 9224 | tf_op jit(solution)/shard_map/ppermute | solution.py:119
  8.5 14.9 %collective-permute-start.2 = (bf16[3,1,1,512]{3,2,1,0:T(2,128)(2,1)S(1)}, bf16[3,1,1,512]{3,2,1,0:T(2,128)(2,1)S(1)}, u32[]{:S(2)}, u32[]{:S(2)}) collective-permute-start(bf16[3,1,1,512]{3,2,1,0:T(2,128)(2,1)S(1)} %get-tuple-element.94), channel_id=1, source_target_pairs={{0,3},{1,2},{2,5},{3,4},{4,7},{5,6},{6,9},{7,8},{8,11},{9,10},{10,... | collective-permute-start | bytes 9224 | tf_op jit(solution)/shard_map/ppermute | solution.py:119
  9.3 26.4 %collective-permute-start.1 = (bf16[3,1,16,512]{3,2,1,0:T(8,128)(2,1)S(1)}, bf16[3,1,16,512]{3,2,1,0:T(8,128)(2,1)S(1)}, u32[]{:S(2)}, u32[]{:S(2)}) collective-permute-start(bf16[3,1,16,512]{3,2,1,0:T(8,128)(2,1)S(1)} %get-tuple-element.89), channel_id=1, source_target_pairs={{0,30},{2,0},{4,2},{6,4},{8,6},{10,8},{12,10},{14,12},{16,14},{18,... | collective-permute-start | bytes 147464 | tf_op jit(solution)/shard_map/ppermute | solution.py:112
  14.7 20.9 %collective-permute-start = (bf16[3,1,16,512]{3,2,1,0:T(8,128)(2,1)S(1)}, bf16[3,1,16,512]{3,2,1,0:T(8,128)(2,1)S(1)}, u32[]{:S(2)}, u32[]{:S(2)}) collective-permute-start(bf16[3,1,16,512]{3,2,1,0:T(8,128)(2,1)S(1)} %get-tuple-element.90), channel_id=1, source_target_pairs={{0,2},{2,4},{4,6},{6,8},{8,10},{10,12},{12,14},{14,16},{16,18},{18... | collective-permute-start | bytes 147464 | tf_op jit(solution)/shard_map/ppermute | solution.py:111
  16.5 23.2 %copy-start.38 = (bf16[512,1024]{1,0:T(8,128)(2,1)S(1)}, bf16[512,1024]{1,0:T(8,128)(2,1)}, u32[]{:S(2)}) copy-start(bf16[512,1024]{1,0:T(8,128)(2,1)} %param.12) | copy-start | bytes 3145732
  17.6 15.5 %all-to-all-start = ((bf16[32,32,128]{2,1,0:T(8,128)(2,1)}), bf16[32,32,128]{2,1,0:T(8,128)(2,1)S(1)}, u32[]{:S(2)}, u32[]{:S(2)}) async-start(bf16[32,32,128]{2,1,0:T(8,128)(2,1)} %shard_map.128), calls=%async_computation | async-start | bytes 524288 | tf_op jit(solution)/shard_map/all_to_all | solution.py:18
  22.4 17.8 %copy-start = (bf16[512,1024]{1,0:T(8,128)(2,1)S(1)}, bf16[512,1024]{1,0:T(8,128)(2,1)}, u32[]{:S(2)}) copy-start(bf16[512,1024]{1,0:T(8,128)(2,1)} %refs_2_.5) | copy-start | bytes 3145732
  36.3 19.4 %all-to-all-start.1 = ((bf16[32,16,128]{2,1,0:T(8,128)(2,1)}), bf16[32,16,128]{2,1,0:T(8,128)(2,1)}, u32[]{:S(2)}, u32[]{:S(2)}) async-start(bf16[32,16,128]{2,1,0:T(8,128)(2,1)} %bitcast.6), calls=%async_computation.1 | async-start | bytes 262144 | tf_op jit(solution)/shard_map/all_to_all | solution.py:18
  58.6 10.6 %copy-start.19 = (f32[3,3,512]{2,1,0:T(4,128)S(1)}, f32[3,3,512]{2,1,0:T(4,128)}, u32[]{:S(2)}) copy-start(f32[3,3,512]{2,1,0:T(4,128)} %kernel_ref.1) | copy-start | bytes 55300
  58.6 19.2 %copy-start.14 = (bf16[16,2,16,128]{3,2,1,0:T(8,128)(2,1)S(1)}, bf16[16,2,16,128]{3,2,1,0:T(8,128)(2,1)}, u32[]{:S(2)}) copy-start(bf16[16,2,16,128]{3,2,1,0:T(8,128)(2,1)} %copy-done.13) | copy-start | bytes 393220
  63.4 14.4 %all-to-all-start.2 = ((bf16[32,16,128]{2,1,0:T(8,128)(2,1)}), bf16[32,16,128]{2,1,0:T(8,128)(2,1)S(1)}, u32[]{:S(2)}, u32[]{:S(2)}) async-start(bf16[32,16,128]{2,1,0:T(8,128)(2,1)} %bitcast.11), calls=%async_computation.2 | async-start | bytes 262144 | tf_op jit(solution)/shard_map/all_to_all | solution.py:18
  95.9 20.1 %copy-start.32 = (bf16[1024,128]{1,0:T(8,128)(2,1)}, bf16[1024,128]{1,0:T(8,128)(2,1)S(1)}, u32[]{:S(2)}) copy-start(bf16[1024,128]{1,0:T(8,128)(2,1)S(1)} %get-tuple-element.66.refs_3_) | copy-start | bytes 786436
  95.9 20.1 %copy-start.36 = (bf16[512,128]{1,0:T(8,128)(2,1)}, bf16[512,128]{1,0:T(8,128)(2,1)S(1)}, u32[]{:S(2)}) copy-start(bf16[512,128]{1,0:T(8,128)(2,1)S(1)} %get-tuple-element.69.refs_6_) | copy-start | bytes 393220
  109.3 11.2 %all-to-all-start.5 = ((bf16[32,16,128]{2,1,0:T(8,128)(2,1)}), bf16[32,16,128]{2,1,0:T(8,128)(2,1)S(1)}, u32[]{:S(2)}, u32[]{:S(2)}) async-start(bf16[32,16,128]{2,1,0:T(8,128)(2,1)} %bitcast.18), calls=%async_computation.5 | async-start | bytes 262144 | tf_op jit(solution)/shard_map/all_to_all | solution.py:18
  112.2 1.5 copy-start.10
  123.4 1.5 copy-start.11
  124.9 3.5 %copy-start.27 = (bf16[3,1024,128]{2,1,0:T(8,128)(2,1)S(1)}, bf16[3,1024,128]{2,1,0:T(8,128)(2,1)}, u32[]{:S(2)}) copy-start(bf16[3,1024,128]{2,1,0:T(8,128)(2,1)} %copy-done.26) | copy-start | bytes 2359300
  124.9 3.5 %copy-start.29 = (bf16[3,512,128]{2,1,0:T(8,128)(2,1)S(1)}, bf16[3,512,128]{2,1,0:T(8,128)(2,1)}, u32[]{:S(2)}) copy-start(bf16[3,512,128]{2,1,0:T(8,128)(2,1)} %copy-done.28) | copy-start | bytes 1179652
  124.9 3.5 %copy-start.31 = (bf16[1024,128]{1,0:T(8,128)(2,1)S(1)}, bf16[1024,128]{1,0:T(8,128)(2,1)}, u32[]{:S(2)}) copy-start(bf16[1024,128]{1,0:T(8,128)(2,1)} %copy-done.30) | copy-start | bytes 786436
  124.9 3.5 %copy-start.33 = (bf16[1024,128]{1,0:T(8,128)(2,1)S(1)}, bf16[1024,128]{1,0:T(8,128)(2,1)}, u32[]{:S(2)}) copy-start(bf16[1024,128]{1,0:T(8,128)(2,1)} %copy-done.32) | copy-start | bytes 786436
  124.9 3.5 %copy-start.35 = (bf16[512,128]{1,0:T(8,128)(2,1)S(1)}, bf16[512,128]{1,0:T(8,128)(2,1)}, u32[]{:S(2)}) copy-start(bf16[512,128]{1,0:T(8,128)(2,1)} %copy-done.34) | copy-start | bytes 393220
  124.9 3.5 %copy-start.37 = (bf16[512,128]{1,0:T(8,128)(2,1)S(1)}, bf16[512,128]{1,0:T(8,128)(2,1)}, u32[]{:S(2)}) copy-start(bf16[512,128]{1,0:T(8,128)(2,1)} %copy-done.36) | copy-start | bytes 393220
  131.1 2.7 %collective-permute-start.5 = (bf16[2,256,1024]{2,1,0:T(8,128)(2,1)S(1)}, bf16[2,256,1024]{2,1,0:T(8,128)(2,1)S(1)}, u32[]{:S(2)}, u32[]{:S(2)}) collective-permute-start(bf16[2,256,1024]{2,1,0:T(8,128)(2,1)S(1)} %get-tuple-element.72), channel_id=1, source_target_pairs={{0,2},{2,0},{4,6},{6,4},{8,10},{10,8},{12,14},{14,12},{16,18},{18,... | collective-permute-start | bytes 3145736 | tf_op jit(solution)/shard_map/ppermute | solution.py:683
  131.1 13.3 %all-to-all-start.6 = ((bf16[32,32,128]{2,1,0:T(8,128)(2,1)}), bf16[32,32,128]{2,1,0:T(8,128)(2,1)S(1)}, u32[]{:S(2)}, u32[]{:S(2)}) async-start(bf16[32,32,128]{2,1,0:T(8,128)(2,1)} %get-tuple-element.61), calls=%async_computation.6 | async-start | bytes 524288 | tf_op jit(solution)/shard_map/all_to_all | solution.py:18
  135.3 12.9 %collective-permute-start.6 = (bf16[128,1024]{1,0:T(8,128)(2,1)}, bf16[128,1024]{1,0:T(8,128)(2,1)S(1)}, u32[]{:S(2)}, u32[]{:S(2)}) collective-permute-start(bf16[128,1024]{1,0:T(8,128)(2,1)} %get-tuple-element.75), channel_id=1, source_target_pairs={{0,4},{2,6},{4,0},{6,2},{8,12},{10,14},{12,8},{14,10},{16,20},{18,... | collective-permute-start | bytes 786440 | tf_op jit(solution)/shard_map/ppermute | solution.py:683
  136.9 11.3 %collective-permute-start.7 = (bf16[256,512]{1,0:T(8,128)(2,1)}, bf16[256,512]{1,0:T(8,128)(2,1)S(1)}, u32[]{:S(2)}, u32[]{:S(2)}) collective-permute-start(bf16[256,512]{1,0:T(8,128)(2,1)} %get-tuple-element.76), channel_id=1, source_target_pairs={{0,1},{1,0},{2,3},{3,2},{4,5},{5,4},{6,7},{7,6},{8,9},{9,8},{10,11... | collective-permute-start | bytes 786440 | tf_op jit(solution)/shard_map/ppermute | solution.py:683
  145.6 20.6 %all-to-all-start.7 = ((bf16[32,32,128]{2,1,0:T(8,128)(2,1)}), bf16[32,32,128]{2,1,0:T(8,128)(2,1)S(1)}, u32[]{:S(2)}, u32[]{:S(2)}) async-start(bf16[32,32,128]{2,1,0:T(8,128)(2,1)} %bitcast.21), calls=%async_computation.7 | async-start | bytes 524288 | tf_op jit(solution)/shard_map/all_to_all | solution.py:18
  148.9 7.5 %collective-permute-start.8 = (bf16[128,512]{1,0:T(8,128)(2,1)S(1)}, bf16[128,512]{1,0:T(8,128)(2,1)S(1)}, u32[]{:S(2)}, u32[]{:S(2)}) collective-permute-start(bf16[128,512]{1,0:T(8,128)(2,1)S(1)} %get-tuple-element.79), channel_id=1, source_target_pairs={{0,1},{1,0},{2,3},{3,2},{4,5},{5,4},{6,7},{7,6},{8,9},{9,8},{10,11... | collective-permute-start | bytes 393224 | tf_op jit(solution)/shard_map/ppermute | solution.py:683
  150.6 6.5 %collective-permute-start.9 = (bf16[128,512]{1,0:T(8,128)(2,1)S(1)}, bf16[128,512]{1,0:T(8,128)(2,1)S(1)}, u32[]{:S(2)}, u32[]{:S(2)}) collective-permute-start(bf16[128,512]{1,0:T(8,128)(2,1)S(1)} %get-tuple-element.80), channel_id=1, source_target_pairs={{0,4},{2,6},{4,0},{6,2},{8,12},{10,14},{12,8},{14,10},{16,20},{18,... | collective-permute-start | bytes 393224 | tf_op jit(solution)/shard_map/ppermute | solution.py:683
  157.7 5.0 %collective-permute-start.10 = (bf16[2,64,512]{2,1,0:T(8,128)(2,1)S(1)}, bf16[2,64,512]{2,1,0:T(8,128)(2,1)S(1)}, u32[]{:S(2)}, u32[]{:S(2)}) collective-permute-start(bf16[2,64,512]{2,1,0:T(8,128)(2,1)S(1)} %get-tuple-element.82), channel_id=1, source_target_pairs={{0,8},{2,10},{4,12},{6,14},{8,0},{10,2},{12,4},{14,6},{16,24},{18,... | collective-permute-start | bytes 393224 | tf_op jit(solution)/shard_map/ppermute | solution.py:683
  163.3 5.3 %collective-permute-start.11 = (bf16[2,32,512]{2,1,0:T(8,128)(2,1)S(1)}, bf16[2,32,512]{2,1,0:T(8,128)(2,1)S(1)}, u32[]{:S(2)}, u32[]{:S(2)}) collective-permute-start(bf16[2,32,512]{2,1,0:T(8,128)(2,1)S(1)} %get-tuple-element.84), channel_id=1, source_target_pairs={{0,16},{2,18},{4,20},{6,22},{8,24},{10,26},{12,28},{14,30},{16,0},... | collective-permute-start | bytes 196616 | tf_op jit(solution)/shard_map/ppermute | solution.py:683
  (25 other events, 24.9 us)

commit v4 on v3

--- a/solution.py
+++ b/solution.py
@@ -22,6 +22,14 @@
 
 
 def call(kernel, out_shape, operands, ins, outs, scratch=(), flops=0, moved=0, limit=8):
+    operands = [
+        pltpu.with_memory_space_constraint(value, pltpu.HBM) if kind == "h" else value
+        for kind, value in zip(ins, operands, strict=True)
+    ]
+    out_shape = [
+        pltpu.HBM(value.shape, value.dtype) if kind == "h" else value
+        for kind, value in zip(outs, out_shape, strict=True)
+    ]
     return pl.pallas_call(
         kernel,
         out_shape=out_shape,
@@ -136,70 +144,67 @@
 
 
 def forward_kernel(
-    states_hbm, low_ref, high_ref, before_ref, after_ref, kernel_ref, gain_ref, up_ref,
+    step, states_hbm, low_ref, high_ref, before_ref, after_ref, kernel_ref, gain_ref, up_ref,
     n_hbm, aux_hbm, hid_hbm, slope_hbm, pad_hbm,
-    states_ref, n_ref, aux_ref, hid_ref, slope_ref, pad_ref, sems,
+    state_ref, n_ref, aux_ref, hid_ref, slope_ref, pad_ref, sems,
 ):
-    steps, rows_out, cols_out, channels = states_ref.shape
+    rows_out, cols_out, channels = state_ref.shape
     count = rows_out * cols_out
-    order = list(reversed(range(steps)))
-    arriving = copies(sems, 0, [(states_hbm.at[s], states_ref.at[s]) for s in order])
+    arriving = copies(sems, 0, [(states_hbm.at[step], state_ref)])
     gain = jnp.broadcast_to(gain_ref[...], (count, channels)).T
-    leaving = []
-    for turn, s in enumerate(order):
-        arriving[turn].wait()
-        pad_ref[s, 1 : 1 + rows_out, MARGIN : MARGIN + cols_out] = states_ref[s].astype(jnp.float32)
-        pad_ref[s, :1, MARGIN : MARGIN + cols_out] = low_ref[s].astype(jnp.float32)
-        pad_ref[s, 1 + rows_out :, MARGIN : MARGIN + cols_out] = high_ref[s].astype(jnp.float32)
-        pad_ref[s, :, MARGIN - 1 : MARGIN] = before_ref[s].astype(jnp.float32)
-        pad_ref[s, :, MARGIN + cols_out : MARGIN + cols_out + 1] = after_ref[s].astype(jnp.float32)
-        mixed = pad_ref[s, 1 : 1 + rows_out, MARGIN : MARGIN + cols_out]
-        for col_tap in range(3):
-            place = MARGIN - 1 + col_tap
-            shifted_cols = pad_ref[s, :, place : place + cols_out]
-            for row_tap in range(3):
-                tap = kernel_ref[row_tap, col_tap : col_tap + 1]
-                mixed = mixed + tap[None] * shifted_cols[row_tap : row_tap + rows_out]
-        mixed = mixed.reshape(count, channels).T
-        inv_root = lax.rsqrt(jnp.mean(mixed * mixed, axis=0, keepdims=True) + EPSILON)
-        normed = mixed * inv_root
-        narrow = (normed * gain).astype(jnp.bfloat16)
-        pre = jnp.dot(up_ref[...], narrow, preferred_element_type=jnp.float32)
-        sigmoid = jax.nn.sigmoid(pre)
-        n_ref[s] = narrow
-        aux_ref[s, :channels] = normed
-        aux_ref[s, channels : 2 * channels] = gain
-        aux_ref[s, 2 * channels :] = jnp.broadcast_to(inv_root, (8, count))
-        hid_ref[s] = (pre * sigmoid).astype(jnp.bfloat16)
-        slope_ref[s] = sigmoid * (1.0 + pre * (1.0 - sigmoid))
-        pairs = [(slope_ref, slope_hbm), (aux_ref, aux_hbm), (n_ref, n_hbm), (hid_ref, hid_hbm), (pad_ref, pad_hbm)]
-        leaving += copies(sems, steps + 5 * turn, [(src.at[s], dst.at[s]) for src, dst in pairs])
-    finish(leaving)
-
-
-def forward_parts(states, around, kernel, norm_gain, w_up_t):
-    steps, rows_out, cols_out, channels = states.shape
+    aux_ref[channels : 2 * channels] = gain
+    pad_ref[:1, MARGIN : MARGIN + cols_out] = low_ref[step].astype(jnp.float32)
+    pad_ref[1 + rows_out :, MARGIN : MARGIN + cols_out] = high_ref[step].astype(jnp.float32)
+    pad_ref[:, MARGIN - 1 : MARGIN] = before_ref[step].astype(jnp.float32)
+    pad_ref[:, MARGIN + cols_out : MARGIN + cols_out + 1] = after_ref[step].astype(jnp.float32)
+    finish(arriving)
+    mixed = state_ref[...].astype(jnp.float32)
+    pad_ref[1 : 1 + rows_out, MARGIN : MARGIN + cols_out] = mixed
+    leaving = copies(sems, 1, [(pad_ref, pad_hbm)])
+    for col_tap in range(3):
+        place = MARGIN - 1 + col_tap
+        shifted_cols = pad_ref[:, place : place + cols_out]
+        for row_tap in range(3):
+            tap = kernel_ref[row_tap, col_tap : col_tap + 1]
+            mixed = mixed + tap[None] * shifted_cols[row_tap : row_tap + rows_out]
+    mixed = mixed.reshape(count, channels).T
+    inv_root = lax.rsqrt(jnp.mean(mixed * mixed, axis=0, keepdims=True) + EPSILON)
+    normed = mixed * inv_root
+    narrow = (normed * gain).astype(jnp.bfloat16)
+    n_ref[...] = narrow
+    aux_ref[:channels] = normed
+    aux_ref[2 * channels :] = jnp.broadcast_to(inv_root, (8, count))
+    leaving += copies(sems, 2, [(n_ref, n_hbm), (aux_ref, aux_hbm)])
+    pre = jnp.dot(up_ref[...], narrow, preferred_element_type=jnp.float32)
+    sigmoid = jax.nn.sigmoid(pre)
+    hid_ref[...] = (pre * sigmoid).astype(jnp.bfloat16)
+    slope_ref[...] = sigmoid * (1.0 + pre * (1.0 - sigmoid))
+    finish(leaving + copies(sems, 4, [(hid_ref, hid_hbm), (slope_ref, slope_hbm)]))
+
+
+def forward_parts(step, states, around, kernel, norm_gain, w_up_t):
+    _, rows_out, cols_out, channels = states.shape
     hid = w_up_t.shape[0]
     count = rows_out * cols_out
     shapes = [
-        ((steps, channels, count), jnp.bfloat16),
-        ((steps, 2 * channels + 8, count), jnp.float32),
-        ((steps, hid, count), jnp.bfloat16),
-        ((steps, hid, count), jnp.float32),
-        ((steps, rows_out + 2, cols_out + 2 * MARGIN, channels), jnp.float32),
+        ((channels, count), jnp.bfloat16),
+        ((2 * channels + 8, count), jnp.float32),
+        ((hid, count), jnp.bfloat16),
+        ((hid, count), jnp.float32),
+        ((rows_out + 2, cols_out + 2 * MARGIN, channels), jnp.float32),
     ]
     return call(
-        forward_kernel,
+        functools.partial(forward_kernel, step),
         [jax.ShapeDtypeStruct(*shape) for shape in shapes],
         [states, *around, kernel, norm_gain.reshape(1, channels), w_up_t],
         "hvvvvvvv",
         "hhhhh",
-        scratch=[pltpu.VMEM(states.shape, jnp.bfloat16)]
+        scratch=[pltpu.VMEM(states.shape[1:], jnp.bfloat16)]
         + [pltpu.VMEM(*shape) for shape in shapes]
-        + [pltpu.SemaphoreType.DMA((6 * steps,))],
-        flops=2 * steps * count * hid * channels,
-        moved=2**23,
-        limit=20,
+        + [pltpu.SemaphoreType.DMA((6,))],
+        flops=2 * count * hid * channels,
+        moved=2**22,
+        limit=12,
     )
 
 
@@ -218,13 +223,14 @@
 
 
 def stencil_kernel(steps, tile, *refs):
-    pad_hbm, *field_hbm, out_ref, pad_ref, field_ref, sems = refs
-    arriving = copies(sems, 0, [(pad_hbm.at[s], pad_ref.at[k]) for k, s in enumerate(steps)])
-    arriving += copies(sems, len(steps), [(ref, field_ref.at[k]) for k, ref in enumerate(field_hbm)])
+    *inputs, out_ref, pad_ref, field_ref, sems = refs
+    pad_hbm, field_hbm = inputs[:steps], inputs[steps:]
+    arriving = copies(sems, 0, [(ref, pad_ref.at[k]) for k, ref in enumerate(pad_hbm)])
+    arriving += copies(sems, steps, [(ref, field_ref.at[k]) for k, ref in enumerate(field_hbm)])
     total = None
-    for k in range(len(steps)):
+    for k in range(steps):
         arriving[k].wait()
-        arriving[len(steps) + k].wait()
+        arriving[steps + k].wait()
         rows = stencil_sums(pad_ref.at[k], field_ref[k], tile)
         total = rows if total is None else [a + b for a, b in zip(total, rows)]
     out_ref[...] = jnp.zeros_like(out_ref)
@@ -232,25 +238,26 @@
         out_ref[k : k + 1] = row
 
 
-def stencil_terms(steps, tile, pad, fields):
+def stencil_terms(tile, pads, fields):
+    steps = len(fields)
     channels, count = fields[0].shape
     return call(
         functools.partial(stencil_kernel, steps, tile),
         [jax.ShapeDtypeStruct((ROWS, channels), jnp.float32)],
-        [pad, *fields],
-        "h" * (1 + len(fields)),
+        [*pads, *fields],
+        "h" * 2 * steps,
         "v",
         scratch=[
-            pltpu.VMEM((len(steps), *pad.shape[1:]), jnp.float32),
-            pltpu.VMEM((len(steps), channels, count), jnp.bfloat16),
-            pltpu.SemaphoreType.DMA((2 * len(steps),)),
+            pltpu.VMEM((steps, *pads[0].shape), jnp.float32),
+            pltpu.VMEM((steps, channels, count), jnp.bfloat16),
+            pltpu.SemaphoreType.DMA((2 * steps,)),
         ],
         moved=2**21,
         limit=12,
     )[0]
 
 
-def network_kernel(step, tile, with_before, with_sums, *refs):
+def network_kernel(tile, with_before, with_sums, *refs):
     refs = list(refs)
     take = lambda: refs.pop(0)
     moved_ref, down_ref, up_ref, slope_hbm, aux_hbm = (take() for _ in range(5))
@@ -259,11 +266,11 @@
     out_hbm, grad_hbm, saved_hbm = take(), take(), take()
     term_hbm = None if with_sums else take()
     slope_ref, aux_ref, before_ref, out_ref, grad_ref, pad_ref, sems = refs
-    pairs = [(slope_hbm.at[step], slope_ref), (aux_hbm.at[step], aux_ref)]
+    pairs = [(slope_hbm, slope_ref), (aux_hbm, aux_ref)]
     if with_before:
         pairs.append((before_hbm, before_ref))
     if with_sums:
-        pairs.append((pad_hbm.at[step], pad_ref))
+        pairs.append((pad_hbm, pad_ref))
     arriving = copies(sems, 0, pairs)
     leaving = copies(sems, 4, [(moved_ref, saved_hbm)])
     moved = moved_ref[...]
@@ -302,7 +309,7 @@
     finish(leaving + copies(sems, 6, [(out_ref, out_hbm)]))
 
 
-def network_back(step, tile, devices, moved, w_down_t, w_up, slope, aux, before, pad=None, sums=None):
+def network_back(tile, devices, moved, w_down_t, w_up, slope, aux, before, pad=None, sums=None):
     channels, count = moved.shape
     hid = w_down_t.shape[0]
     with_before, with_sums = before is not None, pad is not None
@@ -314,18 +321,18 @@
     operands += [before] if with_before else []
     operands += [pad, sums] if with_sums else []
     return call(
-        functools.partial(network_kernel, step, tile, with_before, with_sums),
+        functools.partial(network_kernel, tile, with_before, with_sums),
         out,
         operands,
         "vvvhh" + "h" * with_before + "hv" * with_sums,
         "h" * len(out),
         scratch=[
             pltpu.VMEM((hid, count), jnp.float32),
-            pltpu.VMEM(aux.shape[1:], jnp.float32),
+            pltpu.VMEM(aux.shape, jnp.float32),
             pltpu.VMEM((channels, count), jnp.float32),
             pltpu.VMEM(out_shape, jnp.bfloat16),
             pltpu.VMEM((hid, count), jnp.bfloat16),
-            pltpu.VMEM(pad.shape[1:] if with_sums else (8, count), jnp.float32),
+            pltpu.VMEM(pad.shape if with_sums else (8, count), jnp.float32),
             pltpu.SemaphoreType.DMA((8,)),
         ],
         flops=4 * count * hid * channels,
@@ -594,17 +601,16 @@
 
 def gradient_kernel(row_groups, bit_ref, *refs):
     *inputs, send_ref, keep_ref, left_ref, right_ref, sems = refs
-    steps = len(inputs) // 2 - 1
-    narrow_hbm, hidden_hbm = inputs[:2]
-    grads_hbm, moved_hbm = inputs[2 : 2 + steps], inputs[2 + steps :]
+    steps = len(inputs) // 4
+    narrow_hbm, hidden_hbm, grads_hbm, moved_hbm = (inputs[k * steps : (k + 1) * steps] for k in range(4))
     channels, hid = left_ref.shape[1], right_ref.shape[1]
-    count = narrow_hbm.shape[2]
+    count = narrow_hbm[0].shape[1]
     arriving = []
     for k in range(2):
         for s in range(steps):
             lanes = pl.ds(s * count, count)
-            left = narrow_hbm.at[s] if k == 0 else moved_hbm[s]
-            right = grads_hbm[s] if k == 0 else hidden_hbm.at[s]
+            left = narrow_hbm[s] if k == 0 else moved_hbm[s]
+            right = grads_hbm[s] if k == 0 else hidden_hbm[s]
             pairs = [(left, left_ref.at[k, :, lanes]), (right, right_ref.at[k, :, lanes])]
             arriving += copies(sems, 2 * (k * steps + s), pairs)
     chunk = channels // (2 * row_groups)
@@ -684,8 +690,9 @@
 
 
 def projection_sums(narrow, hidden, grads, moved):
-    steps, channels, count = narrow.shape
-    hid = hidden.shape[1]
+    steps = len(narrow)
+    channels, count = narrow[0].shape
+    hid = hidden[0].shape[0]
     lon, lat = lax.axis_size("lon"), lax.axis_size("lat")
     if lat != 2 or lon != 16:
         lanes_both = (((1,), (1,)), ((), ()))
@@ -701,8 +708,8 @@
     send, keep = call(
         functools.partial(gradient_kernel, groups),
         [sds(shape, jnp.bfloat16), sds(shape, jnp.bfloat16)],
-        [bits, narrow, hidden, *grads, *moved],
-        "shh" + "h" * 2 * steps,
+        [bits, *narrow, *hidden, *grads, *moved],
+        "s" + "h" * 4 * steps,
         "vv",
         scratch=[
             pltpu.VMEM((2, channels, steps * count), jnp.bfloat16),
@@ -760,7 +767,9 @@
             return blocks
         return jnp.concatenate([blocks[:, :share], blocks[:, padded_share : padded_share + share]], axis=1)
 
-    arrived = as_grid(exchanged(packed(cotangent, bilinear, devices)))
+    blocks = packed(cotangent, bilinear, devices)
+    blocks, states_later = lax.optimization_barrier((blocks, states))
+    arrived = as_grid(exchanged(blocks))
     group = me * share // group_size
     moves = jnp.stack([lon_move[:, group], lat_move[:, group]], axis=1)
     grid_now, weights = spatial("first", steps - 1, tile, padded_share, arrived, None, None, moves[steps - 1])
@@ -768,31 +777,33 @@
     taps = lax.dynamic_slice_in_dim(kernel.reshape(9, channels), me * share, share, 1).T
     taps = jnp.pad(taps, ((0, padded_share - share), (0, count - 9)))
 
-    around = edges(states)
+    around = edges(states_later)
     w_up_t, w_down_t = w_up.T, w_down.T
     grid_now, around = lax.optimization_barrier((grid_now, around))
-    narrow, aux, hidden, slope, pad = forward_parts(states, around, kernel, norm_gain, w_up_t)
+    order = list(reversed(range(steps)))
+    forward = {s: forward_parts(s, states, around, kernel, norm_gain, w_up_t) for s in order}
+    narrow, aux, hidden, slope, pad = ({s: forward[s][k] for s in order} for k in range(5))
 
     moved, grads, fields = {}, {}, {}
     term = None
-    for s in reversed(range(steps)):
+    for s in order:
         here = as_rows(exchanged(grid_now.reshape(devices, padded_share, count)))
-        common = (s, tile, devices, here, w_down_t, w_up, slope, aux, term)
+        common = (tile, devices, here, w_down_t, w_up, slope[s], aux[s], term)
         if s > 0:
             fields[s], grads[s], moved[s], term = network_back(*common)
             arrived = as_grid(exchanged(as_blocks(fields[s])))
             (grid_now,) = spatial("mid", s - 1, tile, padded_share, arrived, taps, weights, moves[s - 1])
         else:
             later = list(fields)
-            sums = stencil_terms(later, tile, pad, [fields[k] for k in later])
-            blocks, grads[s], moved[s] = network_back(*common, pad, sums)
+            sums = stencil_terms(tile, [pad[k] for k in later], [fields[k] for k in later])
+            blocks, grads[s], moved[s] = network_back(*common, pad[s], sums)
             arrived = as_grid(exchanged(as_pairs(blocks)))
             (grid_now,) = spatial("last", None, tile, padded_share, arrived, taps, None, None)
 
     arrived = exchanged(grid_now.reshape(devices, 2 * padded_share, count))
     grad_state, grad_kernel, grad_gain = final_parts(from_pairs(arrived), channels)
-    by_step = lambda values: [values[s] for s in range(steps)]
-    grad_up, grad_down = projection_sums(narrow, hidden, by_step(grads), by_step(moved))
+    by_step = lambda values: [values[s] for s in order]
+    grad_up, grad_down = projection_sums(*map(by_step, (narrow, hidden, grads, moved)))
     return (grad_state.reshape(cotangent.shape), grad_up, grad_down, grad_kernel, grad_gain.reshape(channels))
 
 

time: 171 us -> 143 us (0.84)
  local copies, waits for them, and re-layouts: 28.3 us -> 5.18 us
  blocking collectives: 20.7 us -> 11.2 us
  Pallas kernels: 35.1 us -> 43.2 us
  waiting for transfers between devices: 37.1 us -> 33.6 us
  starting transfers between devices: 45 us -> 47.7 us
    unnamed x83 -> x13, local copies, waits for them, and re-layouts: 26.4 us -> 2.88 us
    all_to_all x2 -> x1, blocking collectives: 20.7 us -> 11.2 us  [exchanged(): return lax.all_to_all(blocks, AXES, split_axis=0, concat_axis=0, tiled=True)]
    pallas_call x17 -> x19, Pallas kernels: 35.1 us -> 43.2 us  [call(): pl.pallas_call(kernel, out_shape=out_shape, in_specs=[pl.BlockSpec(memory...]
    all_to_all x6 -> x7, waiting for transfers between devices: 27.9 us -> 24.3 us  [exchanged(): return lax.all_to_all(blocks, AXES, split_axis=0, concat_axis=0, tiled=True)]
    all_to_all x6 -> x7, starting transfers between devices: 21.8 us -> 24.9 us  [exchanged(): return lax.all_to_all(blocks, AXES, split_axis=0, concat_axis=0, tiled=True)]
  transfers between devices with their start and end apart: 18 -> 19, of which waited for: 8 -> 9; matrix products, arithmetic and copies ran while one was open for 2% -> 3% of each run, Pallas kernels for 10% -> 14%
where the time goes in v4:
time: 143 us; the launch traced here: 142 us
  starting transfers between devices  47.7 us (33%)
  Pallas kernels  43.2 us (30%)
  waiting for transfers between devices  33.6 us (23%)
  blocking collectives  11.2 us (8%)
  local copies, waits for them, and re-layouts  5.18 us (4%)
    pallas_call x19, Pallas kernels, call(): pl.pallas_call(kernel, out_shape=out_shape, in_specs=[pl.BlockSpec(memory...  43.2 us
    all_to_all x7, starting transfers between devices, exchanged(): return lax.all_to_all(blocks, AXES, split_axis=0, concat_axis=0, tiled=True)  24.9 us
    all_to_all x7, waiting for transfers between devices, exchanged(): return lax.all_to_all(blocks, AXES, split_axis=0, concat_axis=0, tiled=True)  24.3 us
    all_to_all x1, blocking collectives, exchanged(): return lax.all_to_all(blocks, AXES, split_axis=0, concat_axis=0, tiled=True)  11.2 us
    ppermute x7, starting transfers between devices, swapped(): return lax.ppermute(value, axis, [(i, i ^ 1 << bit) for i in range(count)])  11.2 us
    ppermute x7, waiting for transfers between devices, swapped(): return lax.ppermute(value, axis, [(i, i ^ 1 << bit) for i in range(count)])  9.24 us
    ppermute x3, starting transfers between devices, sent(): return lax.ppermute(value, AXES, both)  7.22 us
    ppermute x1, starting transfers between devices, edges(): lax.ppermute(value, 'lon', [(i, (i - 1) % lon) for i in range(lon)])  4.43 us
  transfers between devices with their start and end apart: 19, of which 9 were waited for; matrix products, arithmetic and copies ran while one was open for 3% of the time, Pallas kernels for 14%

profile of v4, /device:TPU:0, one launch (start us, length us, event | category | flops | bytes accessed | tf_op | source)
XLA Modules:
  0.0 142.2 jit_solution(1495010863980146731)
XLA Ops:
  0.7 1.9 %shard_map.128 = bf16[32,32,128]{2,1,0:T(8,128)(2,1)} custom-call(bf16[128,512]{1,0:T(8,128)(2,1)} %bitcast.53, f32[12,8,16]{2,1,0:T(8,128)} %bitcast.55), custom_call_target="tpu_custom_call" | custom-call | bytes 524288 | tf_op jit(solution)/shard_map/pallas_call | solution.py:33
  2.6 7.3 %all-to-all-start = ((bf16[32,32,128]{2,1,0:T(8,128)(2,1)}), bf16[32,32,128]{2,1,0:T(8,128)(2,1)S(1)}, u32[]{:S(2)}, u32[]{:S(2)}) async-start(bf16[32,32,128]{2,1,0:T(8,128)(2,1)} %shard_map.128), calls=%async_computation | async-start | bytes 524288 | tf_op jit(solution)/shard_map/all_to_all | solution.py:18
  10.0 1.8 %collective-permute-start.3 = (bf16[3,8,1,512]{3,2,1,0:T(2,128)(2,1)S(1)}, bf16[3,8,1,512]{3,2,1,0:T(2,128)(2,1)S(1)}, u32[]{:S(2)}, u32[]{:S(2)}) collective-permute-start(bf16[3,8,1,512]{3,2,1,0:T(2,128)(2,1)S(1)} %broadcast_select_fusion.2), channel_id=1, source_target_pairs={{0,1},{1,0},{2,3},{3,2},{4,5},{5,4},{6,7},{7,6},{8,9},{9,8},{10,11... | collective-permute-start | bytes 73736 | tf_op jit(solution)/shard_map/ppermute | solution.py:127
  11.9 5.3 %collective-permute-start.4 = (bf16[3,1,1,512]{3,2,1,0:T(2,128)(2,1)S(1)}, bf16[3,1,1,512]{3,2,1,0:T(2,128)(2,1)S(1)}, u32[]{:S(2)}, u32[]{:S(2)}) collective-permute-start(bf16[3,1,1,512]{3,2,1,0:T(2,128)(2,1)S(1)} %get-tuple-element.117), channel_id=1, source_target_pairs={{0,31},{1,30},{2,1},{3,0},{4,3},{5,2},{6,5},{7,4},{8,7},{9,6},{10,... | collective-permute-start | bytes 9224 | tf_op jit(solution)/shard_map/ppermute | solution.py:127
  17.3 4.4 %collective-permute-start.1 = (bf16[3,1,16,512]{3,2,1,0:T(8,128)(2,1)S(1)}, bf16[3,1,16,512]{3,2,1,0:T(8,128)(2,1)S(1)}, u32[]{:S(2)}, u32[]{:S(2)}) collective-permute-start(bf16[3,1,16,512]{3,2,1,0:T(8,128)(2,1)S(1)} %get-tuple-element.113), channel_id=1, source_target_pairs={{0,30},{2,0},{4,2},{6,4},{8,6},{10,8},{12,10},{14,12},{16,14},{18,... | collective-permute-start | bytes 147464 | tf_op jit(solution)/shard_map/ppermute | solution.py:120
  24.6 3.7 %all-to-all-start.1 = ((bf16[32,16,128]{2,1,0:T(8,128)(2,1)}), bf16[32,16,128]{2,1,0:T(8,128)(2,1)S(1)}, u32[]{:S(2)}, u32[]{:S(2)}) async-start(bf16[32,16,128]{2,1,0:T(8,128)(2,1)} %bitcast.54), calls=%async_computation.1 | async-start | bytes 262144 | tf_op jit(solution)/shard_map/all_to_all | solution.py:18
  31.1 3.1 %shard_map.130 = (bf16[512,128]{1,0:T(8,128)(2,1)}, f32[1032,128]{1,0:T(8,128)}, bf16[1024,128]{1,0:T(8,128)(2,1)}, f32[1024,128]{1,0:T(8,128)}, f32[10,32,512]{2,1,0:T(8,128)}) custom-call(bf16[3,8,16,512]{3,2,1,0:T(8,128)(2,1)} %states_hbm.5, bf16[3,1,16,512]{3,2,1,0:T(8,128)(2,1)S(1)} %collective-permute-done.low_ref, ...), custom_call_target="tpu_custom_call" | custom-call | flops 134217728 | bytes 4194304 | tf_op jit(solution)/shard_map/pallas_call | solution.py:33
  34.2 2.7 %all-to-all-done.1 = bf16[32,16,128]{2,1,0:T(8,128)(2,1)S(1)} async-done(((bf16[32,16,128]{2,1,0:T(8,128)(2,1)}), bf16[32,16,128]{2,1,0:T(8,128)(2,1)S(1)}, u32[]{:S(2)}, u32[]{:S(2)}) %all-to-all-start.1) | async-done | bytes 131104 | tf_op jit(solution)/shard_map/all_to_all | solution.py:18
  36.9 3.3 %shard_map.131 = (bf16[512,128]{1,0:T(8,128)(2,1)}, bf16[1024,128]{1,0:T(8,128)(2,1)}, bf16[512,128]{1,0:T(8,128)(2,1)}, f32[512,128]{1,0:T(8,128)}) custom-call(bf16[512,128]{1,0:T(8,128)(2,1)S(1)} %bitcast.41, bf16[1024,512]{1,0:T(8,128)(2,1)S(1)} %bitcast.35, bf16[512,1024]{1,0:T(8,128)(2,1)S(1)} %copy-done, f32[1024,128]{1,0:T(8,128)} %get-tuple-element.67.refs_3_, ...), custom_call_target="tpu_custom_call" | custom-call | flops 268435456 | bytes 4194304 | tf_op jit(solution)/shard_map/pallas_call | solution.py:33
  40.3 3.1 %all-to-all-start.2 = ((bf16[32,16,128]{2,1,0:T(8,128)(2,1)}), bf16[32,16,128]{2,1,0:T(8,128)(2,1)S(1)}, u32[]{:S(2)}, u32[]{:S(2)}) async-start(bf16[32,16,128]{2,1,0:T(8,128)(2,1)} %bitcast.49), calls=%async_computation.2 | async-start | bytes 262144 | tf_op jit(solution)/shard_map/all_to_all | solution.py:18
  44.9 7.1 %all-to-all-done.2 = bf16[32,16,128]{2,1,0:T(8,128)(2,1)S(1)} async-done(((bf16[32,16,128]{2,1,0:T(8,128)(2,1)}), bf16[32,16,128]{2,1,0:T(8,128)(2,1)S(1)}, u32[]{:S(2)}, u32[]{:S(2)}) %all-to-all-start.2) | async-done | bytes 131104 | tf_op jit(solution)/shard_map/all_to_all | solution.py:18
  52.0 3.7 %shard_map.132 = bf16[16,2,16,128]{3,2,1,0:T(8,128)(2,1)} custom-call(s32[2]{0:T(128)S(1)} %get-tuple-element.120.refs_0_, bf16[16,2,16,128]{3,2,1,0:T(8,128)(2,1)S(1)} %bitcast.43, f32[16,128]{1,0:T(8,128)S(1)} %pad.4.refs_2_.refs_1_, bf16[16,2,16,128]{3,2,1,0:T(8,128)(2,1)} %get-tuple-element.70.refs_3_), custom_call_target="tpu_custom_call" | custom-call | flops 4194304 | bytes 1048576 | tf_op jit(solution)/shard_map/pallas_call | solution.py:33
  55.7 2.6 %all-to-all-start.3 = ((bf16[32,16,128]{2,1,0:T(8,128)(2,1)}), bf16[32,16,128]{2,1,0:T(8,128)(2,1)S(1)}, u32[]{:S(2)}, u32[]{:S(2)}) async-start(bf16[32,16,128]{2,1,0:T(8,128)(2,1)} %bitcast.52), calls=%async_computation.3 | async-start | bytes 262144 | tf_op jit(solution)/shard_map/all_to_all | solution.py:18
  58.3 3.1 %shard_map.133 = (bf16[512,128]{1,0:T(8,128)(2,1)}, f32[1032,128]{1,0:T(8,128)}, bf16[1024,128]{1,0:T(8,128)(2,1)}, f32[1024,128]{1,0:T(8,128)}, f32[10,32,512]{2,1,0:T(8,128)}) custom-call(bf16[3,8,16,512]{3,2,1,0:T(8,128)(2,1)} %states_hbm.5, bf16[3,1,16,512]{3,2,1,0:T(8,128)(2,1)S(1)} %collective-permute-done.low_ref, ...), custom_call_target="tpu_custom_call" | custom-call | flops 134217728 | bytes 4194304 | tf_op jit(solution)/shard_map/pallas_call | solution.py:33
  61.5 5.5 %all-to-all-done.3 = bf16[32,16,128]{2,1,0:T(8,128)(2,1)S(1)} async-done(((bf16[32,16,128]{2,1,0:T(8,128)(2,1)}), bf16[32,16,128]{2,1,0:T(8,128)(2,1)S(1)}, u32[]{:S(2)}, u32[]{:S(2)}) %all-to-all-start.3) | async-done | bytes 131104 | tf_op jit(solution)/shard_map/all_to_all | solution.py:18
  66.9 3.4 %shard_map.134 = (bf16[512,128]{1,0:T(8,128)(2,1)}, bf16[1024,128]{1,0:T(8,128)(2,1)}, bf16[512,128]{1,0:T(8,128)(2,1)}, f32[512,128]{1,0:T(8,128)}) custom-call(bf16[512,128]{1,0:T(8,128)(2,1)S(1)} %bitcast.42, bf16[1024,512]{1,0:T(8,128)(2,1)S(1)} %bitcast.36, bf16[512,1024]{1,0:T(8,128)(2,1)S(1)} %copy-done, f32[1024,128]{1,0:T(8,128)} %get-tuple-element.71.refs_3_, ...), custom_call_target="tpu_custom_call" | custom-call | flops 268435456 | bytes 4194304 | tf_op jit(solution)/shard_map/pallas_call | solution.py:33
  70.3 11.2 %all_to_all.40 = bf16[32,16,128]{2,1,0:T(8,128)(2,1)S(1)} all-to-all(bf16[32,16,128]{2,1,0:T(8,128)(2,1)} %bitcast.50), channel_id=1, replica_groups=mesh['lon'=16,'lat'=2] {'lon','lat'}, dimensions={0} | all-to-all | bytes 262144 | tf_op jit(solution)/shard_map/all_to_all | solution.py:18
  81.5 3.7 %shard_map.135 = bf16[16,2,16,128]{3,2,1,0:T(8,128)(2,1)} custom-call(s32[2]{0:T(128)S(1)} %get-tuple-element.121.refs_0_, bf16[16,2,16,128]{3,2,1,0:T(8,128)(2,1)S(1)} %bitcast.44, f32[16,128]{1,0:T(8,128)S(1)} %pad.4.refs_2_.refs_1_, bf16[16,2,16,128]{3,2,1,0:T(8,128)(2,1)} %get-tuple-element.70.refs_3_), custom_call_target="tpu_custom_call" | custom-call | flops 4194304 | bytes 1048576 | tf_op jit(solution)/shard_map/pallas_call | solution.py:33
  85.2 2.8 %all-to-all-start.5 = ((bf16[32,16,128]{2,1,0:T(8,128)(2,1)}), bf16[32,16,128]{2,1,0:T(8,128)(2,1)S(1)}, u32[]{:S(2)}, u32[]{:S(2)}) async-start(bf16[32,16,128]{2,1,0:T(8,128)(2,1)} %bitcast.51), calls=%async_computation.5 | async-start | bytes 262144 | tf_op jit(solution)/shard_map/all_to_all | solution.py:18
  88.1 3.1 %shard_map.136 = (bf16[512,128]{1,0:T(8,128)(2,1)}, f32[1032,128]{1,0:T(8,128)}, bf16[1024,128]{1,0:T(8,128)(2,1)}, f32[1024,128]{1,0:T(8,128)}, f32[10,32,512]{2,1,0:T(8,128)}) custom-call(bf16[3,8,16,512]{3,2,1,0:T(8,128)(2,1)} %states_hbm.5, bf16[3,1,16,512]{3,2,1,0:T(8,128)(2,1)S(1)} %collective-permute-done.low_ref, ...), custom_call_target="tpu_custom_call" | custom-call | flops 134217728 | bytes 4194304 | tf_op jit(solution)/shard_map/pallas_call | solution.py:33
  91.2 2.2 %shard_map.137.refs_7_ = f32[16,512]{1,0:T(8,128)S(1)} custom-call(f32[10,32,512]{2,1,0:T(8,128)} %get-tuple-element.79.refs_0_, f32[10,32,512]{2,1,0:T(8,128)} %get-tuple-element.80.refs_1_, bf16[512,128]{1,0:T(8,128)(2,1)} %get-tuple-element.69.refs_2_, bf16[512,128]{1,0:T(8,128)(2,1)} %get-tuple-element.74.refs_3_), custom_call_target="tpu_custom_call" | custom-call | bytes 2097152 | tf_op jit(solution)/shard_map/pallas_call | solution.py:33
  93.4 3.0 %all-to-all-done.5 = bf16[32,16,128]{2,1,0:T(8,128)(2,1)S(1)} async-done(((bf16[32,16,128]{2,1,0:T(8,128)(2,1)}), bf16[32,16,128]{2,1,0:T(8,128)(2,1)S(1)}, u32[]{:S(2)}, u32[]{:S(2)}) %all-to-all-start.5) | async-done | bytes 131104 | tf_op jit(solution)/shard_map/all_to_all | solution.py:18
  96.4 3.9 %shard_map.138 = (bf16[32,32,128]{2,1,0:T(8,128)(2,1)}, bf16[1024,128]{1,0:T(8,128)(2,1)}, bf16[512,128]{1,0:T(8,128)(2,1)}) custom-call(bf16[512,128]{1,0:T(8,128)(2,1)S(1)} %bitcast.40, bf16[1024,512]{1,0:T(8,128)(2,1)S(1)} %bitcast.37, bf16[512,1024]{1,0:T(8,128)(2,1)S(1)} %copy-done, f32[1024,128]{1,0:T(8,128)} %get-tuple-element.75.refs_3_, ...), custom_call_target="tpu_custom_call" | custom-call | flops 268435456 | bytes 4194304 | tf_op jit(solution)/shard_map/pallas_call | solution.py:33
  100.3 3.4 %shard_map.141 = (bf16[2,256,1024]{2,1,0:T(8,128)(2,1)S(1)}, bf16[2,256,1024]{2,1,0:T(8,128)(2,1)S(1)}) custom-call(s32[5]{0:T(128)S(1)} %stack.27.bit_ref, bf16[512,128]{1,0:T(8,128)(2,1)} %get-tuple-element.83.refs_0_, bf16[512,128]{1,0:T(8,128)(2,1)} %get-tuple-element.84.refs_1_, bf16[512,128]{1,0:T(8,128)(2,1)} %get-tuple-element.85.refs_2_, ...), custom_call_target="tpu_custom_call" | custom-call | flops 3221225472 | bytes 6291456 | tf_op jit(solution)/shard_map/pallas_call | solution.py:33
  103.9 2.8 %all-to-all-start.6 = ((bf16[32,32,128]{2,1,0:T(8,128)(2,1)}), bf16[32,32,128]{2,1,0:T(8,128)(2,1)S(1)}, u32[]{:S(2)}, u32[]{:S(2)}) async-start(bf16[32,32,128]{2,1,0:T(8,128)(2,1)} %get-tuple-element.81), calls=%async_computation.6 | async-start | bytes 524288 | tf_op jit(solution)/shard_map/all_to_all | solution.py:18
  108.2 1.8 %collective-permute-start.6 = (bf16[128,1024]{1,0:T(8,128)(2,1)}, bf16[128,1024]{1,0:T(8,128)(2,1)S(1)}, u32[]{:S(2)}, u32[]{:S(2)}) collective-permute-start(bf16[128,1024]{1,0:T(8,128)(2,1)} %get-tuple-element.99), channel_id=1, source_target_pairs={{0,4},{2,6},{4,0},{6,2},{8,12},{10,14},{12,8},{14,10},{16,20},{18,... | collective-permute-start | bytes 786440 | tf_op jit(solution)/shard_map/ppermute | solution.py:689
  111.4 5.9 %all-to-all-done.6 = bf16[32,32,128]{2,1,0:T(8,128)(2,1)S(1)} async-done(((bf16[32,32,128]{2,1,0:T(8,128)(2,1)}), bf16[32,32,128]{2,1,0:T(8,128)(2,1)S(1)}, u32[]{:S(2)}, u32[]{:S(2)}) %all-to-all-start.6) | async-done | bytes 262176 | tf_op jit(solution)/shard_map/all_to_all | solution.py:18
  118.5 2.6 %all-to-all-start.7 = ((bf16[32,32,128]{2,1,0:T(8,128)(2,1)}), bf16[32,32,128]{2,1,0:T(8,128)(2,1)S(1)}, u32[]{:S(2)}, u32[]{:S(2)}) async-start(bf16[32,32,128]{2,1,0:T(8,128)(2,1)} %bitcast.48), calls=%async_computation.7 | async-start | bytes 524288 | tf_op jit(solution)/shard_map/all_to_all | solution.py:18
  125.0 4.3 %collective-permute-done.8.refs_2_ = bf16[128,512]{1,0:T(8,128)(2,1)S(1)} collective-permute-done((bf16[128,512]{1,0:T(8,128)(2,1)S(1)}, bf16[128,512]{1,0:T(8,128)(2,1)S(1)}, u32[]{:S(2)}, u32[]{:S(2)}) %collective-permute-start.8) | collective-permute-done | bytes 131104 | tf_op jit(solution)/shard_map/ppermute | solution.py:689
  130.6 1.8 %collective-permute-start.10 = (bf16[2,64,512]{2,1,0:T(8,128)(2,1)S(1)}, bf16[2,64,512]{2,1,0:T(8,128)(2,1)S(1)}, u32[]{:S(2)}, u32[]{:S(2)}) collective-permute-start(bf16[2,64,512]{2,1,0:T(8,128)(2,1)S(1)} %get-tuple-element.106), channel_id=1, source_target_pairs={{0,8},{2,10},{4,12},{6,14},{8,0},{10,2},{12,4},{14,6},{16,24},{18,... | collective-permute-start | bytes 393224 | tf_op jit(solution)/shard_map/ppermute | solution.py:689
  132.4 3.2 %collective-permute-done.10.refs_1_ = bf16[2,64,512]{2,1,0:T(8,128)(2,1)S(1)} collective-permute-done((bf16[2,64,512]{2,1,0:T(8,128)(2,1)S(1)}, bf16[2,64,512]{2,1,0:T(8,128)(2,1)S(1)}, u32[]{:S(2)}, u32[]{:S(2)}) %collective-permute-start.10) | collective-permute-done | bytes 131104 | tf_op jit(solution)/shard_map/ppermute | solution.py:689
  136.2 2.9 %collective-permute-start.11 = (bf16[2,32,512]{2,1,0:T(8,128)(2,1)S(1)}, bf16[2,32,512]{2,1,0:T(8,128)(2,1)S(1)}, u32[]{:S(2)}, u32[]{:S(2)}) collective-permute-start(bf16[2,32,512]{2,1,0:T(8,128)(2,1)S(1)} %get-tuple-element.108), channel_id=1, source_target_pairs={{0,16},{2,18},{4,20},{6,22},{8,24},{10,26},{12,28},{14,30},{16,0},... | collective-permute-start | bytes 196616 | tf_op jit(solution)/shard_map/ppermute | solution.py:689
  (51 shorter events, 20.4 us)
Async XLA Ops:
  0.6 9.3 %copy-start.3 = (bf16[3,8,16,512]{3,2,1,0:T(8,128)(2,1)S(1)}, bf16[3,8,16,512]{3,2,1,0:T(8,128)(2,1)}, u32[]{:S(2)}) copy-start(bf16[3,8,16,512]{3,2,1,0:T(8,128)(2,1)} %states_hbm.5) | copy-start | bytes 1179652
  0.6 27.7 %copy-start = (bf16[512,1024]{1,0:T(8,128)(2,1)S(1)}, bf16[512,1024]{1,0:T(8,128)(2,1)}, u32[]{:S(2)}) copy-start(bf16[512,1024]{1,0:T(8,128)(2,1)} %refs_2_.5) | copy-start | bytes 3145732
  2.6 20.3 %all-to-all-start = ((bf16[32,32,128]{2,1,0:T(8,128)(2,1)}), bf16[32,32,128]{2,1,0:T(8,128)(2,1)S(1)}, u32[]{:S(2)}, u32[]{:S(2)}) async-start(bf16[32,32,128]{2,1,0:T(8,128)(2,1)} %shard_map.128), calls=%async_computation | async-start | bytes 524288 | tf_op jit(solution)/shard_map/all_to_all | solution.py:18
  10.0 12.6 %collective-permute-start.3 = (bf16[3,8,1,512]{3,2,1,0:T(2,128)(2,1)S(1)}, bf16[3,8,1,512]{3,2,1,0:T(2,128)(2,1)S(1)}, u32[]{:S(2)}, u32[]{:S(2)}) collective-permute-start(bf16[3,8,1,512]{3,2,1,0:T(2,128)(2,1)S(1)} %broadcast_select_fusion.2), channel_id=1, source_target_pairs={{0,1},{1,0},{2,3},{3,2},{4,5},{5,4},{6,7},{7,6},{8,9},{9,8},{10,11... | collective-permute-start | bytes 73736 | tf_op jit(solution)/shard_map/ppermute | solution.py:127
  11.8 10.8 %collective-permute-start.2 = (bf16[3,1,1,512]{3,2,1,0:T(2,128)(2,1)S(1)}, bf16[3,1,1,512]{3,2,1,0:T(2,128)(2,1)S(1)}, u32[]{:S(2)}, u32[]{:S(2)}) collective-permute-start(bf16[3,1,1,512]{3,2,1,0:T(2,128)(2,1)S(1)} %get-tuple-element.118), channel_id=1, source_target_pairs={{0,3},{1,2},{2,5},{3,4},{4,7},{5,6},{6,9},{7,8},{8,11},{9,10},{10,... | collective-permute-start | bytes 9224 | tf_op jit(solution)/shard_map/ppermute | solution.py:127
  11.9 10.8 %collective-permute-start.4 = (bf16[3,1,1,512]{3,2,1,0:T(2,128)(2,1)S(1)}, bf16[3,1,1,512]{3,2,1,0:T(2,128)(2,1)S(1)}, u32[]{:S(2)}, u32[]{:S(2)}) collective-permute-start(bf16[3,1,1,512]{3,2,1,0:T(2,128)(2,1)S(1)} %get-tuple-element.117), channel_id=1, source_target_pairs={{0,31},{1,30},{2,1},{3,0},{4,3},{5,2},{6,5},{7,4},{8,7},{9,6},{10,... | collective-permute-start | bytes 9224 | tf_op jit(solution)/shard_map/ppermute | solution.py:127
  17.2 7.3 %collective-permute-start = (bf16[3,1,16,512]{3,2,1,0:T(8,128)(2,1)S(1)}, bf16[3,1,16,512]{3,2,1,0:T(8,128)(2,1)S(1)}, u32[]{:S(2)}, u32[]{:S(2)}) collective-permute-start(bf16[3,1,16,512]{3,2,1,0:T(8,128)(2,1)S(1)} %get-tuple-element.114), channel_id=1, source_target_pairs={{0,2},{2,4},{4,6},{6,8},{8,10},{10,12},{12,14},{14,16},{16,18},{18... | collective-permute-start | bytes 147464 | tf_op jit(solution)/shard_map/ppermute | solution.py:119
  17.3 7.3 %collective-permute-start.1 = (bf16[3,1,16,512]{3,2,1,0:T(8,128)(2,1)S(1)}, bf16[3,1,16,512]{3,2,1,0:T(8,128)(2,1)S(1)}, u32[]{:S(2)}, u32[]{:S(2)}) collective-permute-start(bf16[3,1,16,512]{3,2,1,0:T(8,128)(2,1)S(1)} %get-tuple-element.113), channel_id=1, source_target_pairs={{0,30},{2,0},{4,2},{6,4},{8,6},{10,8},{12,10},{14,12},{16,14},{18,... | collective-permute-start | bytes 147464 | tf_op jit(solution)/shard_map/ppermute | solution.py:120
  24.6 12.4 %all-to-all-start.1 = ((bf16[32,16,128]{2,1,0:T(8,128)(2,1)}), bf16[32,16,128]{2,1,0:T(8,128)(2,1)S(1)}, u32[]{:S(2)}, u32[]{:S(2)}) async-start(bf16[32,16,128]{2,1,0:T(8,128)(2,1)} %bitcast.54), calls=%async_computation.1 | async-start | bytes 262144 | tf_op jit(solution)/shard_map/all_to_all | solution.py:18
  28.9 1.5 %copy-start.1 = (f32[3,3,512]{2,1,0:T(4,128)S(1)}, f32[3,3,512]{2,1,0:T(4,128)}, u32[]{:S(2)}) copy-start(f32[3,3,512]{2,1,0:T(4,128)} %kernel_ref.5) | copy-start | bytes 55300
  30.4 0.7 copy-start.2
  40.3 11.7 %all-to-all-start.2 = ((bf16[32,16,128]{2,1,0:T(8,128)(2,1)}), bf16[32,16,128]{2,1,0:T(8,128)(2,1)S(1)}, u32[]{:S(2)}, u32[]{:S(2)}) async-start(bf16[32,16,128]{2,1,0:T(8,128)(2,1)} %bitcast.49), calls=%async_computation.2 | async-start | bytes 262144 | tf_op jit(solution)/shard_map/all_to_all | solution.py:18
  55.7 11.2 %all-to-all-start.3 = ((bf16[32,16,128]{2,1,0:T(8,128)(2,1)}), bf16[32,16,128]{2,1,0:T(8,128)(2,1)S(1)}, u32[]{:S(2)}, u32[]{:S(2)}) async-start(bf16[32,16,128]{2,1,0:T(8,128)(2,1)} %bitcast.52), calls=%async_computation.3 | async-start | bytes 262144 | tf_op jit(solution)/shard_map/all_to_all | solution.py:18
  85.2 11.2 %all-to-all-start.5 = ((bf16[32,16,128]{2,1,0:T(8,128)(2,1)}), bf16[32,16,128]{2,1,0:T(8,128)(2,1)S(1)}, u32[]{:S(2)}, u32[]{:S(2)}) async-start(bf16[32,16,128]{2,1,0:T(8,128)(2,1)} %bitcast.51), calls=%async_computation.5 | async-start | bytes 262144 | tf_op jit(solution)/shard_map/all_to_all | solution.py:18
  103.8 2.9 %collective-permute-start.5 = (bf16[2,256,1024]{2,1,0:T(8,128)(2,1)S(1)}, bf16[2,256,1024]{2,1,0:T(8,128)(2,1)S(1)}, u32[]{:S(2)}, u32[]{:S(2)}) collective-permute-start(bf16[2,256,1024]{2,1,0:T(8,128)(2,1)S(1)} %get-tuple-element.96), channel_id=1, source_target_pairs={{0,2},{2,0},{4,6},{6,4},{8,10},{10,8},{12,14},{14,12},{16,18},{18,... | collective-permute-start | bytes 3145736 | tf_op jit(solution)/shard_map/ppermute | solution.py:689
  103.9 13.5 %all-to-all-start.6 = ((bf16[32,32,128]{2,1,0:T(8,128)(2,1)}), bf16[32,32,128]{2,1,0:T(8,128)(2,1)S(1)}, u32[]{:S(2)}, u32[]{:S(2)}) async-start(bf16[32,32,128]{2,1,0:T(8,128)(2,1)} %get-tuple-element.81), calls=%async_computation.6 | async-start | bytes 524288 | tf_op jit(solution)/shard_map/all_to_all | solution.py:18
  108.2 13.0 %collective-permute-start.6 = (bf16[128,1024]{1,0:T(8,128)(2,1)}, bf16[128,1024]{1,0:T(8,128)(2,1)S(1)}, u32[]{:S(2)}, u32[]{:S(2)}) collective-permute-start(bf16[128,1024]{1,0:T(8,128)(2,1)} %get-tuple-element.99), channel_id=1, source_target_pairs={{0,4},{2,6},{4,0},{6,2},{8,12},{10,14},{12,8},{14,10},{16,20},{18,... | collective-permute-start | bytes 786440 | tf_op jit(solution)/shard_map/ppermute | solution.py:689
  110.0 11.2 %collective-permute-start.7 = (bf16[256,512]{1,0:T(8,128)(2,1)}, bf16[256,512]{1,0:T(8,128)(2,1)S(1)}, u32[]{:S(2)}, u32[]{:S(2)}) collective-permute-start(bf16[256,512]{1,0:T(8,128)(2,1)} %get-tuple-element.100), channel_id=1, source_target_pairs={{0,1},{1,0},{2,3},{3,2},{4,5},{5,4},{6,7},{7,6},{8,9},{9,8},{10,11... | collective-permute-start | bytes 786440 | tf_op jit(solution)/shard_map/ppermute | solution.py:689
  118.5 20.6 %all-to-all-start.7 = ((bf16[32,32,128]{2,1,0:T(8,128)(2,1)}), bf16[32,32,128]{2,1,0:T(8,128)(2,1)S(1)}, u32[]{:S(2)}, u32[]{:S(2)}) async-start(bf16[32,32,128]{2,1,0:T(8,128)(2,1)} %bitcast.48), calls=%async_computation.7 | async-start | bytes 524288 | tf_op jit(solution)/shard_map/all_to_all | solution.py:18
  121.8 7.5 %collective-permute-start.8 = (bf16[128,512]{1,0:T(8,128)(2,1)S(1)}, bf16[128,512]{1,0:T(8,128)(2,1)S(1)}, u32[]{:S(2)}, u32[]{:S(2)}) collective-permute-start(bf16[128,512]{1,0:T(8,128)(2,1)S(1)} %get-tuple-element.103), channel_id=1, source_target_pairs={{0,1},{1,0},{2,3},{3,2},{4,5},{5,4},{6,7},{7,6},{8,9},{9,8},{10,11... | collective-permute-start | bytes 393224 | tf_op jit(solution)/shard_map/ppermute | solution.py:689
  123.5 6.5 %collective-permute-start.9 = (bf16[128,512]{1,0:T(8,128)(2,1)S(1)}, bf16[128,512]{1,0:T(8,128)(2,1)S(1)}, u32[]{:S(2)}, u32[]{:S(2)}) collective-permute-start(bf16[128,512]{1,0:T(8,128)(2,1)S(1)} %get-tuple-element.104), channel_id=1, source_target_pairs={{0,4},{2,6},{4,0},{6,2},{8,12},{10,14},{12,8},{14,10},{16,20},{18,... | collective-permute-start | bytes 393224 | tf_op jit(solution)/shard_map/ppermute | solution.py:689
  130.6 5.0 %collective-permute-start.10 = (bf16[2,64,512]{2,1,0:T(8,128)(2,1)S(1)}, bf16[2,64,512]{2,1,0:T(8,128)(2,1)S(1)}, u32[]{:S(2)}, u32[]{:S(2)}) collective-permute-start(bf16[2,64,512]{2,1,0:T(8,128)(2,1)S(1)} %get-tuple-element.106), channel_id=1, source_target_pairs={{0,8},{2,10},{4,12},{6,14},{8,0},{10,2},{12,4},{14,6},{16,24},{18,... | collective-permute-start | bytes 393224 | tf_op jit(solution)/shard_map/ppermute | solution.py:689
  136.2 5.3 %collective-permute-start.11 = (bf16[2,32,512]{2,1,0:T(8,128)(2,1)S(1)}, bf16[2,32,512]{2,1,0:T(8,128)(2,1)S(1)}, u32[]{:S(2)}, u32[]{:S(2)}) collective-permute-start(bf16[2,32,512]{2,1,0:T(8,128)(2,1)S(1)} %get-tuple-element.108), channel_id=1, source_target_pairs={{0,16},{2,18},{4,20},{6,22},{8,24},{10,26},{12,28},{14,30},{16,0},... | collective-permute-start | bytes 196616 | tf_op jit(solution)/shard_map/ppermute | solution.py:689

commit v5 on v4

v5 whole, which is shorter than its diff:
```python
import functools

import jax
import jax.numpy as jnp
from jax import lax
from jax.experimental import pallas as pl
from jax.experimental.pallas import tpu as pltpu
from jax.sharding import PartitionSpec as P

EPSILON = 1e-06
AXES = ("lon", "lat")
ROWS = 16
LAT_REACH = 2
LON_REACH = 8
MIB = 1024 * 1024


def exchanged(blocks):
    return lax.all_to_all(blocks, AXES, split_axis=0, concat_axis=0, tiled=True)


SPACES = {"s": pltpu.SMEM, "v": pltpu.VMEM, "h": pltpu.HBM}


def call(kernel, out_shape, operands, ins, outs, scratch=(), flops=0, moved=0, limit=8):
    operands = [
        pltpu.with_memory_space_constraint(value, pltpu.HBM) if kind == "h" else value
        for kind, value in zip(ins, operands, strict=True)
    ]
    out_shape = [
        pltpu.HBM(value.shape, value.dtype) if kind == "h" else value
        for kind, value in zip(outs, out_shape, strict=True)
    ]
    return pl.pallas_call(
        kernel,
        out_shape=out_shape,
        in_specs=[pl.BlockSpec(memory_space=SPACES[kind]) for kind in ins],
        out_specs=[pl.BlockSpec(memory_space=SPACES[kind]) for kind in outs],
        scratch_shapes=scratch,
        compiler_params=pltpu.CompilerParams(vmem_limit_bytes=limit * MIB),
        cost_estimate=pl.CostEstimate(flops=flops, bytes_accessed=moved, transcendentals=0),
    )(*operands)


def copies(sems, first, pairs):
    started = [pltpu.make_async_copy(src, dst, sems.at[first + k]) for k, (src, dst) in enumerate(pairs)]
    for copy in started:
        copy.start()
    return started


def finish(started):
    for copy in started:
        copy.wait()


def split_three(value, lane, width):
    value = jnp.where(lane < width, value, 0.0)
    result = jnp.zeros_like(value)
    for k in range(3):
        piece = value.astype(jnp.bfloat16).astype(jnp.float32)
        result = result + (pltpu.roll(piece, k * width, 1) if k else piece)
        value = value - piece
    return result.astype(jnp.bfloat16)


def join_three(value, width):
    lanes = value.shape[1]
    return value + pltpu.roll(value, lanes - width, 1) + pltpu.roll(value, lanes - 2 * width, 1)


def pack_kernel(cotangent_hbm, weight_hbm, out_hbm, cotangent_ref, weight_ref, out_ref, sems):
    started = copies(sems, 0, [(cotangent_hbm, cotangent_ref), (weight_hbm, weight_ref)])
    channels = cotangent_ref.shape[1]
    devices, _, count = out_ref.shape
    share = channels // devices
    started[1].wait()
    rows = weight_ref.shape[0]
    weights = jnp.concatenate([weight_ref[:, i] for i in range(weight_ref.shape[1])], axis=1)
    weights = jnp.concatenate([weights, jnp.zeros((ROWS - rows, count), jnp.float32)], axis=0)
    weights = weights.astype(jnp.bfloat16)
    out_ref[:, share:] = jnp.broadcast_to(weights[None], (devices, ROWS, count))
    started[0].wait()
    turned = cotangent_ref[...].astype(jnp.float32).T.astype(jnp.bfloat16)
    out_ref[:, :share] = turned.reshape(devices, share, count)
    finish(copies(sems, 2, [(out_ref, out_hbm)]))


def packed(cotangent, bilinear, devices):
    rows_out, cols_out, channels = cotangent.shape
    steps, corners = bilinear.shape[:2]
    count = rows_out * cols_out
    share = channels // devices
    if share % ROWS:
        blocks = cotangent.reshape(count, channels).T.reshape(devices, share, count)
        blocks = jnp.pad(blocks, ((0, 0), (0, -share % ROWS), (0, 0)))
        weights = bilinear.reshape(steps * corners, count).astype(jnp.bfloat16)
        weights = jnp.pad(weights, ((0, ROWS - steps * corners), (0, 0)))
        return jnp.concatenate([blocks, jnp.broadcast_to(weights[None], (devices, ROWS, count))], axis=1)
    shape = (devices, share + ROWS, count)
    return call(
        pack_kernel,
        [jax.ShapeDtypeStruct(shape, jnp.bfloat16)],
        [cotangent.reshape(count, channels), bilinear.reshape(steps * corners, rows_out, cols_out)],
        "hh",
        "h",
        scratch=[
            pltpu.VMEM((count, channels), jnp.bfloat16),
            pltpu.VMEM((steps * corners, rows_out, cols_out), jnp.float32),
            pltpu.VMEM(shape, jnp.bfloat16),
            pltpu.SemaphoreType.DMA((3,)),
        ],
        moved=2**19,
    )[0]


def lon_edges(states):
    lon = lax.axis_size("lon")
    ahead = lambda value: lax.ppermute(value, "lon", [(i, (i + 1) % lon) for i in range(lon)])
    behind = lambda value: lax.ppermute(value, "lon", [(i, (i - 1) % lon) for i in range(lon)])
    return ahead(states[:, -1:]), behind(states[:, :1])


def lat_edges(states, low, high):
    lat, lat_at = lax.axis_size("lat"), lax.axis_index("lat")
    column = lambda place: jnp.concatenate([part[:, :, place] for part in (low, states, high)], axis=1)
    first, last = column(slice(0, 1)), column(slice(-1, None))
    if lat == 2:
        arrived = lax.ppermute(jnp.where(lat_at == 0, last, first), "lat", [(0, 1), (1, 0)])
        return jnp.where(lat_at == 0, 0, arrived), jnp.where(lat_at == 0, arrived, 0)
    return (
        lax.ppermute(last, "lat", [(i, i + 1) for i in range(lat - 1)]),
        lax.ppermute(first, "lat", [(i + 1, i) for i in range(lat - 1)]),
    )


MARGIN = 8


def forward_kernel(
    step, states_hbm, low_ref, high_ref, before_ref, after_ref, kernel_ref, gain_ref, up_ref,
    n_hbm, turned_hbm, inv_hbm, hid_hbm, slope_hbm, pad_hbm,
    n_ref, turned_ref, inv_ref, hid_ref, slope_ref, pad_ref, state_ref, wide_ref, sems,
):
    rows_out, cols_out, channels = state_ref.shape
    count = rows_out * cols_out
    arriving = copies(sems, 0, [(states_hbm.at[step], state_ref)])
    wide_ref[:1, MARGIN : MARGIN + cols_out] = low_ref[step].astype(jnp.float32)
    wide_ref[1 + rows_out :, MARGIN : MARGIN + cols_out] = high_ref[step].astype(jnp.float32)
    wide_ref[:, MARGIN - 1 : MARGIN] = before_ref[step].astype(jnp.float32)
    wide_ref[:, MARGIN + cols_out : MARGIN + cols_out + 1] = after_ref[step].astype(jnp.float32)
    finish(arriving)
    mixed = state_ref[...].astype(jnp.float32)
    wide_ref[1 : 1 + rows_out, MARGIN : MARGIN + cols_out] = mixed
    pad_ref[...] = wide_ref[...].astype(jnp.bfloat16)
    leaving = copies(sems, 1, [(pad_ref, pad_hbm)])
    for col_tap in range(3):
        place = MARGIN - 1 + col_tap
        shifted_cols = wide_ref[:, place : place + cols_out]
        for row_tap in range(3):
            tap = kernel_ref[row_tap, col_tap : col_tap + 1]
            mixed = mixed + tap[None] * shifted_cols[row_tap : row_tap + rows_out]
    mixed = mixed.reshape(count, channels)
    inv_root = lax.rsqrt(jnp.mean(mixed * mixed, axis=1, keepdims=True) + EPSILON)
    narrow = mixed * inv_root * gain_ref[...]
    n_ref[...] = narrow.astype(jnp.bfloat16)
    inv_ref[...] = jnp.broadcast_to(inv_root, inv_ref.shape)
    leaving += copies(sems, 2, [(n_ref, n_hbm), (inv_ref, inv_hbm)])
    pre = jnp.dot(n_ref[...], up_ref[...], preferred_element_type=jnp.float32)
    sigmoid = jax.nn.sigmoid(pre)
    slope_ref[...] = (sigmoid * (1.0 + pre * (1.0 - sigmoid))).astype(jnp.bfloat16)
    leaving += copies(sems, 4, [(slope_ref, slope_hbm)])
    hid_ref[...] = (pre * sigmoid).astype(jnp.bfloat16)
    turned_ref[...] = narrow.T.astype(jnp.bfloat16)
    finish(leaving + copies(sems, 5, [(hid_ref, hid_hbm), (turned_ref, turned_hbm)]))


def forward_parts(step, states, around, kernel, norm_gain, w_up):
    _, rows_out, cols_out, channels = states.shape
    hid = w_up.shape[1]
    count = rows_out * cols_out
    wide = (rows_out + 2, cols_out + 2 * MARGIN, channels)
    shapes = [
        ((count, channels), jnp.bfloat16),
        ((channels, count), jnp.bfloat16),
        ((count, 128), jnp.float32),
        ((count, hid), jnp.bfloat16),
        ((count, hid), jnp.bfloat16),
        (wide, jnp.bfloat16),
    ]
    return call(
        functools.partial(forward_kernel, step),
        [jax.ShapeDtypeStruct(*shape) for shape in shapes],
        [states, *around, kernel, norm_gain, w_up],
        "hvvvvvvv",
        "hhhhhh",
        scratch=[pltpu.VMEM(*shape) for shape in shapes]
        + [pltpu.VMEM(states.shape[1:], jnp.bfloat16), pltpu.VMEM(wide, jnp.float32), pltpu.SemaphoreType.DMA((7,))],
        flops=2 * count * hid * channels,
        moved=2**22,
        limit=12,
    )


def transposed(value):
    return value.astype(jnp.float32).T.astype(jnp.bfloat16)


LANES_BOTH = (((1,), (1,)), ((), ()))


def network_kernel(moved_ref, down_ref, up_ref, gain_ref, slope_hbm, n_hbm, inv_hbm, out_hbm, grad_hbm, saved_hbm, *refs):
    slope_ref, n_ref, inv_ref, out_ref, grad_ref, sems = refs
    arriving = copies(sems, 0, [(slope_hbm, slope_ref), (n_hbm, n_ref), (inv_hbm, inv_ref)])
    leaving = copies(sems, 3, [(moved_ref, saved_hbm)])
    moved = moved_ref[...].astype(jnp.float32).T
    grad_hidden = jnp.dot(moved.astype(jnp.bfloat16), down_ref[...], preferred_element_type=jnp.float32)
    arriving[0].wait()
    grad_pre = (grad_hidden * slope_ref[...].astype(jnp.float32)).astype(jnp.bfloat16)
    grad_ref[...] = grad_pre
    leaving += copies(sems, 4, [(grad_ref, grad_hbm)])
    grad_n = lax.dot_general(grad_pre, up_ref[...], LANES_BOTH, preferred_element_type=jnp.float32)
    finish(arriving[1:])
    narrow, gain = n_ref[...].astype(jnp.float32), gain_ref[...]
    mean = jnp.mean(grad_n * narrow, axis=1, keepdims=True)
    field = moved + inv_ref[:, :1] * (grad_n * gain - narrow * (mean / gain))
    out_ref[...] = field.T.astype(jnp.bfloat16)
    finish(leaving + copies(sems, 5, [(out_ref, out_hbm)]))


def network_back(moved, w_down, w_up, norm_gain, slope, narrow, inv_root):
    channels, count = moved.shape
    hid = w_down.shape[1]
    shapes = [((channels, count), jnp.bfloat16), ((count, hid), jnp.bfloat16), ((channels, count), jnp.bfloat16)]
    return call(
        network_kernel,
        [jax.ShapeDtypeStruct(*shape) for shape in shapes],
        [moved, w_down, w_up, norm_gain, slope, narrow, inv_root],
        "vvvvhhh",
        "hhh",
        scratch=[pltpu.VMEM(value.shape, value.dtype) for value in (slope, narrow, inv_root)]
        + [pltpu.VMEM(*shape) for shape in shapes[:2]]
        + [pltpu.SemaphoreType.DMA((6,))],
        flops=4 * count * hid * channels,
        moved=4 * 2**20,
        limit=12,
    )


def stencil_sums(pad_ref, field, tile):
    rows_out, cols_out = tile
    field = field.reshape(rows_out, cols_out, -1)
    padded = pad_ref[...].astype(jnp.float32)
    result = [None] * 9
    for col_tap in range(3):
        place = MARGIN - 1 + col_tap
        shifted_cols = padded[:, place : place + cols_out]
        for row_tap in range(3):
            products = jnp.sum(shifted_cols[row_tap : row_tap + rows_out] * field, axis=0)
            result[3 * row_tap + col_tap] = jnp.sum(products, axis=0, keepdims=True)
    return result


def sums_kernel(steps, tile, last, *refs):
    up_ref, gain_ref, *refs = refs
    inputs, refs = refs[: 4 * steps], refs[4 * steps :]
    if last:
        before_ref, out_hbm, *refs, out_ref = refs
    else:
        out_ref, *refs = refs
    pads, fields, grads, narrows, sems = refs
    places = [(ref, place.at[k]) for k in range(steps) for ref, place in zip(inputs[4 * k : 4 * k + 4], refs[:4])]
    arriving = copies(sems, 0, places)
    channels, count = fields.shape[1:]
    rows, term = None, None
    for k in range(steps):
        finish(arriving[4 * k : 4 * k + 4])
        grad_n = lax.dot_general(grads[k], up_ref[...], LANES_BOTH, preferred_element_type=jnp.float32)
        product = grad_n * narrows[k].astype(jnp.float32)
        term = product if term is None else term + product
        more = stencil_sums(pads.at[k], fields[k].astype(jnp.float32).T, tile)
        rows = more if rows is None else [a + b for a, b in zip(rows, more)]
    rows = rows + [jnp.sum(term, axis=0, keepdims=True) / gain_ref[...], jnp.zeros((6, channels), jnp.float32)]
    sums = jnp.concatenate(rows, axis=0)
    if not last:
        out_ref[...] = sums
        return
    sums = jnp.concatenate([sums + before_ref[...], jnp.zeros((count - ROWS, channels), jnp.float32)], axis=0).T
    lane = lax.broadcasted_iota(jnp.int32, (channels, count), 1)
    devices = out_ref.shape[0]
    share = channels // devices
    out_ref[:, :share] = fields[0].reshape(devices, share, count)
    out_ref[:, share:] = split_three(sums, lane, ROWS).reshape(devices, share, count)
    finish(copies(sems, 4 * steps, [(out_ref, out_hbm)]))


def channel_sums(tile, devices, w_up, norm_gain, pads, fields, grads, narrows, before):
    steps = len(fields)
    last = before is not None
    channels, count = fields[0].shape
    shape = (devices, 2 * channels // devices, count) if last else (ROWS, channels)
    dtype = jnp.bfloat16 if last else jnp.float32
    inputs = [value for group in zip(pads, fields, grads, narrows) for value in group]
    return call(
        functools.partial(sums_kernel, steps, tile, last),
        [jax.ShapeDtypeStruct(shape, dtype)],
        [w_up, norm_gain, *inputs] + [before] * last,
        "vv" + "h" * 4 * steps + "v" * last,
        "h" if last else "v",
        scratch=[pltpu.VMEM((steps, *value.shape), value.dtype) for value in inputs[:4]]
        + [pltpu.SemaphoreType.DMA((4 * steps + 1,))]
        + [pltpu.VMEM(shape, dtype)] * last,
        moved=2**21,
        limit=12,
    )[0]


def final_kernel(arrived_ref, state_hbm, taps_ref, gain_ref, state_ref, sems):
    devices, rows, count = arrived_ref.shape
    share = rows // 2
    channels = devices * share
    state = arrived_ref[:, :share].reshape(channels, count).astype(jnp.float32)
    state_ref[...] = state.T.astype(jnp.bfloat16)
    leaving = copies(sems, 0, [(state_ref, state_hbm)])
    sums = arrived_ref[:, share:].reshape(channels, count).astype(jnp.float32)
    sums = join_three(sums, ROWS).T
    for k in range(9):
        taps_ref[k // 3, k % 3 : k % 3 + 1] = sums[k : k + 1]
    gain_ref[...] = sums[9:10]
    finish(leaving)


def final_parts(arrived, channels):
    devices, rows, count = arrived.shape
    sds = jax.ShapeDtypeStruct
    return call(
        final_kernel,
        [sds((count, channels), jnp.bfloat16), sds((3, 3, channels), jnp.float32), sds((1, channels), jnp.float32)],
        [arrived],
        "v",
        "hvv",
        scratch=[pltpu.VMEM((count, channels), jnp.bfloat16), pltpu.SemaphoreType.DMA((1,))],
        moved=2**19,
    )


def spatial_kernel(mode, step, near_lon, near_lat, *refs):
    refs = list(refs)
    take = lambda: refs.pop(0)
    with_move, with_stencil = mode != "last", mode != "first"
    move_ref = take() if with_move else None
    in_ref = take()
    kern_ref = take() if with_stencil else None
    weight_hbm = take() if mode == "mid" else None
    out_hbm = take()
    saved_hbm = take() if mode == "first" else None
    out_ref, sems = take(), take()
    spread_ref, weight_ref = (take(), take()) if with_move else (None, None)
    tiles_lon, tiles_lat, _, lanes = in_ref.shape
    rows = out_ref.shape[2] if with_move else out_ref.shape[2] // 2
    started = []
    if mode == "mid":
        arriving = copies(sems, 0, [(weight_hbm, weight_ref)])
    if mode == "first":
        weight_ref[...] = in_ref[:, :, rows:]
        started += copies(sems, 0, [(weight_ref, saved_hbm)])
    lane = lax.broadcasted_iota(jnp.int32, (rows, lanes), 1)
    col = lax.rem(lane, near_lat)
    lat_last, lat_first = col == near_lat - 1, col == 0
    lon_last, lon_first = lane >= lanes - near_lat, lane < near_lat
    tiles = [(a, b) for a in range(tiles_lon) for b in range(tiles_lat)]

    def turn(value, steps):
        return pltpu.roll(value, steps % lanes if isinstance(steps, int) else steps, 1)

    def lat_after(grid):
        turned = {key: turn(value, -1) for key, value in grid.items()}
        wrapped = {key: turn(grid[key], near_lat - 1) for key in tiles if key[1] > 0}
        return {(a, b): jnp.where(lat_last, wrapped.get((a, b + 1), 0.0), turned[a, b]) for a, b in tiles}

    def lat_before(grid):
        turned = {key: turn(value, 1) for key, value in grid.items()}
        wrapped = {key: turn(grid[key], 1 - near_lat) for key in tiles if key[1] < tiles_lat - 1}
        return {(a, b): jnp.where(lat_first, wrapped.get((a, b - 1), 0.0), turned[a, b]) for a, b in tiles}

    def lon_after(grid):
        return {
            (a, b): turn(jnp.where(lon_first, grid[(a + 1) % tiles_lon, b], grid[a, b]), -near_lat) for a, b in tiles
        }

    def lon_before(grid):
        return {(a, b): turn(jnp.where(lon_last, grid[(a - 1) % tiles_lon, b], grid[a, b]), near_lat) for a, b in tiles}

    grid = {(a, b): in_ref[a, b, :rows].astype(jnp.float32) for a, b in tiles}
    if with_stencil:
        taps = [
            [jnp.broadcast_to(kern_ref[:, 3 * a + b : 3 * a + b + 1], (rows, lanes)) for b in range(3)] for a in range(3)
        ]
        by_col = [lat_after(grid), grid, lat_before(grid)]
        mix = [
            {key: sum(taps[row][c] * by_col[c][key] for c in range(1, 3)) + taps[row][0] * by_col[0][key] for key in tiles}
            for row in range(3)
        ]
        high, low = lon_after(mix[0]), lon_before(mix[2])
        grid = {key: grid[key] + mix[1][key] + (high[key] + low[key]) for key in tiles}
    if not with_move:
        for a, b in tiles:
            out_ref[a, b, :rows] = grid[a, b].astype(jnp.bfloat16)
        sums = jnp.sum(in_ref[:, :, rows:].astype(jnp.float32), axis=(0, 1))
        sums = split_three(join_three(sums, ROWS), lane, ROWS)
        out_ref[:, :, rows:] = jnp.broadcast_to(sums[None, None], (tiles_lon, tiles_lat, rows, lanes))
        finish(copies(sems, 1, [(out_ref, out_hbm)]))
        return

    if mode == "mid":
        grid = {key: value.astype(jnp.bfloat16).astype(jnp.float32) for key, value in grid.items()}
        finish(arriving)
    weights = {}
    for a, b in tiles:
        four = weight_ref[a, b].astype(jnp.float32)[4 * step : 4 * step + 4]
        weights[a, b] = [jnp.broadcast_to(four[k : k + 1], (rows, lanes)) for k in range(4)]
    weighted = [{key: weights[key][k] * grid[key] for key in tiles} for k in range(4)]
    own, lon = lat_after(weighted[2]), lat_after(weighted[3])
    lon = lon_after({key: weighted[1][key] + lon[key] for key in tiles})
    for a, b in tiles:
        value = (weighted[0][a, b] + own[a, b] + lon[a, b]).astype(jnp.bfloat16).astype(jnp.float32)
        for place in range(a, tiles_lon + LON_REACH, tiles_lon):
            spread_ref[place, b] = value
    spread_ref[:, tiles_lat:] = jnp.zeros((tiles_lon + LON_REACH, LAT_REACH, rows, lanes), jnp.float32)

    lon_move, lat_move = move_ref[0], move_ref[1]
    far_lon, off_lon = lon_move // near_lon, lax.rem(lon_move, near_lon)
    far_lat, off_lat = lat_move // near_lat, lax.rem(lat_move, near_lat)
    shift = off_lon * near_lat + off_lat
    turn_here = lax.rem(2 * lanes - shift, lanes)
    turn_next = lax.rem(2 * lanes - shift + near_lat, lanes)
    same_lon = lane >= off_lon * near_lat
    same_lat = col + off_lat < near_lat
    half = tiles_lon // 2
    for a in range(tiles_lon):
        met = [
            jnp.where(same_lon, spread_ref[far_lon + a, far_lat + b], spread_ref[far_lon + a + 1, far_lat + b])
            for b in range(tiles_lat + 1)
        ]
        for b in range(tiles_lat):
            value = jnp.where(same_lat, turn(met[b], turn_here), turn(met[b + 1], turn_next))
            out_ref[a, b] = value.astype(jnp.bfloat16)
        if (a + 1) % half == 0:
            part = pl.ds(a + 1 - half, half)
            started += copies(sems, 1 + a // half, [(out_ref.at[part], out_hbm.at[part])])
    finish(started)


def spatial(mode, step, tile, rows, field, kern, weights, moves):
    tiles_lon, tiles_lat, _, lanes = field.shape
    with_move, with_stencil = mode != "last", mode != "first"
    operands = ([moves] if with_move else []) + [field]
    operands += [kern] if with_stencil else []
    operands += [weights] if mode == "mid" else []
    out_shape = (tiles_lon, tiles_lat, rows if with_move else 2 * rows, lanes)
    weight_shape = (tiles_lon, tiles_lat, ROWS, lanes)
    sds = jax.ShapeDtypeStruct
    out = [sds(out_shape, jnp.bfloat16)] + ([sds(weight_shape, jnp.bfloat16)] if mode == "first" else [])
    scratch = [pltpu.VMEM(out_shape, jnp.bfloat16), pltpu.SemaphoreType.DMA((3,))]
    if with_move:
        spread_shape = (tiles_lon + LON_REACH, tiles_lat + LAT_REACH, rows, lanes)
        scratch += [pltpu.VMEM(spread_shape, jnp.float32), pltpu.VMEM(weight_shape, jnp.bfloat16)]
    return call(
        functools.partial(spatial_kernel, mode, step, *tile),
        out,
        operands,
        "s" * with_move + "v" + "v" * with_stencil + "h" * (mode == "mid"),
        "h" * len(out),
        scratch=scratch,
        flops=2**22,
        moved=2**20,
        limit=max(8, 14 * tiles_lon * tiles_lat * rows * lanes * 4 // MIB),
    )


def halved(value, axis, bit, dim):
    count = lax.axis_size(axis)
    mine = lax.axis_index(axis) >> bit & 1
    kept = lax.dynamic_index_in_dim(value, mine, dim, keepdims=False)
    sent = lax.dynamic_index_in_dim(value, 1 - mine, dim, keepdims=False).astype(jnp.bfloat16)
    arrived = lax.ppermute(sent, axis, [(i, i ^ (1 << bit)) for i in range(count)])
    return kept + arrived.astype(jnp.float32)


def scattered(value, lat_first):
    channels, hid = value.shape
    lon_bits = lax.axis_size("lon").bit_length() - 1
    lat_bits = lax.axis_size("lat").bit_length() - 1
    rows = channels >> lon_bits
    value = value.reshape(*([2] * lon_bits), rows, *([2] * lat_bits), hid >> lat_bits)

    def over_lon(value, bit, left):
        return halved(value, "lon", bit, left.index(bit)), [k for k in left if k != bit]

    left_lon = list(range(lon_bits))[::-1]
    left_lat = list(range(lat_bits))[::-1]
    order = [("lon", 0), ("lon", 1)] + [("lat", k) for k in range(lat_bits)]
    if lat_first:
        order = [("lon", 0)] + [("lat", k) for k in range(lat_bits)] + [("lon", 1)]
    order += [("lon", k) for k in range(2, lon_bits)]
    for axis, bit in order:
        if axis == "lon":
            value, left_lon = over_lon(value, bit, left_lon)
        else:
            value = halved(value, "lat", bit, len(left_lon) + 1 + left_lat.index(bit))
            left_lat.remove(bit)
    return value


def gradient_kernel(row_groups, bit_ref, *refs):
    *inputs, send_ref, keep_ref, left_ref, right_ref, sems = refs
    steps = len(inputs) // 4
    count = inputs[0].shape[1]
    arriving = []
    for k in range(2):
        for s in range(steps):
            part = pl.ds(s * count, count)
            pairs = [(inputs[2 * k * steps + s], left_ref.at[k, :, part])]
            pairs += [(inputs[(2 * k + 1) * steps + s], right_ref.at[k, part])]
            arriving += copies(sems, 2 * (k * steps + s), pairs)
    chunk = left_ref.shape[1] // (2 * row_groups)
    for k in range(2):
        finish(arriving[2 * k * steps : 2 * (k + 1) * steps])
        for which, out_ref in ((1 - bit_ref[0], send_ref), (bit_ref[0], keep_ref)):
            rows = []
            for p in range(row_groups):
                start = pl.multiple_of((2 * p + which) * chunk, chunk)
                rows.append(left_ref[k, pl.ds(start, chunk)])
            rows = jnp.concatenate(rows, axis=0)
            out_ref[k] = jnp.dot(rows, right_ref[k], preferred_element_type=jnp.float32).astype(jnp.bfloat16)


def halves_kernel(plan, together, bit_ref, *refs):
    refs = list(refs)
    count = len(plan)
    joint_in = len(refs) == 2 + (2 if together else 2 * count)
    if joint_in:
        kept, arrived = refs[0], refs[1]
        kept, arrived = [kept.at[k] for k in range(count)], [arrived.at[k] for k in range(count)]
        refs = refs[2:]
    else:
        kept, arrived = refs[:count], refs[count : 2 * count]
        refs = refs[2 * count :]
    if together:
        sends, keeps = [refs[0].at[k] for k in range(count)], [refs[1].at[k] for k in range(count)]
    else:
        sends, keeps = refs[:count], refs[count:]
    for k, (dim, groups, bit_at) in enumerate(plan):
        bit = bit_ref[bit_at]
        size = kept[k].shape[dim] // (2 * groups)
        for which, out_ref in ((1 - bit, sends[k]), (bit, keeps[k])):
            for p in range(groups):
                start = pl.multiple_of((2 * p + which) * size, size)
                place = (pl.ds(start, size),) if dim == 0 else (slice(None), pl.ds(start, size))
                goal = (pl.ds(p * size, size),) if dim == 0 else (slice(None), pl.ds(p * size, size))
                value = kept[k][place].astype(jnp.float32) + arrived[k][place].astype(jnp.float32)
                out_ref[goal] = value.astype(out_ref.dtype)


def halves(plan, together, bits, kept, arrived):
    shapes = []
    arrays = [kept[k] for k in range(len(plan))] if isinstance(kept, (list, tuple)) else kept
    for k, (dim, _, _) in enumerate(plan):
        shape = list(arrays[k].shape if isinstance(arrays, list) else arrays.shape[1:])
        shape[dim] //= 2
        shapes.append(tuple(shape))
    sds = jax.ShapeDtypeStruct
    if together:
        shape = (len(plan), *shapes[0])
        out = [sds(shape, jnp.bfloat16), sds(shape, jnp.float32)]
    else:
        out = [sds(shape, jnp.bfloat16) for shape in shapes] + [sds(shape, jnp.float32) for shape in shapes]
    operands = [*kept, *arrived] if isinstance(kept, (list, tuple)) else [kept, arrived]
    return call(
        functools.partial(halves_kernel, plan, together),
        out,
        [bits, *operands],
        "s" + "v" * len(operands),
        "v" * len(out),
        moved=2**20,
        limit=12,
    )


def last_sum_kernel(kept_ref, arrived_ref, up_ref, down_ref):
    up_ref[...] = kept_ref[0] + arrived_ref[0].astype(jnp.float32)
    down_ref[...] = kept_ref[1] + arrived_ref[1].astype(jnp.float32)


def swapped(value, axis, bit):
    count = lax.axis_size(axis)
    return lax.ppermute(value, axis, [(i, i ^ (1 << bit)) for i in range(count)])


def projection_sums(narrow, hidden, grads, moved):
    steps = len(narrow)
    channels, count = narrow[0].shape
    hid = hidden[0].shape[1]
    lon, lat = lax.axis_size("lon"), lax.axis_size("lat")
    if lat != 2 or lon != 16:
        dots = lambda left, right: sum(
            jnp.dot(left[s], right[s], preferred_element_type=jnp.float32) for s in range(steps)
        )
        return scattered(dots(narrow, grads), False), scattered(dots(moved, hidden), True)
    here = lax.axis_index("lon")
    bits = jnp.stack([here >> k & 1 for k in range(4)] + [lax.axis_index("lat")]).astype(jnp.int32)
    sds = jax.ShapeDtypeStruct
    groups = lon // 2
    shape = (2, channels // 2, hid)
    send, keep = call(
        functools.partial(gradient_kernel, groups),
        [sds(shape, jnp.bfloat16), sds(shape, jnp.bfloat16)],
        [bits, *narrow, *grads, *moved, *hidden],
        "s" + "h" * 4 * steps,
        "vv",
        scratch=[
            pltpu.VMEM((2, channels, steps * count), jnp.bfloat16),
            pltpu.VMEM((2, steps * count, hid), jnp.bfloat16),
            pltpu.SemaphoreType.DMA((4 * steps,)),
        ],
        flops=12 * 2**28,
        moved=6 * 2**20,
        limit=16,
    )
    arrived = swapped(send, "lon", 0)
    send_up, send_down, *keep = halves(((0, groups // 2, 1), (1, 1, 4)), False, bits, keep, arrived)
    arrived = [swapped(send_up, "lon", 1), swapped(send_down, "lat", 0)]
    send_up, send_down, *keep = halves(((1, 1, 4), (0, groups // 2, 1)), False, bits, keep, arrived)
    arrived = [swapped(send_up, "lat", 0), swapped(send_down, "lon", 1)]
    send, keep = halves(((0, groups // 4, 2), (0, groups // 4, 2)), True, bits, keep, arrived)
    arrived = swapped(send, "lon", 2)
    send, keep = halves(((0, groups // 8, 3), (0, groups // 8, 3)), True, bits, keep, arrived)
    arrived = swapped(send, "lon", 3)
    out = sds((channels // lon, hid // lat), jnp.float32)
    return call(last_sum_kernel, [out, out], [keep, arrived], "vv", "vv", moved=2**18)


def local(cotangent, states, w_up, w_down, norm_gain, kernel, bilinear, lon_move, lat_move):
    steps, rows_out, cols_out, channels = states.shape
    tiles_lon, tiles_lat = lax.axis_size("lon"), lax.axis_size("lat")
    devices = tiles_lon * tiles_lat
    count = rows_out * cols_out
    tile = (rows_out, cols_out)
    share = channels // devices
    padded_share = -(-share // ROWS) * ROWS
    whole_share = share == padded_share
    group_size = channels // lon_move.shape[1]
    me = lax.axis_index("lon") * tiles_lat + lax.axis_index("lat")

    def as_blocks(value):
        value = value.reshape(devices, share, count)
        return value if whole_share else jnp.pad(value, ((0, 0), (0, padded_share - share), (0, 0)))

    def as_rows(blocks):
        return blocks[:, :share].reshape(channels, count)

    def as_grid(blocks):
        return blocks.reshape(tiles_lon, tiles_lat, *blocks.shape[1:])

    def as_pairs(blocks):
        if whole_share:
            return blocks
        parts = [blocks[:, :share], blocks[:, share:]]
        parts = [jnp.pad(part, ((0, 0), (0, padded_share - share), (0, 0))) for part in parts]
        return jnp.concatenate(parts, axis=1)

    def from_pairs(blocks):
        if whole_share:
            return blocks
        return jnp.concatenate([blocks[:, :share], blocks[:, padded_share : padded_share + share]], axis=1)

    blocks = packed(cotangent, bilinear, devices)
    blocks, states_later = lax.optimization_barrier((blocks, states))
    arrived = as_grid(exchanged(blocks))
    group = me * share // group_size
    moves = jnp.stack([lon_move[:, group], lat_move[:, group]], axis=1)
    grid_now, weights = spatial("first", steps - 1, tile, padded_share, arrived, None, None, moves[steps - 1])

    taps = lax.dynamic_slice_in_dim(kernel.reshape(9, channels), me * share, share, 1).T
    taps = jnp.pad(taps, ((0, padded_share - share), (0, count - 9)))

    low, high = lon_edges(states_later)
    grid_now, low, high = lax.optimization_barrier((grid_now, low, high))
    around = (low, high, *lat_edges(states, low, high))
    order = list(reversed(range(steps)))
    gain = norm_gain.reshape(1, channels)
    forward = {s: forward_parts(s, states, around, kernel, gain, w_up) for s in order}

    moved, grads, fields = {}, {}, {}
    sums = None
    by_step = lambda values, steps_now: [values[s] for s in steps_now]

    def sums_of(steps_now, before):
        parts = [[forward[s][5] for s in steps_now], by_step(fields, steps_now), by_step(grads, steps_now)]
        return channel_sums(tile, devices, w_up, gain, *parts, [forward[s][0] for s in steps_now], before)

    for s in order:
        here = as_rows(exchanged(grid_now.reshape(devices, padded_share, count)))
        if s == order[-1]:
            sums = sums_of(order[:-1], None)
            here, sums = lax.optimization_barrier((here, sums))
        elif s != order[0]:
            here, forward = lax.optimization_barrier((here, forward))
        narrow, _, inv_root, _, slope, _ = forward[s]
        fields[s], grads[s], moved[s] = network_back(here, w_down, w_up, gain, slope, narrow, inv_root)
        if s > 0:
            arrived = as_grid(exchanged(as_blocks(fields[s])))
            (grid_now,) = spatial("mid", s - 1, tile, padded_share, arrived, taps, weights, moves[s - 1])
    arrived = as_grid(exchanged(as_pairs(sums_of(order[-1:], sums))))
    (grid_now,) = spatial("last", None, tile, padded_share, arrived, taps, None, None)

    arrived = exchanged(grid_now.reshape(devices, 2 * padded_share, count))
    grad_state, grad_kernel, grad_gain = final_parts(from_pairs(arrived), channels)
    narrow, hidden = ([forward[s][k] for s in order] for k in (1, 3))
    grad_up, grad_down = projection_sums(narrow, hidden, by_step(grads, order), by_step(moved, order))
    return (grad_state.reshape(cotangent.shape), grad_up, grad_down, grad_kernel, grad_gain.reshape(channels))


def solution(mesh):
    placed = (
        P("lon", "lat", None),
        P(None, "lon", "lat", None),
        P(),
        P(),
        P(),
        P(),
        P(None, None, "lon", "lat"),
        P(),
        P(),
    )
    return jax.shard_map(
        local,
        mesh=mesh,
        in_specs=placed,
        out_specs=(P("lon", "lat", None), P("lon", "lat"), P("lon", "lat"), P(), P()),
        check_vma=False,
    )
```

time: 143 us -> 140 us (0.979)
  waiting for transfers between devices: 33.6 us -> 43.8 us
  starting transfers between devices: 47.7 us -> 39.7 us
  local copies, waits for them, and re-layouts: 5.18 us -> 1.29 us
  Pallas kernels: 43.2 us -> 41.2 us
    all_to_all x7, waiting for transfers between devices: 24.3 us -> 33.9 us  [exchanged(): return lax.all_to_all(blocks, AXES, split_axis=0, concat_axis=0, tiled=True)]
    ppermute x5 -> x3, starting transfers between devices: 11.7 us -> 5.49 us  [the longest x1 4.19 us: lon_edges(): lax.ppermute(value, 'lon', [(i, (i - 1) % lon) for i in range(lon)])]
    pallas_call x19 -> x20, Pallas kernels: 43.2 us -> 41.2 us  [call(): pl.pallas_call(kernel, out_shape=out_shape, in_specs=[pl.BlockSpec(memory...]
    unnamed x13 -> x19, local copies, waits for them, and re-layouts: 2.88 us -> 0.91 us
    all_to_all x7, starting transfers between devices: 24.9 us -> 23.1 us  [exchanged(): return lax.all_to_all(blocks, AXES, split_axis=0, concat_axis=0, tiled=True)]
  transfers between devices with their start and end apart: 19 -> 17, of which waited for: 9 -> 11; matrix products, arithmetic and copies ran while one was open for 3% -> 0% of each run, Pallas kernels for 14% -> 15%
where the time goes in v5:
time: 140 us; the launch traced here: 139 us
  waiting for transfers between devices  43.8 us (31%)
  Pallas kernels  41.2 us (29%)
  starting transfers between devices  39.7 us (28%)
  blocking collectives  11.4 us (8%)
    pallas_call x20, Pallas kernels, call(): pl.pallas_call(kernel, out_shape=out_shape, in_specs=[pl.BlockSpec(memory...  41.2 us
    all_to_all x7, waiting for transfers between devices, exchanged(): return lax.all_to_all(blocks, AXES, split_axis=0, concat_axis=0, tiled=True)  33.9 us
    all_to_all x7, starting transfers between devices, exchanged(): return lax.all_to_all(blocks, AXES, split_axis=0, concat_axis=0, tiled=True)  23.1 us
    all_to_all x1, blocking collectives, exchanged(): return lax.all_to_all(blocks, AXES, split_axis=0, concat_axis=0, tiled=True)  11.4 us
    ppermute x7, starting transfers between devices, swapped(): return lax.ppermute(value, axis, [(i, i ^ 1 << bit) for i in range(count)])  11.1 us
    ppermute x7, waiting for transfers between devices, swapped(): return lax.ppermute(value, axis, [(i, i ^ 1 << bit) for i in range(count)])  9.25 us
    ppermute x1, starting transfers between devices, lon_edges(): lax.ppermute(value, 'lon', [(i, (i - 1) % lon) for i in range(lon)])  4.19 us
  transfers between devices with their start and end apart: 17, of which 11 were waited for; matrix products, arithmetic and copies ran while one was open for 0% of the time, Pallas kernels for 15%

profile of v5, /device:TPU:0, one launch (start us, length us, event | category | flops | bytes accessed | tf_op | source)
XLA Modules:
  0.0 138.8 jit_solution(475873578032602025)
XLA Ops:
  0.7 1.8 %shard_map.128 = bf16[32,32,128]{2,1,0:T(8,128)(2,1)} custom-call(bf16[128,512]{1,0:T(8,128)(2,1)} %bitcast.50, f32[12,8,16]{2,1,0:T(8,128)} %bitcast.51), custom_call_target="tpu_custom_call" | custom-call | bytes 524288 | tf_op jit(solution)/shard_map/pallas_call | solution.py:34
  2.5 7.3 %all-to-all-start = ((bf16[32,32,128]{2,1,0:T(8,128)(2,1)}), bf16[32,32,128]{2,1,0:T(8,128)(2,1)S(1)}, u32[]{:S(2)}, u32[]{:S(2)}) async-start(bf16[32,32,128]{2,1,0:T(8,128)(2,1)} %shard_map.128), calls=%async_computation | async-start | bytes 524288 | tf_op jit(solution)/shard_map/all_to_all | solution.py:19
  10.2 4.2 %collective-permute-start.1 = (bf16[3,1,16,512]{3,2,1,0:T(8,128)(2,1)S(1)}, bf16[3,1,16,512]{3,2,1,0:T(8,128)(2,1)S(1)}, u32[]{:S(2)}, u32[]{:S(2)}) collective-permute-start(bf16[3,1,16,512]{3,2,1,0:T(8,128)(2,1)S(1)} %get-tuple-element.151), channel_id=1, source_target_pairs={{0,30},{2,0},{4,2},{6,4},{8,6},{10,8},{12,10},{14,12},{16,14},{18,... | collective-permute-start | bytes 147464 | tf_op jit(solution)/shard_map/ppermute | solution.py:120
  14.6 6.3 %all-to-all-done = bf16[32,32,128]{2,1,0:T(8,128)(2,1)S(1)} async-done(((bf16[32,32,128]{2,1,0:T(8,128)(2,1)}), bf16[32,32,128]{2,1,0:T(8,128)(2,1)S(1)}, u32[]{:S(2)}, u32[]{:S(2)}) %all-to-all-start) | async-done | bytes 262176 | tf_op jit(solution)/shard_map/all_to_all | solution.py:19
  20.9 1.7 %shard_map.129 = (bf16[16,2,16,128]{3,2,1,0:T(8,128)(2,1)}, bf16[16,2,16,128]{3,2,1,0:T(8,128)(2,1)}) custom-call(s32[2]{0:T(128)S(1)} %get-tuple-element.160.refs_0_, bf16[16,2,32,128]{3,2,1,0:T(8,128)(2,1)S(1)} %bitcast.30), custom_call_target="tpu_custom_call" | custom-call | flops 4194304 | bytes 1048576 | tf_op jit(solution)/shard_map/pallas_call | solution.py:34
  23.9 2.7 %all-to-all-start.1 = ((bf16[32,16,128]{2,1,0:T(8,128)(2,1)}), bf16[32,16,128]{2,1,0:T(8,128)(2,1)S(1)}, u32[]{:S(2)}, u32[]{:S(2)}) async-start(bf16[32,16,128]{2,1,0:T(8,128)(2,1)} %bitcast.6), calls=%async_computation.1 | async-start | bytes 262144 | tf_op jit(solution)/shard_map/all_to_all | solution.py:19
  27.4 2.8 %shard_map.130 = (bf16[128,512]{1,0:T(8,128)(2,1)}, bf16[512,128]{1,0:T(8,128)(2,1)}, f32[128,128]{1,0:T(8,128)}, bf16[128,1024]{1,0:T(8,128)(2,1)}, bf16[128,10...) custom-call(bf16[3,8,16,512]{3,2,1,0:T(8,128)(2,1)} %states_hbm.5, ...), custom_call_target="tpu_custom_call" | custom-call | flops 134217728 | bytes 4194304 | tf_op jit(solution)/shard_map/pallas_call | solution.py:34
  30.1 5.1 %all-to-all-done.1 = bf16[32,16,128]{2,1,0:T(8,128)(2,1)S(1)} async-done(((bf16[32,16,128]{2,1,0:T(8,128)(2,1)}), bf16[32,16,128]{2,1,0:T(8,128)(2,1)S(1)}, u32[]{:S(2)}, u32[]{:S(2)}) %all-to-all-start.1) | async-done | bytes 131104 | tf_op jit(solution)/shard_map/all_to_all | solution.py:19
  35.3 2.6 %shard_map.131 = (bf16[512,128]{1,0:T(8,128)(2,1)}, bf16[128,1024]{1,0:T(8,128)(2,1)}, bf16[512,128]{1,0:T(8,128)(2,1)}) custom-call(bf16[512,128]{1,0:T(8,128)(2,1)S(1)} %bitcast.34, bf16[512,1024]{1,0:T(8,128)(2,1)S(1)} %copy-done.1, bf16[512,1024]{1,0:T(8,128)(2,1)S(1)} %copy-done, f32[1,512]{1,0:T(1,128)S(1)} %bitcast.38, ...), custom_call_target="tpu_custom_call" | custom-call | flops 268435456 | bytes 4194304 | tf_op jit(solution)/shard_map/pallas_call | solution.py:34
  37.9 2.6 %all-to-all-start.2 = ((bf16[32,16,128]{2,1,0:T(8,128)(2,1)}), bf16[32,16,128]{2,1,0:T(8,128)(2,1)S(1)}, u32[]{:S(2)}, u32[]{:S(2)}) async-start(bf16[32,16,128]{2,1,0:T(8,128)(2,1)} %bitcast.46), calls=%async_computation.2 | async-start | bytes 262144 | tf_op jit(solution)/shard_map/all_to_all | solution.py:19
  40.7 8.4 %all-to-all-done.2 = bf16[32,16,128]{2,1,0:T(8,128)(2,1)S(1)} async-done(((bf16[32,16,128]{2,1,0:T(8,128)(2,1)}), bf16[32,16,128]{2,1,0:T(8,128)(2,1)S(1)}, u32[]{:S(2)}, u32[]{:S(2)}) %all-to-all-start.2) | async-done | bytes 131104 | tf_op jit(solution)/shard_map/all_to_all | solution.py:19
  49.1 2.6 %shard_map.132 = bf16[16,2,16,128]{3,2,1,0:T(8,128)(2,1)} custom-call(s32[2]{0:T(128)S(1)} %get-tuple-element.161.refs_0_, bf16[16,2,16,128]{3,2,1,0:T(8,128)(2,1)S(1)} %bitcast.35, f32[16,128]{1,0:T(8,128)S(1)} %pad.4.refs_2_.refs_1_, bf16[16,2,16,128]{3,2,1,0:T(8,128)(2,1)} %get-tuple-element.87.refs_3_), custom_call_target="tpu_custom_call" | custom-call | flops 4194304 | bytes 1048576 | tf_op jit(solution)/shard_map/pallas_call | solution.py:34
  51.8 2.6 %all-to-all-start.3 = ((bf16[32,16,128]{2,1,0:T(8,128)(2,1)}), bf16[32,16,128]{2,1,0:T(8,128)(2,1)S(1)}, u32[]{:S(2)}, u32[]{:S(2)}) async-start(bf16[32,16,128]{2,1,0:T(8,128)(2,1)} %bitcast.49), calls=%async_computation.3 | async-start | bytes 262144 | tf_op jit(solution)/shard_map/all_to_all | solution.py:19
  54.3 2.8 %shard_map.133 = (bf16[128,512]{1,0:T(8,128)(2,1)}, bf16[512,128]{1,0:T(8,128)(2,1)}, f32[128,128]{1,0:T(8,128)}, bf16[128,1024]{1,0:T(8,128)(2,1)}, bf16[128,10...) custom-call(bf16[3,8,16,512]{3,2,1,0:T(8,128)(2,1)} %states_hbm.5, ...), custom_call_target="tpu_custom_call" | custom-call | flops 134217728 | bytes 4194304 | tf_op jit(solution)/shard_map/pallas_call | solution.py:34
  57.1 2.8 %shard_map.134 = (bf16[128,512]{1,0:T(8,128)(2,1)}, bf16[512,128]{1,0:T(8,128)(2,1)}, f32[128,128]{1,0:T(8,128)}, bf16[128,1024]{1,0:T(8,128)(2,1)}, bf16[128,10...) custom-call(bf16[3,8,16,512]{3,2,1,0:T(8,128)(2,1)} %states_hbm.5, ...), custom_call_target="tpu_custom_call" | custom-call | flops 134217728 | bytes 4194304 | tf_op jit(solution)/shard_map/pallas_call | solution.py:34
  59.9 3.1 %all-to-all-done.3 = bf16[32,16,128]{2,1,0:T(8,128)(2,1)S(1)} async-done(((bf16[32,16,128]{2,1,0:T(8,128)(2,1)}), bf16[32,16,128]{2,1,0:T(8,128)(2,1)S(1)}, u32[]{:S(2)}, u32[]{:S(2)}) %all-to-all-start.3) | async-done | bytes 131104 | tf_op jit(solution)/shard_map/all_to_all | solution.py:19
  63.0 2.6 %shard_map.135 = (bf16[512,128]{1,0:T(8,128)(2,1)}, bf16[128,1024]{1,0:T(8,128)(2,1)}, bf16[512,128]{1,0:T(8,128)(2,1)}) custom-call(bf16[512,128]{1,0:T(8,128)(2,1)S(1)} %bitcast.33, bf16[512,1024]{1,0:T(8,128)(2,1)S(1)} %copy-done.1, bf16[512,1024]{1,0:T(8,128)(2,1)S(1)} %copy-done, f32[1,512]{1,0:T(1,128)S(1)} %bitcast.41, ...), custom_call_target="tpu_custom_call" | custom-call | flops 268435456 | bytes 4194304 | tf_op jit(solution)/shard_map/pallas_call | solution.py:34
  65.6 11.4 %all_to_all.40 = bf16[32,16,128]{2,1,0:T(8,128)(2,1)S(1)} all-to-all(bf16[32,16,128]{2,1,0:T(8,128)(2,1)} %bitcast.47), channel_id=1, replica_groups=mesh['lon'=16,'lat'=2] {'lon','lat'}, dimensions={0} | all-to-all | bytes 262144 | tf_op jit(solution)/shard_map/all_to_all | solution.py:19
  77.0 2.6 %shard_map.136 = bf16[16,2,16,128]{3,2,1,0:T(8,128)(2,1)} custom-call(s32[2]{0:T(128)S(1)} %get-tuple-element.159.refs_0_, bf16[16,2,16,128]{3,2,1,0:T(8,128)(2,1)S(1)} %bitcast.36, f32[16,128]{1,0:T(8,128)S(1)} %pad.4.refs_2_.refs_1_, bf16[16,2,16,128]{3,2,1,0:T(8,128)(2,1)} %get-tuple-element.87.refs_3_), custom_call_target="tpu_custom_call" | custom-call | flops 4194304 | bytes 1048576 | tf_op jit(solution)/shard_map/pallas_call | solution.py:34
  79.6 2.8 %all-to-all-start.5 = ((bf16[32,16,128]{2,1,0:T(8,128)(2,1)}), bf16[32,16,128]{2,1,0:T(8,128)(2,1)S(1)}, u32[]{:S(2)}, u32[]{:S(2)}) async-start(bf16[32,16,128]{2,1,0:T(8,128)(2,1)} %bitcast.48), calls=%async_computation.5 | async-start | bytes 262144 | tf_op jit(solution)/shard_map/all_to_all | solution.py:19
  82.5 2.7 %shard_map.137.refs_6_ = f32[16,512]{1,0:T(8,128)S(1)} custom-call(bf16[512,1024]{1,0:T(8,128)(2,1)S(1)} %copy-done, f32[1,512]{1,0:T(1,128)S(1)} %bitcast.42, bf16[10,32,512]{2,1,0:T(8,128)(2,1)} %get-tuple-element.109.refs_2_, bf16[512,128]{1,0:T(8,128)(2,1)} %get-tuple-element.86.refs_3_, bf16[128,1024]{1,0:T(8,128)(2,1)} %get-tuple-element.110.refs_4_.refs_3_, ...), custom_call_target="tpu_custom_call" | custom-call | bytes 2097152 | tf_op jit(solution)/shard_map/pallas_call | solution.py:34
  85.2 5.6 %all-to-all-done.5 = bf16[32,16,128]{2,1,0:T(8,128)(2,1)S(1)} async-done(((bf16[32,16,128]{2,1,0:T(8,128)(2,1)}), bf16[32,16,128]{2,1,0:T(8,128)(2,1)S(1)}, u32[]{:S(2)}, u32[]{:S(2)}) %all-to-all-start.5) | async-done | bytes 131104 | tf_op jit(solution)/shard_map/all_to_all | solution.py:19
  90.8 2.6 %shard_map.138 = (bf16[512,128]{1,0:T(8,128)(2,1)}, bf16[128,1024]{1,0:T(8,128)(2,1)}, bf16[512,128]{1,0:T(8,128)(2,1)}) custom-call(bf16[512,128]{1,0:T(8,128)(2,1)S(1)} %bitcast.32, bf16[512,1024]{1,0:T(8,128)(2,1)S(1)} %copy-done.1, bf16[512,1024]{1,0:T(8,128)(2,1)S(1)} %copy-done, f32[1,512]{1,0:T(1,128)S(1)} %bitcast.43, ...), custom_call_target="tpu_custom_call" | custom-call | flops 268435456 | bytes 4194304 | tf_op jit(solution)/shard_map/pallas_call | solution.py:34
  93.5 4.2 %shard_map.142 = (bf16[2,256,1024]{2,1,0:T(8,128)(2,1)}, bf16[2,256,1024]{2,1,0:T(8,128)(2,1)S(1)}) custom-call(s32[5]{0:T(128)S(1)} %stack.27.bit_ref, bf16[512,128]{1,0:T(8,128)(2,1)} %get-tuple-element.122.refs_0_, bf16[512,128]{1,0:T(8,128)(2,1)} %get-tuple-element.123.refs_1_, bf16[512,128]{1,0:T(8,128)(2,1)} %get-tuple-element.124.refs_2_, ...), custom_call_target="tpu_custom_call" | custom-call | flops 3221225472 | bytes 6291456 | tf_op jit(solution)/shard_map/pallas_call | solution.py:34
  97.7 2.8 %shard_map.139 = bf16[32,32,128]{2,1,0:T(8,128)(2,1)} custom-call(bf16[512,1024]{1,0:T(8,128)(2,1)S(1)} %copy-done, f32[1,512]{1,0:T(1,128)S(1)} %bitcast.44, bf16[10,32,512]{2,1,0:T(8,128)(2,1)} %get-tuple-element.103.refs_2_, bf16[512,128]{1,0:T(8,128)(2,1)} %get-tuple-element.118.refs_3_, bf16[128,1024]{1,0:T(8,128)(2,1)} %get-tuple-element.119.refs_4_.refs_5_, ...), custom_call_target="tpu_custom_call" | custom-call | bytes 2097152 | tf_op jit(solution)/shard_map/pallas_call | solution.py:34
  100.6 2.6 %all-to-all-start.6 = ((bf16[32,32,128]{2,1,0:T(8,128)(2,1)}), bf16[32,32,128]{2,1,0:T(8,128)(2,1)S(1)}, u32[]{:S(2)}, u32[]{:S(2)}) async-start(bf16[32,32,128]{2,1,0:T(8,128)(2,1)} %shard_map.139), calls=%async_computation.6 | async-start | bytes 524288 | tf_op jit(solution)/shard_map/all_to_all | solution.py:19
  108.5 5.4 %all-to-all-done.6 = bf16[32,32,128]{2,1,0:T(8,128)(2,1)S(1)} async-done(((bf16[32,32,128]{2,1,0:T(8,128)(2,1)}), bf16[32,32,128]{2,1,0:T(8,128)(2,1)S(1)}, u32[]{:S(2)}, u32[]{:S(2)}) %all-to-all-start.6) | async-done | bytes 262176 | tf_op jit(solution)/shard_map/all_to_all | solution.py:19
  115.1 2.6 %all-to-all-start.7 = ((bf16[32,32,128]{2,1,0:T(8,128)(2,1)}), bf16[32,32,128]{2,1,0:T(8,128)(2,1)S(1)}, u32[]{:S(2)}, u32[]{:S(2)}) async-start(bf16[32,32,128]{2,1,0:T(8,128)(2,1)} %bitcast.45), calls=%async_computation.7 | async-start | bytes 524288 | tf_op jit(solution)/shard_map/all_to_all | solution.py:19
  121.6 4.2 %collective-permute-done.6.refs_2_ = bf16[128,512]{1,0:T(8,128)(2,1)S(1)} collective-permute-done((bf16[128,512]{1,0:T(8,128)(2,1)S(1)}, bf16[128,512]{1,0:T(8,128)(2,1)S(1)}, u32[]{:S(2)}, u32[]{:S(2)}) %collective-permute-start.6) | collective-permute-done | bytes 131104 | tf_op jit(solution)/shard_map/ppermute | solution.py:597
  127.2 1.8 %collective-permute-start.8 = (bf16[2,64,512]{2,1,0:T(8,128)(2,1)S(1)}, bf16[2,64,512]{2,1,0:T(8,128)(2,1)S(1)}, u32[]{:S(2)}, u32[]{:S(2)}) collective-permute-start(bf16[2,64,512]{2,1,0:T(8,128)(2,1)S(1)} %get-tuple-element.142), channel_id=1, source_target_pairs={{0,8},{2,10},{4,12},{6,14},{8,0},{10,2},{12,4},{14,6},{16,24},{18,... | collective-permute-start | bytes 393224 | tf_op jit(solution)/shard_map/ppermute | solution.py:597
  129.0 3.2 %collective-permute-done.8.refs_1_ = bf16[2,64,512]{2,1,0:T(8,128)(2,1)S(1)} collective-permute-done((bf16[2,64,512]{2,1,0:T(8,128)(2,1)S(1)}, bf16[2,64,512]{2,1,0:T(8,128)(2,1)S(1)}, u32[]{:S(2)}, u32[]{:S(2)}) %collective-permute-start.8) | collective-permute-done | bytes 131104 | tf_op jit(solution)/shard_map/ppermute | solution.py:597
  132.8 2.9 %collective-permute-start.9 = (bf16[2,32,512]{2,1,0:T(8,128)(2,1)S(1)}, bf16[2,32,512]{2,1,0:T(8,128)(2,1)S(1)}, u32[]{:S(2)}, u32[]{:S(2)}) collective-permute-start(bf16[2,32,512]{2,1,0:T(8,128)(2,1)S(1)} %get-tuple-element.144), channel_id=1, source_target_pairs={{0,16},{2,18},{4,20},{6,22},{8,24},{10,26},{12,28},{14,30},{16,0},... | collective-permute-start | bytes 196616 | tf_op jit(solution)/shard_map/ppermute | solution.py:597
  (55 shorter events, 18.2 us)
Async XLA Ops:
  0.6 9.2 %copy-start.6 = (bf16[3,8,16,512]{3,2,1,0:T(8,128)(2,1)S(1)}, bf16[3,8,16,512]{3,2,1,0:T(8,128)(2,1)}, u32[]{:S(2)}) copy-start(bf16[3,8,16,512]{3,2,1,0:T(8,128)(2,1)} %states_hbm.5) | copy-start | bytes 1179652
  0.6 13.7 %copy-start.7 = (s32[3,4]{1,0:T(4,128)S(1)}, s32[3,4]{1,0:T(4,128)}, u32[]{:S(2)}) copy-start(s32[3,4]{1,0:T(4,128)} %param.17) | copy-start | bytes 148
  0.7 13.7 %copy-start.8 = (s32[3,4]{1,0:T(4,128)S(1)}, s32[3,4]{1,0:T(4,128)}, u32[]{:S(2)}) copy-start(s32[3,4]{1,0:T(4,128)} %param.16) | copy-start | bytes 148
  2.5 24.8 %copy-start = (bf16[512,1024]{1,0:T(8,128)(2,1)S(1)}, bf16[512,1024]{1,0:T(8,128)(2,1)}, u32[]{:S(2)}) copy-start(bf16[512,1024]{1,0:T(8,128)(2,1)} %refs_0_.3) | copy-start | bytes 3145732
  2.5 18.4 %all-to-all-start = ((bf16[32,32,128]{2,1,0:T(8,128)(2,1)}), bf16[32,32,128]{2,1,0:T(8,128)(2,1)S(1)}, u32[]{:S(2)}, u32[]{:S(2)}) async-start(bf16[32,32,128]{2,1,0:T(8,128)(2,1)} %shard_map.128), calls=%async_computation | async-start | bytes 524288 | tf_op jit(solution)/shard_map/all_to_all | solution.py:19
  9.9 12.8 %collective-permute-start = (bf16[3,1,16,512]{3,2,1,0:T(8,128)(2,1)S(1)}, bf16[3,1,16,512]{3,2,1,0:T(8,128)(2,1)S(1)}, u32[]{:S(2)}, u32[]{:S(2)}) collective-permute-start(bf16[3,1,16,512]{3,2,1,0:T(8,128)(2,1)S(1)} %get-tuple-element.152), channel_id=1, source_target_pairs={{0,2},{2,4},{4,6},{6,8},{8,10},{10,12},{12,14},{14,16},{16,18},{18... | collective-permute-start | bytes 147464 | tf_op jit(solution)/shard_map/ppermute | solution.py:119
  10.2 12.5 %collective-permute-start.1 = (bf16[3,1,16,512]{3,2,1,0:T(8,128)(2,1)S(1)}, bf16[3,1,16,512]{3,2,1,0:T(8,128)(2,1)S(1)}, u32[]{:S(2)}, u32[]{:S(2)}) collective-permute-start(bf16[3,1,16,512]{3,2,1,0:T(8,128)(2,1)S(1)} %get-tuple-element.151), channel_id=1, source_target_pairs={{0,30},{2,0},{4,2},{6,4},{8,6},{10,8},{12,10},{14,12},{16,14},{18,... | collective-permute-start | bytes 147464 | tf_op jit(solution)/shard_map/ppermute | solution.py:120
  22.7 4.6 %copy-start.4 = (f32[3,3,512]{2,1,0:T(4,128)S(1)}, f32[3,3,512]{2,1,0:T(4,128)}, u32[]{:S(2)}) copy-start(f32[3,3,512]{2,1,0:T(4,128)} %kernel_ref.5) | copy-start | bytes 55300
  22.7 4.6 %copy-start.5 = (f32[512]{0:T(512)S(1)}, f32[512]{0:T(512)}, u32[]{:S(2)}) copy-start(f32[512]{0:T(512)} %param.13) | copy-start | bytes 6148
  22.9 4.3 %collective-permute-start.2 = (bf16[3,10,1,512]{3,2,1,0:T(2,128)(2,1)S(1)}, bf16[3,10,1,512]{3,2,1,0:T(2,128)(2,1)S(1)}, u32[]{:S(2)}, u32[]{:S(2)}) collective-permute-start(bf16[3,10,1,512]{3,2,1,0:T(2,128)(2,1)S(1)} %broadcast_select_fusion.2), channel_id=1, source_target_pairs={{0,1},{1,0},{2,3},{3,2},{4,5},{5,4},{6,7},{7,6},{8,9},{9,8},{10,11... | collective-permute-start | bytes 92168 | tf_op jit(solution)/shard_map/ppermute | solution.py:129
  23.9 11.3 %copy-start.1 = (bf16[512,1024]{1,0:T(8,128)(2,1)S(1)}, bf16[512,1024]{1,0:T(8,128)(2,1)}, u32[]{:S(2)}) copy-start(bf16[512,1024]{1,0:T(8,128)(2,1)} %down_ref.5) | copy-start | bytes 3145732
  23.9 11.3 %all-to-all-start.1 = ((bf16[32,16,128]{2,1,0:T(8,128)(2,1)}), bf16[32,16,128]{2,1,0:T(8,128)(2,1)S(1)}, u32[]{:S(2)}, u32[]{:S(2)}) async-start(bf16[32,16,128]{2,1,0:T(8,128)(2,1)} %bitcast.6), calls=%async_computation.1 | async-start | bytes 262144 | tf_op jit(solution)/shard_map/all_to_all | solution.py:19
  37.9 11.2 %all-to-all-start.2 = ((bf16[32,16,128]{2,1,0:T(8,128)(2,1)}), bf16[32,16,128]{2,1,0:T(8,128)(2,1)S(1)}, u32[]{:S(2)}, u32[]{:S(2)}) async-start(bf16[32,16,128]{2,1,0:T(8,128)(2,1)} %bitcast.46), calls=%async_computation.2 | async-start | bytes 262144 | tf_op jit(solution)/shard_map/all_to_all | solution.py:19
  51.8 11.2 %all-to-all-start.3 = ((bf16[32,16,128]{2,1,0:T(8,128)(2,1)}), bf16[32,16,128]{2,1,0:T(8,128)(2,1)S(1)}, u32[]{:S(2)}, u32[]{:S(2)}) async-start(bf16[32,16,128]{2,1,0:T(8,128)(2,1)} %bitcast.49), calls=%async_computation.3 | async-start | bytes 262144 | tf_op jit(solution)/shard_map/all_to_all | solution.py:19
  79.6 11.2 %all-to-all-start.5 = ((bf16[32,16,128]{2,1,0:T(8,128)(2,1)}), bf16[32,16,128]{2,1,0:T(8,128)(2,1)S(1)}, u32[]{:S(2)}, u32[]{:S(2)}) async-start(bf16[32,16,128]{2,1,0:T(8,128)(2,1)} %bitcast.48), calls=%async_computation.5 | async-start | bytes 262144 | tf_op jit(solution)/shard_map/all_to_all | solution.py:19
  97.7 5.5 %collective-permute-start.3 = (bf16[2,256,1024]{2,1,0:T(8,128)(2,1)}, bf16[2,256,1024]{2,1,0:T(8,128)(2,1)S(1)}, u32[]{:S(2)}, u32[]{:S(2)}) collective-permute-start(bf16[2,256,1024]{2,1,0:T(8,128)(2,1)} %get-tuple-element.132), channel_id=1, source_target_pairs={{0,2},{2,0},{4,6},{6,4},{8,10},{10,8},{12,14},{14,12},{16,18},{18,... | collective-permute-start | bytes 3145736 | tf_op jit(solution)/shard_map/ppermute | solution.py:597
  100.6 13.3 %all-to-all-start.6 = ((bf16[32,32,128]{2,1,0:T(8,128)(2,1)}), bf16[32,32,128]{2,1,0:T(8,128)(2,1)S(1)}, u32[]{:S(2)}, u32[]{:S(2)}) async-start(bf16[32,32,128]{2,1,0:T(8,128)(2,1)} %shard_map.139), calls=%async_computation.6 | async-start | bytes 524288 | tf_op jit(solution)/shard_map/all_to_all | solution.py:19
  104.6 0.8 copy-start.2
  105.4 12.3 %collective-permute-start.4 = (bf16[128,1024]{1,0:T(8,128)(2,1)}, bf16[128,1024]{1,0:T(8,128)(2,1)S(1)}, u32[]{:S(2)}, u32[]{:S(2)}) collective-permute-start(bf16[128,1024]{1,0:T(8,128)(2,1)} %get-tuple-element.135), channel_id=1, source_target_pairs={{0,4},{2,6},{4,0},{6,2},{8,12},{10,14},{12,8},{14,10},{16,20},{18,... | collective-permute-start | bytes 786440 | tf_op jit(solution)/shard_map/ppermute | solution.py:597
  107.0 10.7 %collective-permute-start.5 = (bf16[256,512]{1,0:T(8,128)(2,1)S(1)}, bf16[256,512]{1,0:T(8,128)(2,1)S(1)}, u32[]{:S(2)}, u32[]{:S(2)}) collective-permute-start(bf16[256,512]{1,0:T(8,128)(2,1)S(1)} %get-tuple-element.136), channel_id=1, source_target_pairs={{0,1},{1,0},{2,3},{3,2},{4,5},{5,4},{6,7},{7,6},{8,9},{9,8},{10,11... | collective-permute-start | bytes 786440 | tf_op jit(solution)/shard_map/ppermute | solution.py:597
  113.9 3.8 %copy-start.3 = (f32[256,512]{1,0:T(8,128)S(1)}, f32[256,512]{1,0:T(8,128)}, u32[]{:S(2)}) copy-start(f32[256,512]{1,0:T(8,128)} %copy-done.2) | copy-start | bytes 1572868
  115.1 20.6 %all-to-all-start.7 = ((bf16[32,32,128]{2,1,0:T(8,128)(2,1)}), bf16[32,32,128]{2,1,0:T(8,128)(2,1)S(1)}, u32[]{:S(2)}, u32[]{:S(2)}) async-start(bf16[32,32,128]{2,1,0:T(8,128)(2,1)} %bitcast.45), calls=%async_computation.7 | async-start | bytes 524288 | tf_op jit(solution)/shard_map/all_to_all | solution.py:19
  118.4 7.4 %collective-permute-start.6 = (bf16[128,512]{1,0:T(8,128)(2,1)S(1)}, bf16[128,512]{1,0:T(8,128)(2,1)S(1)}, u32[]{:S(2)}, u32[]{:S(2)}) collective-permute-start(bf16[128,512]{1,0:T(8,128)(2,1)S(1)} %get-tuple-element.139), channel_id=1, source_target_pairs={{0,1},{1,0},{2,3},{3,2},{4,5},{5,4},{6,7},{7,6},{8,9},{9,8},{10,11... | collective-permute-start | bytes 393224 | tf_op jit(solution)/shard_map/ppermute | solution.py:597
  120.1 6.5 %collective-permute-start.7 = (bf16[128,512]{1,0:T(8,128)(2,1)S(1)}, bf16[128,512]{1,0:T(8,128)(2,1)S(1)}, u32[]{:S(2)}, u32[]{:S(2)}) collective-permute-start(bf16[128,512]{1,0:T(8,128)(2,1)S(1)} %get-tuple-element.140), channel_id=1, source_target_pairs={{0,4},{2,6},{4,0},{6,2},{8,12},{10,14},{12,8},{14,10},{16,20},{18,... | collective-permute-start | bytes 393224 | tf_op jit(solution)/shard_map/ppermute | solution.py:597
  127.2 5.0 %collective-permute-start.8 = (bf16[2,64,512]{2,1,0:T(8,128)(2,1)S(1)}, bf16[2,64,512]{2,1,0:T(8,128)(2,1)S(1)}, u32[]{:S(2)}, u32[]{:S(2)}) collective-permute-start(bf16[2,64,512]{2,1,0:T(8,128)(2,1)S(1)} %get-tuple-element.142), channel_id=1, source_target_pairs={{0,8},{2,10},{4,12},{6,14},{8,0},{10,2},{12,4},{14,6},{16,24},{18,... | collective-permute-start | bytes 393224 | tf_op jit(solution)/shard_map/ppermute | solution.py:597
  132.8 5.3 %collective-permute-start.9 = (bf16[2,32,512]{2,1,0:T(8,128)(2,1)S(1)}, bf16[2,32,512]{2,1,0:T(8,128)(2,1)S(1)}, u32[]{:S(2)}, u32[]{:S(2)}) collective-permute-start(bf16[2,32,512]{2,1,0:T(8,128)(2,1)S(1)} %get-tuple-element.144), channel_id=1, source_target_pairs={{0,16},{2,18},{4,20},{6,22},{8,24},{10,26},{12,28},{14,30},{16,0},... | collective-permute-start | bytes 196616 | tf_op jit(solution)/shard_map/ppermute | solution.py:597

commit v6 on v5

v6 whole, which is shorter than its diff:
```python
import functools

import jax
import jax.numpy as jnp
from jax import lax
from jax.experimental import pallas as pl
from jax.experimental.pallas import tpu as pltpu
from jax.sharding import PartitionSpec as P

EPSILON = 1e-06
AXES = ("lon", "lat")
ROWS = 16
LAT_REACH = 2
LON_REACH = 8
MIB = 1024 * 1024


def exchanged(blocks):
    return lax.all_to_all(blocks, AXES, split_axis=0, concat_axis=0, tiled=True)


SPACES = {"s": pltpu.SMEM, "v": pltpu.VMEM, "p": pltpu.VMEM, "h": pltpu.HBM}
PINNED = {"p": pltpu.VMEM, "h": pltpu.HBM}


def call(kernel, out_shape, operands, ins, outs, scratch=(), flops=0, moved=0, limit=8):
    operands = [
        pltpu.with_memory_space_constraint(value, PINNED[kind]) if kind in PINNED else value
        for kind, value in zip(ins, operands, strict=True)
    ]
    out_shape = [
        PINNED[kind](value.shape, value.dtype) if kind in PINNED else value
        for kind, value in zip(outs, out_shape, strict=True)
    ]
    return pl.pallas_call(
        kernel,
        out_shape=out_shape,
        in_specs=[pl.BlockSpec(memory_space=SPACES[kind]) for kind in ins],
        out_specs=[pl.BlockSpec(memory_space=SPACES[kind]) for kind in outs],
        scratch_shapes=scratch,
        compiler_params=pltpu.CompilerParams(vmem_limit_bytes=limit * MIB),
        cost_estimate=pl.CostEstimate(flops=flops, bytes_accessed=moved, transcendentals=0),
    )(*operands)


def copies(sems, first, pairs):
    started = [pltpu.make_async_copy(src, dst, sems.at[first + k]) for k, (src, dst) in enumerate(pairs)]
    for copy in started:
        copy.start()
    return started


def finish(started):
    for copy in started:
        copy.wait()


PIECES = 3


def pieces_of(value):
    parts = []
    for _ in range(PIECES):
        parts.append(value.astype(jnp.bfloat16))
        value = value - parts[-1].astype(jnp.float32)
    return jnp.concatenate(parts, axis=0)


def whole_of(parts):
    rows = parts.shape[0] // PIECES
    parts = parts.astype(jnp.float32)
    return (parts[:rows] + parts[rows : 2 * rows]) + parts[2 * rows :]


def pack_kernel(cotangent_hbm, weight_hbm, out_hbm, cotangent_ref, weight_ref, out_ref, sems):
    started = copies(sems, 0, [(cotangent_hbm, cotangent_ref), (weight_hbm, weight_ref)])
    channels = cotangent_ref.shape[1]
    devices, _, count = out_ref.shape
    share = channels // devices
    started[1].wait()
    rows = weight_ref.shape[0]
    weights = jnp.concatenate([weight_ref[:, i] for i in range(weight_ref.shape[1])], axis=1)
    weights = jnp.concatenate([weights, jnp.zeros((ROWS - rows, count), jnp.float32)], axis=0)
    weights = weights.astype(jnp.bfloat16)
    out_ref[:, share:] = jnp.broadcast_to(weights[None], (devices, ROWS, count))
    started[0].wait()
    turned = cotangent_ref[...].astype(jnp.float32).T.astype(jnp.bfloat16)
    out_ref[:, :share] = turned.reshape(devices, share, count)
    finish(copies(sems, 2, [(out_ref, out_hbm)]))


def packed(cotangent, bilinear, devices):
    rows_out, cols_out, channels = cotangent.shape
    steps, corners = bilinear.shape[:2]
    count = rows_out * cols_out
    share = channels // devices
    if share % ROWS:
        blocks = cotangent.reshape(count, channels).T.reshape(devices, share, count)
        blocks = jnp.pad(blocks, ((0, 0), (0, -share % ROWS), (0, 0)))
        weights = bilinear.reshape(steps * corners, count).astype(jnp.bfloat16)
        weights = jnp.pad(weights, ((0, ROWS - steps * corners), (0, 0)))
        return jnp.concatenate([blocks, jnp.broadcast_to(weights[None], (devices, ROWS, count))], axis=1)
    shape = (devices, share + ROWS, count)
    return call(
        pack_kernel,
        [jax.ShapeDtypeStruct(shape, jnp.bfloat16)],
        [cotangent.reshape(count, channels), bilinear.reshape(steps * corners, rows_out, cols_out)],
        "hh",
        "h",
        scratch=[
            pltpu.VMEM((count, channels), jnp.bfloat16),
            pltpu.VMEM((steps * corners, rows_out, cols_out), jnp.float32),
            pltpu.VMEM(shape, jnp.bfloat16),
            pltpu.SemaphoreType.DMA((3,)),
        ],
        moved=2**19,
    )[0]


def lat_edges(states):
    lat, lat_at = lax.axis_size("lat"), lax.axis_index("lat")
    first, last = states[:, :, :1], states[:, :, -1:]
    if lat == 2:
        arrived = lax.ppermute(jnp.where(lat_at == 0, last, first), "lat", [(0, 1), (1, 0)])
        return jnp.where(lat_at == 0, 0, arrived), jnp.where(lat_at == 0, arrived, 0)
    return (
        lax.ppermute(last, "lat", [(i, i + 1) for i in range(lat - 1)]),
        lax.ppermute(first, "lat", [(i + 1, i) for i in range(lat - 1)]),
    )


def lon_edges(states, before, after):
    lon = lax.axis_size("lon")
    ahead = lambda value: lax.ppermute(value, "lon", [(i, (i + 1) % lon) for i in range(lon)])
    behind = lambda value: lax.ppermute(value, "lon", [(i, (i - 1) % lon) for i in range(lon)])
    row = lambda place: jnp.concatenate([part[:, place] for part in (before, states, after)], axis=2)
    return ahead(row(slice(-1, None))), behind(row(slice(0, 1)))


MARGIN = 8


def forward_kernel(
    step, states_ref, before_ref, after_ref, low_ref, high_ref, kernel_ref, gain_ref, up_ref,
    n_hbm, turned_hbm, inv_hbm, hid_hbm, slope_hbm, pad_hbm,
    n_ref, turned_ref, inv_ref, hid_ref, slope_ref, pad_ref, wide_ref, sems,
):
    rows_out, cols_out, channels = states_ref.shape[1:]
    count = rows_out * cols_out
    mixed = states_ref[step].astype(jnp.float32)
    fill_margins(wide_ref, before_ref[step], after_ref[step], low_ref[step], high_ref[step], mixed)
    pad_ref[...] = wide_ref[...].astype(jnp.bfloat16)
    leaving = copies(sems, 1, [(pad_ref, pad_hbm)])
    for col_tap in range(3):
        place = MARGIN - 1 + col_tap
        shifted_cols = wide_ref[:, place : place + cols_out]
        for row_tap in range(3):
            tap = kernel_ref[row_tap, col_tap : col_tap + 1]
            mixed = mixed + tap[None] * shifted_cols[row_tap : row_tap + rows_out]
    mixed = mixed.reshape(count, channels)
    inv_root = lax.rsqrt(jnp.mean(mixed * mixed, axis=1, keepdims=True) + EPSILON)
    narrow = mixed * inv_root * gain_ref[...]
    n_ref[...] = narrow.astype(jnp.bfloat16)
    inv_ref[...] = jnp.broadcast_to(inv_root, inv_ref.shape)
    leaving += copies(sems, 2, [(n_ref, n_hbm), (inv_ref, inv_hbm)])
    pre = jnp.dot(n_ref[...], up_ref[...], preferred_element_type=jnp.float32)
    sigmoid = jax.nn.sigmoid(pre)
    slope_ref[...] = (sigmoid * (1.0 + pre * (1.0 - sigmoid))).astype(jnp.bfloat16)
    leaving += copies(sems, 4, [(slope_ref, slope_hbm)])
    hid_ref[...] = (pre * sigmoid).astype(jnp.bfloat16)
    turned_ref[...] = narrow.T.astype(jnp.bfloat16)
    finish(leaving + copies(sems, 5, [(hid_ref, hid_hbm), (turned_ref, turned_hbm)]))


def forward_parts(step, states, around, kernel, norm_gain, w_up):
    _, rows_out, cols_out, channels = states.shape
    hid = w_up.shape[1]
    count = rows_out * cols_out
    wide = (rows_out + 2, cols_out + 2 * MARGIN, channels)
    shapes = [
        ((count, channels), jnp.bfloat16),
        ((channels, count), jnp.bfloat16),
        ((count, 128), jnp.float32),
        ((count, hid), jnp.bfloat16),
        ((count, hid), jnp.bfloat16),
        (wide, jnp.bfloat16),
    ]
    return call(
        functools.partial(forward_kernel, step),
        [jax.ShapeDtypeStruct(*shape) for shape in shapes],
        [states, *around, kernel, norm_gain, w_up],
        "vvvvvvvv",
        "hhhhhh",
        scratch=[pltpu.VMEM(*shape) for shape in shapes]
        + [pltpu.VMEM(wide, jnp.float32), pltpu.SemaphoreType.DMA((7,))],
        flops=2 * count * hid * channels,
        moved=2**22,
        limit=12,
    )


def transposed(value):
    return value.astype(jnp.float32).T.astype(jnp.bfloat16)


LANES_BOTH = (((1,), (1,)), ((), ()))


def network_kernel(moved_ref, down_ref, up_ref, gain_ref, slope_hbm, n_hbm, inv_hbm, out_hbm, grad_hbm, saved_hbm, *refs):
    slope_ref, n_ref, inv_ref, out_ref, grad_ref, sems = refs
    arriving = copies(sems, 0, [(slope_hbm, slope_ref), (n_hbm, n_ref), (inv_hbm, inv_ref)])
    leaving = copies(sems, 3, [(moved_ref, saved_hbm)])
    moved = moved_ref[...].astype(jnp.float32).T
    grad_hidden = jnp.dot(moved.astype(jnp.bfloat16), down_ref[...], preferred_element_type=jnp.float32)
    arriving[0].wait()
    grad_pre = (grad_hidden * slope_ref[...].astype(jnp.float32)).astype(jnp.bfloat16)
    grad_ref[...] = grad_pre
    leaving += copies(sems, 4, [(grad_ref, grad_hbm)])
    grad_n = lax.dot_general(grad_pre, up_ref[...], LANES_BOTH, preferred_element_type=jnp.float32)
    finish(arriving[1:])
    narrow, gain = n_ref[...].astype(jnp.float32), gain_ref[...]
    mean = jnp.mean(grad_n * narrow, axis=1, keepdims=True)
    field = moved + inv_ref[:, :1] * (grad_n * gain - narrow * (mean / gain))
    out_ref[...] = field.T.astype(jnp.bfloat16)
    finish(leaving + copies(sems, 5, [(out_ref, out_hbm)]))


def network_back(moved, w_down, w_up, norm_gain, slope, narrow, inv_root):
    channels, count = moved.shape
    hid = w_down.shape[1]
    shapes = [((channels, count), jnp.bfloat16), ((count, hid), jnp.bfloat16), ((channels, count), jnp.bfloat16)]
    return call(
        network_kernel,
        [jax.ShapeDtypeStruct(*shape) for shape in shapes],
        [moved, w_down, w_up, norm_gain, slope, narrow, inv_root],
        "vvvvhhh",
        "hhh",
        scratch=[pltpu.VMEM(value.shape, value.dtype) for value in (slope, narrow, inv_root)]
        + [pltpu.VMEM(*shape) for shape in shapes[:2]]
        + [pltpu.SemaphoreType.DMA((6,))],
        flops=4 * count * hid * channels,
        moved=4 * 2**20,
        limit=12,
    )


def stencil_sums(pad_ref, field, tile):
    rows_out, cols_out = tile
    field = field.reshape(rows_out, cols_out, -1)
    padded = pad_ref[...].astype(jnp.float32)
    result = [None] * 9
    for col_tap in range(3):
        place = MARGIN - 1 + col_tap
        shifted_cols = padded[:, place : place + cols_out]
        for row_tap in range(3):
            products = jnp.sum(shifted_cols[row_tap : row_tap + rows_out] * field, axis=0)
            result[3 * row_tap + col_tap] = jnp.sum(products, axis=0, keepdims=True)
    return result


def sums_rows(rows, term, gain):
    rows = rows + [jnp.sum(term, axis=0, keepdims=True) / gain, jnp.zeros((ROWS - 10, term.shape[1]), jnp.float32)]
    return jnp.concatenate(rows, axis=0)


def sums_kernel(steps, tile, up_ref, gain_ref, *refs):
    inputs, (out_ref, *refs) = refs[: 4 * steps], refs[4 * steps :]
    pads, fields, grads, narrows, sems = refs
    places = [(ref, place.at[k]) for k in range(steps) for ref, place in zip(inputs[4 * k : 4 * k + 4], refs[:4])]
    arriving = copies(sems, 0, places)
    rows, term = None, None
    for k in range(steps):
        finish(arriving[4 * k : 4 * k + 4])
        grad_n = lax.dot_general(grads[k], up_ref[...], LANES_BOTH, preferred_element_type=jnp.float32)
        product = grad_n * narrows[k].astype(jnp.float32)
        term = product if term is None else term + product
        more = stencil_sums(pads.at[k], fields[k].astype(jnp.float32).T, tile)
        rows = more if rows is None else [a + b for a, b in zip(rows, more)]
    out_ref[...] = sums_rows(rows, term, gain_ref[...])


def channel_sums(tile, w_up, norm_gain, pads, fields, grads, narrows):
    steps = len(fields)
    inputs = [value for group in zip(pads, fields, grads, narrows) for value in group]
    return call(
        functools.partial(sums_kernel, steps, tile),
        [jax.ShapeDtypeStruct((ROWS, fields[0].shape[0]), jnp.float32)],
        [w_up, norm_gain, *inputs],
        "vv" + "h" * 4 * steps,
        "v",
        scratch=[pltpu.VMEM((steps, *value.shape), value.dtype) for value in inputs[:4]]
        + [pltpu.SemaphoreType.DMA((4 * steps,))],
        moved=2**21,
        limit=12,
    )[0]


QUADRANTS = 4


def lon_bit(at):
    return lax.axis_index("lon") >> at & 1


def last_kernel(steps, tile, lon_groups, moved_ref, down_ref, up_ref, gain_ref, sums_ref, *refs):
    slope_hbm, n_hbm, inv_hbm, pad_hbm, *refs = refs
    inputs, refs = refs[: 4 * steps - 2], refs[4 * steps - 2 :]
    field_ref, total_ref, send_ref, keep_ref, slope_ref, n_ref, inv_ref, pad_ref, left_ref, right_ref, sems = refs
    arriving = copies(
        sems, 0, [(slope_hbm, slope_ref), (n_hbm, n_ref), (inv_hbm, inv_ref), (pad_hbm, pad_ref)]
    )
    count = slope_ref.shape[0]
    part = lambda s: pl.ds(s * count, count)
    narrows, grads = inputs[:steps], inputs[steps : 2 * steps - 1]
    moveds, hiddens = inputs[2 * steps - 1 : 3 * steps - 2], inputs[3 * steps - 2 :]
    pairs = [(ref, left_ref.at[0, :, part(s)]) for s, ref in enumerate(narrows)]
    pairs += [(ref, right_ref.at[0, part(s)]) for s, ref in enumerate(grads)]
    pairs += [(ref, left_ref.at[1, :, part(s)]) for s, ref in enumerate(moveds)]
    pairs += [(ref, right_ref.at[1, part(s)]) for s, ref in enumerate(hiddens)]
    later = copies(sems, 4, pairs)
    left_ref[1, :, (steps - 1) * count :] = moved_ref[...]
    moved = moved_ref[...].astype(jnp.float32).T
    channels = moved.shape[1]
    grad_hidden = jnp.dot(moved.astype(jnp.bfloat16), down_ref[...], preferred_element_type=jnp.float32)
    arriving[0].wait()
    grad_pre = (grad_hidden * slope_ref[...].astype(jnp.float32)).astype(jnp.bfloat16)
    right_ref[0, (steps - 1) * count :] = grad_pre
    grad_n = lax.dot_general(grad_pre, up_ref[...], LANES_BOTH, preferred_element_type=jnp.float32)
    finish(arriving[1:])
    narrow, gain = n_ref[...].astype(jnp.float32), gain_ref[...]
    term = grad_n * narrow
    mean = jnp.mean(term, axis=1, keepdims=True)
    field = moved + inv_ref[:, :1] * (grad_n * gain - narrow * (mean / gain))
    narrow_field = field.astype(jnp.bfloat16)
    field_ref[...] = narrow_field
    total = sums_ref[...] + sums_rows(stencil_sums(pad_ref, narrow_field.astype(jnp.float32), tile), term, gain)
    total_ref[...] = total
    finish(later)
    if send_ref.ndim == 3:
        for k in range(2):
            send_ref[k] = jnp.dot(left_ref[k], right_ref[k], preferred_element_type=jnp.float32).astype(jnp.bfloat16)
        keep_ref[...] = jnp.zeros_like(keep_ref)
        return
    quadrant_rows = channels // 4
    send_ref[2 * QUADRANTS * quadrant_rows :] = pieces_of(total)
    chunk = channels // (4 * lon_groups)
    width = right_ref.shape[2] // 2
    for k in range(2):
        rows = []
        for core in (1 - lon_bit(0), lon_bit(0)):
            for x in range(2):
                for z in range(lon_groups):
                    start = pl.multiple_of((4 * z + 2 * x + core) * chunk, chunk)
                    rows.append(left_ref[k, pl.ds(start, chunk)])
        rows = jnp.concatenate(rows, axis=0)
        value = jnp.dot(rows, right_ref[k], preferred_element_type=jnp.float32).astype(jnp.bfloat16)
        size = lon_groups * chunk
        for q in range(QUADRANTS):
            x, lat = q // 2, q % 2
            columns = slice(lat * width, (lat + 1) * width)
            start = (k * QUADRANTS + q) * quadrant_rows
            send_ref[start : start + quadrant_rows] = value[x * size : (x + 1) * size, columns]
            keep_ref[k, q] = value[(2 + x) * size : (3 + x) * size, columns]


def last_step(tile, moved, w_down, w_up, norm_gain, sums, forward, grads, moveds):
    steps = len(forward)
    channels, count = moved.shape
    hid = w_down.shape[1]
    narrow, _, inv_root, _, slope, pad = forward[-1]
    lon_groups = lax.axis_size("lon") // 4
    by_quadrant = lax.axis_size("lat") == 2 and lon_groups == 4
    send = (2, channels, hid)
    keep = (8, 128)
    if by_quadrant:
        send = (2 * channels + PIECES * ROWS, hid // 2)
        keep = (2, QUADRANTS, channels // 4, hid // 2)
    sds = jax.ShapeDtypeStruct
    inputs = [parts[1] for parts in forward] + grads + moveds + [parts[3] for parts in forward]
    return call(
        functools.partial(last_kernel, steps, tile, lon_groups),
        [
            sds((count, channels), jnp.bfloat16),
            sds((ROWS, channels), jnp.float32),
            sds(send, jnp.bfloat16),
            sds(keep, jnp.bfloat16),
        ],
        [moved, w_down, w_up, norm_gain, sums, slope, narrow, inv_root, pad, *inputs],
        "vvvvv" + "h" * (4 + len(inputs)),
        "vppp",
        scratch=[pltpu.VMEM(value.shape, value.dtype) for value in (slope, narrow, inv_root, pad)]
        + [pltpu.VMEM((2, channels, steps * count), jnp.bfloat16), pltpu.VMEM((2, steps * count, hid), jnp.bfloat16)]
        + [pltpu.SemaphoreType.DMA((len(inputs) + 4,))],
        flops=2**31,
        moved=6 * 2**20,
        limit=20,
    )


def fill_margins(wide_ref, before, after, low, high, middle):
    rows_out, cols_out, _ = middle.shape
    around = slice(MARGIN - 1, MARGIN + cols_out + 1)
    wide_ref[:1, around] = low.astype(jnp.float32)
    wide_ref[1 + rows_out :, around] = high.astype(jnp.float32)
    wide_ref[1 : 1 + rows_out, MARGIN - 1 : MARGIN] = before.astype(jnp.float32)
    wide_ref[1 : 1 + rows_out, MARGIN + cols_out : MARGIN + cols_out + 1] = after.astype(jnp.float32)
    wide_ref[1 : 1 + rows_out, MARGIN : MARGIN + cols_out] = middle


def final_kernel(field_ref, before_ref, after_ref, low_ref, high_ref, kernel_ref, out_ref, wide_ref):
    rows_out, cols_out, _ = field_ref.shape
    result = field_ref[...].astype(jnp.float32)
    fill_margins(wide_ref, before_ref[0], after_ref[0], low_ref[0], high_ref[0], result)
    for col_tap in range(3):
        place = MARGIN + 1 - col_tap
        shifted_cols = wide_ref[:, place : place + cols_out]
        for row_tap in range(3):
            tap = kernel_ref[row_tap, col_tap : col_tap + 1]
            result = result + tap[None] * shifted_cols[2 - row_tap : 2 - row_tap + rows_out]
    out_ref[...] = result.astype(jnp.bfloat16)


def final_parts(field, around, kernel):
    rows_out, cols_out, channels = field.shape
    return call(
        final_kernel,
        [jax.ShapeDtypeStruct(field.shape, jnp.bfloat16)],
        [field, *around, kernel],
        "v" * 6,
        "v",
        scratch=[pltpu.VMEM((rows_out + 2, cols_out + 2 * MARGIN, channels), jnp.float32)],
        moved=2**19,
    )[0]


def spatial_kernel(mode, step, near_lon, near_lat, *refs):
    refs = list(refs)
    take = lambda: refs.pop(0)
    with_stencil = mode != "first"
    move_hbm = take()
    in_ref = take()
    kern_ref = take() if with_stencil else None
    weight_hbm = take() if mode == "mid" else None
    out_hbm = take()
    saved_hbm = take() if mode == "first" else None
    out_ref, sems = take(), take()
    spread_ref, weight_ref, move_ref = take(), take(), take()
    moving = copies(sems, 3, [(move_hbm, move_ref)])
    tiles_lon, tiles_lat, _, lanes = in_ref.shape
    rows = out_ref.shape[2]
    started = []
    if mode == "mid":
        arriving = copies(sems, 0, [(weight_hbm, weight_ref)])
    if mode == "first":
        weight_ref[...] = in_ref[:, :, rows:]
        started += copies(sems, 0, [(weight_ref, saved_hbm)])
    lane = lax.broadcasted_iota(jnp.int32, (rows, lanes), 1)
    col = lax.rem(lane, near_lat)
    lat_last, lat_first = col == near_lat - 1, col == 0
    lon_last, lon_first = lane >= lanes - near_lat, lane < near_lat
    tiles = [(a, b) for a in range(tiles_lon) for b in range(tiles_lat)]

    def turn(value, steps):
        return pltpu.roll(value, steps % lanes if isinstance(steps, int) else steps, 1)

    def lat_after(grid):
        turned = {key: turn(value, -1) for key, value in grid.items()}
        wrapped = {key: turn(grid[key], near_lat - 1) for key in tiles if key[1] > 0}
        return {(a, b): jnp.where(lat_last, wrapped.get((a, b + 1), 0.0), turned[a, b]) for a, b in tiles}

    def lat_before(grid):
        turned = {key: turn(value, 1) for key, value in grid.items()}
        wrapped = {key: turn(grid[key], 1 - near_lat) for key in tiles if key[1] < tiles_lat - 1}
        return {(a, b): jnp.where(lat_first, wrapped.get((a, b - 1), 0.0), turned[a, b]) for a, b in tiles}

    def lon_after(grid):
        return {
            (a, b): turn(jnp.where(lon_first, grid[(a + 1) % tiles_lon, b], grid[a, b]), -near_lat) for a, b in tiles
        }

    def lon_before(grid):
        return {(a, b): turn(jnp.where(lon_last, grid[(a - 1) % tiles_lon, b], grid[a, b]), near_lat) for a, b in tiles}

    grid = {(a, b): in_ref[a, b, :rows].astype(jnp.float32) for a, b in tiles}
    if with_stencil:
        taps = [
            [jnp.broadcast_to(kern_ref[:, 3 * a + b : 3 * a + b + 1], (rows, lanes)) for b in range(3)] for a in range(3)
        ]
        by_col = [lat_after(grid), grid, lat_before(grid)]
        mix = [
            {key: sum(taps[row][c] * by_col[c][key] for c in range(1, 3)) + taps[row][0] * by_col[0][key] for key in tiles}
            for row in range(3)
        ]
        high, low = lon_after(mix[0]), lon_before(mix[2])
        grid = {key: grid[key] + mix[1][key] + (high[key] + low[key]) for key in tiles}
    if mode == "mid":
        grid = {key: value.astype(jnp.bfloat16).astype(jnp.float32) for key, value in grid.items()}
        finish(arriving)
    weights = {}
    for a, b in tiles:
        four = weight_ref[a, b].astype(jnp.float32)[4 * step : 4 * step + 4]
        weights[a, b] = [jnp.broadcast_to(four[k : k + 1], (rows, lanes)) for k in range(4)]
    weighted = [{key: weights[key][k] * grid[key] for key in tiles} for k in range(4)]
    own, lon = lat_after(weighted[2]), lat_after(weighted[3])
    lon = lon_after({key: weighted[1][key] + lon[key] for key in tiles})
    for a, b in tiles:
        value = (weighted[0][a, b] + own[a, b] + lon[a, b]).astype(jnp.bfloat16).astype(jnp.float32)
        for place in range(a, tiles_lon + LON_REACH, tiles_lon):
            spread_ref[place, b] = value
    spread_ref[:, tiles_lat:] = jnp.zeros((tiles_lon + LON_REACH, LAT_REACH, rows, lanes), jnp.float32)

    finish(moving)
    lon_move, lat_move = move_ref[step, 0], move_ref[step, 1]
    far_lon, off_lon = lon_move // near_lon, lax.rem(lon_move, near_lon)
    far_lat, off_lat = lat_move // near_lat, lax.rem(lat_move, near_lat)
    shift = off_lon * near_lat + off_lat
    turn_here = lax.rem(2 * lanes - shift, lanes)
    turn_next = lax.rem(2 * lanes - shift + near_lat, lanes)
    same_lon = lane >= off_lon * near_lat
    same_lat = col + off_lat < near_lat
    half = tiles_lon // 2
    for a in range(tiles_lon):
        met = [
            jnp.where(same_lon, spread_ref[far_lon + a, far_lat + b], spread_ref[far_lon + a + 1, far_lat + b])
            for b in range(tiles_lat + 1)
        ]
        for b in range(tiles_lat):
            value = jnp.where(same_lat, turn(met[b], turn_here), turn(met[b + 1], turn_next))
            out_ref[a, b] = value.astype(jnp.bfloat16)
        if (a + 1) % half == 0:
            part = pl.ds(a + 1 - half, half)
            started += copies(sems, 1 + a // half, [(out_ref.at[part], out_hbm.at[part])])
    finish(started)


def spatial(mode, step, tile, rows, field, kern, weights, moves):
    tiles_lon, tiles_lat, _, lanes = field.shape
    with_stencil = mode != "first"
    operands = [moves, field]
    operands += [kern] if with_stencil else []
    operands += [weights] if mode == "mid" else []
    out_shape = (tiles_lon, tiles_lat, rows, lanes)
    weight_shape = (tiles_lon, tiles_lat, ROWS, lanes)
    sds = jax.ShapeDtypeStruct
    out = [sds(out_shape, jnp.bfloat16)] + ([sds(weight_shape, jnp.bfloat16)] if mode == "first" else [])
    scratch = [pltpu.VMEM(out_shape, jnp.bfloat16), pltpu.SemaphoreType.DMA((4,))]
    spread_shape = (tiles_lon + LON_REACH, tiles_lat + LAT_REACH, rows, lanes)
    scratch += [pltpu.VMEM(spread_shape, jnp.float32), pltpu.VMEM(weight_shape, jnp.bfloat16)]
    scratch += [pltpu.SMEM(moves.shape, jnp.int32)]
    return call(
        functools.partial(spatial_kernel, mode, step, *tile),
        out,
        operands,
        "hv" + "v" * with_stencil + "h" * (mode == "mid"),
        "h" * len(out),
        scratch=scratch,
        flops=2**22,
        moved=2**20,
        limit=max(8, 14 * tiles_lon * tiles_lat * rows * lanes * 4 // MIB),
    )


def halved(value, axis, bit, dim):
    count = lax.axis_size(axis)
    mine = lax.axis_index(axis) >> bit & 1
    kept = lax.dynamic_index_in_dim(value, mine, dim, keepdims=False)
    sent = lax.dynamic_index_in_dim(value, 1 - mine, dim, keepdims=False).astype(jnp.bfloat16)
    arrived = lax.ppermute(sent, axis, [(i, i ^ (1 << bit)) for i in range(count)])
    return kept + arrived.astype(jnp.float32)


def scattered(value, lat_first):
    channels, hid = value.shape
    lon_bits = lax.axis_size("lon").bit_length() - 1
    lat_bits = lax.axis_size("lat").bit_length() - 1
    rows = channels >> lon_bits
    value = value.reshape(*([2] * lon_bits), rows, *([2] * lat_bits), hid >> lat_bits)

    def over_lon(value, bit, left):
        return halved(value, "lon", bit, left.index(bit)), [k for k in left if k != bit]

    left_lon = list(range(lon_bits))[::-1]
    left_lat = list(range(lat_bits))[::-1]
    order = [("lon", 0), ("lon", 1)] + [("lat", k) for k in range(lat_bits)]
    if lat_first:
        order = [("lon", 0)] + [("lat", k) for k in range(lat_bits)] + [("lon", 1)]
    order += [("lon", k) for k in range(2, lon_bits)]
    for axis, bit in order:
        if axis == "lon":
            value, left_lon = over_lon(value, bit, left_lon)
        else:
            value = halved(value, "lat", bit, len(left_lon) + 1 + left_lat.index(bit))
            left_lat.remove(bit)
    return value


def add_parts(pairs, kept, arrived):
    for q, out_ref, place in pairs:
        value = kept(q).astype(jnp.float32) + arrived(q).astype(jnp.float32)
        out_ref[place] = value.astype(out_ref.dtype)


def quadrant_kernel(kept_ref, total_ref, arrived_ref, send_ref, keep_ref, chip_ref):
    core, x, lat = lon_bit(0), lon_bit(1), lax.axis_index("lat")
    rows = kept_ref.shape[2]
    for k in range(2):
        for j in range(2):
            kept = (1 - core) * (2 * x + j) + core * (2 * j + lat)
            sent = (1 - core) * (2 * (1 - x) + j) + core * (2 * j + 1 - lat)
            pairs = [(sent, send_ref, pl.ds((2 * k + j) * rows, rows)), (kept, keep_ref, (k, j))]
            arrived = lambda q: arrived_ref[pl.ds(pl.multiple_of((k * QUADRANTS + q) * rows, rows), rows)]
            add_parts(pairs, lambda q: kept_ref[k, q], arrived)
    chip = total_ref[...] + whole_of(arrived_ref[2 * QUADRANTS * rows :])
    chip_ref[...] = chip
    send_ref[4 * rows :] = pieces_of(chip)


def half_kernel(kept_ref, chip_ref, arrived_ref, send_ref, keep_ref, beside_ref):
    core, x, lat = lon_bit(0), lon_bit(1), lax.axis_index("lat")
    mine = (1 - core) * lat + core * x
    rows = kept_ref.shape[2]
    for k in range(2):
        pairs = [(1 - mine, send_ref, pl.ds(k * rows, rows)), (mine, keep_ref, k)]
        arrived = lambda q: arrived_ref[pl.ds(pl.multiple_of((2 * k + q) * rows, rows), rows)]
        add_parts(pairs, lambda q: kept_ref[k, q], arrived)
    sums = PIECES * ROWS
    beside = arrived_ref[4 * rows :]
    beside_ref[...] = whole_of(beside)
    send_ref[2 * rows : 2 * rows + sums] = pieces_of(chip_ref[...])
    send_ref[2 * rows + sums :] = beside


def rows_kernel(groups, bit_at, *refs):
    kept_ref, *total_refs, arrived_ref, send_ref, keep_ref, total_ref = refs
    bit = lon_bit(bit_at)
    rows = kept_ref.shape[1]
    chunk = rows // (2 * groups)
    for k in range(2):
        for p in range(groups):
            goal = pl.ds(p * chunk, chunk)
            places = [pl.multiple_of((2 * p + which) * chunk, chunk) for which in (1 - bit, bit)]
            pairs = [
                (places[0], send_ref, pl.ds(k * groups * chunk + p * chunk, chunk)),
                (places[1], keep_ref, (k, goal)),
            ]
            arrived = lambda q: arrived_ref[pl.ds(pl.multiple_of(k * rows + q, chunk), chunk)]
            add_parts(pairs, lambda q: kept_ref[k, pl.ds(q, chunk)], arrived)
    total = add_sums(total_refs, arrived_ref, 2 * rows)
    total_ref[...] = total
    send_ref[2 * groups * chunk :] = pieces_of(total)


def add_sums(total_refs, arrived_ref, start):
    size = PIECES * ROWS
    arrived = whole_of(arrived_ref[start : start + size])
    if len(total_refs) == 1:
        return total_refs[0][...] + arrived
    chip, beside = (ref[...] for ref in total_refs)
    return (chip + whole_of(arrived_ref[start + size :])) + (beside + arrived)


def last_sum_kernel(kept_ref, total_ref, arrived_ref, up_ref, down_ref, taps_ref, gain_ref):
    rows = kept_ref.shape[1]
    up_ref[...] = kept_ref[0] + arrived_ref[:rows].astype(jnp.float32)
    down_ref[...] = kept_ref[1] + arrived_ref[rows : 2 * rows].astype(jnp.float32)
    total = add_sums([total_ref], arrived_ref, 2 * rows)
    for k in range(9):
        taps_ref[k // 3, k % 3 : k % 3 + 1] = total[k : k + 1]
    gain_ref[...] = total[9:10]


def all_sums(send, keep, total):
    lon, lat = lax.axis_size("lon"), lax.axis_size("lat")
    channels = total.shape[1]
    if send.ndim == 3:
        parts = [scattered(send[k].astype(jnp.float32), k == 1) for k in range(2)]
        total = lax.psum(total, AXES)
        return (*parts, total[:9].reshape(3, 3, channels), total[9])
    places = [(i, j) for i in range(lon) for j in range(lat)]
    flat = lambda i, j: i * lat + j

    def traded(value, partner):
        return lax.ppermute(value, AXES, [(flat(i, j), flat(*partner(i, j))) for i, j in places])

    sds = jax.ShapeDtypeStruct

    def stage(kernel, shape, kept, totals, arrived, sums):
        sent = 2 * shape[-2] * (shape[1] if len(shape) == 4 else 1) + PIECES * ROWS * sums
        out = [sds((sent, shape[-1]), jnp.bfloat16), sds(shape, jnp.float32), sds(total.shape, jnp.float32)]
        operands = [kept, *totals, arrived]
        return call(kernel, out, operands, "v" * len(operands), "ppp", moved=2**20, limit=12)

    rows, width = keep.shape[2:]
    arrived = traded(send, lambda i, j: (i ^ 1, j))
    send, keep, chip = stage(quadrant_kernel, (2, 2, rows, width), keep, [total], arrived, 1)
    arrived = traded(send, lambda i, j: (i, j ^ 1) if i & 1 else (i ^ 2, j))
    send, keep, beside = stage(half_kernel, (2, rows, width), keep, [chip], arrived, 2)
    arrived = traded(send, lambda i, j: (i ^ 2, j) if i & 1 else (i, j ^ 1))
    kernel = functools.partial(rows_kernel, 2, 2)
    send, keep, total = stage(kernel, (2, rows // 2, width), keep, [chip, beside], arrived, 1)
    arrived = traded(send, lambda i, j: (i ^ 4, j))
    kernel = functools.partial(rows_kernel, 1, 3)
    send, keep, total = stage(kernel, (2, rows // 4, width), keep, [total], arrived, 1)
    arrived = traded(send, lambda i, j: (i ^ 8, j))
    part = sds((rows // 4, width), jnp.float32)
    out = [part, part, sds((3, 3, channels), jnp.float32), sds((1, channels), jnp.float32)]
    up, down, taps, gain = call(last_sum_kernel, out, [keep, total, arrived], "vvv", "vvvv", moved=2**18)
    return up, down, taps, gain.reshape(channels)


def local(cotangent, states, w_up, w_down, norm_gain, kernel, bilinear, lon_move, lat_move):
    steps, rows_out, cols_out, channels = states.shape
    tiles_lon, tiles_lat = lax.axis_size("lon"), lax.axis_size("lat")
    devices = tiles_lon * tiles_lat
    count = rows_out * cols_out
    tile = (rows_out, cols_out)
    share = channels // devices
    padded_share = -(-share // ROWS) * ROWS
    whole_share = share == padded_share
    group_size = channels // lon_move.shape[1]
    me = lax.axis_index("lon") * tiles_lat + lax.axis_index("lat")

    def as_blocks(value):
        value = value.reshape(devices, share, count)
        return value if whole_share else jnp.pad(value, ((0, 0), (0, padded_share - share), (0, 0)))

    def as_rows(blocks):
        return blocks[:, :share].reshape(channels, count)

    def as_grid(blocks):
        return blocks.reshape(tiles_lon, tiles_lat, *blocks.shape[1:])

    blocks = packed(cotangent, bilinear, devices)
    blocks, states_later = lax.optimization_barrier((blocks, states))
    arrived = as_grid(exchanged(blocks))
    group = me * share // group_size
    moves = jnp.stack([lon_move[:, group], lat_move[:, group]], axis=1)
    grid_now, weights = spatial("first", steps - 1, tile, padded_share, arrived, None, None, moves)

    taps = lax.dynamic_slice_in_dim(kernel.reshape(9, channels), me * share, share, 1).T
    taps = jnp.pad(taps, ((0, padded_share - share), (0, count - 9)))

    before, after = lat_edges(states_later)
    grid_now, before, after = lax.optimization_barrier((grid_now, before, after))
    around = (before, after, *lon_edges(states, before, after))
    order = list(reversed(range(steps)))
    gain = norm_gain.reshape(1, channels)
    forward = {s: forward_parts(s, states, around, kernel, gain, w_up) for s in order}

    moved, grads, fields = {}, {}, {}
    for s in order[:-1]:
        here = as_rows(exchanged(grid_now.reshape(devices, padded_share, count)))
        if s != order[0]:
            here, forward = lax.optimization_barrier((here, forward))
        narrow, _, inv_root, _, slope, _ = forward[s]
        fields[s], grads[s], moved[s] = network_back(here, w_down, w_up, gain, slope, narrow, inv_root)
        arrived = as_grid(exchanged(as_blocks(fields[s])))
        (grid_now,) = spatial("mid", s - 1, tile, padded_share, arrived, taps, weights, moves)

    here = as_rows(exchanged(grid_now.reshape(devices, padded_share, count)))
    earlier = lambda values: [values[s] for s in order[:-1]]
    pads, narrows = ([forward[s][k] for s in order[:-1]] for k in (5, 0))
    sums = channel_sums(tile, w_up, gain, pads, earlier(fields), earlier(grads), narrows)
    here, sums = lax.optimization_barrier((here, sums))
    parts = ([forward[s] for s in order], earlier(grads), earlier(moved))
    field, total, send, keep = last_step(tile, here, w_down, w_up, gain, sums, *parts)
    field = field.reshape(cotangent.shape)
    before, after = lat_edges(field[None])
    grad_state = final_parts(field, (before, after, *lon_edges(field[None], before, after)), kernel)
    return (grad_state, *all_sums(send, keep, total))


def solution(mesh):
    placed = (
        P("lon", "lat", None),
        P(None, "lon", "lat", None),
        P(),
        P(),
        P(),
        P(),
        P(None, None, "lon", "lat"),
        P(),
        P(),
    )
    return jax.shard_map(
        local,
        mesh=mesh,
        in_specs=placed,
        out_specs=(P("lon", "lat", None), P("lon", "lat"), P("lon", "lat"), P(), P()),
        check_vma=False,
    )
```

time: 140 us -> 129 us (0.921)
  waiting for transfers between devices: 43.8 us -> 58.7 us
  Pallas kernels: 41.2 us -> 26.8 us
  starting transfers between devices: 39.7 us -> 27.9 us
  other arithmetic: 0.35 us -> 2.01 us
    ppermute x7 -> x5, waiting for transfers between devices: 9.25 us -> 26.2 us  [traded(): lax.ppermute(value, AXES, [(flat(i, j), flat(*partner(i, j))) for i, j in...]
    pallas_call x20 -> x17, Pallas kernels: 41.2 us -> 26.8 us  [call(): pl.pallas_call(kernel, out_shape=out_shape, in_specs=[pl.BlockSpec(memory...]
    ppermute x7 -> x5, starting transfers between devices: 11.1 us -> 0.84 us  [traded(): lax.ppermute(value, AXES, [(flat(i, j), flat(*partner(i, j))) for i, j in...]
    all_to_all x7 -> x5, waiting for transfers between devices: 33.9 us -> 23.8 us  [exchanged(): return lax.all_to_all(blocks, AXES, split_axis=0, concat_axis=0, tiled=True)]
    ppermute x1 -> x2, waiting for transfers between devices: 0.01 us -> 4.06 us  [lon_edges(): lax.ppermute(value, 'lon', [(i, (i + 1) % lon) for i in range(lon)])]
    all_to_all x7 -> x5, starting transfers between devices: 23.1 us -> 19.5 us  [exchanged(): return lax.all_to_all(blocks, AXES, split_axis=0, concat_axis=0, tiled=True)]
    ppermute x1 -> x2, waiting for transfers between devices: 0.01 us -> 2.34 us  [lon_edges(): lax.ppermute(value, 'lon', [(i, (i - 1) % lon) for i in range(lon)])]
    ppermute x1 -> x2, starting transfers between devices: 1 us -> 2.91 us  [lat_edges(): lax.ppermute(jnp.where(lat_at == 0, last, first), 'lat', [(0, 1), (1, 0)])]
  transfers between devices with their start and end apart: 17 -> 16, of which waited for: 11 -> 13; matrix products, arithmetic and copies ran while one was open for 0% -> 2% of each run, Pallas kernels for 15% -> 7%
where the time goes in v6:
time: 129 us; the launch traced here: 128 us
  waiting for transfers between devices  58.7 us (46%)
  starting transfers between devices  27.9 us (22%)
  Pallas kernels  26.8 us (21%)
  blocking collectives  11.2 us (9%)
  other arithmetic  2.01 us (2%)
    pallas_call x17, Pallas kernels, call(): pl.pallas_call(kernel, out_shape=out_shape, in_specs=[pl.BlockSpec(memory...  26.8 us
    ppermute x5, waiting for transfers between devices, traded(): lax.ppermute(value, AXES, [(flat(i, j), flat(*partner(i, j))) for i, j in...  26.2 us
    all_to_all x5, waiting for transfers between devices, exchanged(): return lax.all_to_all(blocks, AXES, split_axis=0, concat_axis=0, tiled=True)  23.8 us
    all_to_all x5, starting transfers between devices, exchanged(): return lax.all_to_all(blocks, AXES, split_axis=0, concat_axis=0, tiled=True)  19.5 us
    all_to_all x1, blocking collectives, exchanged(): return lax.all_to_all(blocks, AXES, split_axis=0, concat_axis=0, tiled=True)  11.2 us
    ppermute x2, starting transfers between devices, lon_edges(): lax.ppermute(value, 'lon', [(i, (i - 1) % lon) for i in range(lon)])  4.44 us
    ppermute x2, waiting for transfers between devices, lon_edges(): lax.ppermute(value, 'lon', [(i, (i + 1) % lon) for i in range(lon)])  4.06 us
    ppermute x2, starting transfers between devices, lat_edges(): lax.ppermute(jnp.where(lat_at == 0, last, first), 'lat', [(0, 1), (1, 0)])  2.91 us
  transfers between devices with their start and end apart: 16, of which 13 were waited for; matrix products, arithmetic and copies ran while one was open for 2% of the time, Pallas kernels for 7%

profile of v6, /device:TPU:0, one launch (start us, length us, event | category | flops | bytes accessed | tf_op | source)
XLA Modules:
  0.0 127.9 jit_solution(14231900363848468830)
XLA Ops:
  0.7 1.9 %shard_map.128 = bf16[32,32,128]{2,1,0:T(8,128)(2,1)} custom-call(bf16[128,512]{1,0:T(8,128)(2,1)} %bitcast.38, f32[12,8,16]{2,1,0:T(8,128)} %bitcast.40), custom_call_target="tpu_custom_call" | custom-call | bytes 524288 | tf_op jit(solution)/shard_map/pallas_call | solution.py:35
  2.6 7.3 %all-to-all-start = ((bf16[32,32,128]{2,1,0:T(8,128)(2,1)}), bf16[32,32,128]{2,1,0:T(8,128)(2,1)S(1)}, u32[]{:S(2)}, u32[]{:S(2)}) async-start(bf16[32,32,128]{2,1,0:T(8,128)(2,1)} %shard_map.128), calls=%async_computation | async-start | bytes 524288 | tf_op jit(solution)/shard_map/all_to_all | solution.py:19
  11.0 1.8 %collective-permute-start = (bf16[3,8,1,512]{3,2,1,0:T(2,128)(2,1)S(1)}, bf16[3,8,1,512]{3,2,1,0:T(2,128)(2,1)S(1)}, u32[]{:S(2)}, u32[]{:S(2)}) collective-permute-start(bf16[3,8,1,512]{3,2,1,0:T(2,128)(2,1)S(1)} %broadcast_select_fusion.2), channel_id=1, source_target_pairs={{0,1},{1,0},{2,3},{3,2},{4,5},{5,4},{6,7},{7,6},{8,9},{9,8},{10,11... | collective-permute-start | bytes 73736 | tf_op jit(solution)/shard_map/ppermute | solution.py:124
  13.7 2.4 %collective-permute-done = bf16[3,8,1,512]{3,2,1,0:T(2,128)(2,1)S(1)} collective-permute-done((bf16[3,8,1,512]{3,2,1,0:T(2,128)(2,1)S(1)}, bf16[3,8,1,512]{3,2,1,0:T(2,128)(2,1)S(1)}, u32[]{:S(2)}, u32[]{:S(2)}) %collective-permute-start) | collective-permute-done | bytes 24608 | tf_op jit(solution)/shard_map/ppermute | solution.py:124
  16.1 4.5 %all-to-all-done = bf16[32,32,128]{2,1,0:T(8,128)(2,1)S(1)} async-done(((bf16[32,32,128]{2,1,0:T(8,128)(2,1)}), bf16[32,32,128]{2,1,0:T(8,128)(2,1)S(1)}, u32[]{:S(2)}, u32[]{:S(2)}) %all-to-all-start) | async-done | bytes 262176 | tf_op jit(solution)/shard_map/all_to_all | solution.py:19
  20.6 1.5 %shard_map.129 = (bf16[16,2,16,128]{3,2,1,0:T(8,128)(2,1)}, bf16[16,2,16,128]{3,2,1,0:T(8,128)(2,1)}) custom-call(s32[3,2]{1,0:T(4,128)} %pad_add_fusion.refs_0_, bf16[16,2,32,128]{3,2,1,0:T(8,128)(2,1)S(1)} %bitcast.18), custom_call_target="tpu_custom_call" | custom-call | flops 4194304 | bytes 1048576 | tf_op jit(solution)/shard_map/pallas_call | solution.py:35
  22.2 2.7 %all-to-all-start.1 = ((bf16[32,16,128]{2,1,0:T(8,128)(2,1)}), bf16[32,16,128]{2,1,0:T(8,128)(2,1)S(1)}, u32[]{:S(2)}, u32[]{:S(2)}) async-start(bf16[32,16,128]{2,1,0:T(8,128)(2,1)} %bitcast.39), calls=%async_computation.1 | async-start | bytes 262144 | tf_op jit(solution)/shard_map/all_to_all | solution.py:19
  25.2 4.4 %collective-permute-start.2 = (bf16[3,1,18,512]{3,2,1,0:T(8,128)(2,1)S(1)}, bf16[3,1,18,512]{3,2,1,0:T(8,128)(2,1)S(1)}, u32[]{:S(2)}, u32[]{:S(2)}) collective-permute-start(bf16[3,1,18,512]{3,2,1,0:T(8,128)(2,1)S(1)} %pad_maximum_fusion.1), channel_id=1, source_target_pairs={{0,30},{2,0},{4,2},{6,4},{8,6},{10,8},{12,10},{14,12},{16,14},{18,... | collective-permute-start | bytes 165896 | tf_op jit(solution)/shard_map/ppermute | solution.py:135
  29.6 3.9 %collective-permute-done.1.low_ref = bf16[3,1,18,512]{3,2,1,0:T(8,128)(2,1)S(1)} collective-permute-done((bf16[3,1,18,512]{3,2,1,0:T(8,128)(2,1)S(1)}, bf16[3,1,18,512]{3,2,1,0:T(8,128)(2,1)S(1)}, u32[]{:S(2)}, u32[]{:S(2)}) %collective-permute-start.1) | collective-permute-done | bytes 55328 | tf_op jit(solution)/shard_map/ppermute | solution.py:134
  33.4 1.7 %shard_map.130 = (bf16[128,512]{1,0:T(8,128)(2,1)}, bf16[512,128]{1,0:T(8,128)(2,1)}, f32[128,128]{1,0:T(8,128)}, bf16[128,1024]{1,0:T(8,128)(2,1)}, bf16[128,10...) custom-call(bf16[3,8,16,512]{3,2,1,0:T(8,128)(2,1)S(1)} %copy-done.1, ...), custom_call_target="tpu_custom_call" | custom-call | flops 134217728 | bytes 4194304 | tf_op jit(solution)/shard_map/pallas_call | solution.py:35
  35.2 2.6 %shard_map.131 = (bf16[512,128]{1,0:T(8,128)(2,1)}, bf16[128,1024]{1,0:T(8,128)(2,1)}, bf16[512,128]{1,0:T(8,128)(2,1)}) custom-call(bf16[512,128]{1,0:T(8,128)(2,1)S(1)} %bitcast.19, bf16[512,1024]{1,0:T(8,128)(2,1)S(1)} %copy-done.2, bf16[512,1024]{1,0:T(8,128)(2,1)S(1)} %copy-done, f32[1,512]{1,0:T(1,128)S(1)} %bitcast.28, ...), custom_call_target="tpu_custom_call" | custom-call | flops 268435456 | bytes 4194304 | tf_op jit(solution)/shard_map/pallas_call | solution.py:35
  37.9 4.1 %all-to-all-start.2 = ((bf16[32,16,128]{2,1,0:T(8,128)(2,1)}), bf16[32,16,128]{2,1,0:T(8,128)(2,1)S(1)}, u32[]{:S(2)}, u32[]{:S(2)}) async-start(bf16[32,16,128]{2,1,0:T(8,128)(2,1)} %bitcast.34), calls=%async_computation.2 | async-start | bytes 262144 | tf_op jit(solution)/shard_map/all_to_all | solution.py:19
  42.1 8.4 %all-to-all-done.2 = bf16[32,16,128]{2,1,0:T(8,128)(2,1)S(1)} async-done(((bf16[32,16,128]{2,1,0:T(8,128)(2,1)}), bf16[32,16,128]{2,1,0:T(8,128)(2,1)S(1)}, u32[]{:S(2)}, u32[]{:S(2)}) %all-to-all-start.2) | async-done | bytes 131104 | tf_op jit(solution)/shard_map/all_to_all | solution.py:19
  50.6 2.1 %shard_map.132 = bf16[16,2,16,128]{3,2,1,0:T(8,128)(2,1)} custom-call(s32[3,2]{1,0:T(4,128)} %pad_add_fusion.refs_0_, bf16[16,2,16,128]{3,2,1,0:T(8,128)(2,1)S(1)} %bitcast.21, f32[16,128]{1,0:T(8,128)S(1)} %pad.4.refs_2_, bf16[16,2,16,128]{3,2,1,0:T(8,128)(2,1)} %get-tuple-element.85.refs_3_), custom_call_target="tpu_custom_call" | custom-call | flops 4194304 | bytes 1048576 | tf_op jit(solution)/shard_map/pallas_call | solution.py:35
  52.7 2.6 %all-to-all-start.3 = ((bf16[32,16,128]{2,1,0:T(8,128)(2,1)}), bf16[32,16,128]{2,1,0:T(8,128)(2,1)S(1)}, u32[]{:S(2)}, u32[]{:S(2)}) async-start(bf16[32,16,128]{2,1,0:T(8,128)(2,1)} %bitcast.35), calls=%async_computation.3 | async-start | bytes 262144 | tf_op jit(solution)/shard_map/all_to_all | solution.py:19
  55.3 1.7 %shard_map.134 = (bf16[128,512]{1,0:T(8,128)(2,1)}, bf16[512,128]{1,0:T(8,128)(2,1)}, f32[128,128]{1,0:T(8,128)}, bf16[128,1024]{1,0:T(8,128)(2,1)}, bf16[128,10...) custom-call(bf16[3,8,16,512]{3,2,1,0:T(8,128)(2,1)S(1)} %copy-done.1, ...), custom_call_target="tpu_custom_call" | custom-call | flops 134217728 | bytes 4194304 | tf_op jit(solution)/shard_map/pallas_call | solution.py:35
  57.0 1.7 %shard_map.133 = (bf16[128,512]{1,0:T(8,128)(2,1)}, bf16[512,128]{1,0:T(8,128)(2,1)}, f32[128,128]{1,0:T(8,128)}, bf16[128,1024]{1,0:T(8,128)(2,1)}, bf16[128,10...) custom-call(bf16[3,8,16,512]{3,2,1,0:T(8,128)(2,1)S(1)} %copy-done.1, ...), custom_call_target="tpu_custom_call" | custom-call | flops 134217728 | bytes 4194304 | tf_op jit(solution)/shard_map/pallas_call | solution.py:35
  58.8 5.1 %all-to-all-done.3 = bf16[32,16,128]{2,1,0:T(8,128)(2,1)S(1)} async-done(((bf16[32,16,128]{2,1,0:T(8,128)(2,1)}), bf16[32,16,128]{2,1,0:T(8,128)(2,1)S(1)}, u32[]{:S(2)}, u32[]{:S(2)}) %all-to-all-start.3) | async-done | bytes 131104 | tf_op jit(solution)/shard_map/all_to_all | solution.py:19
  63.9 2.6 %shard_map.135 = (bf16[512,128]{1,0:T(8,128)(2,1)}, bf16[128,1024]{1,0:T(8,128)(2,1)}, bf16[512,128]{1,0:T(8,128)(2,1)}) custom-call(bf16[512,128]{1,0:T(8,128)(2,1)S(1)} %bitcast.20, bf16[512,1024]{1,0:T(8,128)(2,1)S(1)} %copy-done.2, bf16[512,1024]{1,0:T(8,128)(2,1)S(1)} %copy-done, f32[1,512]{1,0:T(1,128)S(1)} %bitcast.31, ...), custom_call_target="tpu_custom_call" | custom-call | flops 268435456 | bytes 4194304 | tf_op jit(solution)/shard_map/pallas_call | solution.py:35
  66.5 11.2 %all_to_all.30 = bf16[32,16,128]{2,1,0:T(8,128)(2,1)S(1)} all-to-all(bf16[32,16,128]{2,1,0:T(8,128)(2,1)} %bitcast.36), channel_id=1, replica_groups=mesh['lon'=16,'lat'=2] {'lon','lat'}, dimensions={0} | all-to-all | bytes 262144 | tf_op jit(solution)/shard_map/all_to_all | solution.py:19
  77.7 2.1 %shard_map.136 = bf16[16,2,16,128]{3,2,1,0:T(8,128)(2,1)} custom-call(s32[3,2]{1,0:T(4,128)} %pad_add_fusion.refs_0_, bf16[16,2,16,128]{3,2,1,0:T(8,128)(2,1)S(1)} %bitcast.22, f32[16,128]{1,0:T(8,128)S(1)} %pad.4.refs_2_, bf16[16,2,16,128]{3,2,1,0:T(8,128)(2,1)} %get-tuple-element.85.refs_3_), custom_call_target="tpu_custom_call" | custom-call | flops 4194304 | bytes 1048576 | tf_op jit(solution)/shard_map/pallas_call | solution.py:35
  79.9 2.8 %all-to-all-start.5 = ((bf16[32,16,128]{2,1,0:T(8,128)(2,1)}), bf16[32,16,128]{2,1,0:T(8,128)(2,1)S(1)}, u32[]{:S(2)}, u32[]{:S(2)}) async-start(bf16[32,16,128]{2,1,0:T(8,128)(2,1)} %bitcast.37), calls=%async_computation.5 | async-start | bytes 262144 | tf_op jit(solution)/shard_map/all_to_all | solution.py:19
  82.7 2.7 %shard_map.137.sums_ref = f32[16,512]{1,0:T(8,128)S(1)} custom-call(bf16[512,1024]{1,0:T(8,128)(2,1)S(1)} %copy-done, f32[1,512]{1,0:T(1,128)S(1)} %bitcast.32, bf16[10,32,512]{2,1,0:T(8,128)(2,1)} %get-tuple-element.106.refs_0_, bf16[512,128]{1,0:T(8,128)(2,1)} %get-tuple-element.84.refs_1_, bf16[128,1024]{1,0:T(8,128)(2,1)} %get-tuple-element.107.refs_2_.refs_7_, ...), custom_call_target="tpu_custom_call" | custom-call | bytes 2097152 | tf_op jit(solution)/shard_map/pallas_call | solution.py:35
  85.4 5.7 %all-to-all-done.5 = bf16[32,16,128]{2,1,0:T(8,128)(2,1)S(1)} async-done(((bf16[32,16,128]{2,1,0:T(8,128)(2,1)}), bf16[32,16,128]{2,1,0:T(8,128)(2,1)S(1)}, u32[]{:S(2)}, u32[]{:S(2)}) %all-to-all-start.5) | async-done | bytes 131104 | tf_op jit(solution)/shard_map/all_to_all | solution.py:19
  91.1 3.6 %shard_map.138 = (bf16[128,512]{1,0:T(8,128)(2,1)S(1)}, f32[16,512]{1,0:T(8,128)S(1)}, bf16[1072,512]{1,0:T(8,128)(2,1)S(1)}, bf16[2,4,128,512]{3,2,1,0:T(8,128)(2,1)S(1)}) custom-call(bf16[512,128]{1,0:T(8,128)(2,1)S(1)} %bitcast.26, bf16[512,1024]{1,0:T(8,128)(2,1)S(1)} %copy-done.2, bf16[512,1024]{1,0:T(8,128)(2,1)S(1)} %copy-done, ...), custom_call_target="tpu_custom_call" | custom-call | flops 2147483648 | bytes 6291456 | tf_op jit(solution)/shard_map/pallas_call | solution.py:35
  94.8 2.7 %collective-permute-done.6.arrived_ref = bf16[1072,512]{1,0:T(8,128)(2,1)S(1)} collective-permute-done((bf16[1072,512]{1,0:T(8,128)(2,1)S(1)}, bf16[1072,512]{1,0:T(8,128)(2,1)S(1)}, u32[]{:S(2)}, u32[]{:S(2)}) %collective-permute-start.6) | collective-permute-done | bytes 1097760 | tf_op jit(solution)/shard_map/ppermute | solution.py:683
  99.0 8.6 %collective-permute-done.7.arrived_ref = bf16[560,512]{1,0:T(8,128)(2,1)S(1)} collective-permute-done((bf16[560,512]{1,0:T(8,128)(2,1)S(1)}, bf16[560,512]{1,0:T(8,128)(2,1)S(1)}, u32[]{:S(2)}, u32[]{:S(2)}) %collective-permute-start.7) | collective-permute-done | bytes 573472 | tf_op jit(solution)/shard_map/ppermute | solution.py:683
  108.1 7.1 %collective-permute-done.8.refs_3_ = bf16[352,512]{1,0:T(8,128)(2,1)S(1)} collective-permute-done((bf16[352,512]{1,0:T(8,128)(2,1)S(1)}, bf16[352,512]{1,0:T(8,128)(2,1)S(1)}, u32[]{:S(2)}, u32[]{:S(2)}) %collective-permute-start.8) | collective-permute-done | bytes 360480 | tf_op jit(solution)/shard_map/ppermute | solution.py:683
  115.4 5.4 %collective-permute-done.9.refs_2_ = bf16[176,512]{1,0:T(8,128)(2,1)S(1)} collective-permute-done((bf16[176,512]{1,0:T(8,128)(2,1)S(1)}, bf16[176,512]{1,0:T(8,128)(2,1)S(1)}, u32[]{:S(2)}, u32[]{:S(2)}) %collective-permute-start.9) | collective-permute-done | bytes 180256 | tf_op jit(solution)/shard_map/ppermute | solution.py:683
  121.3 2.3 %collective-permute-done.5.high_ref = bf16[1,1,18,512]{3,2,1,0:T(8,128)(2,1)S(1)} collective-permute-done((bf16[1,1,18,512]{3,2,1,0:T(8,128)(2,1)S(1)}, bf16[1,1,18,512]{3,2,1,0:T(8,128)(2,1)S(1)}, u32[]{:S(2)}, u32[]{:S(2)}) %collective-permute-start.5) | collective-permute-done | bytes 18464 | tf_op jit(solution)/shard_map/ppermute | solution.py:135
  123.7 1.1 shard_map.139
  124.8 2.4 %collective-permute-done.10.arrived_ref = bf16[112,512]{1,0:T(8,128)(2,1)S(1)} collective-permute-done((bf16[112,512]{1,0:T(8,128)(2,1)S(1)}, bf16[112,512]{1,0:T(8,128)(2,1)S(1)}, u32[]{:S(2)}, u32[]{:S(2)}) %collective-permute-start.10) | collective-permute-done | bytes 114720 | tf_op jit(solution)/shard_map/ppermute | solution.py:683
  (52 shorter events, 5.9 us)
Async XLA Ops:
  0.6 12.2 %copy-start.1 = (bf16[3,8,16,512]{3,2,1,0:T(8,128)(2,1)S(1)}, bf16[3,8,16,512]{3,2,1,0:T(8,128)(2,1)}, u32[]{:S(2)}) copy-start(bf16[3,8,16,512]{3,2,1,0:T(8,128)(2,1)} %states_ref.5) | copy-start | bytes 1179652
  0.6 12.3 %copy-start.5 = (s32[3,4]{1,0:T(4,128)S(1)}, s32[3,4]{1,0:T(4,128)}, u32[]{:S(2)}) copy-start(s32[3,4]{1,0:T(4,128)} %param.17) | copy-start | bytes 148
  0.7 12.3 %copy-start.6 = (s32[3,4]{1,0:T(4,128)S(1)}, s32[3,4]{1,0:T(4,128)}, u32[]{:S(2)}) copy-start(s32[3,4]{1,0:T(4,128)} %param.16) | copy-start | bytes 148
  0.7 32.8 %copy-start = (bf16[512,1024]{1,0:T(8,128)(2,1)S(1)}, bf16[512,1024]{1,0:T(8,128)(2,1)}, u32[]{:S(2)}) copy-start(bf16[512,1024]{1,0:T(8,128)(2,1)} %up_ref.13) | copy-start | bytes 3145732
  0.7 32.7 %copy-start.3 = (f32[3,3,512]{2,1,0:T(4,128)S(1)}, f32[3,3,512]{2,1,0:T(4,128)}, u32[]{:S(2)}) copy-start(f32[3,3,512]{2,1,0:T(4,128)} %kernel_ref.7) | copy-start | bytes 55300
  0.7 32.7 %copy-start.4 = (f32[512]{0:T(512)S(1)}, f32[512]{0:T(512)}, u32[]{:S(2)}) copy-start(f32[512]{0:T(512)} %param.13) | copy-start | bytes 6148
  2.6 18.0 %all-to-all-start = ((bf16[32,32,128]{2,1,0:T(8,128)(2,1)}), bf16[32,32,128]{2,1,0:T(8,128)(2,1)S(1)}, u32[]{:S(2)}, u32[]{:S(2)}) async-start(bf16[32,32,128]{2,1,0:T(8,128)(2,1)} %shard_map.128), calls=%async_computation | async-start | bytes 524288 | tf_op jit(solution)/shard_map/all_to_all | solution.py:19
  11.0 5.0 %collective-permute-start = (bf16[3,8,1,512]{3,2,1,0:T(2,128)(2,1)S(1)}, bf16[3,8,1,512]{3,2,1,0:T(2,128)(2,1)S(1)}, u32[]{:S(2)}, u32[]{:S(2)}) collective-permute-start(bf16[3,8,1,512]{3,2,1,0:T(2,128)(2,1)S(1)} %broadcast_select_fusion.2), channel_id=1, source_target_pairs={{0,1},{1,0},{2,3},{3,2},{4,5},{5,4},{6,7},{7,6},{8,9},{9,8},{10,11... | collective-permute-start | bytes 73736 | tf_op jit(solution)/shard_map/ppermute | solution.py:124
  22.1 13.0 %copy-start.2 = (bf16[512,1024]{1,0:T(8,128)(2,1)S(1)}, bf16[512,1024]{1,0:T(8,128)(2,1)}, u32[]{:S(2)}) copy-start(bf16[512,1024]{1,0:T(8,128)(2,1)} %down_ref.5) | copy-start | bytes 3145732
  22.2 13.0 %all-to-all-start.1 = ((bf16[32,16,128]{2,1,0:T(8,128)(2,1)}), bf16[32,16,128]{2,1,0:T(8,128)(2,1)S(1)}, u32[]{:S(2)}, u32[]{:S(2)}) async-start(bf16[32,16,128]{2,1,0:T(8,128)(2,1)} %bitcast.39), calls=%async_computation.1 | async-start | bytes 262144 | tf_op jit(solution)/shard_map/all_to_all | solution.py:19
  25.0 8.4 %collective-permute-start.1 = (bf16[3,1,18,512]{3,2,1,0:T(8,128)(2,1)S(1)}, bf16[3,1,18,512]{3,2,1,0:T(8,128)(2,1)S(1)}, u32[]{:S(2)}, u32[]{:S(2)}) collective-permute-start(bf16[3,1,18,512]{3,2,1,0:T(8,128)(2,1)S(1)} %pad_maximum_fusion), channel_id=1, source_target_pairs={{0,2},{2,4},{4,6},{6,8},{8,10},{10,12},{12,14},{14,16},{16,18},{18... | collective-permute-start | bytes 165896 | tf_op jit(solution)/shard_map/ppermute | solution.py:134
  25.2 8.2 %collective-permute-start.2 = (bf16[3,1,18,512]{3,2,1,0:T(8,128)(2,1)S(1)}, bf16[3,1,18,512]{3,2,1,0:T(8,128)(2,1)S(1)}, u32[]{:S(2)}, u32[]{:S(2)}) collective-permute-start(bf16[3,1,18,512]{3,2,1,0:T(8,128)(2,1)S(1)} %pad_maximum_fusion.1), channel_id=1, source_target_pairs={{0,30},{2,0},{4,2},{6,4},{8,6},{10,8},{12,10},{14,12},{16,14},{18,... | collective-permute-start | bytes 165896 | tf_op jit(solution)/shard_map/ppermute | solution.py:135
  37.9 12.7 %all-to-all-start.2 = ((bf16[32,16,128]{2,1,0:T(8,128)(2,1)}), bf16[32,16,128]{2,1,0:T(8,128)(2,1)S(1)}, u32[]{:S(2)}, u32[]{:S(2)}) async-start(bf16[32,16,128]{2,1,0:T(8,128)(2,1)} %bitcast.34), calls=%async_computation.2 | async-start | bytes 262144 | tf_op jit(solution)/shard_map/all_to_all | solution.py:19
  52.7 11.2 %all-to-all-start.3 = ((bf16[32,16,128]{2,1,0:T(8,128)(2,1)}), bf16[32,16,128]{2,1,0:T(8,128)(2,1)S(1)}, u32[]{:S(2)}, u32[]{:S(2)}) async-start(bf16[32,16,128]{2,1,0:T(8,128)(2,1)} %bitcast.35), calls=%async_computation.3 | async-start | bytes 262144 | tf_op jit(solution)/shard_map/all_to_all | solution.py:19
  79.9 11.2 %all-to-all-start.5 = ((bf16[32,16,128]{2,1,0:T(8,128)(2,1)}), bf16[32,16,128]{2,1,0:T(8,128)(2,1)S(1)}, u32[]{:S(2)}, u32[]{:S(2)}) async-start(bf16[32,16,128]{2,1,0:T(8,128)(2,1)} %bitcast.37), calls=%async_computation.5 | async-start | bytes 262144 | tf_op jit(solution)/shard_map/all_to_all | solution.py:19
  94.7 2.8 %collective-permute-start.6 = (bf16[1072,512]{1,0:T(8,128)(2,1)S(1)}, bf16[1072,512]{1,0:T(8,128)(2,1)S(1)}, u32[]{:S(2)}, u32[]{:S(2)}) collective-permute-start(bf16[1072,512]{1,0:T(8,128)(2,1)S(1)} %get-tuple-element.128), channel_id=1, source_target_pairs={{0,2},{1,3},{2,0},{3,1},{4,6},{5,7},{6,4},{7,5},{8,10},{9,11},{10,... | collective-permute-start | bytes 3293192 | tf_op jit(solution)/shard_map/ppermute | solution.py:683
  97.8 9.8 %collective-permute-start.7 = (bf16[560,512]{1,0:T(8,128)(2,1)S(1)}, bf16[560,512]{1,0:T(8,128)(2,1)S(1)}, u32[]{:S(2)}, u32[]{:S(2)}) collective-permute-start(bf16[560,512]{1,0:T(8,128)(2,1)S(1)} %get-tuple-element.131), channel_id=1, source_target_pairs={{0,4},{1,5},{2,3},{3,2},{4,0},{5,1},{6,7},{7,6},{8,12},{9,13},{10,... | collective-permute-start | bytes 1720328 | tf_op jit(solution)/shard_map/ppermute | solution.py:683
  97.9 10.2 %collective-permute-start.3 = (bf16[1,8,1,512]{3,2,1,0:T(2,128)(2,1)S(1)}, bf16[1,8,1,512]{3,2,1,0:T(2,128)(2,1)S(1)}, u32[]{:S(2)}, u32[]{:S(2)}) collective-permute-start(bf16[1,8,1,512]{3,2,1,0:T(2,128)(2,1)S(1)} %broadcast_select_fusion.5), channel_id=1, source_target_pairs={{0,1},{1,0},{2,3},{3,2},{4,5},{5,4},{6,7},{7,6},{8,9},{9,8},{10,11... | collective-permute-start | bytes 24584 | tf_op jit(solution)/shard_map/ppermute | solution.py:124
  107.7 7.5 %collective-permute-start.8 = (bf16[352,512]{1,0:T(8,128)(2,1)S(1)}, bf16[352,512]{1,0:T(8,128)(2,1)S(1)}, u32[]{:S(2)}, u32[]{:S(2)}) collective-permute-start(bf16[352,512]{1,0:T(8,128)(2,1)S(1)} %get-tuple-element.134), channel_id=1, source_target_pairs={{0,1},{1,0},{2,6},{3,7},{4,5},{5,4},{6,2},{7,3},{8,9},{9,8},{10,14... | collective-permute-start | bytes 1081352 | tf_op jit(solution)/shard_map/ppermute | solution.py:683
  115.2 5.6 %collective-permute-start.9 = (bf16[176,512]{1,0:T(8,128)(2,1)S(1)}, bf16[176,512]{1,0:T(8,128)(2,1)S(1)}, u32[]{:S(2)}, u32[]{:S(2)}) collective-permute-start(bf16[176,512]{1,0:T(8,128)(2,1)S(1)} %get-tuple-element.137), channel_id=1, source_target_pairs={{0,8},{1,9},{2,10},{3,11},{4,12},{5,13},{6,14},{7,15},{8,0},{9,1},... | collective-permute-start | bytes 540680 | tf_op jit(solution)/shard_map/ppermute | solution.py:683
  115.3 6.0 %collective-permute-start.4 = (bf16[1,1,18,512]{3,2,1,0:T(8,128)(2,1)S(1)}, bf16[1,1,18,512]{3,2,1,0:T(8,128)(2,1)S(1)}, u32[]{:S(2)}, u32[]{:S(2)}) collective-permute-start(bf16[1,1,18,512]{3,2,1,0:T(8,128)(2,1)S(1)} %pad_maximum_fusion.2), channel_id=1, source_target_pairs={{0,2},{2,4},{4,6},{6,8},{8,10},{10,12},{12,14},{14,16},{16,18},{18... | collective-permute-start | bytes 55304 | tf_op jit(solution)/shard_map/ppermute | solution.py:134
  120.8 6.4 %collective-permute-start.10 = (bf16[112,512]{1,0:T(8,128)(2,1)S(1)}, bf16[112,512]{1,0:T(8,128)(2,1)S(1)}, u32[]{:S(2)}, u32[]{:S(2)}) collective-permute-start(bf16[112,512]{1,0:T(8,128)(2,1)S(1)} %get-tuple-element.140), channel_id=1, source_target_pairs={{0,16},{1,17},{2,18},{3,19},{4,20},{5,21},{6,22},{7,23},{8,24},{9,... | collective-permute-start | bytes 344072 | tf_op jit(solution)/shard_map/ppermute | solution.py:683
  121.1 2.6 %collective-permute-start.5 = (bf16[1,1,18,512]{3,2,1,0:T(8,128)(2,1)S(1)}, bf16[1,1,18,512]{3,2,1,0:T(8,128)(2,1)S(1)}, u32[]{:S(2)}, u32[]{:S(2)}) collective-permute-start(bf16[1,1,18,512]{3,2,1,0:T(8,128)(2,1)S(1)} %pad_maximum_fusion.3), channel_id=1, source_target_pairs={{0,30},{2,0},{4,2},{6,4},{8,6},{10,8},{12,10},{14,12},{16,14},{18,... | collective-permute-start | bytes 55304 | tf_op jit(solution)/shard_map/ppermute | solution.py:135

commit v7 on v6

--- a/solution.py
+++ b/solution.py
@@ -56,20 +56,24 @@
 
 
 PIECES = 3
+SUMS = 10
+SUM_ROWS = 32
 
 
 def pieces_of(value):
+    value = value[:SUMS]
     parts = []
     for _ in range(PIECES):
-        parts.append(value.astype(jnp.bfloat16))
-        value = value - parts[-1].astype(jnp.float32)
-    return jnp.concatenate(parts, axis=0)
+        parts.append(value.astype(jnp.bfloat16).astype(jnp.float32))
+        value = value - parts[-1]
+    parts.append(jnp.zeros((SUM_ROWS - PIECES * SUMS, value.shape[1]), jnp.float32))
+    return jnp.concatenate(parts, axis=0).astype(jnp.bfloat16)
 
 
 def whole_of(parts):
-    rows = parts.shape[0] // PIECES
     parts = parts.astype(jnp.float32)
-    return (parts[:rows] + parts[rows : 2 * rows]) + parts[2 * rows :]
+    total = (parts[:SUMS] + parts[SUMS : 2 * SUMS]) + parts[2 * SUMS : 3 * SUMS]
+    return jnp.concatenate([total, jnp.zeros((ROWS - SUMS, parts.shape[1]), jnp.float32)], axis=0)
 
 
 def pack_kernel(cotangent_hbm, weight_hbm, out_hbm, cotangent_ref, weight_ref, out_ref, sems):
@@ -117,11 +121,12 @@
     )[0]
 
 
-def lat_edges(states):
+def lat_edges(states, held=lambda value: value):
     lat, lat_at = lax.axis_size("lat"), lax.axis_index("lat")
     first, last = states[:, :, :1], states[:, :, -1:]
     if lat == 2:
         arrived = lax.ppermute(jnp.where(lat_at == 0, last, first), "lat", [(0, 1), (1, 0)])
+        arrived = held(arrived)
         return jnp.where(lat_at == 0, 0, arrived), jnp.where(lat_at == 0, arrived, 0)
     return (
         lax.ppermute(last, "lat", [(i, i + 1) for i in range(lat - 1)]),
@@ -302,83 +307,83 @@
     return lax.axis_index("lon") >> at & 1
 
 
-def last_kernel(steps, tile, lon_groups, moved_ref, down_ref, up_ref, gain_ref, sums_ref, *refs):
+def gradient_quadrants(left_ref, right_ref, send_ref, keep_ref):
+    channels, width = left_ref.shape[0], right_ref.shape[1] // 2
+    if keep_ref.ndim == 2:
+        send_ref[:channels] = jnp.dot(left_ref[...], right_ref[...], preferred_element_type=jnp.float32).astype(jnp.bfloat16)
+        keep_ref[...] = jnp.zeros_like(keep_ref)
+        return
+    size = channels // QUADRANTS
+    groups = lax.axis_size("lon") // 4
+    chunk = size // groups
+    rows = []
+    for core in (1 - lon_bit(0), lon_bit(0)):
+        for x in range(2):
+            for z in range(groups):
+                start = pl.multiple_of((4 * z + 2 * x + core) * chunk, chunk)
+                rows.append(left_ref[pl.ds(start, chunk)])
+    rows = jnp.concatenate(rows, axis=0)
+    value = jnp.dot(rows, right_ref[...], preferred_element_type=jnp.float32).astype(jnp.bfloat16)
+    for q in range(QUADRANTS):
+        x, lat = q // 2, q % 2
+        columns = slice(lat * width, (lat + 1) * width)
+        send_ref[q * size : (q + 1) * size] = value[x * size : (x + 1) * size, columns]
+        keep_ref[q] = value[(2 + x) * size : (3 + x) * size, columns]
+
+
+def quadrant_shapes(channels, hid, sums):
+    if lax.axis_size("lat") != 2 or lax.axis_size("lon") != 16:
+        return (channels, hid), (8, 128)
+    return (channels + SUM_ROWS * sums, hid // 2), (QUADRANTS, channels // QUADRANTS, hid // 2)
+
+
+def side_by_side(refs, goal_ref, axis):
+    size = refs[0].shape[axis]
+    places = [pl.ds(s * size, size) for s in range(len(refs))]
+    return [(ref, goal_ref.at[:, place] if axis else goal_ref.at[place]) for ref, place in zip(refs, places)]
+
+
+def last_kernel(steps, tile, moved_ref, down_ref, up_ref, gain_ref, sums_ref, *refs):
     slope_hbm, n_hbm, inv_hbm, pad_hbm, *refs = refs
-    inputs, refs = refs[: 4 * steps - 2], refs[4 * steps - 2 :]
+    inputs, refs = refs[: 2 * steps - 1], refs[2 * steps - 1 :]
     field_ref, total_ref, send_ref, keep_ref, slope_ref, n_ref, inv_ref, pad_ref, left_ref, right_ref, sems = refs
     arriving = copies(
         sems, 0, [(slope_hbm, slope_ref), (n_hbm, n_ref), (inv_hbm, inv_ref), (pad_hbm, pad_ref)]
     )
     count = slope_ref.shape[0]
-    part = lambda s: pl.ds(s * count, count)
-    narrows, grads = inputs[:steps], inputs[steps : 2 * steps - 1]
-    moveds, hiddens = inputs[2 * steps - 1 : 3 * steps - 2], inputs[3 * steps - 2 :]
-    pairs = [(ref, left_ref.at[0, :, part(s)]) for s, ref in enumerate(narrows)]
-    pairs += [(ref, right_ref.at[0, part(s)]) for s, ref in enumerate(grads)]
-    pairs += [(ref, left_ref.at[1, :, part(s)]) for s, ref in enumerate(moveds)]
-    pairs += [(ref, right_ref.at[1, part(s)]) for s, ref in enumerate(hiddens)]
+    pairs = side_by_side(inputs[:steps], left_ref, 1) + side_by_side(inputs[steps:], right_ref, 0)
     later = copies(sems, 4, pairs)
-    left_ref[1, :, (steps - 1) * count :] = moved_ref[...]
     moved = moved_ref[...].astype(jnp.float32).T
-    channels = moved.shape[1]
     grad_hidden = jnp.dot(moved.astype(jnp.bfloat16), down_ref[...], preferred_element_type=jnp.float32)
     arriving[0].wait()
     grad_pre = (grad_hidden * slope_ref[...].astype(jnp.float32)).astype(jnp.bfloat16)
-    right_ref[0, (steps - 1) * count :] = grad_pre
+    right_ref[(steps - 1) * count :] = grad_pre
     grad_n = lax.dot_general(grad_pre, up_ref[...], LANES_BOTH, preferred_element_type=jnp.float32)
     finish(arriving[1:])
     narrow, gain = n_ref[...].astype(jnp.float32), gain_ref[...]
     term = grad_n * narrow
     mean = jnp.mean(term, axis=1, keepdims=True)
     field = moved + inv_ref[:, :1] * (grad_n * gain - narrow * (mean / gain))
-    narrow_field = field.astype(jnp.bfloat16)
-    field_ref[...] = narrow_field
-    total = sums_ref[...] + sums_rows(stencil_sums(pad_ref, narrow_field.astype(jnp.float32), tile), term, gain)
+    field = field.astype(jnp.bfloat16)
+    field_ref[...] = field
+    total = sums_ref[...] + sums_rows(stencil_sums(pad_ref, field.astype(jnp.float32), tile), term, gain)
     total_ref[...] = total
     finish(later)
-    if send_ref.ndim == 3:
-        for k in range(2):
-            send_ref[k] = jnp.dot(left_ref[k], right_ref[k], preferred_element_type=jnp.float32).astype(jnp.bfloat16)
-        keep_ref[...] = jnp.zeros_like(keep_ref)
-        return
-    quadrant_rows = channels // 4
-    send_ref[2 * QUADRANTS * quadrant_rows :] = pieces_of(total)
-    chunk = channels // (4 * lon_groups)
-    width = right_ref.shape[2] // 2
-    for k in range(2):
-        rows = []
-        for core in (1 - lon_bit(0), lon_bit(0)):
-            for x in range(2):
-                for z in range(lon_groups):
-                    start = pl.multiple_of((4 * z + 2 * x + core) * chunk, chunk)
-                    rows.append(left_ref[k, pl.ds(start, chunk)])
-        rows = jnp.concatenate(rows, axis=0)
-        value = jnp.dot(rows, right_ref[k], preferred_element_type=jnp.float32).astype(jnp.bfloat16)
-        size = lon_groups * chunk
-        for q in range(QUADRANTS):
-            x, lat = q // 2, q % 2
-            columns = slice(lat * width, (lat + 1) * width)
-            start = (k * QUADRANTS + q) * quadrant_rows
-            send_ref[start : start + quadrant_rows] = value[x * size : (x + 1) * size, columns]
-            keep_ref[k, q] = value[(2 + x) * size : (3 + x) * size, columns]
-
-
-def last_step(tile, moved, w_down, w_up, norm_gain, sums, forward, grads, moveds):
+    gradient_quadrants(left_ref, right_ref, send_ref, keep_ref)
+    if keep_ref.ndim > 2:
+        send_ref[left_ref.shape[0] :] = pieces_of(total)
+
+
+def last_step(tile, moved, w_down, w_up, norm_gain, sums, forward, grads):
     steps = len(forward)
     channels, count = moved.shape
     hid = w_down.shape[1]
     narrow, _, inv_root, _, slope, pad = forward[-1]
-    lon_groups = lax.axis_size("lon") // 4
-    by_quadrant = lax.axis_size("lat") == 2 and lon_groups == 4
-    send = (2, channels, hid)
-    keep = (8, 128)
-    if by_quadrant:
-        send = (2 * channels + PIECES * ROWS, hid // 2)
-        keep = (2, QUADRANTS, channels // 4, hid // 2)
+    send, keep = quadrant_shapes(channels, hid, 1)
     sds = jax.ShapeDtypeStruct
-    inputs = [parts[1] for parts in forward] + grads + moveds + [parts[3] for parts in forward]
+    inputs = [parts[1] for parts in forward] + grads
     return call(
-        functools.partial(last_kernel, steps, tile, lon_groups),
+        functools.partial(last_kernel, steps, tile),
         [
             sds((count, channels), jnp.bfloat16),
             sds((ROWS, channels), jnp.float32),
@@ -389,11 +394,40 @@
         "vvvvv" + "h" * (4 + len(inputs)),
         "vppp",
         scratch=[pltpu.VMEM(value.shape, value.dtype) for value in (slope, narrow, inv_root, pad)]
-        + [pltpu.VMEM((2, channels, steps * count), jnp.bfloat16), pltpu.VMEM((2, steps * count, hid), jnp.bfloat16)]
+        + [pltpu.VMEM((channels, steps * count), jnp.bfloat16), pltpu.VMEM((steps * count, hid), jnp.bfloat16)]
         + [pltpu.SemaphoreType.DMA((len(inputs) + 4,))],
-        flops=2**31,
+        flops=2**30,
         moved=6 * 2**20,
         limit=20,
+    )
+
+
+def down_kernel(steps, moved_ref, *refs):
+    inputs, (send_ref, keep_ref, left_ref, right_ref, sems) = refs[: 2 * steps - 1], refs[2 * steps - 1 :]
+    count = moved_ref.shape[1]
+    pairs = side_by_side(inputs[: steps - 1], left_ref, 1) + side_by_side(inputs[steps - 1 :], right_ref, 0)
+    arriving = copies(sems, 0, pairs)
+    left_ref[:, (steps - 1) * count :] = moved_ref[...]
+    finish(arriving)
+    gradient_quadrants(left_ref, right_ref, send_ref, keep_ref)
+
+
+def down_gradients(moved, forward, moveds):
+    steps = len(forward)
+    channels, count = moved.shape
+    hid = forward[0][3].shape[1]
+    inputs = moveds + [parts[3] for parts in forward]
+    return call(
+        functools.partial(down_kernel, steps),
+        [jax.ShapeDtypeStruct(shape, jnp.bfloat16) for shape in quadrant_shapes(channels, hid, 0)],
+        [moved, *inputs],
+        "v" + "h" * len(inputs),
+        "pp",
+        scratch=[pltpu.VMEM((channels, steps * count), jnp.bfloat16), pltpu.VMEM((steps * count, hid), jnp.bfloat16)]
+        + [pltpu.SemaphoreType.DMA((len(inputs),))],
+        flops=2**29,
+        moved=2**21,
+        limit=16,
     )
 
 
@@ -600,112 +634,163 @@
         out_ref[place] = value.astype(out_ref.dtype)
 
 
-def quadrant_kernel(kept_ref, total_ref, arrived_ref, send_ref, keep_ref, chip_ref):
-    core, x, lat = lon_bit(0), lon_bit(1), lax.axis_index("lat")
-    rows = kept_ref.shape[2]
-    for k in range(2):
-        for j in range(2):
-            kept = (1 - core) * (2 * x + j) + core * (2 * j + lat)
-            sent = (1 - core) * (2 * (1 - x) + j) + core * (2 * j + 1 - lat)
-            pairs = [(sent, send_ref, pl.ds((2 * k + j) * rows, rows)), (kept, keep_ref, (k, j))]
-            arrived = lambda q: arrived_ref[pl.ds(pl.multiple_of((k * QUADRANTS + q) * rows, rows), rows)]
-            add_parts(pairs, lambda q: kept_ref[k, q], arrived)
-    chip = total_ref[...] + whole_of(arrived_ref[2 * QUADRANTS * rows :])
-    chip_ref[...] = chip
-    send_ref[4 * rows :] = pieces_of(chip)
-
-
-def half_kernel(kept_ref, chip_ref, arrived_ref, send_ref, keep_ref, beside_ref):
-    core, x, lat = lon_bit(0), lon_bit(1), lax.axis_index("lat")
-    mine = (1 - core) * lat + core * x
-    rows = kept_ref.shape[2]
-    for k in range(2):
-        pairs = [(1 - mine, send_ref, pl.ds(k * rows, rows)), (mine, keep_ref, k)]
-        arrived = lambda q: arrived_ref[pl.ds(pl.multiple_of((2 * k + q) * rows, rows), rows)]
-        add_parts(pairs, lambda q: kept_ref[k, q], arrived)
-    sums = PIECES * ROWS
-    beside = arrived_ref[4 * rows :]
-    beside_ref[...] = whole_of(beside)
-    send_ref[2 * rows : 2 * rows + sums] = pieces_of(chip_ref[...])
-    send_ref[2 * rows + sums :] = beside
-
-
-def rows_kernel(groups, bit_at, *refs):
-    kept_ref, *total_refs, arrived_ref, send_ref, keep_ref, total_ref = refs
+def first_axis(flip):
+    core = lon_bit(0)
+    return 1 - core if flip else core
+
+
+def quadrant_kernel(flip, *refs):
+    kept_ref, *total_refs, arrived_ref, send_ref, keep_ref = refs[: 4 + len(refs) // 6]
+    axis, x, lat = first_axis(flip), lon_bit(1), lax.axis_index("lat")
+    rows = kept_ref.shape[1]
+    for j in range(2):
+        kept = (1 - axis) * (2 * x + j) + axis * (2 * j + lat)
+        sent = (1 - axis) * (2 * (1 - x) + j) + axis * (2 * j + 1 - lat)
+        pairs = [(sent, send_ref, pl.ds(j * rows, rows)), (kept, keep_ref, j)]
+        arrived = lambda q: arrived_ref[pl.ds(pl.multiple_of(q * rows, rows), rows)]
+        add_parts(pairs, lambda q: kept_ref[q], arrived)
+    if total_refs:
+        chip = total_refs[0][...] + whole_of(arrived_ref[QUADRANTS * rows :])
+        refs[-1][...] = chip
+        send_ref[2 * rows :] = pieces_of(chip)
+
+
+def half_kernel(flip, *refs):
+    kept_ref, *total_refs, arrived_ref, send_ref, keep_ref = refs[: 4 + len(refs) // 6]
+    axis, x, lat = first_axis(flip), lon_bit(1), lax.axis_index("lat")
+    mine = (1 - axis) * lat + axis * x
+    rows = kept_ref.shape[1]
+    pairs = [(1 - mine, send_ref, pl.ds(0, rows)), (mine, keep_ref, slice(None))]
+    arrived = lambda q: arrived_ref[pl.ds(pl.multiple_of(q * rows, rows), rows)]
+    add_parts(pairs, lambda q: kept_ref[q], arrived)
+    if total_refs:
+        beside = arrived_ref[2 * rows :]
+        refs[-1][...] = whole_of(beside)
+        send_ref[rows : rows + SUM_ROWS] = pieces_of(total_refs[0][...])
+        send_ref[rows + SUM_ROWS :] = beside
+
+
+def rows_kernel(groups, bit_at, totals, *refs):
+    kept_ref, *refs = refs
+    total_refs, (arrived_ref, send_ref, keep_ref, *total_ref) = refs[:totals], refs[totals:]
     bit = lon_bit(bit_at)
-    rows = kept_ref.shape[1]
+    rows = kept_ref.shape[0]
     chunk = rows // (2 * groups)
-    for k in range(2):
-        for p in range(groups):
-            goal = pl.ds(p * chunk, chunk)
-            places = [pl.multiple_of((2 * p + which) * chunk, chunk) for which in (1 - bit, bit)]
-            pairs = [
-                (places[0], send_ref, pl.ds(k * groups * chunk + p * chunk, chunk)),
-                (places[1], keep_ref, (k, goal)),
-            ]
-            arrived = lambda q: arrived_ref[pl.ds(pl.multiple_of(k * rows + q, chunk), chunk)]
-            add_parts(pairs, lambda q: kept_ref[k, pl.ds(q, chunk)], arrived)
-    total = add_sums(total_refs, arrived_ref, 2 * rows)
-    total_ref[...] = total
-    send_ref[2 * groups * chunk :] = pieces_of(total)
+    for p in range(groups):
+        goal = pl.ds(p * chunk, chunk)
+        places = [pl.multiple_of((2 * p + which) * chunk, chunk) for which in (1 - bit, bit)]
+        pairs = [(places[0], send_ref, goal), (places[1], keep_ref, goal)]
+        add_parts(pairs, lambda q: kept_ref[pl.ds(q, chunk)], lambda q: arrived_ref[pl.ds(q, chunk)])
+    if totals:
+        total = add_sums(total_refs, arrived_ref, rows)
+        total_ref[0][...] = total
+        send_ref[rows // 2 :] = pieces_of(total)
 
 
 def add_sums(total_refs, arrived_ref, start):
-    size = PIECES * ROWS
-    arrived = whole_of(arrived_ref[start : start + size])
+    arrived = whole_of(arrived_ref[start : start + SUM_ROWS])
     if len(total_refs) == 1:
         return total_refs[0][...] + arrived
     chip, beside = (ref[...] for ref in total_refs)
-    return (chip + whole_of(arrived_ref[start + size :])) + (beside + arrived)
-
-
-def last_sum_kernel(kept_ref, total_ref, arrived_ref, up_ref, down_ref, taps_ref, gain_ref):
-    rows = kept_ref.shape[1]
-    up_ref[...] = kept_ref[0] + arrived_ref[:rows].astype(jnp.float32)
-    down_ref[...] = kept_ref[1] + arrived_ref[rows : 2 * rows].astype(jnp.float32)
-    total = add_sums([total_ref], arrived_ref, 2 * rows)
+    return (chip + whole_of(arrived_ref[start + SUM_ROWS :])) + (beside + arrived)
+
+
+def finish_kernel(kept_ref, total_ref, arrived_ref, kept_down_ref, arrived_down_ref, up_hbm, down_hbm, taps_ref, gain_ref, *refs):
+    up_ref, down_ref, sems = refs
+    rows = kept_ref.shape[0]
+    down_ref[...] = kept_down_ref[...] + arrived_down_ref[...].astype(jnp.float32)
+    leaving = copies(sems, 0, [(down_ref, down_hbm)])
+    up_ref[...] = kept_ref[...] + arrived_ref[:rows].astype(jnp.float32)
+    leaving += copies(sems, 1, [(up_ref, up_hbm)])
+    total = add_sums([total_ref], arrived_ref, rows)
     for k in range(9):
         taps_ref[k // 3, k % 3 : k % 3 + 1] = total[k : k + 1]
     gain_ref[...] = total[9:10]
-
-
-def all_sums(send, keep, total):
+    finish(leaving)
+
+
+def after(value, first):
+    return lax.optimization_barrier((value, first))[0]
+
+
+def halving(flip, send, keep, total):
     lon, lat = lax.axis_size("lon"), lax.axis_size("lat")
-    channels = total.shape[1]
-    if send.ndim == 3:
-        parts = [scattered(send[k].astype(jnp.float32), k == 1) for k in range(2)]
-        total = lax.psum(total, AXES)
-        return (*parts, total[:9].reshape(3, 3, channels), total[9])
     places = [(i, j) for i in range(lon) for j in range(lat)]
     flat = lambda i, j: i * lat + j
-
-    def traded(value, partner):
-        return lax.ppermute(value, AXES, [(flat(i, j), flat(*partner(i, j))) for i, j in places])
-
+    along_lat = lambda i: (i & 1) != flip
     sds = jax.ShapeDtypeStruct
-
-    def stage(kernel, shape, kept, totals, arrived, sums):
-        sent = 2 * shape[-2] * (shape[1] if len(shape) == 4 else 1) + PIECES * ROWS * sums
-        out = [sds((sent, shape[-1]), jnp.bfloat16), sds(shape, jnp.float32), sds(total.shape, jnp.float32)]
-        operands = [kept, *totals, arrived]
-        return call(kernel, out, operands, "v" * len(operands), "ppp", moved=2**20, limit=12)
-
-    rows, width = keep.shape[2:]
-    arrived = traded(send, lambda i, j: (i ^ 1, j))
-    send, keep, chip = stage(quadrant_kernel, (2, 2, rows, width), keep, [total], arrived, 1)
-    arrived = traded(send, lambda i, j: (i, j ^ 1) if i & 1 else (i ^ 2, j))
-    send, keep, beside = stage(half_kernel, (2, rows, width), keep, [chip], arrived, 2)
-    arrived = traded(send, lambda i, j: (i ^ 2, j) if i & 1 else (i, j ^ 1))
-    kernel = functools.partial(rows_kernel, 2, 2)
-    send, keep, total = stage(kernel, (2, rows // 2, width), keep, [chip, beside], arrived, 1)
-    arrived = traded(send, lambda i, j: (i ^ 4, j))
-    kernel = functools.partial(rows_kernel, 1, 3)
-    send, keep, total = stage(kernel, (2, rows // 4, width), keep, [total], arrived, 1)
-    arrived = traded(send, lambda i, j: (i ^ 8, j))
-    part = sds((rows // 4, width), jnp.float32)
+    rows, width = keep.shape[1:]
+    sums = [] if total is None else [total]
+    with_sums = len(sums)
+    plan = [
+        (lambda i, j: (i ^ 1, j), functools.partial(quadrant_kernel, flip), (2, rows, width), 1),
+        (
+            lambda i, j: (i, j ^ 1) if along_lat(i) else (i ^ 2, j),
+            functools.partial(half_kernel, flip),
+            (rows, width),
+            2,
+        ),
+        (
+            lambda i, j: (i ^ 2, j) if along_lat(i) else (i, j ^ 1),
+            functools.partial(rows_kernel, 2, 2, 2 * with_sums),
+            (rows // 2, width),
+            1,
+        ),
+        (lambda i, j: (i ^ 4, j), functools.partial(rows_kernel, 1, 3, with_sums), (rows // 4, width), 1),
+    ]
+    for at, (partner, kernel, shape, parts) in enumerate(plan):
+        send = yield send
+        arrived = lax.ppermute(send, AXES, [(flat(i, j), flat(*partner(i, j))) for i, j in places])
+        arrived = yield arrived
+        sent = shape[-2] * (shape[0] if len(shape) == 3 else 1) + SUM_ROWS * parts * with_sums
+        out = [sds((sent, shape[-1]), jnp.bfloat16), sds(shape, jnp.float32)]
+        out += [sds(value.shape, jnp.float32) for value in sums[:1]]
+        operands = [keep, *sums, arrived]
+        send, keep, *more = call(kernel, out, operands, "v" * len(operands), "p" * len(out), moved=2**19, limit=12)
+        sums = sums + more if at == 1 else more
+    send = yield send
+    arrived = lax.ppermute(send, AXES, [(flat(i, j), flat(i ^ 8, j)) for i, j in places])
+    yield (keep, *sums, arrived)
+
+
+def all_sums(up, down, total, field, kernel):
+    channels = total.shape[1]
+    field = field[None]
+    if up[1].ndim == 2:
+        parts = [scattered(send.astype(jnp.float32), flip) for flip, (send, _) in enumerate((up, down))]
+        total = lax.psum(total, AXES)
+        around = lat_edges(field)
+        state = final_parts(field[0], (*around, *lon_edges(field, *around)), kernel)
+        return (state, *parts, total[:9].reshape(3, 3, channels), total[9])
+    ahead, behind = halving(False, *up, total), halving(True, *down, None)
+    send, later = next(ahead), next(behind)
+    arrived = ahead.send(send)
+    send = ahead.send(after(arrived, later))
+    field = after(field, send)
+    arrived_later = behind.send(after(later, send))
+    later = behind.send(arrived_later)
+    around = lat_edges(field, lambda value: after(value, later))
+    state = final_parts(field[0], (*around, *lon_edges(field, *around)), kernel)
+    for at in range(1, 4):
+        arrived = ahead.send(send)
+        arrived_later = behind.send(later)
+        send = ahead.send(after(arrived, later))
+        later = behind.send(after(arrived_later, send))
+    final_ahead = ahead.send(send)
+    final_behind = behind.send(later)
+    sds = jax.ShapeDtypeStruct
+    part = sds(final_ahead[0].shape, jnp.float32)
     out = [part, part, sds((3, 3, channels), jnp.float32), sds((1, channels), jnp.float32)]
-    up, down, taps, gain = call(last_sum_kernel, out, [keep, total, arrived], "vvv", "vvvv", moved=2**18)
-    return up, down, taps, gain.reshape(channels)
+    up, down, taps, gain = call(
+        finish_kernel,
+        out,
+        [*final_ahead, *final_behind],
+        "vvvvv",
+        "hhvv",
+        scratch=[pltpu.VMEM(part.shape, part.dtype)] * 2 + [pltpu.SemaphoreType.DMA((2,))],
+        moved=2**18,
+    )
+    return state, up, down, taps, gain.reshape(channels)
 
 
 def local(cotangent, states, w_up, w_down, norm_gain, kernel, bilinear, lon_move, lat_move):
@@ -740,9 +825,9 @@
     taps = lax.dynamic_slice_in_dim(kernel.reshape(9, channels), me * share, share, 1).T
     taps = jnp.pad(taps, ((0, padded_share - share), (0, count - 9)))
 
-    before, after = lat_edges(states_later)
-    grid_now, before, after = lax.optimization_barrier((grid_now, before, after))
-    around = (before, after, *lon_edges(states, before, after))
+    around = lat_edges(states_later)
+    grid_now, *around = lax.optimization_barrier((grid_now, *around))
+    around = (*around, *lon_edges(states, *around))
     order = list(reversed(range(steps)))
     gain = norm_gain.reshape(1, channels)
     forward = {s: forward_parts(s, states, around, kernel, gain, w_up) for s in order}
@@ -762,12 +847,11 @@
     pads, narrows = ([forward[s][k] for s in order[:-1]] for k in (5, 0))
     sums = channel_sums(tile, w_up, gain, pads, earlier(fields), earlier(grads), narrows)
     here, sums = lax.optimization_barrier((here, sums))
-    parts = ([forward[s] for s in order], earlier(grads), earlier(moved))
-    field, total, send, keep = last_step(tile, here, w_down, w_up, gain, sums, *parts)
+    parts = [forward[s] for s in order]
+    field, total, send, keep = last_step(tile, here, w_down, w_up, gain, sums, parts, earlier(grads))
+    down = down_gradients(here, parts, earlier(moved))
     field = field.reshape(cotangent.shape)
-    before, after = lat_edges(field[None])
-    grad_state = final_parts(field, (before, after, *lon_edges(field[None], before, after)), kernel)
-    return (grad_state, *all_sums(send, keep, total))
+    return all_sums((send, keep), down, total, field, kernel)
 
 
 def solution(mesh):

time: 129 us -> 126 us (0.977)
  waiting for transfers between devices: 58.7 us -> 47.6 us
  starting transfers between devices: 27.9 us -> 35.6 us
  Pallas kernels: 26.8 us -> 28.9 us
    ppermute x5 -> x10, waiting for transfers between devices: 26.2 us -> 13.4 us  [the longest x8 13.4 us: halving(): lax.ppermute(send, AXES, [(flat(i, j), flat(*partner(i, j))) for i, j in...]
    ppermute x5 -> x10, starting transfers between devices: 0.84 us -> 7.26 us  [the longest x8 4.63 us: halving(): lax.ppermute(send, AXES, [(flat(i, j), flat(*partner(i, j))) for i, j in...]
    pallas_call x17 -> x22, Pallas kernels: 26.8 us -> 28.9 us  [call(): pl.pallas_call(kernel, out_shape=out_shape, in_specs=[pl.BlockSpec(memory...]
    ppermute x2, waiting for transfers between devices: 2.39 us -> 3.91 us  [lat_edges(): lax.ppermute(jnp.where(lat_at == 0, last, first), 'lat', [(0, 1), (1, 0)])]
    ppermute x2, starting transfers between devices: 4.44 us -> 5.9 us  [lon_edges(): lax.ppermute(value, 'lon', [(i, (i - 1) % lon) for i in range(lon)])]
  transfers between devices with their start and end apart: 16 -> 21, of which waited for: 13 -> 13; matrix products, arithmetic and copies ran while one was open for 2% -> 1% of each run, Pallas kernels for 7% -> 9%
where the time goes in v7:
time: 126 us
  waiting for transfers between devices  47.6 us (38%)
  starting transfers between devices  35.6 us (28%)
  Pallas kernels  28.9 us (23%)
  blocking collectives  11.2 us (9%)
    pallas_call x22, Pallas kernels, call(): pl.pallas_call(kernel, out_shape=out_shape, in_specs=[pl.BlockSpec(memory...  28.9 us
    all_to_all x5, waiting for transfers between devices, exchanged(): return lax.all_to_all(blocks, AXES, split_axis=0, concat_axis=0, tiled=True)  24.9 us
    all_to_all x5, starting transfers between devices, exchanged(): return lax.all_to_all(blocks, AXES, split_axis=0, concat_axis=0, tiled=True)  19.3 us
    ppermute x8, waiting for transfers between devices, halving(): lax.ppermute(send, AXES, [(flat(i, j), flat(*partner(i, j))) for i, j in...  13.4 us
    all_to_all x1, blocking collectives, exchanged(): return lax.all_to_all(blocks, AXES, split_axis=0, concat_axis=0, tiled=True)  11.2 us
    ppermute x2, starting transfers between devices, lon_edges(): lax.ppermute(value, 'lon', [(i, (i - 1) % lon) for i in range(lon)])  5.9 us
    ppermute x8, starting transfers between devices, halving(): lax.ppermute(send, AXES, [(flat(i, j), flat(*partner(i, j))) for i, j in...  4.63 us
    ppermute x2, waiting for transfers between devices, lat_edges(): lax.ppermute(jnp.where(lat_at == 0, last, first), 'lat', [(0, 1), (1, 0)])  3.91 us
  transfers between devices with their start and end apart: 21, of which 13 were waited for; matrix products, arithmetic and copies ran while one was open for 1% of the time, Pallas kernels for 9%

profile of v7, /device:TPU:0, one launch (start us, length us, event | category | flops | bytes accessed | tf_op | source)
XLA Modules:
  0.0 125.9 jit_solution(370949745512749275)
XLA Ops:
  0.7 1.8 %shard_map.128 = bf16[32,32,128]{2,1,0:T(8,128)(2,1)} custom-call(bf16[128,512]{1,0:T(8,128)(2,1)} %bitcast.39, f32[12,8,16]{2,1,0:T(8,128)} %bitcast.41), custom_call_target="tpu_custom_call" | custom-call | bytes 524288 | tf_op jit(solution)/shard_map/pallas_call | solution.py:35
  2.5 7.3 %all-to-all-start = ((bf16[32,32,128]{2,1,0:T(8,128)(2,1)}), bf16[32,32,128]{2,1,0:T(8,128)(2,1)S(1)}, u32[]{:S(2)}, u32[]{:S(2)}) async-start(bf16[32,32,128]{2,1,0:T(8,128)(2,1)} %shard_map.128), calls=%async_computation | async-start | bytes 524288 | tf_op jit(solution)/shard_map/all_to_all | solution.py:19
  9.9 1.8 %collective-permute-start = (bf16[3,8,1,512]{3,2,1,0:T(2,128)(2,1)S(1)}, bf16[3,8,1,512]{3,2,1,0:T(2,128)(2,1)S(1)}, u32[]{:S(2)}, u32[]{:S(2)}) collective-permute-start(bf16[3,8,1,512]{3,2,1,0:T(2,128)(2,1)S(1)} %broadcast_select_fusion.2), channel_id=1, source_target_pairs={{0,1},{1,0},{2,3},{3,2},{4,5},{5,4},{6,7},{7,6},{8,9},{9,8},{10,11... | collective-permute-start | bytes 73736 | tf_op jit(solution)/shard_map/ppermute | solution.py:128
  12.5 2.2 %collective-permute-done = bf16[3,8,1,512]{3,2,1,0:T(2,128)(2,1)S(1)} collective-permute-done((bf16[3,8,1,512]{3,2,1,0:T(2,128)(2,1)S(1)}, bf16[3,8,1,512]{3,2,1,0:T(2,128)(2,1)S(1)}, u32[]{:S(2)}, u32[]{:S(2)}) %collective-permute-start) | collective-permute-done | bytes 24608 | tf_op jit(solution)/shard_map/ppermute | solution.py:128
  14.9 5.7 %all-to-all-done = bf16[32,32,128]{2,1,0:T(8,128)(2,1)S(1)} async-done(((bf16[32,32,128]{2,1,0:T(8,128)(2,1)}), bf16[32,32,128]{2,1,0:T(8,128)(2,1)S(1)}, u32[]{:S(2)}, u32[]{:S(2)}) %all-to-all-start) | async-done | bytes 262176 | tf_op jit(solution)/shard_map/all_to_all | solution.py:19
  20.5 1.5 %shard_map.129 = (bf16[16,2,16,128]{3,2,1,0:T(8,128)(2,1)}, bf16[16,2,16,128]{3,2,1,0:T(8,128)(2,1)}) custom-call(s32[3,2]{1,0:T(4,128)} %pad_add_fusion.refs_0_, bf16[16,2,32,128]{3,2,1,0:T(8,128)(2,1)S(1)} %bitcast.18), custom_call_target="tpu_custom_call" | custom-call | flops 4194304 | bytes 1048576 | tf_op jit(solution)/shard_map/pallas_call | solution.py:35
  22.1 2.6 %all-to-all-start.1 = ((bf16[32,16,128]{2,1,0:T(8,128)(2,1)}), bf16[32,16,128]{2,1,0:T(8,128)(2,1)S(1)}, u32[]{:S(2)}, u32[]{:S(2)}) async-start(bf16[32,16,128]{2,1,0:T(8,128)(2,1)} %bitcast.40), calls=%async_computation.1 | async-start | bytes 262144 | tf_op jit(solution)/shard_map/all_to_all | solution.py:19
  25.0 4.4 %collective-permute-start.2 = (bf16[3,1,18,512]{3,2,1,0:T(8,128)(2,1)S(1)}, bf16[3,1,18,512]{3,2,1,0:T(8,128)(2,1)S(1)}, u32[]{:S(2)}, u32[]{:S(2)}) collective-permute-start(bf16[3,1,18,512]{3,2,1,0:T(8,128)(2,1)S(1)} %pad_maximum_fusion.1), channel_id=1, source_target_pairs={{0,30},{2,0},{4,2},{6,4},{8,6},{10,8},{12,10},{14,12},{16,14},{18,... | collective-permute-start | bytes 165896 | tf_op jit(solution)/shard_map/ppermute | solution.py:140
  29.4 3.8 %collective-permute-done.1.low_ref = bf16[3,1,18,512]{3,2,1,0:T(8,128)(2,1)S(1)} collective-permute-done((bf16[3,1,18,512]{3,2,1,0:T(8,128)(2,1)S(1)}, bf16[3,1,18,512]{3,2,1,0:T(8,128)(2,1)S(1)}, u32[]{:S(2)}, u32[]{:S(2)}) %collective-permute-start.1) | collective-permute-done | bytes 55328 | tf_op jit(solution)/shard_map/ppermute | solution.py:139
  33.2 1.7 %shard_map.130 = (bf16[128,512]{1,0:T(8,128)(2,1)}, bf16[512,128]{1,0:T(8,128)(2,1)}, f32[128,128]{1,0:T(8,128)}, bf16[128,1024]{1,0:T(8,128)(2,1)}, bf16[128,10...) custom-call(bf16[3,8,16,512]{3,2,1,0:T(8,128)(2,1)S(1)} %copy-done.1, ...), custom_call_target="tpu_custom_call" | custom-call | flops 134217728 | bytes 4194304 | tf_op jit(solution)/shard_map/pallas_call | solution.py:35
  35.0 2.7 %shard_map.131 = (bf16[512,128]{1,0:T(8,128)(2,1)}, bf16[128,1024]{1,0:T(8,128)(2,1)}, bf16[512,128]{1,0:T(8,128)(2,1)}) custom-call(bf16[512,128]{1,0:T(8,128)(2,1)S(1)} %bitcast.19, bf16[512,1024]{1,0:T(8,128)(2,1)S(1)} %copy-done.2, bf16[512,1024]{1,0:T(8,128)(2,1)S(1)} %copy-done, f32[1,512]{1,0:T(1,128)S(1)} %bitcast.29, ...), custom_call_target="tpu_custom_call" | custom-call | flops 268435456 | bytes 4194304 | tf_op jit(solution)/shard_map/pallas_call | solution.py:35
  37.6 4.1 %all-to-all-start.2 = ((bf16[32,16,128]{2,1,0:T(8,128)(2,1)}), bf16[32,16,128]{2,1,0:T(8,128)(2,1)S(1)}, u32[]{:S(2)}, u32[]{:S(2)}) async-start(bf16[32,16,128]{2,1,0:T(8,128)(2,1)} %bitcast.35), calls=%async_computation.2 | async-start | bytes 262144 | tf_op jit(solution)/shard_map/all_to_all | solution.py:19
  41.9 8.4 %all-to-all-done.2 = bf16[32,16,128]{2,1,0:T(8,128)(2,1)S(1)} async-done(((bf16[32,16,128]{2,1,0:T(8,128)(2,1)}), bf16[32,16,128]{2,1,0:T(8,128)(2,1)S(1)}, u32[]{:S(2)}, u32[]{:S(2)}) %all-to-all-start.2) | async-done | bytes 131104 | tf_op jit(solution)/shard_map/all_to_all | solution.py:19
  50.4 2.1 %shard_map.132 = bf16[16,2,16,128]{3,2,1,0:T(8,128)(2,1)} custom-call(s32[3,2]{1,0:T(4,128)} %pad_add_fusion.refs_0_, bf16[16,2,16,128]{3,2,1,0:T(8,128)(2,1)S(1)} %bitcast.21, f32[16,128]{1,0:T(8,128)S(1)} %pad.4.refs_2_, bf16[16,2,16,128]{3,2,1,0:T(8,128)(2,1)} %get-tuple-element.105.refs_3_), custom_call_target="tpu_custom_call" | custom-call | flops 4194304 | bytes 1048576 | tf_op jit(solution)/shard_map/pallas_call | solution.py:35
  52.5 2.6 %all-to-all-start.3 = ((bf16[32,16,128]{2,1,0:T(8,128)(2,1)}), bf16[32,16,128]{2,1,0:T(8,128)(2,1)S(1)}, u32[]{:S(2)}, u32[]{:S(2)}) async-start(bf16[32,16,128]{2,1,0:T(8,128)(2,1)} %bitcast.36), calls=%async_computation.3 | async-start | bytes 262144 | tf_op jit(solution)/shard_map/all_to_all | solution.py:19
  55.1 1.7 %shard_map.134 = (bf16[128,512]{1,0:T(8,128)(2,1)}, bf16[512,128]{1,0:T(8,128)(2,1)}, f32[128,128]{1,0:T(8,128)}, bf16[128,1024]{1,0:T(8,128)(2,1)}, bf16[128,10...) custom-call(bf16[3,8,16,512]{3,2,1,0:T(8,128)(2,1)S(1)} %copy-done.1, ...), custom_call_target="tpu_custom_call" | custom-call | flops 134217728 | bytes 4194304 | tf_op jit(solution)/shard_map/pallas_call | solution.py:35
  56.8 1.7 %shard_map.133 = (bf16[128,512]{1,0:T(8,128)(2,1)}, bf16[512,128]{1,0:T(8,128)(2,1)}, f32[128,128]{1,0:T(8,128)}, bf16[128,1024]{1,0:T(8,128)(2,1)}, bf16[128,10...) custom-call(bf16[3,8,16,512]{3,2,1,0:T(8,128)(2,1)S(1)} %copy-done.1, ...), custom_call_target="tpu_custom_call" | custom-call | flops 134217728 | bytes 4194304 | tf_op jit(solution)/shard_map/pallas_call | solution.py:35
  58.6 5.1 %all-to-all-done.3 = bf16[32,16,128]{2,1,0:T(8,128)(2,1)S(1)} async-done(((bf16[32,16,128]{2,1,0:T(8,128)(2,1)}), bf16[32,16,128]{2,1,0:T(8,128)(2,1)S(1)}, u32[]{:S(2)}, u32[]{:S(2)}) %all-to-all-start.3) | async-done | bytes 131104 | tf_op jit(solution)/shard_map/all_to_all | solution.py:19
  63.7 2.7 %shard_map.135 = (bf16[512,128]{1,0:T(8,128)(2,1)}, bf16[128,1024]{1,0:T(8,128)(2,1)}, bf16[512,128]{1,0:T(8,128)(2,1)}) custom-call(bf16[512,128]{1,0:T(8,128)(2,1)S(1)} %bitcast.20, bf16[512,1024]{1,0:T(8,128)(2,1)S(1)} %copy-done.2, bf16[512,1024]{1,0:T(8,128)(2,1)S(1)} %copy-done, f32[1,512]{1,0:T(1,128)S(1)} %bitcast.32, ...), custom_call_target="tpu_custom_call" | custom-call | flops 268435456 | bytes 4194304 | tf_op jit(solution)/shard_map/pallas_call | solution.py:35
  66.4 11.2 %all_to_all.30 = bf16[32,16,128]{2,1,0:T(8,128)(2,1)S(1)} all-to-all(bf16[32,16,128]{2,1,0:T(8,128)(2,1)} %bitcast.37), channel_id=1, replica_groups=mesh['lon'=16,'lat'=2] {'lon','lat'}, dimensions={0} | all-to-all | bytes 262144 | tf_op jit(solution)/shard_map/all_to_all | solution.py:19
  77.6 2.1 %shard_map.136 = bf16[16,2,16,128]{3,2,1,0:T(8,128)(2,1)} custom-call(s32[3,2]{1,0:T(4,128)} %pad_add_fusion.refs_0_, bf16[16,2,16,128]{3,2,1,0:T(8,128)(2,1)S(1)} %bitcast.22, f32[16,128]{1,0:T(8,128)S(1)} %pad.4.refs_2_, bf16[16,2,16,128]{3,2,1,0:T(8,128)(2,1)} %get-tuple-element.105.refs_3_), custom_call_target="tpu_custom_call" | custom-call | flops 4194304 | bytes 1048576 | tf_op jit(solution)/shard_map/pallas_call | solution.py:35
  79.7 2.8 %all-to-all-start.5 = ((bf16[32,16,128]{2,1,0:T(8,128)(2,1)}), bf16[32,16,128]{2,1,0:T(8,128)(2,1)S(1)}, u32[]{:S(2)}, u32[]{:S(2)}) async-start(bf16[32,16,128]{2,1,0:T(8,128)(2,1)} %bitcast.38), calls=%async_computation.5 | async-start | bytes 262144 | tf_op jit(solution)/shard_map/all_to_all | solution.py:19
  82.5 2.7 %shard_map.137.sums_ref = f32[16,512]{1,0:T(8,128)S(1)} custom-call(bf16[512,1024]{1,0:T(8,128)(2,1)S(1)} %copy-done, f32[1,512]{1,0:T(1,128)S(1)} %bitcast.33, bf16[10,32,512]{2,1,0:T(8,128)(2,1)} %get-tuple-element.126.refs_0_, bf16[512,128]{1,0:T(8,128)(2,1)} %get-tuple-element.104.refs_1_, bf16[128,1024]{1,0:T(8,128)(2,1)} %get-tuple-element.127.refs_2_.refs_7_, ...), custom_call_target="tpu_custom_call" | custom-call | bytes 2097152 | tf_op jit(solution)/shard_map/pallas_call | solution.py:35
  85.2 5.7 %all-to-all-done.5 = bf16[32,16,128]{2,1,0:T(8,128)(2,1)S(1)} async-done(((bf16[32,16,128]{2,1,0:T(8,128)(2,1)}), bf16[32,16,128]{2,1,0:T(8,128)(2,1)S(1)}, u32[]{:S(2)}, u32[]{:S(2)}) %all-to-all-start.5) | async-done | bytes 131104 | tf_op jit(solution)/shard_map/all_to_all | solution.py:19
  90.9 3.0 %shard_map.138 = (bf16[128,512]{1,0:T(8,128)(2,1)S(1)}, f32[16,512]{1,0:T(8,128)S(1)}, bf16[544,512]{1,0:T(8,128)(2,1)S(1)}, bf16[4,128,512]{2,1,0:T(8,128)(2,1)S(1)}) custom-call(bf16[512,128]{1,0:T(8,128)(2,1)S(1)} %bitcast.26, bf16[512,1024]{1,0:T(8,128)(2,1)S(1)} %copy-done.2, bf16[512,1024]{1,0:T(8,128)(2,1)S(1)} %copy-done, f32[1,512]{1,0:T(1,128)S(1)} %bitcast.34, ...), custom_call_target="tpu_custom_call" | custom-call | flops 1073741824 | bytes 6291456 | tf_op jit(solution)/shard_map/pallas_call | solution.py:35
  94.0 2.0 %shard_map.139 = (bf16[512,512]{1,0:T(8,128)(2,1)S(1)}, bf16[4,128,512]{2,1,0:T(8,128)(2,1)S(1)}) custom-call(bf16[512,128]{1,0:T(8,128)(2,1)S(1)} %bitcast.27, bf16[512,128]{1,0:T(8,128)(2,1)} %get-tuple-element.144.refs_0_, bf16[512,128]{1,0:T(8,128)(2,1)} %get-tuple-element.145.refs_1_, bf16[128,1024]{1,0:T(8,128)(2,1)} %get-tuple-element.146.refs_2_, ...), custom_call_target="tpu_custom_call" | custom-call | flops 536870912 | bytes 2097152 | tf_op jit(solution)/shard_map/pallas_call | solution.py:35
  99.1 1.7 %collective-permute-done.4 = bf16[1,8,1,512]{3,2,1,0:T(2,128)(2,1)S(1)} collective-permute-done((bf16[1,8,1,512]{3,2,1,0:T(2,128)(2,1)S(1)}, bf16[1,8,1,512]{3,2,1,0:T(2,128)(2,1)S(1)}, u32[]{:S(2)}, u32[]{:S(2)}) %collective-permute-start.4) | collective-permute-done | bytes 8224 | tf_op jit(solution)/shard_map/ppermute | solution.py:128
  100.8 4.7 %collective-permute-done.8.refs_2_ = bf16[288,512]{1,0:T(8,128)(2,1)S(1)} collective-permute-done((bf16[288,512]{1,0:T(8,128)(2,1)S(1)}, bf16[288,512]{1,0:T(8,128)(2,1)S(1)}, u32[]{:S(2)}, u32[]{:S(2)}) %collective-permute-start.8) | collective-permute-done | bytes 294944 | tf_op jit(solution)/shard_map/ppermute | solution.py:743
  106.8 5.5 %collective-permute-done.9.refs_3_ = bf16[192,512]{1,0:T(8,128)(2,1)S(1)} collective-permute-done((bf16[192,512]{1,0:T(8,128)(2,1)S(1)}, bf16[192,512]{1,0:T(8,128)(2,1)S(1)}, u32[]{:S(2)}, u32[]{:S(2)}) %collective-permute-start.9) | collective-permute-done | bytes 196640 | tf_op jit(solution)/shard_map/ppermute | solution.py:743
  112.5 2.1 %collective-permute-start.14 = (bf16[64,512]{1,0:T(8,128)(2,1)S(1)}, bf16[64,512]{1,0:T(8,128)(2,1)S(1)}, u32[]{:S(2)}, u32[]{:S(2)}) collective-permute-start(bf16[64,512]{1,0:T(8,128)(2,1)S(1)} %get-tuple-element.172), channel_id=1, source_target_pairs={{0,8},{1,9},{2,10},{3,11},{4,12},{5,13},{6,14},{7,15},{8,0},{9,1},... | collective-permute-start | bytes 196616 | tf_op jit(solution)/shard_map/ppermute | solution.py:743
  114.7 2.4 %collective-permute-done.11.refs_2_ = bf16[96,512]{1,0:T(8,128)(2,1)S(1)} collective-permute-done((bf16[96,512]{1,0:T(8,128)(2,1)S(1)}, bf16[96,512]{1,0:T(8,128)(2,1)S(1)}, u32[]{:S(2)}, u32[]{:S(2)}) %collective-permute-start.11) | collective-permute-done | bytes 98336 | tf_op jit(solution)/shard_map/ppermute | solution.py:743
  117.8 2.4 %collective-permute-start.15 = (bf16[32,512]{1,0:T(8,128)(2,1)S(1)}, bf16[32,512]{1,0:T(8,128)(2,1)S(1)}, u32[]{:S(2)}, u32[]{:S(2)}) collective-permute-start(bf16[32,512]{1,0:T(8,128)(2,1)S(1)} %get-tuple-element.180), channel_id=1, source_target_pairs={{0,16},{1,17},{2,18},{3,19},{4,20},{5,21},{6,22},{7,23},{8,24},{9,... | collective-permute-start | bytes 98312 | tf_op jit(solution)/shard_map/ppermute | solution.py:752
  (67 shorter events, 12.3 us)
Async XLA Ops:
  0.6 9.2 %copy-start.1 = (bf16[3,8,16,512]{3,2,1,0:T(8,128)(2,1)S(1)}, bf16[3,8,16,512]{3,2,1,0:T(8,128)(2,1)}, u32[]{:S(2)}) copy-start(bf16[3,8,16,512]{3,2,1,0:T(8,128)(2,1)} %states_ref.5) | copy-start | bytes 1179652
  0.6 11.1 %copy-start.5 = (s32[3,4]{1,0:T(4,128)S(1)}, s32[3,4]{1,0:T(4,128)}, u32[]{:S(2)}) copy-start(s32[3,4]{1,0:T(4,128)} %param.17) | copy-start | bytes 148
  0.7 11.1 %copy-start.6 = (s32[3,4]{1,0:T(4,128)S(1)}, s32[3,4]{1,0:T(4,128)}, u32[]{:S(2)}) copy-start(s32[3,4]{1,0:T(4,128)} %param.16) | copy-start | bytes 148
  2.5 30.7 %copy-start = (bf16[512,1024]{1,0:T(8,128)(2,1)S(1)}, bf16[512,1024]{1,0:T(8,128)(2,1)}, u32[]{:S(2)}) copy-start(bf16[512,1024]{1,0:T(8,128)(2,1)} %up_ref.13) | copy-start | bytes 3145732
  2.5 18.0 %all-to-all-start = ((bf16[32,32,128]{2,1,0:T(8,128)(2,1)}), bf16[32,32,128]{2,1,0:T(8,128)(2,1)S(1)}, u32[]{:S(2)}, u32[]{:S(2)}) async-start(bf16[32,32,128]{2,1,0:T(8,128)(2,1)} %shard_map.128), calls=%async_computation | async-start | bytes 524288 | tf_op jit(solution)/shard_map/all_to_all | solution.py:19
  9.9 4.8 %collective-permute-start = (bf16[3,8,1,512]{3,2,1,0:T(2,128)(2,1)S(1)}, bf16[3,8,1,512]{3,2,1,0:T(2,128)(2,1)S(1)}, u32[]{:S(2)}, u32[]{:S(2)}) collective-permute-start(bf16[3,8,1,512]{3,2,1,0:T(2,128)(2,1)S(1)} %broadcast_select_fusion.2), channel_id=1, source_target_pairs={{0,1},{1,0},{2,3},{3,2},{4,5},{5,4},{6,7},{7,6},{8,9},{9,8},{10,11... | collective-permute-start | bytes 73736 | tf_op jit(solution)/shard_map/ppermute | solution.py:128
  22.1 11.2 %copy-start.3 = (f32[3,3,512]{2,1,0:T(4,128)S(1)}, f32[3,3,512]{2,1,0:T(4,128)}, u32[]{:S(2)}) copy-start(f32[3,3,512]{2,1,0:T(4,128)} %kernel_ref.7) | copy-start | bytes 55300
  22.1 11.2 %copy-start.4 = (f32[512]{0:T(512)S(1)}, f32[512]{0:T(512)}, u32[]{:S(2)}) copy-start(f32[512]{0:T(512)} %param.13) | copy-start | bytes 6148
  22.1 12.9 %all-to-all-start.1 = ((bf16[32,16,128]{2,1,0:T(8,128)(2,1)}), bf16[32,16,128]{2,1,0:T(8,128)(2,1)S(1)}, u32[]{:S(2)}, u32[]{:S(2)}) async-start(bf16[32,16,128]{2,1,0:T(8,128)(2,1)} %bitcast.40), calls=%async_computation.1 | async-start | bytes 262144 | tf_op jit(solution)/shard_map/all_to_all | solution.py:19
  24.7 10.3 %copy-start.2 = (bf16[512,1024]{1,0:T(8,128)(2,1)S(1)}, bf16[512,1024]{1,0:T(8,128)(2,1)}, u32[]{:S(2)}) copy-start(bf16[512,1024]{1,0:T(8,128)(2,1)} %down_ref.5) | copy-start | bytes 3145732
  24.8 8.4 %collective-permute-start.1 = (bf16[3,1,18,512]{3,2,1,0:T(8,128)(2,1)S(1)}, bf16[3,1,18,512]{3,2,1,0:T(8,128)(2,1)S(1)}, u32[]{:S(2)}, u32[]{:S(2)}) collective-permute-start(bf16[3,1,18,512]{3,2,1,0:T(8,128)(2,1)S(1)} %pad_maximum_fusion), channel_id=1, source_target_pairs={{0,2},{2,4},{4,6},{6,8},{8,10},{10,12},{12,14},{14,16},{16,18},{18... | collective-permute-start | bytes 165896 | tf_op jit(solution)/shard_map/ppermute | solution.py:139
  25.0 8.2 %collective-permute-start.2 = (bf16[3,1,18,512]{3,2,1,0:T(8,128)(2,1)S(1)}, bf16[3,1,18,512]{3,2,1,0:T(8,128)(2,1)S(1)}, u32[]{:S(2)}, u32[]{:S(2)}) collective-permute-start(bf16[3,1,18,512]{3,2,1,0:T(8,128)(2,1)S(1)} %pad_maximum_fusion.1), channel_id=1, source_target_pairs={{0,30},{2,0},{4,2},{6,4},{8,6},{10,8},{12,10},{14,12},{16,14},{18,... | collective-permute-start | bytes 165896 | tf_op jit(solution)/shard_map/ppermute | solution.py:140
  37.6 12.7 %all-to-all-start.2 = ((bf16[32,16,128]{2,1,0:T(8,128)(2,1)}), bf16[32,16,128]{2,1,0:T(8,128)(2,1)S(1)}, u32[]{:S(2)}, u32[]{:S(2)}) async-start(bf16[32,16,128]{2,1,0:T(8,128)(2,1)} %bitcast.35), calls=%async_computation.2 | async-start | bytes 262144 | tf_op jit(solution)/shard_map/all_to_all | solution.py:19
  52.5 11.2 %all-to-all-start.3 = ((bf16[32,16,128]{2,1,0:T(8,128)(2,1)}), bf16[32,16,128]{2,1,0:T(8,128)(2,1)S(1)}, u32[]{:S(2)}, u32[]{:S(2)}) async-start(bf16[32,16,128]{2,1,0:T(8,128)(2,1)} %bitcast.36), calls=%async_computation.3 | async-start | bytes 262144 | tf_op jit(solution)/shard_map/all_to_all | solution.py:19
  79.7 11.2 %all-to-all-start.5 = ((bf16[32,16,128]{2,1,0:T(8,128)(2,1)}), bf16[32,16,128]{2,1,0:T(8,128)(2,1)S(1)}, u32[]{:S(2)}, u32[]{:S(2)}) async-start(bf16[32,16,128]{2,1,0:T(8,128)(2,1)} %bitcast.38), calls=%async_computation.5 | async-start | bytes 262144 | tf_op jit(solution)/shard_map/all_to_all | solution.py:19
  94.0 2.1 %collective-permute-start.3 = (bf16[544,512]{1,0:T(8,128)(2,1)S(1)}, bf16[544,512]{1,0:T(8,128)(2,1)S(1)}, u32[]{:S(2)}, u32[]{:S(2)}) collective-permute-start(bf16[544,512]{1,0:T(8,128)(2,1)S(1)} %get-tuple-element.143), channel_id=1, source_target_pairs={{0,2},{1,3},{2,0},{3,1},{4,6},{5,7},{6,4},{7,5},{8,10},{9,11},{10,... | collective-permute-start | bytes 1671176 | tf_op jit(solution)/shard_map/ppermute | solution.py:743
  96.2 2.1 %collective-permute-start.5 = (bf16[512,512]{1,0:T(8,128)(2,1)S(1)}, bf16[512,512]{1,0:T(8,128)(2,1)S(1)}, u32[]{:S(2)}, u32[]{:S(2)}) collective-permute-start(bf16[512,512]{1,0:T(8,128)(2,1)S(1)} %get-tuple-element.154), channel_id=1, source_target_pairs={{0,2},{1,3},{2,0},{3,1},{4,6},{5,7},{6,4},{7,5},{8,10},{9,11},{10,... | collective-permute-start | bytes 1572872 | tf_op jit(solution)/shard_map/ppermute | solution.py:743
  96.8 8.7 %collective-permute-start.8 = (bf16[288,512]{1,0:T(8,128)(2,1)S(1)}, bf16[288,512]{1,0:T(8,128)(2,1)S(1)}, u32[]{:S(2)}, u32[]{:S(2)}) collective-permute-start(bf16[288,512]{1,0:T(8,128)(2,1)S(1)} %get-tuple-element.151), channel_id=1, source_target_pairs={{0,4},{1,5},{2,3},{3,2},{4,0},{5,1},{6,7},{7,6},{8,12},{9,13},{10,... | collective-permute-start | bytes 884744 | tf_op jit(solution)/shard_map/ppermute | solution.py:743
  96.8 4.0 %collective-permute-start.4 = (bf16[1,8,1,512]{3,2,1,0:T(2,128)(2,1)S(1)}, bf16[1,8,1,512]{3,2,1,0:T(2,128)(2,1)S(1)}, u32[]{:S(2)}, u32[]{:S(2)}) collective-permute-start(bf16[1,8,1,512]{3,2,1,0:T(2,128)(2,1)S(1)} %broadcast_select_fusion.5), channel_id=1, source_target_pairs={{0,1},{1,0},{2,3},{3,2},{4,5},{5,4},{6,7},{7,6},{8,9},{9,8},{10,11... | collective-permute-start | bytes 24584 | tf_op jit(solution)/shard_map/ppermute | solution.py:128
  98.4 7.5 %collective-permute-start.10 = (bf16[256,512]{1,0:T(8,128)(2,1)S(1)}, bf16[256,512]{1,0:T(8,128)(2,1)S(1)}, u32[]{:S(2)}, u32[]{:S(2)}) collective-permute-start(bf16[256,512]{1,0:T(8,128)(2,1)S(1)} %get-tuple-element.155), channel_id=1, source_target_pairs={{0,1},{1,0},{2,6},{3,7},{4,5},{5,4},{6,2},{7,3},{8,9},{9,8},{10,14... | collective-permute-start | bytes 786440 | tf_op jit(solution)/shard_map/ppermute | solution.py:743
  105.6 6.8 %collective-permute-start.9 = (bf16[192,512]{1,0:T(8,128)(2,1)S(1)}, bf16[192,512]{1,0:T(8,128)(2,1)S(1)}, u32[]{:S(2)}, u32[]{:S(2)}) collective-permute-start(bf16[192,512]{1,0:T(8,128)(2,1)S(1)} %get-tuple-element.162), channel_id=1, source_target_pairs={{0,1},{1,0},{2,6},{3,7},{4,5},{5,4},{6,2},{7,3},{8,9},{9,8},{10,14... | collective-permute-start | bytes 589832 | tf_op jit(solution)/shard_map/ppermute | solution.py:743
  106.0 6.5 %collective-permute-start.12 = (bf16[128,512]{1,0:T(8,128)(2,1)S(1)}, bf16[128,512]{1,0:T(8,128)(2,1)S(1)}, u32[]{:S(2)}, u32[]{:S(2)}) collective-permute-start(bf16[128,512]{1,0:T(8,128)(2,1)S(1)} %get-tuple-element.165), channel_id=1, source_target_pairs={{0,4},{1,5},{2,3},{3,2},{4,0},{5,1},{6,7},{7,6},{8,12},{9,13},{10,... | collective-permute-start | bytes 393224 | tf_op jit(solution)/shard_map/ppermute | solution.py:743
  112.4 4.7 %collective-permute-start.11 = (bf16[96,512]{1,0:T(8,128)(2,1)S(1)}, bf16[96,512]{1,0:T(8,128)(2,1)S(1)}, u32[]{:S(2)}, u32[]{:S(2)}) collective-permute-start(bf16[96,512]{1,0:T(8,128)(2,1)S(1)} %get-tuple-element.169), channel_id=1, source_target_pairs={{0,8},{1,9},{2,10},{3,11},{4,12},{5,13},{6,14},{7,15},{8,0},{9,1},... | collective-permute-start | bytes 294920 | tf_op jit(solution)/shard_map/ppermute | solution.py:743
  112.5 5.2 %collective-permute-start.14 = (bf16[64,512]{1,0:T(8,128)(2,1)S(1)}, bf16[64,512]{1,0:T(8,128)(2,1)S(1)}, u32[]{:S(2)}, u32[]{:S(2)}) collective-permute-start(bf16[64,512]{1,0:T(8,128)(2,1)S(1)} %get-tuple-element.172), channel_id=1, source_target_pairs={{0,8},{1,9},{2,10},{3,11},{4,12},{5,13},{6,14},{7,15},{8,0},{9,1},... | collective-permute-start | bytes 196616 | tf_op jit(solution)/shard_map/ppermute | solution.py:743
  114.6 7.1 %collective-permute-start.6 = (bf16[1,1,18,512]{3,2,1,0:T(8,128)(2,1)S(1)}, bf16[1,1,18,512]{3,2,1,0:T(8,128)(2,1)S(1)}, u32[]{:S(2)}, u32[]{:S(2)}) collective-permute-start(bf16[1,1,18,512]{3,2,1,0:T(8,128)(2,1)S(1)} %pad_maximum_fusion.2), channel_id=1, source_target_pairs={{0,2},{2,4},{4,6},{6,8},{8,10},{10,12},{12,14},{14,16},{16,18},{18... | collective-permute-start | bytes 55304 | tf_op jit(solution)/shard_map/ppermute | solution.py:139
  117.1 7.3 %collective-permute-start.13 = (bf16[64,512]{1,0:T(8,128)(2,1)S(1)}, bf16[64,512]{1,0:T(8,128)(2,1)S(1)}, u32[]{:S(2)}, u32[]{:S(2)}) collective-permute-start(bf16[64,512]{1,0:T(8,128)(2,1)S(1)} %get-tuple-element.176), channel_id=1, source_target_pairs={{0,16},{1,17},{2,18},{3,19},{4,20},{5,21},{6,22},{7,23},{8,24},{9,... | collective-permute-start | bytes 196616 | tf_op jit(solution)/shard_map/ppermute | solution.py:752
  117.8 6.6 %collective-permute-start.15 = (bf16[32,512]{1,0:T(8,128)(2,1)S(1)}, bf16[32,512]{1,0:T(8,128)(2,1)S(1)}, u32[]{:S(2)}, u32[]{:S(2)}) collective-permute-start(bf16[32,512]{1,0:T(8,128)(2,1)S(1)} %get-tuple-element.180), channel_id=1, source_target_pairs={{0,16},{1,17},{2,18},{3,19},{4,20},{5,21},{6,22},{7,23},{8,24},{9,... | collective-permute-start | bytes 98312 | tf_op jit(solution)/shard_map/ppermute | solution.py:752
  120.2 3.0 %collective-permute-start.7 = (bf16[1,1,18,512]{3,2,1,0:T(8,128)(2,1)S(1)}, bf16[1,1,18,512]{3,2,1,0:T(8,128)(2,1)S(1)}, u32[]{:S(2)}, u32[]{:S(2)}) collective-permute-start(bf16[1,1,18,512]{3,2,1,0:T(8,128)(2,1)S(1)} %pad_maximum_fusion.3), channel_id=1, source_target_pairs={{0,30},{2,0},{4,2},{6,4},{8,6},{10,8},{12,10},{14,12},{16,14},{18,... | collective-permute-start | bytes 55304 | tf_op jit(solution)/shard_map/ppermute | solution.py:140

commit v8 on v7

--- a/solution.py
+++ b/solution.py
@@ -74,6 +74,10 @@
     parts = parts.astype(jnp.float32)
     total = (parts[:SUMS] + parts[SUMS : 2 * SUMS]) + parts[2 * SUMS : 3 * SUMS]
     return jnp.concatenate([total, jnp.zeros((ROWS - SUMS, parts.shape[1]), jnp.float32)], axis=0)
+
+
+def after(value, first):
+    return lax.optimization_barrier((value, first))[0]
 
 
 def pack_kernel(cotangent_hbm, weight_hbm, out_hbm, cotangent_ref, weight_ref, out_ref, sems):
@@ -145,17 +149,15 @@
 MARGIN = 8
 
 
-def forward_kernel(
-    step, states_ref, before_ref, after_ref, low_ref, high_ref, kernel_ref, gain_ref, up_ref,
-    n_hbm, turned_hbm, inv_hbm, hid_hbm, slope_hbm, pad_hbm,
-    n_ref, turned_ref, inv_ref, hid_ref, slope_ref, pad_ref, wide_ref, sems,
-):
+def forward_math(step, places, sems, leaving, outs):
+    states_ref, before_ref, after_ref, low_ref, high_ref, kernel_ref, gain_ref, up_ref = places
+    n_ref, turned_ref, inv_ref, hid_ref, slope_ref, pad_ref, wide_ref = outs
     rows_out, cols_out, channels = states_ref.shape[1:]
     count = rows_out * cols_out
     mixed = states_ref[step].astype(jnp.float32)
     fill_margins(wide_ref, before_ref[step], after_ref[step], low_ref[step], high_ref[step], mixed)
     pad_ref[...] = wide_ref[...].astype(jnp.bfloat16)
-    leaving = copies(sems, 1, [(pad_ref, pad_hbm)])
+    leaving("pad")
     for col_tap in range(3):
         place = MARGIN - 1 + col_tap
         shifted_cols = wide_ref[:, place : place + cols_out]
@@ -167,22 +169,44 @@
     narrow = mixed * inv_root * gain_ref[...]
     n_ref[...] = narrow.astype(jnp.bfloat16)
     inv_ref[...] = jnp.broadcast_to(inv_root, inv_ref.shape)
-    leaving += copies(sems, 2, [(n_ref, n_hbm), (inv_ref, inv_hbm)])
+    leaving("n", "inv")
     pre = jnp.dot(n_ref[...], up_ref[...], preferred_element_type=jnp.float32)
     sigmoid = jax.nn.sigmoid(pre)
     slope_ref[...] = (sigmoid * (1.0 + pre * (1.0 - sigmoid))).astype(jnp.bfloat16)
-    leaving += copies(sems, 4, [(slope_ref, slope_hbm)])
+    leaving("slope")
     hid_ref[...] = (pre * sigmoid).astype(jnp.bfloat16)
     turned_ref[...] = narrow.T.astype(jnp.bfloat16)
-    finish(leaving + copies(sems, 5, [(hid_ref, hid_hbm), (turned_ref, turned_hbm)]))
-
-
-def forward_parts(step, states, around, kernel, norm_gain, w_up):
+    leaving("hid", "turned")
+
+
+FORWARD = ("n", "turned", "inv", "hid", "slope", "pad")
+
+
+def sender(sems, refs, goals, started):
+    names = list(goals)
+
+    def leave(*which):
+        for name in which:
+            if name in goals:
+                started.extend(copies(sems, names.index(name), [(refs[name], goals[name])]))
+
+    return leave
+
+
+def forward_kernel(step, *refs):
+    places, goals, outs, sems = refs[:8], refs[8:14], refs[14:21], refs[21]
+    started = []
+    leave = sender(sems, dict(zip(FORWARD, outs)), dict(zip(FORWARD, goals)), started)
+    forward_math(step, places, sems, leave, outs)
+    finish(started)
+
+
+def forward_shapes(states, w_up):
     _, rows_out, cols_out, channels = states.shape
     hid = w_up.shape[1]
     count = rows_out * cols_out
     wide = (rows_out + 2, cols_out + 2 * MARGIN, channels)
-    shapes = [
+    return [
         ((count, channels), jnp.bfloat16),
         ((channels, count), jnp.bfloat16),
         ((count, 128), jnp.float32),
@@ -190,44 +214,105 @@
         ((count, hid), jnp.bfloat16),
         (wide, jnp.bfloat16),
     ]
+
+
+def forward_scratch(shapes):
+    scratch = [pltpu.VMEM(*shape) for shape in shapes]
+    return scratch + [pltpu.VMEM(shapes[-1][0], jnp.float32)]
+
+
+def forward_parts(step, states, around, kernel, norm_gain, w_up):
+    shapes = forward_shapes(states, w_up)
     return call(
         functools.partial(forward_kernel, step),
         [jax.ShapeDtypeStruct(*shape) for shape in shapes],
         [states, *around, kernel, norm_gain, w_up],
         "vvvvvvvv",
         "hhhhhh",
-        scratch=[pltpu.VMEM(*shape) for shape in shapes]
-        + [pltpu.VMEM(wide, jnp.float32), pltpu.SemaphoreType.DMA((7,))],
-        flops=2 * count * hid * channels,
+        scratch=forward_scratch(shapes) + [pltpu.SemaphoreType.DMA((6,))],
+        flops=2**27,
         moved=2**22,
         limit=12,
     )
 
 
-def transposed(value):
-    return value.astype(jnp.float32).T.astype(jnp.bfloat16)
-
-
 LANES_BOTH = (((1,), (1,)), ((), ()))
 
 
-def network_kernel(moved_ref, down_ref, up_ref, gain_ref, slope_hbm, n_hbm, inv_hbm, out_hbm, grad_hbm, saved_hbm, *refs):
-    slope_ref, n_ref, inv_ref, out_ref, grad_ref, sems = refs
-    arriving = copies(sems, 0, [(slope_hbm, slope_ref), (n_hbm, n_ref), (inv_hbm, inv_ref)])
-    leaving = copies(sems, 3, [(moved_ref, saved_hbm)])
+def fetch_kernel(*refs):
+    count = len(refs) // 2
+    *pairs, sems = refs
+    finish(copies(sems, 0, list(zip(pairs[:count], pairs[count:]))))
+
+
+def fetched(values, first):
+    values = after(values, first)
+    return call(
+        fetch_kernel,
+        [jax.ShapeDtypeStruct(value.shape, value.dtype) for value in values],
+        values,
+        "h" * len(values),
+        "v" * len(values),
+        scratch=[pltpu.SemaphoreType.DMA((len(values),))],
+        moved=2**19,
+    )
+
+
+def network_math(moved_ref, down_ref, up_ref, gain_ref, slope_ref, n_ref, inv_ref, out_ref, grad_ref, leave):
+    leave("moved")
     moved = moved_ref[...].astype(jnp.float32).T
     grad_hidden = jnp.dot(moved.astype(jnp.bfloat16), down_ref[...], preferred_element_type=jnp.float32)
-    arriving[0].wait()
     grad_pre = (grad_hidden * slope_ref[...].astype(jnp.float32)).astype(jnp.bfloat16)
     grad_ref[...] = grad_pre
-    leaving += copies(sems, 4, [(grad_ref, grad_hbm)])
+    leave("grad")
     grad_n = lax.dot_general(grad_pre, up_ref[...], LANES_BOTH, preferred_element_type=jnp.float32)
-    finish(arriving[1:])
     narrow, gain = n_ref[...].astype(jnp.float32), gain_ref[...]
     mean = jnp.mean(grad_n * narrow, axis=1, keepdims=True)
     field = moved + inv_ref[:, :1] * (grad_n * gain - narrow * (mean / gain))
     out_ref[...] = field.T.astype(jnp.bfloat16)
-    finish(leaving + copies(sems, 5, [(out_ref, out_hbm)]))
+    leave("field")
+
+
+def network_kernel(moved_ref, down_ref, up_ref, gain_ref, slope_ref, n_ref, inv_ref, *refs):
+    *goals, out_ref, grad_ref, sems = refs
+    started = []
+    names = ("field", "grad", "moved")
+    leave = sender(sems, dict(zip(names, (out_ref, grad_ref, moved_ref))), dict(zip(names, goals)), started)
+    network_math(moved_ref, down_ref, up_ref, gain_ref, slope_ref, n_ref, inv_ref, out_ref, grad_ref, leave)
+    finish(started)
+
+
+def first_kernel(step, *refs):
+    (moved_ref, down_ref), places, refs = refs[:2], refs[2:10], refs[10:]
+    goals, outs, (out_ref, grad_ref, sems) = refs[:7], refs[7:14], refs[14:]
+    started = []
+    names = ("n", "turned", "hid", "pad", "field", "grad", "moved")
+    values = dict(zip(FORWARD, outs)) | {"field": out_ref, "grad": grad_ref, "moved": moved_ref}
+    leave = sender(sems, values, dict(zip(names, goals)), started)
+    forward_math(step, places, sems, leave, outs)
+    n_ref, _, inv_ref, _, slope_ref = outs[:5]
+    gain_ref, up_ref = places[6:]
+    network_math(moved_ref, down_ref, up_ref, gain_ref, slope_ref, n_ref, inv_ref, out_ref, grad_ref, leave)
+    finish(started)
+
+
+def first_step(step, moved, w_down, states, around, kernel, norm_gain, w_up):
+    shapes = forward_shapes(states, w_up)
+    channels, count = moved.shape
+    hid = w_down.shape[1]
+    backs = [((channels, count), jnp.bfloat16), ((count, hid), jnp.bfloat16), ((channels, count), jnp.bfloat16)]
+    results = [shapes[k] for k in (0, 1, 3, 5)] + backs
+    return call(
+        functools.partial(first_kernel, step),
+        [jax.ShapeDtypeStruct(*shape) for shape in results],
+        [moved, w_down, states, *around, kernel, norm_gain, w_up],
+        "v" * 10,
+        "h" * 7,
+        scratch=forward_scratch(shapes) + [pltpu.VMEM(*shape) for shape in backs[:2]] + [pltpu.SemaphoreType.DMA((7,))],
+        flops=2**28,
+        moved=2**22,
+        limit=16,
+    )
 
 
 def network_back(moved, w_down, w_up, norm_gain, slope, narrow, inv_root):
@@ -238,14 +323,12 @@
         network_kernel,
         [jax.ShapeDtypeStruct(*shape) for shape in shapes],
         [moved, w_down, w_up, norm_gain, slope, narrow, inv_root],
-        "vvvvhhh",
+        "vvvvvvv",
         "hhh",
-        scratch=[pltpu.VMEM(value.shape, value.dtype) for value in (slope, narrow, inv_root)]
-        + [pltpu.VMEM(*shape) for shape in shapes[:2]]
-        + [pltpu.SemaphoreType.DMA((6,))],
+        scratch=[pltpu.VMEM(*shape) for shape in shapes[:2]] + [pltpu.SemaphoreType.DMA((3,))],
         flops=4 * count * hid * channels,
         moved=4 * 2**20,
-        limit=12,
+        limit=8,
     )
 
 
@@ -344,22 +427,17 @@
 
 
 def last_kernel(steps, tile, moved_ref, down_ref, up_ref, gain_ref, sums_ref, *refs):
-    slope_hbm, n_hbm, inv_hbm, pad_hbm, *refs = refs
+    slope_ref, n_ref, inv_ref, pad_ref, *refs = refs
     inputs, refs = refs[: 2 * steps - 1], refs[2 * steps - 1 :]
-    field_ref, total_ref, send_ref, keep_ref, slope_ref, n_ref, inv_ref, pad_ref, left_ref, right_ref, sems = refs
-    arriving = copies(
-        sems, 0, [(slope_hbm, slope_ref), (n_hbm, n_ref), (inv_hbm, inv_ref), (pad_hbm, pad_ref)]
-    )
+    field_ref, total_ref, send_ref, keep_ref, left_ref, right_ref, sems = refs
     count = slope_ref.shape[0]
     pairs = side_by_side(inputs[:steps], left_ref, 1) + side_by_side(inputs[steps:], right_ref, 0)
-    later = copies(sems, 4, pairs)
+    later = copies(sems, 0, pairs)
     moved = moved_ref[...].astype(jnp.float32).T
     grad_hidden = jnp.dot(moved.astype(jnp.bfloat16), down_ref[...], preferred_element_type=jnp.float32)
-    arriving[0].wait()
     grad_pre = (grad_hidden * slope_ref[...].astype(jnp.float32)).astype(jnp.bfloat16)
     right_ref[(steps - 1) * count :] = grad_pre
     grad_n = lax.dot_general(grad_pre, up_ref[...], LANES_BOTH, preferred_element_type=jnp.float32)
-    finish(arriving[1:])
     narrow, gain = n_ref[...].astype(jnp.float32), gain_ref[...]
     term = grad_n * narrow
     mean = jnp.mean(term, axis=1, keepdims=True)
@@ -374,14 +452,13 @@
         send_ref[left_ref.shape[0] :] = pieces_of(total)
 
 
-def last_step(tile, moved, w_down, w_up, norm_gain, sums, forward, grads):
-    steps = len(forward)
+def last_step(tile, moved, w_down, w_up, norm_gain, sums, near, turned, grads):
+    steps = len(turned)
     channels, count = moved.shape
     hid = w_down.shape[1]
-    narrow, _, inv_root, _, slope, pad = forward[-1]
     send, keep = quadrant_shapes(channels, hid, 1)
     sds = jax.ShapeDtypeStruct
-    inputs = [parts[1] for parts in forward] + grads
+    inputs = turned + grads
     return call(
         functools.partial(last_kernel, steps, tile),
         [
@@ -390,12 +467,11 @@
             sds(send, jnp.bfloat16),
             sds(keep, jnp.bfloat16),
         ],
-        [moved, w_down, w_up, norm_gain, sums, slope, narrow, inv_root, pad, *inputs],
-        "vvvvv" + "h" * (4 + len(inputs)),
+        [moved, w_down, w_up, norm_gain, sums, *near, *inputs],
+        "v" * 9 + "h" * len(inputs),
         "vppp",
-        scratch=[pltpu.VMEM(value.shape, value.dtype) for value in (slope, narrow, inv_root, pad)]
-        + [pltpu.VMEM((channels, steps * count), jnp.bfloat16), pltpu.VMEM((steps * count, hid), jnp.bfloat16)]
-        + [pltpu.SemaphoreType.DMA((len(inputs) + 4,))],
+        scratch=[pltpu.VMEM((channels, steps * count), jnp.bfloat16), pltpu.VMEM((steps * count, hid), jnp.bfloat16)]
+        + [pltpu.SemaphoreType.DMA((len(inputs),))],
         flops=2**30,
         moved=6 * 2**20,
         limit=20,
@@ -412,11 +488,11 @@
     gradient_quadrants(left_ref, right_ref, send_ref, keep_ref)
 
 
-def down_gradients(moved, forward, moveds):
-    steps = len(forward)
+def down_gradients(moved, moveds, hidden):
+    steps = len(hidden)
     channels, count = moved.shape
-    hid = forward[0][3].shape[1]
-    inputs = moveds + [parts[3] for parts in forward]
+    hid = hidden[0].shape[1]
+    inputs = moveds + hidden
     return call(
         functools.partial(down_kernel, steps),
         [jax.ShapeDtypeStruct(shape, jnp.bfloat16) for shape in quadrant_shapes(channels, hid, 0)],
@@ -707,10 +783,6 @@
         taps_ref[k // 3, k % 3 : k % 3 + 1] = total[k : k + 1]
     gain_ref[...] = total[9:10]
     finish(leaving)
-
-
-def after(value, first):
-    return lax.optimization_barrier((value, first))[0]
 
 
 def halving(flip, send, keep, total):
@@ -830,26 +902,40 @@
     around = (*around, *lon_edges(states, *around))
     order = list(reversed(range(steps)))
     gain = norm_gain.reshape(1, channels)
-    forward = {s: forward_parts(s, states, around, kernel, gain, w_up) for s in order}
-
-    moved, grads, fields = {}, {}, {}
-    for s in order[:-1]:
-        here = as_rows(exchanged(grid_now.reshape(devices, padded_share, count)))
-        if s != order[0]:
-            here, forward = lax.optimization_barrier((here, forward))
-        narrow, _, inv_root, _, slope, _ = forward[s]
-        fields[s], grads[s], moved[s] = network_back(here, w_down, w_up, gain, slope, narrow, inv_root)
-        arrived = as_grid(exchanged(as_blocks(fields[s])))
-        (grid_now,) = spatial("mid", s - 1, tile, padded_share, arrived, taps, weights, moves)
-
-    here = as_rows(exchanged(grid_now.reshape(devices, padded_share, count)))
+    now, *others = order
+    forward = {s: forward_parts(s, states, around, kernel, gain, w_up) for s in others}
+    names = {k: {s: forward[s][at] for s in others} for at, k in enumerate(FORWARD)}
+
+    def taken_back(grid):
+        return as_rows(exchanged(grid.reshape(devices, padded_share, count)))
+
+    def spread_on(s, field, grid_kernel=taps):
+        arrived = as_grid(exchanged(as_blocks(field)))
+        return spatial("mid", s, tile, padded_share, arrived, grid_kernel, weights, moves)[0]
+
+    fields, grads, moved = {}, {}, {}
+    (near,) = fetched([w_down], grid_now)
+    here = after(taken_back(grid_now), near)
+    parts = first_step(now, here, near, states, around, kernel, gain, w_up)
+    for k, value in zip(("n", "turned", "hid", "pad"), parts):
+        names[k][now] = value
+    fields[now], grads[now], moved[now] = parts[4:]
+    for s in others:
+        grid_now = spread_on(s, fields[s + 1])
+        here = taken_back(grid_now)
+        wanted = ("slope", "n", "inv") + ("pad",) * (s == others[-1])
+        near = fetched([names[k][s] for k in wanted], grid_now)
+        if s == others[-1]:
+            break
+        here = after(here, (near, forward))
+        fields[s], grads[s], moved[s] = network_back(here, w_down, w_up, gain, *near)
+
     earlier = lambda values: [values[s] for s in order[:-1]]
-    pads, narrows = ([forward[s][k] for s in order[:-1]] for k in (5, 0))
-    sums = channel_sums(tile, w_up, gain, pads, earlier(fields), earlier(grads), narrows)
-    here, sums = lax.optimization_barrier((here, sums))
-    parts = [forward[s] for s in order]
-    field, total, send, keep = last_step(tile, here, w_down, w_up, gain, sums, parts, earlier(grads))
-    down = down_gradients(here, parts, earlier(moved))
+    all_of = lambda values: [values[s] for s in order]
+    sums = channel_sums(tile, w_up, gain, *map(earlier, (names["pad"], fields, grads, names["n"])))
+    here = after(here, (near, sums))
+    field, total, send, keep = last_step(tile, here, w_down, w_up, gain, sums, near, all_of(names["turned"]), earlier(grads))
+    down = down_gradients(here, earlier(moved), all_of(names["hid"]))
     field = field.reshape(cotangent.shape)
     return all_sums((send, keep), down, total, field, kernel)
 

time: 126 us -> 122 us (0.968)
  waiting for transfers between devices: 47.6 us -> 44.1 us
    ppermute x2, waiting for transfers between devices: 3.84 us -> 0.01 us  [lon_edges(): lax.ppermute(value, 'lon', [(i, (i + 1) % lon) for i in range(lon)])]
    pallas_call x22 -> x24, Pallas kernels: 28.9 us -> 28.2 us  [call(): pl.pallas_call(kernel, out_shape=out_shape, in_specs=[pl.BlockSpec(memory...]
  transfers between devices with their start and end apart: 21 -> 21, of which waited for: 13 -> 13; matrix products, arithmetic and copies ran while one was open for 1% -> 1% of each run, Pallas kernels for 9% -> 11%
where the time goes in v8:
time: 122 us
  waiting for transfers between devices  44.1 us (36%)
  starting transfers between devices  35.1 us (29%)
  Pallas kernels  28.2 us (23%)
  blocking collectives  11.2 us (9%)
    pallas_call x24, Pallas kernels, call(): pl.pallas_call(kernel, out_shape=out_shape, in_specs=[pl.BlockSpec(memory...  28.2 us
    all_to_all x5, waiting for transfers between devices, exchanged(): return lax.all_to_all(blocks, AXES, split_axis=0, concat_axis=0, tiled=True)  25.9 us
    all_to_all x5, starting transfers between devices, exchanged(): return lax.all_to_all(blocks, AXES, split_axis=0, concat_axis=0, tiled=True)  18.8 us
    ppermute x8, waiting for transfers between devices, halving(): lax.ppermute(send, AXES, [(flat(i, j), flat(*partner(i, j))) for i, j in...  13.4 us
    all_to_all x1, blocking collectives, exchanged(): return lax.all_to_all(blocks, AXES, split_axis=0, concat_axis=0, tiled=True)  11.2 us
    ppermute x2, starting transfers between devices, lon_edges(): lax.ppermute(value, 'lon', [(i, (i - 1) % lon) for i in range(lon)])  5.9 us
    ppermute x8, starting transfers between devices, halving(): lax.ppermute(send, AXES, [(flat(i, j), flat(*partner(i, j))) for i, j in...  4.63 us
    ppermute x2, waiting for transfers between devices, lat_edges(): lax.ppermute(jnp.where(lat_at == 0, last, first), 'lat', [(0, 1), (1, 0)])  3.25 us
  transfers between devices with their start and end apart: 21, of which 13 were waited for; matrix products, arithmetic and copies ran while one was open for 1% of the time, Pallas kernels for 11%

profile of v8, /device:TPU:0, one launch (start us, length us, event | category | flops | bytes accessed | tf_op | source)
XLA Modules:
  0.0 121.8 jit_solution(15791638834326189083)
XLA Ops:
  0.6 1.8 %shard_map.128 = bf16[32,32,128]{2,1,0:T(8,128)(2,1)} custom-call(bf16[128,512]{1,0:T(8,128)(2,1)} %bitcast.38, f32[12,8,16]{2,1,0:T(8,128)} %bitcast.40), custom_call_target="tpu_custom_call" | custom-call | bytes 524288 | tf_op jit(solution)/shard_map/pallas_call | solution.py:35
  2.5 7.3 %all-to-all-start = ((bf16[32,32,128]{2,1,0:T(8,128)(2,1)}), bf16[32,32,128]{2,1,0:T(8,128)(2,1)S(1)}, u32[]{:S(2)}, u32[]{:S(2)}) async-start(bf16[32,32,128]{2,1,0:T(8,128)(2,1)} %shard_map.128), calls=%async_computation | async-start | bytes 524288 | tf_op jit(solution)/shard_map/all_to_all | solution.py:19
  9.9 1.8 %collective-permute-start = (bf16[3,8,1,512]{3,2,1,0:T(2,128)(2,1)S(1)}, bf16[3,8,1,512]{3,2,1,0:T(2,128)(2,1)S(1)}, u32[]{:S(2)}, u32[]{:S(2)}) collective-permute-start(bf16[3,8,1,512]{3,2,1,0:T(2,128)(2,1)S(1)} %broadcast_select_fusion.2), channel_id=1, source_target_pairs={{0,1},{1,0},{2,3},{3,2},{4,5},{5,4},{6,7},{7,6},{8,9},{9,8},{10,11... | collective-permute-start | bytes 73736 | tf_op jit(solution)/shard_map/ppermute | solution.py:132
  13.2 1.6 %collective-permute-done = bf16[3,8,1,512]{3,2,1,0:T(2,128)(2,1)S(1)} collective-permute-done((bf16[3,8,1,512]{3,2,1,0:T(2,128)(2,1)S(1)}, bf16[3,8,1,512]{3,2,1,0:T(2,128)(2,1)S(1)}, u32[]{:S(2)}, u32[]{:S(2)}) %collective-permute-start) | collective-permute-done | bytes 24608 | tf_op jit(solution)/shard_map/ppermute | solution.py:132
  14.8 5.7 %all-to-all-done = bf16[32,32,128]{2,1,0:T(8,128)(2,1)S(1)} async-done(((bf16[32,32,128]{2,1,0:T(8,128)(2,1)}), bf16[32,32,128]{2,1,0:T(8,128)(2,1)S(1)}, u32[]{:S(2)}, u32[]{:S(2)}) %all-to-all-start) | async-done | bytes 262176 | tf_op jit(solution)/shard_map/all_to_all | solution.py:19
  20.5 1.5 %shard_map.129 = (bf16[16,2,16,128]{3,2,1,0:T(8,128)(2,1)}, bf16[16,2,16,128]{3,2,1,0:T(8,128)(2,1)}) custom-call(s32[3,2]{1,0:T(4,128)} %pad_add_fusion.refs_0_, bf16[16,2,32,128]{3,2,1,0:T(8,128)(2,1)S(1)} %bitcast.18), custom_call_target="tpu_custom_call" | custom-call | flops 4194304 | bytes 1048576 | tf_op jit(solution)/shard_map/pallas_call | solution.py:35
  22.0 2.6 %all-to-all-start.1 = ((bf16[32,16,128]{2,1,0:T(8,128)(2,1)}), bf16[32,16,128]{2,1,0:T(8,128)(2,1)S(1)}, u32[]{:S(2)}, u32[]{:S(2)}) async-start(bf16[32,16,128]{2,1,0:T(8,128)(2,1)} %bitcast.39), calls=%async_computation.1 | async-start | bytes 262144 | tf_op jit(solution)/shard_map/all_to_all | solution.py:19
  24.9 4.4 %collective-permute-start.2 = (bf16[3,1,18,512]{3,2,1,0:T(8,128)(2,1)S(1)}, bf16[3,1,18,512]{3,2,1,0:T(8,128)(2,1)S(1)}, u32[]{:S(2)}, u32[]{:S(2)}) collective-permute-start(bf16[3,1,18,512]{3,2,1,0:T(8,128)(2,1)S(1)} %pad_maximum_fusion.1), channel_id=1, source_target_pairs={{0,30},{2,0},{4,2},{6,4},{8,6},{10,8},{12,10},{14,12},{16,14},{18,... | collective-permute-start | bytes 165896 | tf_op jit(solution)/shard_map/ppermute | solution.py:144
  30.6 3.1 %all-to-all-done.1 = bf16[32,16,128]{2,1,0:T(8,128)(2,1)S(1)} async-done(((bf16[32,16,128]{2,1,0:T(8,128)(2,1)}), bf16[32,16,128]{2,1,0:T(8,128)(2,1)S(1)}, u32[]{:S(2)}, u32[]{:S(2)}) %all-to-all-start.1) | async-done | bytes 131104 | tf_op jit(solution)/shard_map/all_to_all | solution.py:19
  33.7 2.5 %shard_map.131 = (bf16[128,512]{1,0:T(8,128)(2,1)}, bf16[512,128]{1,0:T(8,128)(2,1)}, bf16[128,1024]{1,0:T(8,128)(2,1)}, bf16[10,32,512]{2,1,0:T(8,128)(2,1)}, b...) custom-call(bf16[512,128]{1,0:T(8,128)(2,1)S(1)} %bitcast.19, ...), custom_call_target="tpu_custom_call" | custom-call | flops 268435456 | bytes 4194304 | tf_op jit(solution)/shard_map/pallas_call | solution.py:35
  36.2 3.6 %all-to-all-start.2 = ((bf16[32,16,128]{2,1,0:T(8,128)(2,1)}), bf16[32,16,128]{2,1,0:T(8,128)(2,1)S(1)}, u32[]{:S(2)}, u32[]{:S(2)}) async-start(bf16[32,16,128]{2,1,0:T(8,128)(2,1)} %bitcast.34), calls=%async_computation.2 | async-start | bytes 262144 | tf_op jit(solution)/shard_map/all_to_all | solution.py:19
  40.0 8.4 %all-to-all-done.2 = bf16[32,16,128]{2,1,0:T(8,128)(2,1)S(1)} async-done(((bf16[32,16,128]{2,1,0:T(8,128)(2,1)}), bf16[32,16,128]{2,1,0:T(8,128)(2,1)S(1)}, u32[]{:S(2)}, u32[]{:S(2)}) %all-to-all-start.2) | async-done | bytes 131104 | tf_op jit(solution)/shard_map/all_to_all | solution.py:19
  48.4 2.1 %shard_map.132 = bf16[16,2,16,128]{3,2,1,0:T(8,128)(2,1)} custom-call(s32[3,2]{1,0:T(4,128)} %pad_add_fusion.refs_0_, bf16[16,2,16,128]{3,2,1,0:T(8,128)(2,1)S(1)} %bitcast.21, f32[16,128]{1,0:T(8,128)S(1)} %pad.4.refs_2_, bf16[16,2,16,128]{3,2,1,0:T(8,128)(2,1)} %get-tuple-element.101.refs_3_), custom_call_target="tpu_custom_call" | custom-call | flops 4194304 | bytes 1048576 | tf_op jit(solution)/shard_map/pallas_call | solution.py:35
  50.5 2.6 %all-to-all-start.3 = ((bf16[32,16,128]{2,1,0:T(8,128)(2,1)}), bf16[32,16,128]{2,1,0:T(8,128)(2,1)S(1)}, u32[]{:S(2)}, u32[]{:S(2)}) async-start(bf16[32,16,128]{2,1,0:T(8,128)(2,1)} %bitcast.35), calls=%async_computation.3 | async-start | bytes 262144 | tf_op jit(solution)/shard_map/all_to_all | solution.py:19
  53.1 1.7 %shard_map.135 = (bf16[128,512]{1,0:T(8,128)(2,1)}, bf16[512,128]{1,0:T(8,128)(2,1)}, f32[128,128]{1,0:T(8,128)}, bf16[128,1024]{1,0:T(8,128)(2,1)}, bf16[128,10...) custom-call(bf16[3,8,16,512]{3,2,1,0:T(8,128)(2,1)S(1)} %copy-done.1, ...), custom_call_target="tpu_custom_call" | custom-call | flops 134217728 | bytes 4194304 | tf_op jit(solution)/shard_map/pallas_call | solution.py:35
  54.8 1.7 %shard_map.133 = (bf16[128,512]{1,0:T(8,128)(2,1)}, bf16[512,128]{1,0:T(8,128)(2,1)}, f32[128,128]{1,0:T(8,128)}, bf16[128,1024]{1,0:T(8,128)(2,1)}, bf16[128,10...) custom-call(bf16[3,8,16,512]{3,2,1,0:T(8,128)(2,1)S(1)} %copy-done.1, ...), custom_call_target="tpu_custom_call" | custom-call | flops 134217728 | bytes 4194304 | tf_op jit(solution)/shard_map/pallas_call | solution.py:35
  57.6 4.2 %all-to-all-done.3 = bf16[32,16,128]{2,1,0:T(8,128)(2,1)S(1)} async-done(((bf16[32,16,128]{2,1,0:T(8,128)(2,1)}), bf16[32,16,128]{2,1,0:T(8,128)(2,1)S(1)}, u32[]{:S(2)}, u32[]{:S(2)}) %all-to-all-start.3) | async-done | bytes 131104 | tf_op jit(solution)/shard_map/all_to_all | solution.py:19
  61.7 1.6 %shard_map.136 = (bf16[512,128]{1,0:T(8,128)(2,1)}, bf16[128,1024]{1,0:T(8,128)(2,1)}, bf16[512,128]{1,0:T(8,128)(2,1)}) custom-call(bf16[512,128]{1,0:T(8,128)(2,1)S(1)} %bitcast.20, bf16[512,1024]{1,0:T(8,128)(2,1)S(1)} %copy-done.2, bf16[512,1024]{1,0:T(8,128)(2,1)S(1)} %copy-done, f32[1,512]{1,0:T(1,128)S(1)} %bitcast.31, ...), custom_call_target="tpu_custom_call" | custom-call | flops 268435456 | bytes 4194304 | tf_op jit(solution)/shard_map/pallas_call | solution.py:35
  63.3 11.2 %all_to_all.30 = bf16[32,16,128]{2,1,0:T(8,128)(2,1)S(1)} all-to-all(bf16[32,16,128]{2,1,0:T(8,128)(2,1)} %bitcast.37), channel_id=1, replica_groups=mesh['lon'=16,'lat'=2] {'lon','lat'}, dimensions={0} | all-to-all | bytes 262144 | tf_op jit(solution)/shard_map/all_to_all | solution.py:19
  74.5 2.1 %shard_map.137 = bf16[16,2,16,128]{3,2,1,0:T(8,128)(2,1)} custom-call(s32[3,2]{1,0:T(4,128)} %pad_add_fusion.refs_0_, bf16[16,2,16,128]{3,2,1,0:T(8,128)(2,1)S(1)} %bitcast.22, f32[16,128]{1,0:T(8,128)S(1)} %pad.4.refs_2_, bf16[16,2,16,128]{3,2,1,0:T(8,128)(2,1)} %get-tuple-element.101.refs_3_), custom_call_target="tpu_custom_call" | custom-call | flops 4194304 | bytes 1048576 | tf_op jit(solution)/shard_map/pallas_call | solution.py:35
  76.6 2.8 %all-to-all-start.5 = ((bf16[32,16,128]{2,1,0:T(8,128)(2,1)}), bf16[32,16,128]{2,1,0:T(8,128)(2,1)S(1)}, u32[]{:S(2)}, u32[]{:S(2)}) async-start(bf16[32,16,128]{2,1,0:T(8,128)(2,1)} %bitcast.36), calls=%async_computation.5 | async-start | bytes 262144 | tf_op jit(solution)/shard_map/all_to_all | solution.py:19
  79.4 2.7 %shard_map.139.sums_ref = f32[16,512]{1,0:T(8,128)S(1)} custom-call(bf16[512,1024]{1,0:T(8,128)(2,1)S(1)} %copy-done, f32[1,512]{1,0:T(1,128)S(1)} %bitcast.32, bf16[10,32,512]{2,1,0:T(8,128)(2,1)} %get-tuple-element.130.refs_0_, bf16[512,128]{1,0:T(8,128)(2,1)} %get-tuple-element.100.refs_1_, bf16[128,1024]{1,0:T(8,128)(2,1)} %get-tuple-element.131.refs_2_.refs_7_, ...), custom_call_target="tpu_custom_call" | custom-call | bytes 2097152 | tf_op jit(solution)/shard_map/pallas_call | solution.py:35
  83.3 4.5 %all-to-all-done.5 = bf16[32,16,128]{2,1,0:T(8,128)(2,1)S(1)} async-done(((bf16[32,16,128]{2,1,0:T(8,128)(2,1)}), bf16[32,16,128]{2,1,0:T(8,128)(2,1)S(1)}, u32[]{:S(2)}, u32[]{:S(2)}) %all-to-all-start.5) | async-done | bytes 131104 | tf_op jit(solution)/shard_map/all_to_all | solution.py:19
  87.8 2.0 %shard_map.140 = (bf16[128,512]{1,0:T(8,128)(2,1)S(1)}, f32[16,512]{1,0:T(8,128)S(1)}, bf16[544,512]{1,0:T(8,128)(2,1)S(1)}, bf16[4,128,512]{2,1,0:T(8,128)(2,1)S(1)}) custom-call(bf16[512,128]{1,0:T(8,128)(2,1)S(1)} %bitcast.26, bf16[512,1024]{1,0:T(8,128)(2,1)S(1)} %copy-done.2, bf16[512,1024]{1,0:T(8,128)(2,1)S(1)} %copy-done, f32[1,512]{1,0:T(1,128)S(1)} %bitcast.33, ...), custom_call_target="tpu_custom_call" | custom-call | flops 1073741824 | bytes 6291456 | tf_op jit(solution)/shard_map/pallas_call | solution.py:35
  89.9 2.0 %shard_map.141 = (bf16[512,512]{1,0:T(8,128)(2,1)S(1)}, bf16[4,128,512]{2,1,0:T(8,128)(2,1)S(1)}) custom-call(bf16[512,128]{1,0:T(8,128)(2,1)S(1)} %bitcast.27, bf16[512,128]{1,0:T(8,128)(2,1)} %get-tuple-element.140.refs_0_, bf16[512,128]{1,0:T(8,128)(2,1)} %get-tuple-element.141.refs_1_, bf16[128,1024]{1,0:T(8,128)(2,1)} %get-tuple-element.142.refs_2_, ...), custom_call_target="tpu_custom_call" | custom-call | flops 536870912 | bytes 2097152 | tf_op jit(solution)/shard_map/pallas_call | solution.py:35
  95.0 1.7 %collective-permute-done.4 = bf16[1,8,1,512]{3,2,1,0:T(2,128)(2,1)S(1)} collective-permute-done((bf16[1,8,1,512]{3,2,1,0:T(2,128)(2,1)S(1)}, bf16[1,8,1,512]{3,2,1,0:T(2,128)(2,1)S(1)}, u32[]{:S(2)}, u32[]{:S(2)}) %collective-permute-start.4) | collective-permute-done | bytes 8224 | tf_op jit(solution)/shard_map/ppermute | solution.py:132
  96.8 4.7 %collective-permute-done.8.refs_2_ = bf16[288,512]{1,0:T(8,128)(2,1)S(1)} collective-permute-done((bf16[288,512]{1,0:T(8,128)(2,1)S(1)}, bf16[288,512]{1,0:T(8,128)(2,1)S(1)}, u32[]{:S(2)}, u32[]{:S(2)}) %collective-permute-start.8) | collective-permute-done | bytes 294944 | tf_op jit(solution)/shard_map/ppermute | solution.py:815
  102.7 5.5 %collective-permute-done.9.refs_3_ = bf16[192,512]{1,0:T(8,128)(2,1)S(1)} collective-permute-done((bf16[192,512]{1,0:T(8,128)(2,1)S(1)}, bf16[192,512]{1,0:T(8,128)(2,1)S(1)}, u32[]{:S(2)}, u32[]{:S(2)}) %collective-permute-start.9) | collective-permute-done | bytes 196640 | tf_op jit(solution)/shard_map/ppermute | solution.py:815
  108.4 2.1 %collective-permute-start.14 = (bf16[64,512]{1,0:T(8,128)(2,1)S(1)}, bf16[64,512]{1,0:T(8,128)(2,1)S(1)}, u32[]{:S(2)}, u32[]{:S(2)}) collective-permute-start(bf16[64,512]{1,0:T(8,128)(2,1)S(1)} %get-tuple-element.166), channel_id=1, source_target_pairs={{0,8},{1,9},{2,10},{3,11},{4,12},{5,13},{6,14},{7,15},{8,0},{9,1},... | collective-permute-start | bytes 196616 | tf_op jit(solution)/shard_map/ppermute | solution.py:815
  110.6 2.4 %collective-permute-done.11.refs_2_ = bf16[96,512]{1,0:T(8,128)(2,1)S(1)} collective-permute-done((bf16[96,512]{1,0:T(8,128)(2,1)S(1)}, bf16[96,512]{1,0:T(8,128)(2,1)S(1)}, u32[]{:S(2)}, u32[]{:S(2)}) %collective-permute-start.11) | collective-permute-done | bytes 98336 | tf_op jit(solution)/shard_map/ppermute | solution.py:815
  113.7 2.4 %collective-permute-start.15 = (bf16[32,512]{1,0:T(8,128)(2,1)S(1)}, bf16[32,512]{1,0:T(8,128)(2,1)S(1)}, u32[]{:S(2)}, u32[]{:S(2)}) collective-permute-start(bf16[32,512]{1,0:T(8,128)(2,1)S(1)} %get-tuple-element.174), channel_id=1, source_target_pairs={{0,16},{1,17},{2,18},{3,19},{4,20},{5,21},{6,22},{7,23},{8,24},{9,... | collective-permute-start | bytes 98312 | tf_op jit(solution)/shard_map/ppermute | solution.py:824
  117.6 1.5 %collective-permute-done.7.high_ref = bf16[1,1,18,512]{3,2,1,0:T(8,128)(2,1)S(1)} collective-permute-done((bf16[1,1,18,512]{3,2,1,0:T(8,128)(2,1)S(1)}, bf16[1,1,18,512]{3,2,1,0:T(8,128)(2,1)S(1)}, u32[]{:S(2)}, u32[]{:S(2)}) %collective-permute-start.7) | collective-permute-done | bytes 18464 | tf_op jit(solution)/shard_map/ppermute | solution.py:144
  (69 shorter events, 14.9 us)
Async XLA Ops:
  0.6 9.2 %copy-start.1 = (bf16[3,8,16,512]{3,2,1,0:T(8,128)(2,1)S(1)}, bf16[3,8,16,512]{3,2,1,0:T(8,128)(2,1)}, u32[]{:S(2)}) copy-start(bf16[3,8,16,512]{3,2,1,0:T(8,128)(2,1)} %refs_0_.4) | copy-start | bytes 1179652
  2.5 18.0 %all-to-all-start = ((bf16[32,32,128]{2,1,0:T(8,128)(2,1)}), bf16[32,32,128]{2,1,0:T(8,128)(2,1)S(1)}, u32[]{:S(2)}, u32[]{:S(2)}) async-start(bf16[32,32,128]{2,1,0:T(8,128)(2,1)} %shard_map.128), calls=%async_computation | async-start | bytes 524288 | tf_op jit(solution)/shard_map/all_to_all | solution.py:19
  9.9 4.8 %collective-permute-start = (bf16[3,8,1,512]{3,2,1,0:T(2,128)(2,1)S(1)}, bf16[3,8,1,512]{3,2,1,0:T(2,128)(2,1)S(1)}, u32[]{:S(2)}, u32[]{:S(2)}) collective-permute-start(bf16[3,8,1,512]{3,2,1,0:T(2,128)(2,1)S(1)} %broadcast_select_fusion.2), channel_id=1, source_target_pairs={{0,1},{1,0},{2,3},{3,2},{4,5},{5,4},{6,7},{7,6},{8,9},{9,8},{10,11... | collective-permute-start | bytes 73736 | tf_op jit(solution)/shard_map/ppermute | solution.py:132
  11.8 0.7 copy-start.6
  11.8 0.7 copy-start.5
  22.0 11.7 %all-to-all-start.1 = ((bf16[32,16,128]{2,1,0:T(8,128)(2,1)}), bf16[32,16,128]{2,1,0:T(8,128)(2,1)S(1)}, u32[]{:S(2)}, u32[]{:S(2)}) async-start(bf16[32,16,128]{2,1,0:T(8,128)(2,1)} %bitcast.39), calls=%async_computation.1 | async-start | bytes 262144 | tf_op jit(solution)/shard_map/all_to_all | solution.py:19
  24.7 9.0 %collective-permute-start.1 = (bf16[3,1,18,512]{3,2,1,0:T(8,128)(2,1)S(1)}, bf16[3,1,18,512]{3,2,1,0:T(8,128)(2,1)S(1)}, u32[]{:S(2)}, u32[]{:S(2)}) collective-permute-start(bf16[3,1,18,512]{3,2,1,0:T(8,128)(2,1)S(1)} %pad_maximum_fusion), channel_id=1, source_target_pairs={{0,2},{2,4},{4,6},{6,8},{8,10},{10,12},{12,14},{14,16},{16,18},{18... | collective-permute-start | bytes 165896 | tf_op jit(solution)/shard_map/ppermute | solution.py:143
  24.9 8.8 %copy-start = (bf16[512,1024]{1,0:T(8,128)(2,1)S(1)}, bf16[512,1024]{1,0:T(8,128)(2,1)}, u32[]{:S(2)}) copy-start(bf16[512,1024]{1,0:T(8,128)(2,1)} %up_ref.5) | copy-start | bytes 3145732
  24.9 8.8 %copy-start.3 = (f32[3,3,512]{2,1,0:T(4,128)S(1)}, f32[3,3,512]{2,1,0:T(4,128)}, u32[]{:S(2)}) copy-start(f32[3,3,512]{2,1,0:T(4,128)} %kernel_ref.1) | copy-start | bytes 55300
  24.9 8.7 %collective-permute-start.2 = (bf16[3,1,18,512]{3,2,1,0:T(8,128)(2,1)S(1)}, bf16[3,1,18,512]{3,2,1,0:T(8,128)(2,1)S(1)}, u32[]{:S(2)}, u32[]{:S(2)}) collective-permute-start(bf16[3,1,18,512]{3,2,1,0:T(8,128)(2,1)S(1)} %pad_maximum_fusion.1), channel_id=1, source_target_pairs={{0,30},{2,0},{4,2},{6,4},{8,6},{10,8},{12,10},{14,12},{16,14},{18,... | collective-permute-start | bytes 165896 | tf_op jit(solution)/shard_map/ppermute | solution.py:144
  30.6 3.1 %copy-start.4 = (f32[512]{0:T(512)S(1)}, f32[512]{0:T(512)}, u32[]{:S(2)}) copy-start(f32[512]{0:T(512)} %param.13) | copy-start | bytes 6148
  36.2 12.2 %all-to-all-start.2 = ((bf16[32,16,128]{2,1,0:T(8,128)(2,1)}), bf16[32,16,128]{2,1,0:T(8,128)(2,1)S(1)}, u32[]{:S(2)}, u32[]{:S(2)}) async-start(bf16[32,16,128]{2,1,0:T(8,128)(2,1)} %bitcast.34), calls=%async_computation.2 | async-start | bytes 262144 | tf_op jit(solution)/shard_map/all_to_all | solution.py:19
  50.5 11.2 %all-to-all-start.3 = ((bf16[32,16,128]{2,1,0:T(8,128)(2,1)}), bf16[32,16,128]{2,1,0:T(8,128)(2,1)S(1)}, u32[]{:S(2)}, u32[]{:S(2)}) async-start(bf16[32,16,128]{2,1,0:T(8,128)(2,1)} %bitcast.35), calls=%async_computation.3 | async-start | bytes 262144 | tf_op jit(solution)/shard_map/all_to_all | solution.py:19
  54.8 6.9 %copy-start.2 = (bf16[512,1024]{1,0:T(8,128)(2,1)S(1)}, bf16[512,1024]{1,0:T(8,128)(2,1)}, u32[]{:S(2)}) copy-start(bf16[512,1024]{1,0:T(8,128)(2,1)} %down_ref.3) | copy-start | bytes 3145732
  76.6 11.2 %all-to-all-start.5 = ((bf16[32,16,128]{2,1,0:T(8,128)(2,1)}), bf16[32,16,128]{2,1,0:T(8,128)(2,1)S(1)}, u32[]{:S(2)}, u32[]{:S(2)}) async-start(bf16[32,16,128]{2,1,0:T(8,128)(2,1)} %bitcast.36), calls=%async_computation.5 | async-start | bytes 262144 | tf_op jit(solution)/shard_map/all_to_all | solution.py:19
  89.9 2.1 %collective-permute-start.3 = (bf16[544,512]{1,0:T(8,128)(2,1)S(1)}, bf16[544,512]{1,0:T(8,128)(2,1)S(1)}, u32[]{:S(2)}, u32[]{:S(2)}) collective-permute-start(bf16[544,512]{1,0:T(8,128)(2,1)S(1)} %get-tuple-element.139), channel_id=1, source_target_pairs={{0,2},{1,3},{2,0},{3,1},{4,6},{5,7},{6,4},{7,5},{8,10},{9,11},{10,... | collective-permute-start | bytes 1671176 | tf_op jit(solution)/shard_map/ppermute | solution.py:815
  92.1 2.1 %collective-permute-start.5 = (bf16[512,512]{1,0:T(8,128)(2,1)S(1)}, bf16[512,512]{1,0:T(8,128)(2,1)S(1)}, u32[]{:S(2)}, u32[]{:S(2)}) collective-permute-start(bf16[512,512]{1,0:T(8,128)(2,1)S(1)} %get-tuple-element.148), channel_id=1, source_target_pairs={{0,2},{1,3},{2,0},{3,1},{4,6},{5,7},{6,4},{7,5},{8,10},{9,11},{10,... | collective-permute-start | bytes 1572872 | tf_op jit(solution)/shard_map/ppermute | solution.py:815
  92.7 8.7 %collective-permute-start.8 = (bf16[288,512]{1,0:T(8,128)(2,1)S(1)}, bf16[288,512]{1,0:T(8,128)(2,1)S(1)}, u32[]{:S(2)}, u32[]{:S(2)}) collective-permute-start(bf16[288,512]{1,0:T(8,128)(2,1)S(1)} %get-tuple-element.145), channel_id=1, source_target_pairs={{0,4},{1,5},{2,3},{3,2},{4,0},{5,1},{6,7},{7,6},{8,12},{9,13},{10,... | collective-permute-start | bytes 884744 | tf_op jit(solution)/shard_map/ppermute | solution.py:815
  92.7 4.0 %collective-permute-start.4 = (bf16[1,8,1,512]{3,2,1,0:T(2,128)(2,1)S(1)}, bf16[1,8,1,512]{3,2,1,0:T(2,128)(2,1)S(1)}, u32[]{:S(2)}, u32[]{:S(2)}) collective-permute-start(bf16[1,8,1,512]{3,2,1,0:T(2,128)(2,1)S(1)} %broadcast_select_fusion.5), channel_id=1, source_target_pairs={{0,1},{1,0},{2,3},{3,2},{4,5},{5,4},{6,7},{7,6},{8,9},{9,8},{10,11... | collective-permute-start | bytes 24584 | tf_op jit(solution)/shard_map/ppermute | solution.py:132
  94.3 7.5 %collective-permute-start.10 = (bf16[256,512]{1,0:T(8,128)(2,1)S(1)}, bf16[256,512]{1,0:T(8,128)(2,1)S(1)}, u32[]{:S(2)}, u32[]{:S(2)}) collective-permute-start(bf16[256,512]{1,0:T(8,128)(2,1)S(1)} %get-tuple-element.149), channel_id=1, source_target_pairs={{0,1},{1,0},{2,6},{3,7},{4,5},{5,4},{6,2},{7,3},{8,9},{9,8},{10,14... | collective-permute-start | bytes 786440 | tf_op jit(solution)/shard_map/ppermute | solution.py:815
  101.5 6.8 %collective-permute-start.9 = (bf16[192,512]{1,0:T(8,128)(2,1)S(1)}, bf16[192,512]{1,0:T(8,128)(2,1)S(1)}, u32[]{:S(2)}, u32[]{:S(2)}) collective-permute-start(bf16[192,512]{1,0:T(8,128)(2,1)S(1)} %get-tuple-element.156), channel_id=1, source_target_pairs={{0,1},{1,0},{2,6},{3,7},{4,5},{5,4},{6,2},{7,3},{8,9},{9,8},{10,14... | collective-permute-start | bytes 589832 | tf_op jit(solution)/shard_map/ppermute | solution.py:815
  101.9 6.4 %collective-permute-start.12 = (bf16[128,512]{1,0:T(8,128)(2,1)S(1)}, bf16[128,512]{1,0:T(8,128)(2,1)S(1)}, u32[]{:S(2)}, u32[]{:S(2)}) collective-permute-start(bf16[128,512]{1,0:T(8,128)(2,1)S(1)} %get-tuple-element.159), channel_id=1, source_target_pairs={{0,4},{1,5},{2,3},{3,2},{4,0},{5,1},{6,7},{7,6},{8,12},{9,13},{10,... | collective-permute-start | bytes 393224 | tf_op jit(solution)/shard_map/ppermute | solution.py:815
  108.3 4.7 %collective-permute-start.11 = (bf16[96,512]{1,0:T(8,128)(2,1)S(1)}, bf16[96,512]{1,0:T(8,128)(2,1)S(1)}, u32[]{:S(2)}, u32[]{:S(2)}) collective-permute-start(bf16[96,512]{1,0:T(8,128)(2,1)S(1)} %get-tuple-element.163), channel_id=1, source_target_pairs={{0,8},{1,9},{2,10},{3,11},{4,12},{5,13},{6,14},{7,15},{8,0},{9,1},... | collective-permute-start | bytes 294920 | tf_op jit(solution)/shard_map/ppermute | solution.py:815
  108.4 5.2 %collective-permute-start.14 = (bf16[64,512]{1,0:T(8,128)(2,1)S(1)}, bf16[64,512]{1,0:T(8,128)(2,1)S(1)}, u32[]{:S(2)}, u32[]{:S(2)}) collective-permute-start(bf16[64,512]{1,0:T(8,128)(2,1)S(1)} %get-tuple-element.166), channel_id=1, source_target_pairs={{0,8},{1,9},{2,10},{3,11},{4,12},{5,13},{6,14},{7,15},{8,0},{9,1},... | collective-permute-start | bytes 196616 | tf_op jit(solution)/shard_map/ppermute | solution.py:815
  110.5 7.1 %collective-permute-start.6 = (bf16[1,1,18,512]{3,2,1,0:T(8,128)(2,1)S(1)}, bf16[1,1,18,512]{3,2,1,0:T(8,128)(2,1)S(1)}, u32[]{:S(2)}, u32[]{:S(2)}) collective-permute-start(bf16[1,1,18,512]{3,2,1,0:T(8,128)(2,1)S(1)} %pad_maximum_fusion.2), channel_id=1, source_target_pairs={{0,2},{2,4},{4,6},{6,8},{8,10},{10,12},{12,14},{14,16},{16,18},{18... | collective-permute-start | bytes 55304 | tf_op jit(solution)/shard_map/ppermute | solution.py:143
  113.0 7.3 %collective-permute-start.13 = (bf16[64,512]{1,0:T(8,128)(2,1)S(1)}, bf16[64,512]{1,0:T(8,128)(2,1)S(1)}, u32[]{:S(2)}, u32[]{:S(2)}) collective-permute-start(bf16[64,512]{1,0:T(8,128)(2,1)S(1)} %get-tuple-element.170), channel_id=1, source_target_pairs={{0,16},{1,17},{2,18},{3,19},{4,20},{5,21},{6,22},{7,23},{8,24},{9,... | collective-permute-start | bytes 196616 | tf_op jit(solution)/shard_map/ppermute | solution.py:824
  113.7 6.6 %collective-permute-start.15 = (bf16[32,512]{1,0:T(8,128)(2,1)S(1)}, bf16[32,512]{1,0:T(8,128)(2,1)S(1)}, u32[]{:S(2)}, u32[]{:S(2)}) collective-permute-start(bf16[32,512]{1,0:T(8,128)(2,1)S(1)} %get-tuple-element.174), channel_id=1, source_target_pairs={{0,16},{1,17},{2,18},{3,19},{4,20},{5,21},{6,22},{7,23},{8,24},{9,... | collective-permute-start | bytes 98312 | tf_op jit(solution)/shard_map/ppermute | solution.py:824
  116.1 3.0 %collective-permute-start.7 = (bf16[1,1,18,512]{3,2,1,0:T(8,128)(2,1)S(1)}, bf16[1,1,18,512]{3,2,1,0:T(8,128)(2,1)S(1)}, u32[]{:S(2)}, u32[]{:S(2)}) collective-permute-start(bf16[1,1,18,512]{3,2,1,0:T(8,128)(2,1)S(1)} %pad_maximum_fusion.3), channel_id=1, source_target_pairs={{0,30},{2,0},{4,2},{6,4},{8,6},{10,8},{12,10},{14,12},{16,14},{18,... | collective-permute-start | bytes 55304 | tf_op jit(solution)/shard_map/ppermute | solution.py:144

commit v9 on v8

--- a/solution.py
+++ b/solution.py
@@ -139,6 +139,17 @@
 
 
 def lon_edges(states, before, after):
+    lon = lax.axis_size("lon")
+    even = lax.axis_index("lon") % 2 == 0
+    row = lambda place: jnp.concatenate([part[:, place] for part in (before, states, after)], axis=2)
+    first, last = row(slice(0, 1)), row(slice(-1, None))
+    with_next = lax.ppermute(jnp.where(even, last, first), "lon", [(i, i ^ 1) for i in range(lon)])
+    pairs = [(i, (i - 1) % lon if i % 2 == 0 else (i + 1) % lon) for i in range(lon)]
+    with_last = lax.ppermute(jnp.where(even, first, last), "lon", pairs)
+    return jnp.where(even, with_last, with_next), jnp.where(even, with_next, with_last)
+
+
+def lon_edges_ring(states, before, after):
     lon = lax.axis_size("lon")
     ahead = lambda value: lax.ppermute(value, "lon", [(i, (i + 1) % lon) for i in range(lon)])
     behind = lambda value: lax.ppermute(value, "lon", [(i, (i - 1) % lon) for i in range(lon)])
@@ -899,7 +910,7 @@
 
     around = lat_edges(states_later)
     grid_now, *around = lax.optimization_barrier((grid_now, *around))
-    around = (*around, *lon_edges(states, *around))
+    around = (*around, *lon_edges_ring(states, *around))
     order = list(reversed(range(steps)))
     gain = norm_gain.reshape(1, channels)
     now, *others = order

time: 122 us -> 121 us (level)
  transfers between devices with their start and end apart: 21 -> 21, of which waited for: 13 -> 15; matrix products, arithmetic and copies ran while one was open for 1% -> 1% of each run, Pallas kernels for 11% -> 11%
where the time goes in v9:
time: 121 us; the launch traced here: 120 us
  waiting for transfers between devices  43.3 us (36%)
  starting transfers between devices  34.3 us (28%)
  Pallas kernels  28.2 us (23%)
  blocking collectives  11.2 us (9%)
    pallas_call x24, Pallas kernels, call(): pl.pallas_call(kernel, out_shape=out_shape, in_specs=[pl.BlockSpec(memory...  28.2 us
    all_to_all x5, waiting for transfers between devices, exchanged(): return lax.all_to_all(blocks, AXES, split_axis=0, concat_axis=0, tiled=True)  25.9 us
    all_to_all x5, starting transfers between devices, exchanged(): return lax.all_to_all(blocks, AXES, split_axis=0, concat_axis=0, tiled=True)  18.8 us
    ppermute x8, waiting for transfers between devices, halving(): lax.ppermute(send, AXES, [(flat(i, j), flat(*partner(i, j))) for i, j in...  12.6 us
    all_to_all x1, blocking collectives, exchanged(): return lax.all_to_all(blocks, AXES, split_axis=0, concat_axis=0, tiled=True)  11.2 us
    ppermute x8, starting transfers between devices, halving(): lax.ppermute(send, AXES, [(flat(i, j), flat(*partner(i, j))) for i, j in...  4.63 us
    ppermute x1, starting transfers between devices, lon_edges_ring(): lax.ppermute(value, 'lon', [(i, (i - 1) % lon) for i in range(lon)])  4.38 us
    ppermute x2, waiting for transfers between devices, lat_edges(): lax.ppermute(jnp.where(lat_at == 0, last, first), 'lat', [(0, 1), (1, 0)])  3.25 us
  transfers between devices with their start and end apart: 21, of which 15 were waited for; matrix products, arithmetic and copies ran while one was open for 1% of the time, Pallas kernels for 11%

profile of v9, /device:TPU:0, one launch (start us, length us, event | category | flops | bytes accessed | tf_op | source)
XLA Modules:
  0.0 120.2 jit_solution(9670682796691942360)
XLA Ops:
  0.6 1.9 %shard_map.128 = bf16[32,32,128]{2,1,0:T(8,128)(2,1)} custom-call(bf16[128,512]{1,0:T(8,128)(2,1)} %bitcast.38, f32[12,8,16]{2,1,0:T(8,128)} %bitcast.40), custom_call_target="tpu_custom_call" | custom-call | bytes 524288 | tf_op jit(solution)/shard_map/pallas_call | solution.py:35
  2.5 7.3 %all-to-all-start = ((bf16[32,32,128]{2,1,0:T(8,128)(2,1)}), bf16[32,32,128]{2,1,0:T(8,128)(2,1)S(1)}, u32[]{:S(2)}, u32[]{:S(2)}) async-start(bf16[32,32,128]{2,1,0:T(8,128)(2,1)} %shard_map.128), calls=%async_computation | async-start | bytes 524288 | tf_op jit(solution)/shard_map/all_to_all | solution.py:19
  9.9 1.8 %collective-permute-start = (bf16[3,8,1,512]{3,2,1,0:T(2,128)(2,1)S(1)}, bf16[3,8,1,512]{3,2,1,0:T(2,128)(2,1)S(1)}, u32[]{:S(2)}, u32[]{:S(2)}) collective-permute-start(bf16[3,8,1,512]{3,2,1,0:T(2,128)(2,1)S(1)} %broadcast_select_fusion.2), channel_id=1, source_target_pairs={{0,1},{1,0},{2,3},{3,2},{4,5},{5,4},{6,7},{7,6},{8,9},{9,8},{10,11... | collective-permute-start | bytes 73736 | tf_op jit(solution)/shard_map/ppermute | solution.py:132
  13.2 1.6 %collective-permute-done = bf16[3,8,1,512]{3,2,1,0:T(2,128)(2,1)S(1)} collective-permute-done((bf16[3,8,1,512]{3,2,1,0:T(2,128)(2,1)S(1)}, bf16[3,8,1,512]{3,2,1,0:T(2,128)(2,1)S(1)}, u32[]{:S(2)}, u32[]{:S(2)}) %collective-permute-start) | collective-permute-done | bytes 24608 | tf_op jit(solution)/shard_map/ppermute | solution.py:132
  14.8 5.7 %all-to-all-done = bf16[32,32,128]{2,1,0:T(8,128)(2,1)S(1)} async-done(((bf16[32,32,128]{2,1,0:T(8,128)(2,1)}), bf16[32,32,128]{2,1,0:T(8,128)(2,1)S(1)}, u32[]{:S(2)}, u32[]{:S(2)}) %all-to-all-start) | async-done | bytes 262176 | tf_op jit(solution)/shard_map/all_to_all | solution.py:19
  20.5 1.5 %shard_map.129 = (bf16[16,2,16,128]{3,2,1,0:T(8,128)(2,1)}, bf16[16,2,16,128]{3,2,1,0:T(8,128)(2,1)}) custom-call(s32[3,2]{1,0:T(4,128)} %pad_add_fusion.refs_0_, bf16[16,2,32,128]{3,2,1,0:T(8,128)(2,1)S(1)} %bitcast.18), custom_call_target="tpu_custom_call" | custom-call | flops 4194304 | bytes 1048576 | tf_op jit(solution)/shard_map/pallas_call | solution.py:35
  22.0 2.6 %all-to-all-start.1 = ((bf16[32,16,128]{2,1,0:T(8,128)(2,1)}), bf16[32,16,128]{2,1,0:T(8,128)(2,1)S(1)}, u32[]{:S(2)}, u32[]{:S(2)}) async-start(bf16[32,16,128]{2,1,0:T(8,128)(2,1)} %bitcast.39), calls=%async_computation.1 | async-start | bytes 262144 | tf_op jit(solution)/shard_map/all_to_all | solution.py:19
  25.0 4.4 %collective-permute-start.2 = (bf16[3,1,18,512]{3,2,1,0:T(8,128)(2,1)S(1)}, bf16[3,1,18,512]{3,2,1,0:T(8,128)(2,1)S(1)}, u32[]{:S(2)}, u32[]{:S(2)}) collective-permute-start(bf16[3,1,18,512]{3,2,1,0:T(8,128)(2,1)S(1)} %pad_maximum_fusion.1), channel_id=1, source_target_pairs={{0,30},{2,0},{4,2},{6,4},{8,6},{10,8},{12,10},{14,12},{16,14},{18,... | collective-permute-start | bytes 165896 | tf_op jit(solution)/shard_map/ppermute | solution.py:155
  30.6 3.1 %all-to-all-done.1 = bf16[32,16,128]{2,1,0:T(8,128)(2,1)S(1)} async-done(((bf16[32,16,128]{2,1,0:T(8,128)(2,1)}), bf16[32,16,128]{2,1,0:T(8,128)(2,1)S(1)}, u32[]{:S(2)}, u32[]{:S(2)}) %all-to-all-start.1) | async-done | bytes 131104 | tf_op jit(solution)/shard_map/all_to_all | solution.py:19
  33.7 2.5 %shard_map.131 = (bf16[128,512]{1,0:T(8,128)(2,1)}, bf16[512,128]{1,0:T(8,128)(2,1)}, bf16[128,1024]{1,0:T(8,128)(2,1)}, bf16[10,32,512]{2,1,0:T(8,128)(2,1)}, b...) custom-call(bf16[512,128]{1,0:T(8,128)(2,1)S(1)} %bitcast.19, ...), custom_call_target="tpu_custom_call" | custom-call | flops 268435456 | bytes 4194304 | tf_op jit(solution)/shard_map/pallas_call | solution.py:35
  36.2 3.6 %all-to-all-start.2 = ((bf16[32,16,128]{2,1,0:T(8,128)(2,1)}), bf16[32,16,128]{2,1,0:T(8,128)(2,1)S(1)}, u32[]{:S(2)}, u32[]{:S(2)}) async-start(bf16[32,16,128]{2,1,0:T(8,128)(2,1)} %bitcast.34), calls=%async_computation.2 | async-start | bytes 262144 | tf_op jit(solution)/shard_map/all_to_all | solution.py:19
  39.9 8.4 %all-to-all-done.2 = bf16[32,16,128]{2,1,0:T(8,128)(2,1)S(1)} async-done(((bf16[32,16,128]{2,1,0:T(8,128)(2,1)}), bf16[32,16,128]{2,1,0:T(8,128)(2,1)S(1)}, u32[]{:S(2)}, u32[]{:S(2)}) %all-to-all-start.2) | async-done | bytes 131104 | tf_op jit(solution)/shard_map/all_to_all | solution.py:19
  48.4 2.1 %shard_map.132 = bf16[16,2,16,128]{3,2,1,0:T(8,128)(2,1)} custom-call(s32[3,2]{1,0:T(4,128)} %pad_add_fusion.refs_0_, bf16[16,2,16,128]{3,2,1,0:T(8,128)(2,1)S(1)} %bitcast.21, f32[16,128]{1,0:T(8,128)S(1)} %pad.4.refs_2_, bf16[16,2,16,128]{3,2,1,0:T(8,128)(2,1)} %get-tuple-element.101.refs_3_), custom_call_target="tpu_custom_call" | custom-call | flops 4194304 | bytes 1048576 | tf_op jit(solution)/shard_map/pallas_call | solution.py:35
  50.5 2.6 %all-to-all-start.3 = ((bf16[32,16,128]{2,1,0:T(8,128)(2,1)}), bf16[32,16,128]{2,1,0:T(8,128)(2,1)S(1)}, u32[]{:S(2)}, u32[]{:S(2)}) async-start(bf16[32,16,128]{2,1,0:T(8,128)(2,1)} %bitcast.35), calls=%async_computation.3 | async-start | bytes 262144 | tf_op jit(solution)/shard_map/all_to_all | solution.py:19
  53.1 1.7 %shard_map.135 = (bf16[128,512]{1,0:T(8,128)(2,1)}, bf16[512,128]{1,0:T(8,128)(2,1)}, f32[128,128]{1,0:T(8,128)}, bf16[128,1024]{1,0:T(8,128)(2,1)}, bf16[128,10...) custom-call(bf16[3,8,16,512]{3,2,1,0:T(8,128)(2,1)S(1)} %copy-done.1, ...), custom_call_target="tpu_custom_call" | custom-call | flops 134217728 | bytes 4194304 | tf_op jit(solution)/shard_map/pallas_call | solution.py:35
  54.8 1.7 %shard_map.133 = (bf16[128,512]{1,0:T(8,128)(2,1)}, bf16[512,128]{1,0:T(8,128)(2,1)}, f32[128,128]{1,0:T(8,128)}, bf16[128,1024]{1,0:T(8,128)(2,1)}, bf16[128,10...) custom-call(bf16[3,8,16,512]{3,2,1,0:T(8,128)(2,1)S(1)} %copy-done.1, ...), custom_call_target="tpu_custom_call" | custom-call | flops 134217728 | bytes 4194304 | tf_op jit(solution)/shard_map/pallas_call | solution.py:35
  57.6 4.2 %all-to-all-done.3 = bf16[32,16,128]{2,1,0:T(8,128)(2,1)S(1)} async-done(((bf16[32,16,128]{2,1,0:T(8,128)(2,1)}), bf16[32,16,128]{2,1,0:T(8,128)(2,1)S(1)}, u32[]{:S(2)}, u32[]{:S(2)}) %all-to-all-start.3) | async-done | bytes 131104 | tf_op jit(solution)/shard_map/all_to_all | solution.py:19
  61.7 1.6 %shard_map.136 = (bf16[512,128]{1,0:T(8,128)(2,1)}, bf16[128,1024]{1,0:T(8,128)(2,1)}, bf16[512,128]{1,0:T(8,128)(2,1)}) custom-call(bf16[512,128]{1,0:T(8,128)(2,1)S(1)} %bitcast.20, bf16[512,1024]{1,0:T(8,128)(2,1)S(1)} %copy-done.2, bf16[512,1024]{1,0:T(8,128)(2,1)S(1)} %copy-done, f32[1,512]{1,0:T(1,128)S(1)} %bitcast.31, ...), custom_call_target="tpu_custom_call" | custom-call | flops 268435456 | bytes 4194304 | tf_op jit(solution)/shard_map/pallas_call | solution.py:35
  63.3 11.2 %all_to_all.30 = bf16[32,16,128]{2,1,0:T(8,128)(2,1)S(1)} all-to-all(bf16[32,16,128]{2,1,0:T(8,128)(2,1)} %bitcast.37), channel_id=1, replica_groups=mesh['lon'=16,'lat'=2] {'lon','lat'}, dimensions={0} | all-to-all | bytes 262144 | tf_op jit(solution)/shard_map/all_to_all | solution.py:19
  74.5 2.1 %shard_map.137 = bf16[16,2,16,128]{3,2,1,0:T(8,128)(2,1)} custom-call(s32[3,2]{1,0:T(4,128)} %pad_add_fusion.refs_0_, bf16[16,2,16,128]{3,2,1,0:T(8,128)(2,1)S(1)} %bitcast.22, f32[16,128]{1,0:T(8,128)S(1)} %pad.4.refs_2_, bf16[16,2,16,128]{3,2,1,0:T(8,128)(2,1)} %get-tuple-element.101.refs_3_), custom_call_target="tpu_custom_call" | custom-call | flops 4194304 | bytes 1048576 | tf_op jit(solution)/shard_map/pallas_call | solution.py:35
  76.6 2.8 %all-to-all-start.5 = ((bf16[32,16,128]{2,1,0:T(8,128)(2,1)}), bf16[32,16,128]{2,1,0:T(8,128)(2,1)S(1)}, u32[]{:S(2)}, u32[]{:S(2)}) async-start(bf16[32,16,128]{2,1,0:T(8,128)(2,1)} %bitcast.36), calls=%async_computation.5 | async-start | bytes 262144 | tf_op jit(solution)/shard_map/all_to_all | solution.py:19
  79.4 2.7 %shard_map.139.sums_ref = f32[16,512]{1,0:T(8,128)S(1)} custom-call(bf16[512,1024]{1,0:T(8,128)(2,1)S(1)} %copy-done, f32[1,512]{1,0:T(1,128)S(1)} %bitcast.32, bf16[10,32,512]{2,1,0:T(8,128)(2,1)} %get-tuple-element.130.refs_0_, bf16[512,128]{1,0:T(8,128)(2,1)} %get-tuple-element.100.refs_1_, bf16[128,1024]{1,0:T(8,128)(2,1)} %get-tuple-element.131.refs_2_.refs_7_, ...), custom_call_target="tpu_custom_call" | custom-call | bytes 2097152 | tf_op jit(solution)/shard_map/pallas_call | solution.py:35
  83.3 4.5 %all-to-all-done.5 = bf16[32,16,128]{2,1,0:T(8,128)(2,1)S(1)} async-done(((bf16[32,16,128]{2,1,0:T(8,128)(2,1)}), bf16[32,16,128]{2,1,0:T(8,128)(2,1)S(1)}, u32[]{:S(2)}, u32[]{:S(2)}) %all-to-all-start.5) | async-done | bytes 131104 | tf_op jit(solution)/shard_map/all_to_all | solution.py:19
  87.8 2.0 %shard_map.140 = (bf16[128,512]{1,0:T(8,128)(2,1)S(1)}, f32[16,512]{1,0:T(8,128)S(1)}, bf16[544,512]{1,0:T(8,128)(2,1)S(1)}, bf16[4,128,512]{2,1,0:T(8,128)(2,1)S(1)}) custom-call(bf16[512,128]{1,0:T(8,128)(2,1)S(1)} %bitcast.26, bf16[512,1024]{1,0:T(8,128)(2,1)S(1)} %copy-done.2, bf16[512,1024]{1,0:T(8,128)(2,1)S(1)} %copy-done, f32[1,512]{1,0:T(1,128)S(1)} %bitcast.33, ...), custom_call_target="tpu_custom_call" | custom-call | flops 1073741824 | bytes 6291456 | tf_op jit(solution)/shard_map/pallas_call | solution.py:35
  89.9 2.0 %shard_map.141 = (bf16[512,512]{1,0:T(8,128)(2,1)S(1)}, bf16[4,128,512]{2,1,0:T(8,128)(2,1)S(1)}) custom-call(bf16[512,128]{1,0:T(8,128)(2,1)S(1)} %bitcast.27, bf16[512,128]{1,0:T(8,128)(2,1)} %get-tuple-element.140.refs_0_, bf16[512,128]{1,0:T(8,128)(2,1)} %get-tuple-element.141.refs_1_, bf16[128,1024]{1,0:T(8,128)(2,1)} %get-tuple-element.142.refs_2_, ...), custom_call_target="tpu_custom_call" | custom-call | flops 536870912 | bytes 2097152 | tf_op jit(solution)/shard_map/pallas_call | solution.py:35
  95.0 1.7 %collective-permute-done.4 = bf16[1,8,1,512]{3,2,1,0:T(2,128)(2,1)S(1)} collective-permute-done((bf16[1,8,1,512]{3,2,1,0:T(2,128)(2,1)S(1)}, bf16[1,8,1,512]{3,2,1,0:T(2,128)(2,1)S(1)}, u32[]{:S(2)}, u32[]{:S(2)}) %collective-permute-start.4) | collective-permute-done | bytes 8224 | tf_op jit(solution)/shard_map/ppermute | solution.py:132
  96.7 4.7 %collective-permute-done.8.refs_2_ = bf16[288,512]{1,0:T(8,128)(2,1)S(1)} collective-permute-done((bf16[288,512]{1,0:T(8,128)(2,1)S(1)}, bf16[288,512]{1,0:T(8,128)(2,1)S(1)}, u32[]{:S(2)}, u32[]{:S(2)}) %collective-permute-start.8) | collective-permute-done | bytes 294944 | tf_op jit(solution)/shard_map/ppermute | solution.py:826
  102.7 5.5 %collective-permute-done.9.refs_3_ = bf16[192,512]{1,0:T(8,128)(2,1)S(1)} collective-permute-done((bf16[192,512]{1,0:T(8,128)(2,1)S(1)}, bf16[192,512]{1,0:T(8,128)(2,1)S(1)}, u32[]{:S(2)}, u32[]{:S(2)}) %collective-permute-start.9) | collective-permute-done | bytes 196640 | tf_op jit(solution)/shard_map/ppermute | solution.py:826
  108.4 2.1 %collective-permute-start.14 = (bf16[64,512]{1,0:T(8,128)(2,1)S(1)}, bf16[64,512]{1,0:T(8,128)(2,1)S(1)}, u32[]{:S(2)}, u32[]{:S(2)}) collective-permute-start(bf16[64,512]{1,0:T(8,128)(2,1)S(1)} %get-tuple-element.166), channel_id=1, source_target_pairs={{0,8},{1,9},{2,10},{3,11},{4,12},{5,13},{6,14},{7,15},{8,0},{9,1},... | collective-permute-start | bytes 196616 | tf_op jit(solution)/shard_map/ppermute | solution.py:826
  111.4 1.6 %collective-permute-done.11.refs_2_ = bf16[96,512]{1,0:T(8,128)(2,1)S(1)} collective-permute-done((bf16[96,512]{1,0:T(8,128)(2,1)S(1)}, bf16[96,512]{1,0:T(8,128)(2,1)S(1)}, u32[]{:S(2)}, u32[]{:S(2)}) %collective-permute-start.11) | collective-permute-done | bytes 98336 | tf_op jit(solution)/shard_map/ppermute | solution.py:826
  113.7 2.4 %collective-permute-start.15 = (bf16[32,512]{1,0:T(8,128)(2,1)S(1)}, bf16[32,512]{1,0:T(8,128)(2,1)S(1)}, u32[]{:S(2)}, u32[]{:S(2)}) collective-permute-start(bf16[32,512]{1,0:T(8,128)(2,1)S(1)} %get-tuple-element.174), channel_id=1, source_target_pairs={{0,16},{1,17},{2,18},{3,19},{4,20},{5,21},{6,22},{7,23},{8,24},{9,... | collective-permute-start | bytes 98312 | tf_op jit(solution)/shard_map/ppermute | solution.py:835
  118.7 1.3 %shard_map.151 = (f32[32,512]{1,0:T(8,128)}, f32[32,512]{1,0:T(8,128)}, f32[3,3,512]{2,1,0:T(4,128)}, f32[1,512]{1,0:T(1,128)}) custom-call(f32[32,512]{1,0:T(8,128)S(1)} %get-tuple-element.168.kept_ref, f32[16,512]{1,0:T(8,128)S(1)} %get-tuple-element.169.total_ref, bf16[64,512]{1,0:T(8,128)(2,1)S(1)} %collective-permute-done.13.arrived_ref, ...), custom_call_target="tpu_custom_call" | custom-call | bytes 262144 | tf_op jit(solution)/shard_map/pallas_call | solution.py:35
  (69 shorter events, 14.3 us)
Async XLA Ops:
  0.6 9.2 %copy-start.1 = (bf16[3,8,16,512]{3,2,1,0:T(8,128)(2,1)S(1)}, bf16[3,8,16,512]{3,2,1,0:T(8,128)(2,1)}, u32[]{:S(2)}) copy-start(bf16[3,8,16,512]{3,2,1,0:T(8,128)(2,1)} %refs_0_.4) | copy-start | bytes 1179652
  2.5 18.0 %all-to-all-start = ((bf16[32,32,128]{2,1,0:T(8,128)(2,1)}), bf16[32,32,128]{2,1,0:T(8,128)(2,1)S(1)}, u32[]{:S(2)}, u32[]{:S(2)}) async-start(bf16[32,32,128]{2,1,0:T(8,128)(2,1)} %shard_map.128), calls=%async_computation | async-start | bytes 524288 | tf_op jit(solution)/shard_map/all_to_all | solution.py:19
  9.9 4.8 %collective-permute-start = (bf16[3,8,1,512]{3,2,1,0:T(2,128)(2,1)S(1)}, bf16[3,8,1,512]{3,2,1,0:T(2,128)(2,1)S(1)}, u32[]{:S(2)}, u32[]{:S(2)}) collective-permute-start(bf16[3,8,1,512]{3,2,1,0:T(2,128)(2,1)S(1)} %broadcast_select_fusion.2), channel_id=1, source_target_pairs={{0,1},{1,0},{2,3},{3,2},{4,5},{5,4},{6,7},{7,6},{8,9},{9,8},{10,11... | collective-permute-start | bytes 73736 | tf_op jit(solution)/shard_map/ppermute | solution.py:132
  11.8 0.7 copy-start.6
  11.8 0.7 copy-start.5
  22.0 11.7 %all-to-all-start.1 = ((bf16[32,16,128]{2,1,0:T(8,128)(2,1)}), bf16[32,16,128]{2,1,0:T(8,128)(2,1)S(1)}, u32[]{:S(2)}, u32[]{:S(2)}) async-start(bf16[32,16,128]{2,1,0:T(8,128)(2,1)} %bitcast.39), calls=%async_computation.1 | async-start | bytes 262144 | tf_op jit(solution)/shard_map/all_to_all | solution.py:19
  24.7 9.0 %collective-permute-start.1 = (bf16[3,1,18,512]{3,2,1,0:T(8,128)(2,1)S(1)}, bf16[3,1,18,512]{3,2,1,0:T(8,128)(2,1)S(1)}, u32[]{:S(2)}, u32[]{:S(2)}) collective-permute-start(bf16[3,1,18,512]{3,2,1,0:T(8,128)(2,1)S(1)} %pad_maximum_fusion), channel_id=1, source_target_pairs={{0,2},{2,4},{4,6},{6,8},{8,10},{10,12},{12,14},{14,16},{16,18},{18... | collective-permute-start | bytes 165896 | tf_op jit(solution)/shard_map/ppermute | solution.py:154
  24.9 8.8 %copy-start = (bf16[512,1024]{1,0:T(8,128)(2,1)S(1)}, bf16[512,1024]{1,0:T(8,128)(2,1)}, u32[]{:S(2)}) copy-start(bf16[512,1024]{1,0:T(8,128)(2,1)} %up_ref.5) | copy-start | bytes 3145732
  24.9 8.8 %copy-start.3 = (f32[3,3,512]{2,1,0:T(4,128)S(1)}, f32[3,3,512]{2,1,0:T(4,128)}, u32[]{:S(2)}) copy-start(f32[3,3,512]{2,1,0:T(4,128)} %kernel_ref.1) | copy-start | bytes 55300
  25.0 8.7 %collective-permute-start.2 = (bf16[3,1,18,512]{3,2,1,0:T(8,128)(2,1)S(1)}, bf16[3,1,18,512]{3,2,1,0:T(8,128)(2,1)S(1)}, u32[]{:S(2)}, u32[]{:S(2)}) collective-permute-start(bf16[3,1,18,512]{3,2,1,0:T(8,128)(2,1)S(1)} %pad_maximum_fusion.1), channel_id=1, source_target_pairs={{0,30},{2,0},{4,2},{6,4},{8,6},{10,8},{12,10},{14,12},{16,14},{18,... | collective-permute-start | bytes 165896 | tf_op jit(solution)/shard_map/ppermute | solution.py:155
  30.6 3.1 %copy-start.4 = (f32[512]{0:T(512)S(1)}, f32[512]{0:T(512)}, u32[]{:S(2)}) copy-start(f32[512]{0:T(512)} %param.13) | copy-start | bytes 6148
  36.2 12.2 %all-to-all-start.2 = ((bf16[32,16,128]{2,1,0:T(8,128)(2,1)}), bf16[32,16,128]{2,1,0:T(8,128)(2,1)S(1)}, u32[]{:S(2)}, u32[]{:S(2)}) async-start(bf16[32,16,128]{2,1,0:T(8,128)(2,1)} %bitcast.34), calls=%async_computation.2 | async-start | bytes 262144 | tf_op jit(solution)/shard_map/all_to_all | solution.py:19
  50.5 11.2 %all-to-all-start.3 = ((bf16[32,16,128]{2,1,0:T(8,128)(2,1)}), bf16[32,16,128]{2,1,0:T(8,128)(2,1)S(1)}, u32[]{:S(2)}, u32[]{:S(2)}) async-start(bf16[32,16,128]{2,1,0:T(8,128)(2,1)} %bitcast.35), calls=%async_computation.3 | async-start | bytes 262144 | tf_op jit(solution)/shard_map/all_to_all | solution.py:19
  54.8 6.9 %copy-start.2 = (bf16[512,1024]{1,0:T(8,128)(2,1)S(1)}, bf16[512,1024]{1,0:T(8,128)(2,1)}, u32[]{:S(2)}) copy-start(bf16[512,1024]{1,0:T(8,128)(2,1)} %down_ref.3) | copy-start | bytes 3145732
  76.6 11.2 %all-to-all-start.5 = ((bf16[32,16,128]{2,1,0:T(8,128)(2,1)}), bf16[32,16,128]{2,1,0:T(8,128)(2,1)S(1)}, u32[]{:S(2)}, u32[]{:S(2)}) async-start(bf16[32,16,128]{2,1,0:T(8,128)(2,1)} %bitcast.36), calls=%async_computation.5 | async-start | bytes 262144 | tf_op jit(solution)/shard_map/all_to_all | solution.py:19
  89.9 2.1 %collective-permute-start.3 = (bf16[544,512]{1,0:T(8,128)(2,1)S(1)}, bf16[544,512]{1,0:T(8,128)(2,1)S(1)}, u32[]{:S(2)}, u32[]{:S(2)}) collective-permute-start(bf16[544,512]{1,0:T(8,128)(2,1)S(1)} %get-tuple-element.139), channel_id=1, source_target_pairs={{0,2},{1,3},{2,0},{3,1},{4,6},{5,7},{6,4},{7,5},{8,10},{9,11},{10,... | collective-permute-start | bytes 1671176 | tf_op jit(solution)/shard_map/ppermute | solution.py:826
  92.1 2.1 %collective-permute-start.5 = (bf16[512,512]{1,0:T(8,128)(2,1)S(1)}, bf16[512,512]{1,0:T(8,128)(2,1)S(1)}, u32[]{:S(2)}, u32[]{:S(2)}) collective-permute-start(bf16[512,512]{1,0:T(8,128)(2,1)S(1)} %get-tuple-element.148), channel_id=1, source_target_pairs={{0,2},{1,3},{2,0},{3,1},{4,6},{5,7},{6,4},{7,5},{8,10},{9,11},{10,... | collective-permute-start | bytes 1572872 | tf_op jit(solution)/shard_map/ppermute | solution.py:826
  92.7 8.7 %collective-permute-start.8 = (bf16[288,512]{1,0:T(8,128)(2,1)S(1)}, bf16[288,512]{1,0:T(8,128)(2,1)S(1)}, u32[]{:S(2)}, u32[]{:S(2)}) collective-permute-start(bf16[288,512]{1,0:T(8,128)(2,1)S(1)} %get-tuple-element.145), channel_id=1, source_target_pairs={{0,4},{1,5},{2,3},{3,2},{4,0},{5,1},{6,7},{7,6},{8,12},{9,13},{10,... | collective-permute-start | bytes 884744 | tf_op jit(solution)/shard_map/ppermute | solution.py:826
  92.7 4.0 %collective-permute-start.4 = (bf16[1,8,1,512]{3,2,1,0:T(2,128)(2,1)S(1)}, bf16[1,8,1,512]{3,2,1,0:T(2,128)(2,1)S(1)}, u32[]{:S(2)}, u32[]{:S(2)}) collective-permute-start(bf16[1,8,1,512]{3,2,1,0:T(2,128)(2,1)S(1)} %broadcast_select_fusion.5), channel_id=1, source_target_pairs={{0,1},{1,0},{2,3},{3,2},{4,5},{5,4},{6,7},{7,6},{8,9},{9,8},{10,11... | collective-permute-start | bytes 24584 | tf_op jit(solution)/shard_map/ppermute | solution.py:132
  94.3 7.5 %collective-permute-start.10 = (bf16[256,512]{1,0:T(8,128)(2,1)S(1)}, bf16[256,512]{1,0:T(8,128)(2,1)S(1)}, u32[]{:S(2)}, u32[]{:S(2)}) collective-permute-start(bf16[256,512]{1,0:T(8,128)(2,1)S(1)} %get-tuple-element.149), channel_id=1, source_target_pairs={{0,1},{1,0},{2,6},{3,7},{4,5},{5,4},{6,2},{7,3},{8,9},{9,8},{10,14... | collective-permute-start | bytes 786440 | tf_op jit(solution)/shard_map/ppermute | solution.py:826
  101.5 6.8 %collective-permute-start.9 = (bf16[192,512]{1,0:T(8,128)(2,1)S(1)}, bf16[192,512]{1,0:T(8,128)(2,1)S(1)}, u32[]{:S(2)}, u32[]{:S(2)}) collective-permute-start(bf16[192,512]{1,0:T(8,128)(2,1)S(1)} %get-tuple-element.156), channel_id=1, source_target_pairs={{0,1},{1,0},{2,6},{3,7},{4,5},{5,4},{6,2},{7,3},{8,9},{9,8},{10,14... | collective-permute-start | bytes 589832 | tf_op jit(solution)/shard_map/ppermute | solution.py:826
  101.9 6.4 %collective-permute-start.12 = (bf16[128,512]{1,0:T(8,128)(2,1)S(1)}, bf16[128,512]{1,0:T(8,128)(2,1)S(1)}, u32[]{:S(2)}, u32[]{:S(2)}) collective-permute-start(bf16[128,512]{1,0:T(8,128)(2,1)S(1)} %get-tuple-element.159), channel_id=1, source_target_pairs={{0,4},{1,5},{2,3},{3,2},{4,0},{5,1},{6,7},{7,6},{8,12},{9,13},{10,... | collective-permute-start | bytes 393224 | tf_op jit(solution)/shard_map/ppermute | solution.py:826
  108.3 4.7 %collective-permute-start.11 = (bf16[96,512]{1,0:T(8,128)(2,1)S(1)}, bf16[96,512]{1,0:T(8,128)(2,1)S(1)}, u32[]{:S(2)}, u32[]{:S(2)}) collective-permute-start(bf16[96,512]{1,0:T(8,128)(2,1)S(1)} %get-tuple-element.163), channel_id=1, source_target_pairs={{0,8},{1,9},{2,10},{3,11},{4,12},{5,13},{6,14},{7,15},{8,0},{9,1},... | collective-permute-start | bytes 294920 | tf_op jit(solution)/shard_map/ppermute | solution.py:826
  108.4 5.2 %collective-permute-start.14 = (bf16[64,512]{1,0:T(8,128)(2,1)S(1)}, bf16[64,512]{1,0:T(8,128)(2,1)S(1)}, u32[]{:S(2)}, u32[]{:S(2)}) collective-permute-start(bf16[64,512]{1,0:T(8,128)(2,1)S(1)} %get-tuple-element.166), channel_id=1, source_target_pairs={{0,8},{1,9},{2,10},{3,11},{4,12},{5,13},{6,14},{7,15},{8,0},{9,1},... | collective-permute-start | bytes 196616 | tf_op jit(solution)/shard_map/ppermute | solution.py:826
  110.5 5.6 %collective-permute-start.7 = (bf16[1,1,18,512]{3,2,1,0:T(8,128)(2,1)S(1)}, bf16[1,1,18,512]{3,2,1,0:T(8,128)(2,1)S(1)}, u32[]{:S(2)}, u32[]{:S(2)}) collective-permute-start(bf16[1,1,18,512]{3,2,1,0:T(8,128)(2,1)S(1)} %get-tuple-element.191), channel_id=1, source_target_pairs={{0,2},{2,0},{4,6},{6,4},{8,10},{10,8},{12,14},{14,12},{16,18},{18,... | collective-permute-start | bytes 55304 | tf_op jit(solution)/shard_map/ppermute | solution.py:146
  110.6 6.1 %collective-permute-start.6 = (bf16[1,1,18,512]{3,2,1,0:T(8,128)(2,1)S(1)}, bf16[1,1,18,512]{3,2,1,0:T(8,128)(2,1)S(1)}, u32[]{:S(2)}, u32[]{:S(2)}) collective-permute-start(bf16[1,1,18,512]{3,2,1,0:T(8,128)(2,1)S(1)} %get-tuple-element.192), channel_id=1, source_target_pairs={{0,30},{2,4},{4,2},{6,8},{8,6},{10,12},{12,10},{14,16},{16,14},{18... | collective-permute-start | bytes 55304 | tf_op jit(solution)/shard_map/ppermute | solution.py:148
  113.0 5.4 %collective-permute-start.13 = (bf16[64,512]{1,0:T(8,128)(2,1)S(1)}, bf16[64,512]{1,0:T(8,128)(2,1)S(1)}, u32[]{:S(2)}, u32[]{:S(2)}) collective-permute-start(bf16[64,512]{1,0:T(8,128)(2,1)S(1)} %get-tuple-element.170), channel_id=1, source_target_pairs={{0,16},{1,17},{2,18},{3,19},{4,20},{5,21},{6,22},{7,23},{8,24},{9,... | collective-permute-start | bytes 196616 | tf_op jit(solution)/shard_map/ppermute | solution.py:835
  113.7 5.0 %collective-permute-start.15 = (bf16[32,512]{1,0:T(8,128)(2,1)S(1)}, bf16[32,512]{1,0:T(8,128)(2,1)S(1)}, u32[]{:S(2)}, u32[]{:S(2)}) collective-permute-start(bf16[32,512]{1,0:T(8,128)(2,1)S(1)} %get-tuple-element.174), channel_id=1, source_target_pairs={{0,16},{1,17},{2,18},{3,19},{4,20},{5,21},{6,22},{7,23},{8,24},{9,... | collective-permute-start | bytes 98312 | tf_op jit(solution)/shard_map/ppermute | solution.py:835

commit v10 on v9

--- a/solution.py
+++ b/solution.py
@@ -558,20 +558,18 @@
     refs = list(refs)
     take = lambda: refs.pop(0)
     with_stencil = mode != "first"
-    move_hbm = take()
+    move_ref = take()
     in_ref = take()
     kern_ref = take() if with_stencil else None
-    weight_hbm = take() if mode == "mid" else None
+    weight_ref = take() if mode == "mid" else None
     out_hbm = take()
     saved_hbm = take() if mode == "first" else None
     out_ref, sems = take(), take()
-    spread_ref, weight_ref, move_ref = take(), take(), take()
-    moving = copies(sems, 3, [(move_hbm, move_ref)])
+    spread_ref = take()
+    weight_ref = take() if mode == "first" else weight_ref
     tiles_lon, tiles_lat, _, lanes = in_ref.shape
     rows = out_ref.shape[2]
     started = []
-    if mode == "mid":
-        arriving = copies(sems, 0, [(weight_hbm, weight_ref)])
     if mode == "first":
         weight_ref[...] = in_ref[:, :, rows:]
         started += copies(sems, 0, [(weight_ref, saved_hbm)])
@@ -616,7 +614,6 @@
         grid = {key: grid[key] + mix[1][key] + (high[key] + low[key]) for key in tiles}
     if mode == "mid":
         grid = {key: value.astype(jnp.bfloat16).astype(jnp.float32) for key, value in grid.items()}
-        finish(arriving)
     weights = {}
     for a, b in tiles:
         four = weight_ref[a, b].astype(jnp.float32)[4 * step : 4 * step + 4]
@@ -630,8 +627,7 @@
             spread_ref[place, b] = value
     spread_ref[:, tiles_lat:] = jnp.zeros((tiles_lon + LON_REACH, LAT_REACH, rows, lanes), jnp.float32)
 
-    finish(moving)
-    lon_move, lat_move = move_ref[step, 0], move_ref[step, 1]
+    lon_move, lat_move = (jnp.max(move_ref[2 * step + k : 2 * step + k + 1]) for k in range(2))
     far_lon, off_lon = lon_move // near_lon, lax.rem(lon_move, near_lon)
     far_lat, off_lat = lat_move // near_lat, lax.rem(lat_move, near_lat)
     shift = off_lon * near_lat + off_lat
@@ -666,13 +662,13 @@
     out = [sds(out_shape, jnp.bfloat16)] + ([sds(weight_shape, jnp.bfloat16)] if mode == "first" else [])
     scratch = [pltpu.VMEM(out_shape, jnp.bfloat16), pltpu.SemaphoreType.DMA((4,))]
     spread_shape = (tiles_lon + LON_REACH, tiles_lat + LAT_REACH, rows, lanes)
-    scratch += [pltpu.VMEM(spread_shape, jnp.float32), pltpu.VMEM(weight_shape, jnp.bfloat16)]
-    scratch += [pltpu.SMEM(moves.shape, jnp.int32)]
+    scratch += [pltpu.VMEM(spread_shape, jnp.float32)]
+    scratch += [pltpu.VMEM(weight_shape, jnp.bfloat16)] * (mode == "first")
     return call(
         functools.partial(spatial_kernel, mode, step, *tile),
         out,
         operands,
-        "hv" + "v" * with_stencil + "h" * (mode == "mid"),
+        "vv" + "v" * with_stencil + "v" * (mode == "mid"),
         "h" * len(out),
         scratch=scratch,
         flops=2**22,
@@ -902,43 +898,38 @@
     blocks, states_later = lax.optimization_barrier((blocks, states))
     arrived = as_grid(exchanged(blocks))
     group = me * share // group_size
-    moves = jnp.stack([lon_move[:, group], lat_move[:, group]], axis=1)
+    moves = jnp.stack([lon_move[:, group], lat_move[:, group]], axis=1).reshape(2 * steps, 1)
+    moves = jnp.broadcast_to(jnp.pad(moves, ((0, -2 * steps % 8), (0, 0))), (-(-2 * steps // 8) * 8, 128))
     grid_now, weights = spatial("first", steps - 1, tile, padded_share, arrived, None, None, moves)
 
     taps = lax.dynamic_slice_in_dim(kernel.reshape(9, channels), me * share, share, 1).T
     taps = jnp.pad(taps, ((0, padded_share - share), (0, count - 9)))
 
     around = lat_edges(states_later)
-    grid_now, *around = lax.optimization_barrier((grid_now, *around))
-    around = (*around, *lon_edges_ring(states, *around))
+    around = (*around, *lon_edges(states, *around))
     order = list(reversed(range(steps)))
     gain = norm_gain.reshape(1, channels)
-    now, *others = order
-    forward = {s: forward_parts(s, states, around, kernel, gain, w_up) for s in others}
-    names = {k: {s: forward[s][at] for s in others} for at, k in enumerate(FORWARD)}
+    forward = {s: forward_parts(s, states, around, kernel, gain, w_up) for s in order}
+    names = {k: {s: forward[s][at] for s in order} for at, k in enumerate(FORWARD)}
 
     def taken_back(grid):
         return as_rows(exchanged(grid.reshape(devices, padded_share, count)))
 
     def spread_on(s, field, grid_kernel=taps):
-        arrived = as_grid(exchanged(as_blocks(field)))
-        return spatial("mid", s, tile, padded_share, arrived, grid_kernel, weights, moves)[0]
+        (near,) = fetched([weights], field)
+        arrived = after(as_grid(exchanged(as_blocks(field))), near)
+        return spatial("mid", s, tile, padded_share, arrived, grid_kernel, near, moves)[0]
 
     fields, grads, moved = {}, {}, {}
-    (near,) = fetched([w_down], grid_now)
-    here = after(taken_back(grid_now), near)
-    parts = first_step(now, here, near, states, around, kernel, gain, w_up)
-    for k, value in zip(("n", "turned", "hid", "pad"), parts):
-        names[k][now] = value
-    fields[now], grads[now], moved[now] = parts[4:]
-    for s in others:
-        grid_now = spread_on(s, fields[s + 1])
+    for s in order:
+        if s != order[0]:
+            grid_now = spread_on(s, fields[s + 1])
         here = taken_back(grid_now)
-        wanted = ("slope", "n", "inv") + ("pad",) * (s == others[-1])
+        wanted = ("slope", "n", "inv") + ("pad",) * (s == order[-1])
         near = fetched([names[k][s] for k in wanted], grid_now)
-        if s == others[-1]:
+        if s == order[-1]:
             break
-        here = after(here, (near, forward))
+        here = after(here, (near, forward) if s != order[0] else near)
         fields[s], grads[s], moved[s] = network_back(here, w_down, w_up, gain, *near)
 
     earlier = lambda values: [values[s] for s in order[:-1]]

time: 121 us -> 118 us (0.975)
  blocking collectives: 11.2 us -> 0 us
  waiting for transfers between devices: 43.3 us -> 47.5 us
  starting transfers between devices: 34.3 us -> 37.3 us
  Pallas kernels: 28.2 us -> 29.6 us
    all_to_all x1 -> x0, blocking collectives: 11.2 us -> none  [exchanged(): return lax.all_to_all(blocks, AXES, split_axis=0, concat_axis=0, tiled=True)]
    ppermute x1 -> x2, starting transfers between devices: 0.77 us -> 6.49 us  [lon_edges(): with_last = lax.ppermute(jnp.where(even, first, last), 'lon', pairs)]
    ppermute x2 -> x0, starting transfers between devices: 4.55 us -> none  [the longest x1 4.38 us: lon_edges_ring(): lax.ppermute(value, 'lon', [(i, (i - 1) % lon) for i in range(lon)])]
    all_to_all x5 -> x6, waiting for transfers between devices: 25.9 us -> 29 us  [exchanged(): return lax.all_to_all(blocks, AXES, split_axis=0, concat_axis=0, tiled=True)]
    all_to_all x5 -> x6, starting transfers between devices: 18.8 us -> 20.4 us  [exchanged(): return lax.all_to_all(blocks, AXES, split_axis=0, concat_axis=0, tiled=True)]
    pallas_call x24 -> x27, Pallas kernels: 28.2 us -> 29.6 us  [call(): pl.pallas_call(kernel, out_shape=out_shape, in_specs=[pl.BlockSpec(memory...]
  transfers between devices with their start and end apart: 21 -> 22, of which waited for: 15 -> 15; matrix products, arithmetic and copies ran while one was open for 1% -> 1% of each run, Pallas kernels for 11% -> 15%
where the time goes in v10:
time: 118 us; the launch traced here: 117 us
  waiting for transfers between devices  47.5 us (40%)
  starting transfers between devices  37.3 us (32%)
  Pallas kernels  29.6 us (25%)
  between operations  1.23 us (1%)
    pallas_call x27, Pallas kernels, call(): pl.pallas_call(kernel, out_shape=out_shape, in_specs=[pl.BlockSpec(memory...  29.6 us
    all_to_all x6, waiting for transfers between devices, exchanged(): return lax.all_to_all(blocks, AXES, split_axis=0, concat_axis=0, tiled=True)  29 us
    all_to_all x6, starting transfers between devices, exchanged(): return lax.all_to_all(blocks, AXES, split_axis=0, concat_axis=0, tiled=True)  20.4 us
    ppermute x8, waiting for transfers between devices, halving(): lax.ppermute(send, AXES, [(flat(i, j), flat(*partner(i, j))) for i, j in...  12.6 us
    ppermute x2, starting transfers between devices, lon_edges(): with_last = lax.ppermute(jnp.where(even, first, last), 'lon', pairs)  6.49 us
    ppermute x8, starting transfers between devices, halving(): lax.ppermute(send, AXES, [(flat(i, j), flat(*partner(i, j))) for i, j in...  4.66 us
    ppermute x2, waiting for transfers between devices, lat_edges(): lax.ppermute(jnp.where(lat_at == 0, last, first), 'lat', [(0, 1), (1, 0)])  4.42 us
    ppermute x2, starting transfers between devices, lat_edges(): lax.ppermute(jnp.where(lat_at == 0, last, first), 'lat', [(0, 1), (1, 0)])  2.91 us
  transfers between devices with their start and end apart: 22, of which 15 were waited for; matrix products, arithmetic and copies ran while one was open for 1% of the time, Pallas kernels for 15%

profile of v10, /device:TPU:0, one launch (start us, length us, event | category | flops | bytes accessed | tf_op | source)
XLA Modules:
  0.0 117.2 jit_solution(6271625937081552362)
XLA Ops:
  0.7 1.8 %shard_map.128 = bf16[32,32,128]{2,1,0:T(8,128)(2,1)} custom-call(bf16[128,512]{1,0:T(8,128)(2,1)} %bitcast.41, f32[12,8,16]{2,1,0:T(8,128)} %bitcast.43), custom_call_target="tpu_custom_call" | custom-call | bytes 524288 | tf_op jit(solution)/shard_map/pallas_call | solution.py:35
  2.5 7.3 %all-to-all-start = ((bf16[32,32,128]{2,1,0:T(8,128)(2,1)}), bf16[32,32,128]{2,1,0:T(8,128)(2,1)S(1)}, u32[]{:S(2)}, u32[]{:S(2)}) async-start(bf16[32,32,128]{2,1,0:T(8,128)(2,1)} %shard_map.128), calls=%async_computation | async-start | bytes 524288 | tf_op jit(solution)/shard_map/all_to_all | solution.py:19
  9.9 1.8 %collective-permute-start = (bf16[3,8,1,512]{3,2,1,0:T(2,128)(2,1)S(1)}, bf16[3,8,1,512]{3,2,1,0:T(2,128)(2,1)S(1)}, u32[]{:S(2)}, u32[]{:S(2)}) collective-permute-start(bf16[3,8,1,512]{3,2,1,0:T(2,128)(2,1)S(1)} %broadcast_select_fusion.2), channel_id=1, source_target_pairs={{0,1},{1,0},{2,3},{3,2},{4,5},{5,4},{6,7},{7,6},{8,9},{9,8},{10,11... | collective-permute-start | bytes 73736 | tf_op jit(solution)/shard_map/ppermute | solution.py:132
  12.0 2.7 %collective-permute-done = bf16[3,8,1,512]{3,2,1,0:T(2,128)(2,1)S(1)} collective-permute-done((bf16[3,8,1,512]{3,2,1,0:T(2,128)(2,1)S(1)}, bf16[3,8,1,512]{3,2,1,0:T(2,128)(2,1)S(1)}, u32[]{:S(2)}, u32[]{:S(2)}) %collective-permute-start) | collective-permute-done | bytes 24608 | tf_op jit(solution)/shard_map/ppermute | solution.py:132
  15.1 5.7 %collective-permute-start.1 = (bf16[3,1,18,512]{3,2,1,0:T(8,128)(2,1)S(1)}, bf16[3,1,18,512]{3,2,1,0:T(8,128)(2,1)S(1)}, u32[]{:S(2)}, u32[]{:S(2)}) collective-permute-start(bf16[3,1,18,512]{3,2,1,0:T(8,128)(2,1)S(1)} %get-tuple-element.202), channel_id=1, source_target_pairs={{0,30},{2,4},{4,2},{6,8},{8,6},{10,12},{12,10},{14,16},{16,14},{18... | collective-permute-start | bytes 165896 | tf_op jit(solution)/shard_map/ppermute | solution.py:148
  20.8 1.3 %shard_map.129 = (bf16[16,2,16,128]{3,2,1,0:T(8,128)(2,1)}, bf16[16,2,16,128]{3,2,1,0:T(8,128)(2,1)}) custom-call(s32[8,128]{1,0:T(8,128)S(1)} %broadcast_in_dim.20.refs_0_, bf16[16,2,32,128]{3,2,1,0:T(8,128)(2,1)S(1)} %bitcast.20), custom_call_target="tpu_custom_call" | custom-call | flops 4194304 | bytes 1048576 | tf_op jit(solution)/shard_map/pallas_call | solution.py:35
  22.2 2.6 %all-to-all-start.1 = ((bf16[32,16,128]{2,1,0:T(8,128)(2,1)}), bf16[32,16,128]{2,1,0:T(8,128)(2,1)S(1)}, u32[]{:S(2)}, u32[]{:S(2)}) async-start(bf16[32,16,128]{2,1,0:T(8,128)(2,1)} %bitcast.42), calls=%async_computation.1 | async-start | bytes 262144 | tf_op jit(solution)/shard_map/all_to_all | solution.py:19
  25.5 1.7 %shard_map.130 = (bf16[128,512]{1,0:T(8,128)(2,1)}, bf16[512,128]{1,0:T(8,128)(2,1)}, f32[128,128]{1,0:T(8,128)}, bf16[128,1024]{1,0:T(8,128)(2,1)}, bf16[128,10...) custom-call(bf16[3,8,16,512]{3,2,1,0:T(8,128)(2,1)S(1)} %copy-done.1, ...), custom_call_target="tpu_custom_call" | custom-call | flops 134217728 | bytes 4194304 | tf_op jit(solution)/shard_map/pallas_call | solution.py:35
  28.3 5.1 %all-to-all-done.1 = bf16[32,16,128]{2,1,0:T(8,128)(2,1)S(1)} async-done(((bf16[32,16,128]{2,1,0:T(8,128)(2,1)}), bf16[32,16,128]{2,1,0:T(8,128)(2,1)S(1)}, u32[]{:S(2)}, u32[]{:S(2)}) %all-to-all-start.1) | async-done | bytes 131104 | tf_op jit(solution)/shard_map/all_to_all | solution.py:19
  33.4 1.6 %shard_map.132 = (bf16[512,128]{1,0:T(8,128)(2,1)}, bf16[128,1024]{1,0:T(8,128)(2,1)}, bf16[512,128]{1,0:T(8,128)(2,1)}) custom-call(bf16[512,128]{1,0:T(8,128)(2,1)S(1)} %bitcast.21, bf16[512,1024]{1,0:T(8,128)(2,1)S(1)} %copy-done.2, bf16[512,1024]{1,0:T(8,128)(2,1)S(1)} %copy-done, f32[1,512]{1,0:T(1,128)S(1)} %bitcast.31, ...), custom_call_target="tpu_custom_call" | custom-call | flops 268435456 | bytes 4194304 | tf_op jit(solution)/shard_map/pallas_call | solution.py:35
  35.0 2.6 %all-to-all-start.2 = ((bf16[32,16,128]{2,1,0:T(8,128)(2,1)}), bf16[32,16,128]{2,1,0:T(8,128)(2,1)S(1)}, u32[]{:S(2)}, u32[]{:S(2)}) async-start(bf16[32,16,128]{2,1,0:T(8,128)(2,1)} %bitcast.37), calls=%async_computation.2 | async-start | bytes 262144 | tf_op jit(solution)/shard_map/all_to_all | solution.py:19
  38.7 7.5 %all-to-all-done.2 = bf16[32,16,128]{2,1,0:T(8,128)(2,1)S(1)} async-done(((bf16[32,16,128]{2,1,0:T(8,128)(2,1)}), bf16[32,16,128]{2,1,0:T(8,128)(2,1)S(1)}, u32[]{:S(2)}, u32[]{:S(2)}) %all-to-all-start.2) | async-done | bytes 131104 | tf_op jit(solution)/shard_map/all_to_all | solution.py:19
  46.2 1.7 %shard_map.134 = bf16[16,2,16,128]{3,2,1,0:T(8,128)(2,1)} custom-call(s32[8,128]{1,0:T(8,128)S(1)} %broadcast_in_dim.20.refs_0_, bf16[16,2,16,128]{3,2,1,0:T(8,128)(2,1)S(1)} %bitcast.23, f32[16,128]{1,0:T(8,128)S(1)} %pad.9.refs_2_, bf16[16,2,16,128]{3,2,1,0:T(8,128)(2,1)S(1)} %shard_map.133.refs_3_), custom_call_target="tpu_custom_call" | custom-call | flops 4194304 | bytes 1048576 | tf_op jit(solution)/shard_map/pallas_call | solution.py:35
  47.9 2.6 %all-to-all-start.3 = ((bf16[32,16,128]{2,1,0:T(8,128)(2,1)}), bf16[32,16,128]{2,1,0:T(8,128)(2,1)S(1)}, u32[]{:S(2)}, u32[]{:S(2)}) async-start(bf16[32,16,128]{2,1,0:T(8,128)(2,1)} %bitcast.39), calls=%async_computation.3 | async-start | bytes 262144 | tf_op jit(solution)/shard_map/all_to_all | solution.py:19
  50.5 1.7 %shard_map.137 = (bf16[128,512]{1,0:T(8,128)(2,1)}, bf16[512,128]{1,0:T(8,128)(2,1)}, f32[128,128]{1,0:T(8,128)}, bf16[128,1024]{1,0:T(8,128)(2,1)}, bf16[128,10...) custom-call(bf16[3,8,16,512]{3,2,1,0:T(8,128)(2,1)S(1)} %copy-done.1, ...), custom_call_target="tpu_custom_call" | custom-call | flops 134217728 | bytes 4194304 | tf_op jit(solution)/shard_map/pallas_call | solution.py:35
  52.3 1.7 %shard_map.135 = (bf16[128,512]{1,0:T(8,128)(2,1)}, bf16[512,128]{1,0:T(8,128)(2,1)}, f32[128,128]{1,0:T(8,128)}, bf16[128,1024]{1,0:T(8,128)(2,1)}, bf16[128,10...) custom-call(bf16[3,8,16,512]{3,2,1,0:T(8,128)(2,1)S(1)} %copy-done.1, ...), custom_call_target="tpu_custom_call" | custom-call | flops 134217728 | bytes 4194304 | tf_op jit(solution)/shard_map/pallas_call | solution.py:35
  55.0 4.1 %all-to-all-done.3 = bf16[32,16,128]{2,1,0:T(8,128)(2,1)S(1)} async-done(((bf16[32,16,128]{2,1,0:T(8,128)(2,1)}), bf16[32,16,128]{2,1,0:T(8,128)(2,1)S(1)}, u32[]{:S(2)}, u32[]{:S(2)}) %all-to-all-start.3) | async-done | bytes 131104 | tf_op jit(solution)/shard_map/all_to_all | solution.py:19
  59.2 1.6 %shard_map.138 = (bf16[512,128]{1,0:T(8,128)(2,1)}, bf16[128,1024]{1,0:T(8,128)(2,1)}, bf16[512,128]{1,0:T(8,128)(2,1)}) custom-call(bf16[512,128]{1,0:T(8,128)(2,1)S(1)} %bitcast.22, bf16[512,1024]{1,0:T(8,128)(2,1)S(1)} %copy-done.2, bf16[512,1024]{1,0:T(8,128)(2,1)S(1)} %copy-done, f32[1,512]{1,0:T(1,128)S(1)} %bitcast.34, ...), custom_call_target="tpu_custom_call" | custom-call | flops 268435456 | bytes 4194304 | tf_op jit(solution)/shard_map/pallas_call | solution.py:35
  60.7 2.6 %all-to-all-start.4 = ((bf16[32,16,128]{2,1,0:T(8,128)(2,1)}), bf16[32,16,128]{2,1,0:T(8,128)(2,1)S(1)}, u32[]{:S(2)}, u32[]{:S(2)}) async-start(bf16[32,16,128]{2,1,0:T(8,128)(2,1)} %bitcast.38), calls=%async_computation.4 | async-start | bytes 262144 | tf_op jit(solution)/shard_map/all_to_all | solution.py:19
  64.3 7.7 %all-to-all-done.4 = bf16[32,16,128]{2,1,0:T(8,128)(2,1)S(1)} async-done(((bf16[32,16,128]{2,1,0:T(8,128)(2,1)}), bf16[32,16,128]{2,1,0:T(8,128)(2,1)S(1)}, u32[]{:S(2)}, u32[]{:S(2)}) %all-to-all-start.4) | async-done | bytes 131104 | tf_op jit(solution)/shard_map/all_to_all | solution.py:19
  72.0 1.7 %shard_map.140 = bf16[16,2,16,128]{3,2,1,0:T(8,128)(2,1)} custom-call(s32[8,128]{1,0:T(8,128)S(1)} %broadcast_in_dim.20.refs_0_, bf16[16,2,16,128]{3,2,1,0:T(8,128)(2,1)S(1)} %bitcast.24, f32[16,128]{1,0:T(8,128)S(1)} %pad.9.refs_2_, bf16[16,2,16,128]{3,2,1,0:T(8,128)(2,1)S(1)} %shard_map.139.refs_3_), custom_call_target="tpu_custom_call" | custom-call | flops 4194304 | bytes 1048576 | tf_op jit(solution)/shard_map/pallas_call | solution.py:35
  73.7 2.8 %all-to-all-start.5 = ((bf16[32,16,128]{2,1,0:T(8,128)(2,1)}), bf16[32,16,128]{2,1,0:T(8,128)(2,1)S(1)}, u32[]{:S(2)}, u32[]{:S(2)}) async-start(bf16[32,16,128]{2,1,0:T(8,128)(2,1)} %bitcast.40), calls=%async_computation.5 | async-start | bytes 262144 | tf_op jit(solution)/shard_map/all_to_all | solution.py:19
  76.4 2.7 %shard_map.142.sums_ref = f32[16,512]{1,0:T(8,128)S(1)} custom-call(bf16[512,1024]{1,0:T(8,128)(2,1)S(1)} %copy-done, f32[1,512]{1,0:T(1,128)S(1)} %bitcast.35, bf16[10,32,512]{2,1,0:T(8,128)(2,1)} %get-tuple-element.137.refs_0_, bf16[512,128]{1,0:T(8,128)(2,1)} %get-tuple-element.113.refs_1_, bf16[128,1024]{1,0:T(8,128)(2,1)} %get-tuple-element.150.refs_2_.refs_7_, ...), custom_call_target="tpu_custom_call" | custom-call | bytes 2097152 | tf_op jit(solution)/shard_map/pallas_call | solution.py:35
  80.4 4.5 %all-to-all-done.5 = bf16[32,16,128]{2,1,0:T(8,128)(2,1)S(1)} async-done(((bf16[32,16,128]{2,1,0:T(8,128)(2,1)}), bf16[32,16,128]{2,1,0:T(8,128)(2,1)S(1)}, u32[]{:S(2)}, u32[]{:S(2)}) %all-to-all-start.5) | async-done | bytes 131104 | tf_op jit(solution)/shard_map/all_to_all | solution.py:19
  84.9 2.0 %shard_map.143 = (bf16[128,512]{1,0:T(8,128)(2,1)S(1)}, f32[16,512]{1,0:T(8,128)S(1)}, bf16[544,512]{1,0:T(8,128)(2,1)S(1)}, bf16[4,128,512]{2,1,0:T(8,128)(2,1)S(1)}) custom-call(bf16[512,128]{1,0:T(8,128)(2,1)S(1)} %bitcast.28, bf16[512,1024]{1,0:T(8,128)(2,1)S(1)} %copy-done.2, bf16[512,1024]{1,0:T(8,128)(2,1)S(1)} %copy-done, f32[1,512]{1,0:T(1,128)S(1)} %bitcast.36, ...), custom_call_target="tpu_custom_call" | custom-call | flops 1073741824 | bytes 6291456 | tf_op jit(solution)/shard_map/pallas_call | solution.py:35
  87.0 2.0 %shard_map.144 = (bf16[512,512]{1,0:T(8,128)(2,1)S(1)}, bf16[4,128,512]{2,1,0:T(8,128)(2,1)S(1)}) custom-call(bf16[512,128]{1,0:T(8,128)(2,1)S(1)} %bitcast.29, bf16[512,128]{1,0:T(8,128)(2,1)} %get-tuple-element.157.refs_0_, bf16[512,128]{1,0:T(8,128)(2,1)} %get-tuple-element.158.refs_1_, bf16[128,1024]{1,0:T(8,128)(2,1)} %get-tuple-element.136.refs_2_, ...), custom_call_target="tpu_custom_call" | custom-call | flops 536870912 | bytes 2097152 | tf_op jit(solution)/shard_map/pallas_call | solution.py:35
  92.1 1.7 %collective-permute-done.4 = bf16[1,8,1,512]{3,2,1,0:T(2,128)(2,1)S(1)} collective-permute-done((bf16[1,8,1,512]{3,2,1,0:T(2,128)(2,1)S(1)}, bf16[1,8,1,512]{3,2,1,0:T(2,128)(2,1)S(1)}, u32[]{:S(2)}, u32[]{:S(2)}) %collective-permute-start.4) | collective-permute-done | bytes 8224 | tf_op jit(solution)/shard_map/ppermute | solution.py:132
  93.8 4.7 %collective-permute-done.8.refs_2_ = bf16[288,512]{1,0:T(8,128)(2,1)S(1)} collective-permute-done((bf16[288,512]{1,0:T(8,128)(2,1)S(1)}, bf16[288,512]{1,0:T(8,128)(2,1)S(1)}, u32[]{:S(2)}, u32[]{:S(2)}) %collective-permute-start.8) | collective-permute-done | bytes 294944 | tf_op jit(solution)/shard_map/ppermute | solution.py:822
  99.8 5.5 %collective-permute-done.9.refs_3_ = bf16[192,512]{1,0:T(8,128)(2,1)S(1)} collective-permute-done((bf16[192,512]{1,0:T(8,128)(2,1)S(1)}, bf16[192,512]{1,0:T(8,128)(2,1)S(1)}, u32[]{:S(2)}, u32[]{:S(2)}) %collective-permute-start.9) | collective-permute-done | bytes 196640 | tf_op jit(solution)/shard_map/ppermute | solution.py:822
  105.5 2.1 %collective-permute-start.14 = (bf16[64,512]{1,0:T(8,128)(2,1)S(1)}, bf16[64,512]{1,0:T(8,128)(2,1)S(1)}, u32[]{:S(2)}, u32[]{:S(2)}) collective-permute-start(bf16[64,512]{1,0:T(8,128)(2,1)S(1)} %get-tuple-element.182), channel_id=1, source_target_pairs={{0,8},{1,9},{2,10},{3,11},{4,12},{5,13},{6,14},{7,15},{8,0},{9,1},... | collective-permute-start | bytes 196616 | tf_op jit(solution)/shard_map/ppermute | solution.py:822
  108.4 1.6 %collective-permute-done.11.refs_2_ = bf16[96,512]{1,0:T(8,128)(2,1)S(1)} collective-permute-done((bf16[96,512]{1,0:T(8,128)(2,1)S(1)}, bf16[96,512]{1,0:T(8,128)(2,1)S(1)}, u32[]{:S(2)}, u32[]{:S(2)}) %collective-permute-start.11) | collective-permute-done | bytes 98336 | tf_op jit(solution)/shard_map/ppermute | solution.py:822
  110.7 2.4 %collective-permute-start.15 = (bf16[32,512]{1,0:T(8,128)(2,1)S(1)}, bf16[32,512]{1,0:T(8,128)(2,1)S(1)}, u32[]{:S(2)}, u32[]{:S(2)}) collective-permute-start(bf16[32,512]{1,0:T(8,128)(2,1)S(1)} %get-tuple-element.190), channel_id=1, source_target_pairs={{0,16},{1,17},{2,18},{3,19},{4,20},{5,21},{6,22},{7,23},{8,24},{9,... | collective-permute-start | bytes 98312 | tf_op jit(solution)/shard_map/ppermute | solution.py:831
  (75 shorter events, 16.7 us)
Async XLA Ops:
  0.6 9.2 %copy-start.1 = (bf16[3,8,16,512]{3,2,1,0:T(8,128)(2,1)S(1)}, bf16[3,8,16,512]{3,2,1,0:T(8,128)(2,1)}, u32[]{:S(2)}) copy-start(bf16[3,8,16,512]{3,2,1,0:T(8,128)(2,1)} %refs_0_.5) | copy-start | bytes 1179652
  0.6 11.1 %copy-start.5 = (s32[3,4]{1,0:T(4,128)S(1)}, s32[3,4]{1,0:T(4,128)}, u32[]{:S(2)}) copy-start(s32[3,4]{1,0:T(4,128)} %param.17) | copy-start | bytes 148
  0.7 11.1 %copy-start.6 = (s32[3,4]{1,0:T(4,128)S(1)}, s32[3,4]{1,0:T(4,128)}, u32[]{:S(2)}) copy-start(s32[3,4]{1,0:T(4,128)} %param.16) | copy-start | bytes 148
  2.5 22.3 %copy-start = (bf16[512,1024]{1,0:T(8,128)(2,1)S(1)}, bf16[512,1024]{1,0:T(8,128)(2,1)}, u32[]{:S(2)}) copy-start(bf16[512,1024]{1,0:T(8,128)(2,1)} %up_ref.7) | copy-start | bytes 3145732
  2.5 18.2 %all-to-all-start = ((bf16[32,32,128]{2,1,0:T(8,128)(2,1)}), bf16[32,32,128]{2,1,0:T(8,128)(2,1)S(1)}, u32[]{:S(2)}, u32[]{:S(2)}) async-start(bf16[32,32,128]{2,1,0:T(8,128)(2,1)} %shard_map.128), calls=%async_computation | async-start | bytes 524288 | tf_op jit(solution)/shard_map/all_to_all | solution.py:19
  9.9 4.8 %collective-permute-start = (bf16[3,8,1,512]{3,2,1,0:T(2,128)(2,1)S(1)}, bf16[3,8,1,512]{3,2,1,0:T(2,128)(2,1)S(1)}, u32[]{:S(2)}, u32[]{:S(2)}) collective-permute-start(bf16[3,8,1,512]{3,2,1,0:T(2,128)(2,1)S(1)} %broadcast_select_fusion.2), channel_id=1, source_target_pairs={{0,1},{1,0},{2,3},{3,2},{4,5},{5,4},{6,7},{7,6},{8,9},{9,8},{10,11... | collective-permute-start | bytes 73736 | tf_op jit(solution)/shard_map/ppermute | solution.py:132
  15.0 9.8 %collective-permute-start.2 = (bf16[3,1,18,512]{3,2,1,0:T(8,128)(2,1)S(1)}, bf16[3,1,18,512]{3,2,1,0:T(8,128)(2,1)S(1)}, u32[]{:S(2)}, u32[]{:S(2)}) collective-permute-start(bf16[3,1,18,512]{3,2,1,0:T(8,128)(2,1)S(1)} %get-tuple-element.201), channel_id=1, source_target_pairs={{0,2},{2,0},{4,6},{6,4},{8,10},{10,8},{12,14},{14,12},{16,18},{18,... | collective-permute-start | bytes 165896 | tf_op jit(solution)/shard_map/ppermute | solution.py:146
  15.1 9.8 %collective-permute-start.1 = (bf16[3,1,18,512]{3,2,1,0:T(8,128)(2,1)S(1)}, bf16[3,1,18,512]{3,2,1,0:T(8,128)(2,1)S(1)}, u32[]{:S(2)}, u32[]{:S(2)}) collective-permute-start(bf16[3,1,18,512]{3,2,1,0:T(8,128)(2,1)S(1)} %get-tuple-element.202), channel_id=1, source_target_pairs={{0,30},{2,4},{4,2},{6,8},{8,6},{10,12},{12,10},{14,16},{16,14},{18... | collective-permute-start | bytes 165896 | tf_op jit(solution)/shard_map/ppermute | solution.py:148
  22.2 11.2 %all-to-all-start.1 = ((bf16[32,16,128]{2,1,0:T(8,128)(2,1)}), bf16[32,16,128]{2,1,0:T(8,128)(2,1)S(1)}, u32[]{:S(2)}, u32[]{:S(2)}) async-start(bf16[32,16,128]{2,1,0:T(8,128)(2,1)} %bitcast.42), calls=%async_computation.1 | async-start | bytes 262144 | tf_op jit(solution)/shard_map/all_to_all | solution.py:19
  24.8 0.7 copy-start.3
  24.9 0.7 copy-start.4
  25.5 7.9 %copy-start.2 = (bf16[512,1024]{1,0:T(8,128)(2,1)S(1)}, bf16[512,1024]{1,0:T(8,128)(2,1)}, u32[]{:S(2)}) copy-start(bf16[512,1024]{1,0:T(8,128)(2,1)} %down_ref.5) | copy-start | bytes 3145732
  35.0 11.2 %all-to-all-start.2 = ((bf16[32,16,128]{2,1,0:T(8,128)(2,1)}), bf16[32,16,128]{2,1,0:T(8,128)(2,1)S(1)}, u32[]{:S(2)}, u32[]{:S(2)}) async-start(bf16[32,16,128]{2,1,0:T(8,128)(2,1)} %bitcast.37), calls=%async_computation.2 | async-start | bytes 262144 | tf_op jit(solution)/shard_map/all_to_all | solution.py:19
  47.9 11.2 %all-to-all-start.3 = ((bf16[32,16,128]{2,1,0:T(8,128)(2,1)}), bf16[32,16,128]{2,1,0:T(8,128)(2,1)S(1)}, u32[]{:S(2)}, u32[]{:S(2)}) async-start(bf16[32,16,128]{2,1,0:T(8,128)(2,1)} %bitcast.39), calls=%async_computation.3 | async-start | bytes 262144 | tf_op jit(solution)/shard_map/all_to_all | solution.py:19
  60.7 11.2 %all-to-all-start.4 = ((bf16[32,16,128]{2,1,0:T(8,128)(2,1)}), bf16[32,16,128]{2,1,0:T(8,128)(2,1)S(1)}, u32[]{:S(2)}, u32[]{:S(2)}) async-start(bf16[32,16,128]{2,1,0:T(8,128)(2,1)} %bitcast.38), calls=%async_computation.4 | async-start | bytes 262144 | tf_op jit(solution)/shard_map/all_to_all | solution.py:19
  73.7 11.2 %all-to-all-start.5 = ((bf16[32,16,128]{2,1,0:T(8,128)(2,1)}), bf16[32,16,128]{2,1,0:T(8,128)(2,1)S(1)}, u32[]{:S(2)}, u32[]{:S(2)}) async-start(bf16[32,16,128]{2,1,0:T(8,128)(2,1)} %bitcast.40), calls=%async_computation.5 | async-start | bytes 262144 | tf_op jit(solution)/shard_map/all_to_all | solution.py:19
  86.9 2.1 %collective-permute-start.3 = (bf16[544,512]{1,0:T(8,128)(2,1)S(1)}, bf16[544,512]{1,0:T(8,128)(2,1)S(1)}, u32[]{:S(2)}, u32[]{:S(2)}) collective-permute-start(bf16[544,512]{1,0:T(8,128)(2,1)S(1)} %get-tuple-element.156), channel_id=1, source_target_pairs={{0,2},{1,3},{2,0},{3,1},{4,6},{5,7},{6,4},{7,5},{8,10},{9,11},{10,... | collective-permute-start | bytes 1671176 | tf_op jit(solution)/shard_map/ppermute | solution.py:822
  89.2 2.1 %collective-permute-start.5 = (bf16[512,512]{1,0:T(8,128)(2,1)S(1)}, bf16[512,512]{1,0:T(8,128)(2,1)S(1)}, u32[]{:S(2)}, u32[]{:S(2)}) collective-permute-start(bf16[512,512]{1,0:T(8,128)(2,1)S(1)} %get-tuple-element.164), channel_id=1, source_target_pairs={{0,2},{1,3},{2,0},{3,1},{4,6},{5,7},{6,4},{7,5},{8,10},{9,11},{10,... | collective-permute-start | bytes 1572872 | tf_op jit(solution)/shard_map/ppermute | solution.py:822
  89.7 8.7 %collective-permute-start.8 = (bf16[288,512]{1,0:T(8,128)(2,1)S(1)}, bf16[288,512]{1,0:T(8,128)(2,1)S(1)}, u32[]{:S(2)}, u32[]{:S(2)}) collective-permute-start(bf16[288,512]{1,0:T(8,128)(2,1)S(1)} %get-tuple-element.161), channel_id=1, source_target_pairs={{0,4},{1,5},{2,3},{3,2},{4,0},{5,1},{6,7},{7,6},{8,12},{9,13},{10,... | collective-permute-start | bytes 884744 | tf_op jit(solution)/shard_map/ppermute | solution.py:822
  89.8 4.0 %collective-permute-start.4 = (bf16[1,8,1,512]{3,2,1,0:T(2,128)(2,1)S(1)}, bf16[1,8,1,512]{3,2,1,0:T(2,128)(2,1)S(1)}, u32[]{:S(2)}, u32[]{:S(2)}) collective-permute-start(bf16[1,8,1,512]{3,2,1,0:T(2,128)(2,1)S(1)} %broadcast_select_fusion.9), channel_id=1, source_target_pairs={{0,1},{1,0},{2,3},{3,2},{4,5},{5,4},{6,7},{7,6},{8,9},{9,8},{10,11... | collective-permute-start | bytes 24584 | tf_op jit(solution)/shard_map/ppermute | solution.py:132
  91.4 7.5 %collective-permute-start.10 = (bf16[256,512]{1,0:T(8,128)(2,1)S(1)}, bf16[256,512]{1,0:T(8,128)(2,1)S(1)}, u32[]{:S(2)}, u32[]{:S(2)}) collective-permute-start(bf16[256,512]{1,0:T(8,128)(2,1)S(1)} %get-tuple-element.165), channel_id=1, source_target_pairs={{0,1},{1,0},{2,6},{3,7},{4,5},{5,4},{6,2},{7,3},{8,9},{9,8},{10,14... | collective-permute-start | bytes 786440 | tf_op jit(solution)/shard_map/ppermute | solution.py:822
  98.5 6.8 %collective-permute-start.9 = (bf16[192,512]{1,0:T(8,128)(2,1)S(1)}, bf16[192,512]{1,0:T(8,128)(2,1)S(1)}, u32[]{:S(2)}, u32[]{:S(2)}) collective-permute-start(bf16[192,512]{1,0:T(8,128)(2,1)S(1)} %get-tuple-element.172), channel_id=1, source_target_pairs={{0,1},{1,0},{2,6},{3,7},{4,5},{5,4},{6,2},{7,3},{8,9},{9,8},{10,14... | collective-permute-start | bytes 589832 | tf_op jit(solution)/shard_map/ppermute | solution.py:822
  99.0 6.4 %collective-permute-start.12 = (bf16[128,512]{1,0:T(8,128)(2,1)S(1)}, bf16[128,512]{1,0:T(8,128)(2,1)S(1)}, u32[]{:S(2)}, u32[]{:S(2)}) collective-permute-start(bf16[128,512]{1,0:T(8,128)(2,1)S(1)} %get-tuple-element.175), channel_id=1, source_target_pairs={{0,4},{1,5},{2,3},{3,2},{4,0},{5,1},{6,7},{7,6},{8,12},{9,13},{10,... | collective-permute-start | bytes 393224 | tf_op jit(solution)/shard_map/ppermute | solution.py:822
  105.3 4.7 %collective-permute-start.11 = (bf16[96,512]{1,0:T(8,128)(2,1)S(1)}, bf16[96,512]{1,0:T(8,128)(2,1)S(1)}, u32[]{:S(2)}, u32[]{:S(2)}) collective-permute-start(bf16[96,512]{1,0:T(8,128)(2,1)S(1)} %get-tuple-element.179), channel_id=1, source_target_pairs={{0,8},{1,9},{2,10},{3,11},{4,12},{5,13},{6,14},{7,15},{8,0},{9,1},... | collective-permute-start | bytes 294920 | tf_op jit(solution)/shard_map/ppermute | solution.py:822
  105.5 5.2 %collective-permute-start.14 = (bf16[64,512]{1,0:T(8,128)(2,1)S(1)}, bf16[64,512]{1,0:T(8,128)(2,1)S(1)}, u32[]{:S(2)}, u32[]{:S(2)}) collective-permute-start(bf16[64,512]{1,0:T(8,128)(2,1)S(1)} %get-tuple-element.182), channel_id=1, source_target_pairs={{0,8},{1,9},{2,10},{3,11},{4,12},{5,13},{6,14},{7,15},{8,0},{9,1},... | collective-permute-start | bytes 196616 | tf_op jit(solution)/shard_map/ppermute | solution.py:822
  107.6 5.6 %collective-permute-start.7 = (bf16[1,1,18,512]{3,2,1,0:T(8,128)(2,1)S(1)}, bf16[1,1,18,512]{3,2,1,0:T(8,128)(2,1)S(1)}, u32[]{:S(2)}, u32[]{:S(2)}) collective-permute-start(bf16[1,1,18,512]{3,2,1,0:T(8,128)(2,1)S(1)} %get-tuple-element.211), channel_id=1, source_target_pairs={{0,2},{2,0},{4,6},{6,4},{8,10},{10,8},{12,14},{14,12},{16,18},{18,... | collective-permute-start | bytes 55304 | tf_op jit(solution)/shard_map/ppermute | solution.py:146
  107.6 6.1 %collective-permute-start.6 = (bf16[1,1,18,512]{3,2,1,0:T(8,128)(2,1)S(1)}, bf16[1,1,18,512]{3,2,1,0:T(8,128)(2,1)S(1)}, u32[]{:S(2)}, u32[]{:S(2)}) collective-permute-start(bf16[1,1,18,512]{3,2,1,0:T(8,128)(2,1)S(1)} %get-tuple-element.212), channel_id=1, source_target_pairs={{0,30},{2,4},{4,2},{6,8},{8,6},{10,12},{12,10},{14,16},{16,14},{18... | collective-permute-start | bytes 55304 | tf_op jit(solution)/shard_map/ppermute | solution.py:148
  110.1 5.4 %collective-permute-start.13 = (bf16[64,512]{1,0:T(8,128)(2,1)S(1)}, bf16[64,512]{1,0:T(8,128)(2,1)S(1)}, u32[]{:S(2)}, u32[]{:S(2)}) collective-permute-start(bf16[64,512]{1,0:T(8,128)(2,1)S(1)} %get-tuple-element.186), channel_id=1, source_target_pairs={{0,16},{1,17},{2,18},{3,19},{4,20},{5,21},{6,22},{7,23},{8,24},{9,... | collective-permute-start | bytes 196616 | tf_op jit(solution)/shard_map/ppermute | solution.py:831
  110.7 5.0 %collective-permute-start.15 = (bf16[32,512]{1,0:T(8,128)(2,1)S(1)}, bf16[32,512]{1,0:T(8,128)(2,1)S(1)}, u32[]{:S(2)}, u32[]{:S(2)}) collective-permute-start(bf16[32,512]{1,0:T(8,128)(2,1)S(1)} %get-tuple-element.190), channel_id=1, source_target_pairs={{0,16},{1,17},{2,18},{3,19},{4,20},{5,21},{6,22},{7,23},{8,24},{9,... | collective-permute-start | bytes 98312 | tf_op jit(solution)/shard_map/ppermute | solution.py:831

commit v11 on v10

--- a/solution.py
+++ b/solution.py
@@ -147,14 +147,6 @@
     pairs = [(i, (i - 1) % lon if i % 2 == 0 else (i + 1) % lon) for i in range(lon)]
     with_last = lax.ppermute(jnp.where(even, first, last), "lon", pairs)
     return jnp.where(even, with_last, with_next), jnp.where(even, with_next, with_last)
-
-
-def lon_edges_ring(states, before, after):
-    lon = lax.axis_size("lon")
-    ahead = lambda value: lax.ppermute(value, "lon", [(i, (i + 1) % lon) for i in range(lon)])
-    behind = lambda value: lax.ppermute(value, "lon", [(i, (i - 1) % lon) for i in range(lon)])
-    row = lambda place: jnp.concatenate([part[:, place] for part in (before, states, after)], axis=2)
-    return ahead(row(slice(-1, None))), behind(row(slice(0, 1)))
 
 
 MARGIN = 8
@@ -778,18 +770,16 @@
     return (chip + whole_of(arrived_ref[start + SUM_ROWS :])) + (beside + arrived)
 
 
-def finish_kernel(kept_ref, total_ref, arrived_ref, kept_down_ref, arrived_down_ref, up_hbm, down_hbm, taps_ref, gain_ref, *refs):
-    up_ref, down_ref, sems = refs
+def finish_kernel(kept_ref, total_ref, arrived_ref, kept_down_ref, arrived_down_ref, *refs):
+    *goals, up_ref, down_ref, taps_ref, gain_ref, sems = refs
     rows = kept_ref.shape[0]
-    down_ref[...] = kept_down_ref[...] + arrived_down_ref[...].astype(jnp.float32)
-    leaving = copies(sems, 0, [(down_ref, down_hbm)])
-    up_ref[...] = kept_ref[...] + arrived_ref[:rows].astype(jnp.float32)
-    leaving += copies(sems, 1, [(up_ref, up_hbm)])
     total = add_sums([total_ref], arrived_ref, rows)
     for k in range(9):
         taps_ref[k // 3, k % 3 : k % 3 + 1] = total[k : k + 1]
     gain_ref[...] = total[9:10]
-    finish(leaving)
+    up_ref[...] = kept_ref[...] + arrived_ref[:rows].astype(jnp.float32)
+    down_ref[...] = kept_down_ref[...] + arrived_down_ref[...].astype(jnp.float32)
+    finish(copies(sems, 0, list(zip((up_ref, down_ref, taps_ref, gain_ref), goals))))
 
 
 def halving(flip, send, keep, total):
@@ -854,7 +844,7 @@
         arrived = ahead.send(send)
         arrived_later = behind.send(later)
         send = ahead.send(after(arrived, later))
-        later = behind.send(after(arrived_later, send))
+        later = behind.send(arrived_later)
     final_ahead = ahead.send(send)
     final_behind = behind.send(later)
     sds = jax.ShapeDtypeStruct
@@ -865,8 +855,8 @@
         out,
         [*final_ahead, *final_behind],
         "vvvvv",
-        "hhvv",
-        scratch=[pltpu.VMEM(part.shape, part.dtype)] * 2 + [pltpu.SemaphoreType.DMA((2,))],
+        "hhhh",
+        scratch=[pltpu.VMEM(value.shape, value.dtype) for value in out] + [pltpu.SemaphoreType.DMA((4,))],
         moved=2**18,
     )
     return state, up, down, taps, gain.reshape(channels)

time: 118 us -> 117 us (level)
  no operation moved by 1% of the time
where the time goes in v11:
time: 117 us
  waiting for transfers between devices  47.5 us (41%)
  starting transfers between devices  37.3 us (32%)
  Pallas kernels  29.1 us (25%)
  between operations  1.23 us (1%)
    pallas_call x27, Pallas kernels, call(): pl.pallas_call(kernel, out_shape=out_shape, in_specs=[pl.BlockSpec(memory...  29.1 us
    all_to_all x6, waiting for transfers between devices, exchanged(): return lax.all_to_all(blocks, AXES, split_axis=0, concat_axis=0, tiled=True)  29 us
    all_to_all x6, starting transfers between devices, exchanged(): return lax.all_to_all(blocks, AXES, split_axis=0, concat_axis=0, tiled=True)  20.4 us
    ppermute x8, waiting for transfers between devices, halving(): lax.ppermute(send, AXES, [(flat(i, j), flat(*partner(i, j))) for i, j in...  12.6 us
    ppermute x2, starting transfers between devices, lon_edges(): with_last = lax.ppermute(jnp.where(even, first, last), 'lon', pairs)  6.49 us
    ppermute x8, starting transfers between devices, halving(): lax.ppermute(send, AXES, [(flat(i, j), flat(*partner(i, j))) for i, j in...  4.66 us
    ppermute x2, waiting for transfers between devices, lat_edges(): lax.ppermute(jnp.where(lat_at == 0, last, first), 'lat', [(0, 1), (1, 0)])  4.42 us
    ppermute x2, starting transfers between devices, lat_edges(): lax.ppermute(jnp.where(lat_at == 0, last, first), 'lat', [(0, 1), (1, 0)])  2.91 us
  transfers between devices with their start and end apart: 22, of which 15 were waited for; matrix products, arithmetic and copies ran while one was open for 1% of the time, Pallas kernels for 15%

profile of v11, /device:TPU:0, one launch (start us, length us, event | category | flops | bytes accessed | tf_op | source)
XLA Modules:
  0.0 116.6 jit_solution(2453454689058222727)
XLA Ops:
  0.7 1.8 %shard_map.128 = bf16[32,32,128]{2,1,0:T(8,128)(2,1)} custom-call(bf16[128,512]{1,0:T(8,128)(2,1)} %bitcast.41, f32[12,8,16]{2,1,0:T(8,128)} %bitcast.43), custom_call_target="tpu_custom_call" | custom-call | bytes 524288 | tf_op jit(solution)/shard_map/pallas_call | solution.py:35
  2.5 7.3 %all-to-all-start = ((bf16[32,32,128]{2,1,0:T(8,128)(2,1)}), bf16[32,32,128]{2,1,0:T(8,128)(2,1)S(1)}, u32[]{:S(2)}, u32[]{:S(2)}) async-start(bf16[32,32,128]{2,1,0:T(8,128)(2,1)} %shard_map.128), calls=%async_computation | async-start | bytes 524288 | tf_op jit(solution)/shard_map/all_to_all | solution.py:19
  9.9 1.8 %collective-permute-start = (bf16[3,8,1,512]{3,2,1,0:T(2,128)(2,1)S(1)}, bf16[3,8,1,512]{3,2,1,0:T(2,128)(2,1)S(1)}, u32[]{:S(2)}, u32[]{:S(2)}) collective-permute-start(bf16[3,8,1,512]{3,2,1,0:T(2,128)(2,1)S(1)} %broadcast_select_fusion.2), channel_id=1, source_target_pairs={{0,1},{1,0},{2,3},{3,2},{4,5},{5,4},{6,7},{7,6},{8,9},{9,8},{10,11... | collective-permute-start | bytes 73736 | tf_op jit(solution)/shard_map/ppermute | solution.py:132
  12.0 2.7 %collective-permute-done = bf16[3,8,1,512]{3,2,1,0:T(2,128)(2,1)S(1)} collective-permute-done((bf16[3,8,1,512]{3,2,1,0:T(2,128)(2,1)S(1)}, bf16[3,8,1,512]{3,2,1,0:T(2,128)(2,1)S(1)}, u32[]{:S(2)}, u32[]{:S(2)}) %collective-permute-start) | collective-permute-done | bytes 24608 | tf_op jit(solution)/shard_map/ppermute | solution.py:132
  15.1 5.7 %collective-permute-start.1 = (bf16[3,1,18,512]{3,2,1,0:T(8,128)(2,1)S(1)}, bf16[3,1,18,512]{3,2,1,0:T(8,128)(2,1)S(1)}, u32[]{:S(2)}, u32[]{:S(2)}) collective-permute-start(bf16[3,1,18,512]{3,2,1,0:T(8,128)(2,1)S(1)} %get-tuple-element.196), channel_id=1, source_target_pairs={{0,30},{2,4},{4,2},{6,8},{8,6},{10,12},{12,10},{14,16},{16,14},{18... | collective-permute-start | bytes 165896 | tf_op jit(solution)/shard_map/ppermute | solution.py:148
  20.8 1.3 %shard_map.129 = (bf16[16,2,16,128]{3,2,1,0:T(8,128)(2,1)}, bf16[16,2,16,128]{3,2,1,0:T(8,128)(2,1)}) custom-call(s32[8,128]{1,0:T(8,128)S(1)} %broadcast_in_dim.20.refs_0_, bf16[16,2,32,128]{3,2,1,0:T(8,128)(2,1)S(1)} %bitcast.20), custom_call_target="tpu_custom_call" | custom-call | flops 4194304 | bytes 1048576 | tf_op jit(solution)/shard_map/pallas_call | solution.py:35
  22.2 2.6 %all-to-all-start.1 = ((bf16[32,16,128]{2,1,0:T(8,128)(2,1)}), bf16[32,16,128]{2,1,0:T(8,128)(2,1)S(1)}, u32[]{:S(2)}, u32[]{:S(2)}) async-start(bf16[32,16,128]{2,1,0:T(8,128)(2,1)} %bitcast.42), calls=%async_computation.1 | async-start | bytes 262144 | tf_op jit(solution)/shard_map/all_to_all | solution.py:19
  25.5 1.7 %shard_map.130 = (bf16[128,512]{1,0:T(8,128)(2,1)}, bf16[512,128]{1,0:T(8,128)(2,1)}, f32[128,128]{1,0:T(8,128)}, bf16[128,1024]{1,0:T(8,128)(2,1)}, bf16[128,10...) custom-call(bf16[3,8,16,512]{3,2,1,0:T(8,128)(2,1)S(1)} %copy-done.1, ...), custom_call_target="tpu_custom_call" | custom-call | flops 134217728 | bytes 4194304 | tf_op jit(solution)/shard_map/pallas_call | solution.py:35
  28.3 5.1 %all-to-all-done.1 = bf16[32,16,128]{2,1,0:T(8,128)(2,1)S(1)} async-done(((bf16[32,16,128]{2,1,0:T(8,128)(2,1)}), bf16[32,16,128]{2,1,0:T(8,128)(2,1)S(1)}, u32[]{:S(2)}, u32[]{:S(2)}) %all-to-all-start.1) | async-done | bytes 131104 | tf_op jit(solution)/shard_map/all_to_all | solution.py:19
  33.4 1.6 %shard_map.132 = (bf16[512,128]{1,0:T(8,128)(2,1)}, bf16[128,1024]{1,0:T(8,128)(2,1)}, bf16[512,128]{1,0:T(8,128)(2,1)}) custom-call(bf16[512,128]{1,0:T(8,128)(2,1)S(1)} %bitcast.21, bf16[512,1024]{1,0:T(8,128)(2,1)S(1)} %copy-done.2, bf16[512,1024]{1,0:T(8,128)(2,1)S(1)} %copy-done, f32[1,512]{1,0:T(1,128)S(1)} %bitcast.31, ...), custom_call_target="tpu_custom_call" | custom-call | flops 268435456 | bytes 4194304 | tf_op jit(solution)/shard_map/pallas_call | solution.py:35
  35.0 2.6 %all-to-all-start.2 = ((bf16[32,16,128]{2,1,0:T(8,128)(2,1)}), bf16[32,16,128]{2,1,0:T(8,128)(2,1)S(1)}, u32[]{:S(2)}, u32[]{:S(2)}) async-start(bf16[32,16,128]{2,1,0:T(8,128)(2,1)} %bitcast.37), calls=%async_computation.2 | async-start | bytes 262144 | tf_op jit(solution)/shard_map/all_to_all | solution.py:19
  38.7 7.5 %all-to-all-done.2 = bf16[32,16,128]{2,1,0:T(8,128)(2,1)S(1)} async-done(((bf16[32,16,128]{2,1,0:T(8,128)(2,1)}), bf16[32,16,128]{2,1,0:T(8,128)(2,1)S(1)}, u32[]{:S(2)}, u32[]{:S(2)}) %all-to-all-start.2) | async-done | bytes 131104 | tf_op jit(solution)/shard_map/all_to_all | solution.py:19
  46.2 1.7 %shard_map.134 = bf16[16,2,16,128]{3,2,1,0:T(8,128)(2,1)} custom-call(s32[8,128]{1,0:T(8,128)S(1)} %broadcast_in_dim.20.refs_0_, bf16[16,2,16,128]{3,2,1,0:T(8,128)(2,1)S(1)} %bitcast.23, f32[16,128]{1,0:T(8,128)S(1)} %pad.9.refs_2_, bf16[16,2,16,128]{3,2,1,0:T(8,128)(2,1)S(1)} %shard_map.133.refs_3_), custom_call_target="tpu_custom_call" | custom-call | flops 4194304 | bytes 1048576 | tf_op jit(solution)/shard_map/pallas_call | solution.py:35
  47.9 2.6 %all-to-all-start.3 = ((bf16[32,16,128]{2,1,0:T(8,128)(2,1)}), bf16[32,16,128]{2,1,0:T(8,128)(2,1)S(1)}, u32[]{:S(2)}, u32[]{:S(2)}) async-start(bf16[32,16,128]{2,1,0:T(8,128)(2,1)} %bitcast.39), calls=%async_computation.3 | async-start | bytes 262144 | tf_op jit(solution)/shard_map/all_to_all | solution.py:19
  50.5 1.7 %shard_map.137 = (bf16[128,512]{1,0:T(8,128)(2,1)}, bf16[512,128]{1,0:T(8,128)(2,1)}, f32[128,128]{1,0:T(8,128)}, bf16[128,1024]{1,0:T(8,128)(2,1)}, bf16[128,10...) custom-call(bf16[3,8,16,512]{3,2,1,0:T(8,128)(2,1)S(1)} %copy-done.1, ...), custom_call_target="tpu_custom_call" | custom-call | flops 134217728 | bytes 4194304 | tf_op jit(solution)/shard_map/pallas_call | solution.py:35
  52.3 1.7 %shard_map.135 = (bf16[128,512]{1,0:T(8,128)(2,1)}, bf16[512,128]{1,0:T(8,128)(2,1)}, f32[128,128]{1,0:T(8,128)}, bf16[128,1024]{1,0:T(8,128)(2,1)}, bf16[128,10...) custom-call(bf16[3,8,16,512]{3,2,1,0:T(8,128)(2,1)S(1)} %copy-done.1, ...), custom_call_target="tpu_custom_call" | custom-call | flops 134217728 | bytes 4194304 | tf_op jit(solution)/shard_map/pallas_call | solution.py:35
  55.0 4.1 %all-to-all-done.3 = bf16[32,16,128]{2,1,0:T(8,128)(2,1)S(1)} async-done(((bf16[32,16,128]{2,1,0:T(8,128)(2,1)}), bf16[32,16,128]{2,1,0:T(8,128)(2,1)S(1)}, u32[]{:S(2)}, u32[]{:S(2)}) %all-to-all-start.3) | async-done | bytes 131104 | tf_op jit(solution)/shard_map/all_to_all | solution.py:19
  59.2 1.6 %shard_map.138 = (bf16[512,128]{1,0:T(8,128)(2,1)}, bf16[128,1024]{1,0:T(8,128)(2,1)}, bf16[512,128]{1,0:T(8,128)(2,1)}) custom-call(bf16[512,128]{1,0:T(8,128)(2,1)S(1)} %bitcast.22, bf16[512,1024]{1,0:T(8,128)(2,1)S(1)} %copy-done.2, bf16[512,1024]{1,0:T(8,128)(2,1)S(1)} %copy-done, f32[1,512]{1,0:T(1,128)S(1)} %bitcast.34, ...), custom_call_target="tpu_custom_call" | custom-call | flops 268435456 | bytes 4194304 | tf_op jit(solution)/shard_map/pallas_call | solution.py:35
  60.7 2.6 %all-to-all-start.4 = ((bf16[32,16,128]{2,1,0:T(8,128)(2,1)}), bf16[32,16,128]{2,1,0:T(8,128)(2,1)S(1)}, u32[]{:S(2)}, u32[]{:S(2)}) async-start(bf16[32,16,128]{2,1,0:T(8,128)(2,1)} %bitcast.38), calls=%async_computation.4 | async-start | bytes 262144 | tf_op jit(solution)/shard_map/all_to_all | solution.py:19
  64.3 7.7 %all-to-all-done.4 = bf16[32,16,128]{2,1,0:T(8,128)(2,1)S(1)} async-done(((bf16[32,16,128]{2,1,0:T(8,128)(2,1)}), bf16[32,16,128]{2,1,0:T(8,128)(2,1)S(1)}, u32[]{:S(2)}, u32[]{:S(2)}) %all-to-all-start.4) | async-done | bytes 131104 | tf_op jit(solution)/shard_map/all_to_all | solution.py:19
  72.0 1.7 %shard_map.140 = bf16[16,2,16,128]{3,2,1,0:T(8,128)(2,1)} custom-call(s32[8,128]{1,0:T(8,128)S(1)} %broadcast_in_dim.20.refs_0_, bf16[16,2,16,128]{3,2,1,0:T(8,128)(2,1)S(1)} %bitcast.24, f32[16,128]{1,0:T(8,128)S(1)} %pad.9.refs_2_, bf16[16,2,16,128]{3,2,1,0:T(8,128)(2,1)S(1)} %shard_map.139.refs_3_), custom_call_target="tpu_custom_call" | custom-call | flops 4194304 | bytes 1048576 | tf_op jit(solution)/shard_map/pallas_call | solution.py:35
  73.7 2.8 %all-to-all-start.5 = ((bf16[32,16,128]{2,1,0:T(8,128)(2,1)}), bf16[32,16,128]{2,1,0:T(8,128)(2,1)S(1)}, u32[]{:S(2)}, u32[]{:S(2)}) async-start(bf16[32,16,128]{2,1,0:T(8,128)(2,1)} %bitcast.40), calls=%async_computation.5 | async-start | bytes 262144 | tf_op jit(solution)/shard_map/all_to_all | solution.py:19
  76.4 2.7 %shard_map.142.sums_ref = f32[16,512]{1,0:T(8,128)S(1)} custom-call(bf16[512,1024]{1,0:T(8,128)(2,1)S(1)} %copy-done, f32[1,512]{1,0:T(1,128)S(1)} %bitcast.35, bf16[10,32,512]{2,1,0:T(8,128)(2,1)} %get-tuple-element.134.refs_0_, bf16[512,128]{1,0:T(8,128)(2,1)} %get-tuple-element.110.refs_1_, bf16[128,1024]{1,0:T(8,128)(2,1)} %get-tuple-element.147.refs_2_.refs_7_, ...), custom_call_target="tpu_custom_call" | custom-call | bytes 2097152 | tf_op jit(solution)/shard_map/pallas_call | solution.py:35
  80.4 4.5 %all-to-all-done.5 = bf16[32,16,128]{2,1,0:T(8,128)(2,1)S(1)} async-done(((bf16[32,16,128]{2,1,0:T(8,128)(2,1)}), bf16[32,16,128]{2,1,0:T(8,128)(2,1)S(1)}, u32[]{:S(2)}, u32[]{:S(2)}) %all-to-all-start.5) | async-done | bytes 131104 | tf_op jit(solution)/shard_map/all_to_all | solution.py:19
  84.9 2.0 %shard_map.143 = (bf16[128,512]{1,0:T(8,128)(2,1)S(1)}, f32[16,512]{1,0:T(8,128)S(1)}, bf16[544,512]{1,0:T(8,128)(2,1)S(1)}, bf16[4,128,512]{2,1,0:T(8,128)(2,1)S(1)}) custom-call(bf16[512,128]{1,0:T(8,128)(2,1)S(1)} %bitcast.28, bf16[512,1024]{1,0:T(8,128)(2,1)S(1)} %copy-done.2, bf16[512,1024]{1,0:T(8,128)(2,1)S(1)} %copy-done, f32[1,512]{1,0:T(1,128)S(1)} %bitcast.36, ...), custom_call_target="tpu_custom_call" | custom-call | flops 1073741824 | bytes 6291456 | tf_op jit(solution)/shard_map/pallas_call | solution.py:35
  87.0 2.0 %shard_map.144 = (bf16[512,512]{1,0:T(8,128)(2,1)S(1)}, bf16[4,128,512]{2,1,0:T(8,128)(2,1)S(1)}) custom-call(bf16[512,128]{1,0:T(8,128)(2,1)S(1)} %bitcast.29, bf16[512,128]{1,0:T(8,128)(2,1)} %get-tuple-element.154.refs_0_, bf16[512,128]{1,0:T(8,128)(2,1)} %get-tuple-element.155.refs_1_, bf16[128,1024]{1,0:T(8,128)(2,1)} %get-tuple-element.133.refs_2_, ...), custom_call_target="tpu_custom_call" | custom-call | flops 536870912 | bytes 2097152 | tf_op jit(solution)/shard_map/pallas_call | solution.py:35
  92.1 1.7 %collective-permute-done.4 = bf16[1,8,1,512]{3,2,1,0:T(2,128)(2,1)S(1)} collective-permute-done((bf16[1,8,1,512]{3,2,1,0:T(2,128)(2,1)S(1)}, bf16[1,8,1,512]{3,2,1,0:T(2,128)(2,1)S(1)}, u32[]{:S(2)}, u32[]{:S(2)}) %collective-permute-start.4) | collective-permute-done | bytes 8224 | tf_op jit(solution)/shard_map/ppermute | solution.py:132
  93.8 4.7 %collective-permute-done.8.refs_2_ = bf16[288,512]{1,0:T(8,128)(2,1)S(1)} collective-permute-done((bf16[288,512]{1,0:T(8,128)(2,1)S(1)}, bf16[288,512]{1,0:T(8,128)(2,1)S(1)}, u32[]{:S(2)}, u32[]{:S(2)}) %collective-permute-start.8) | collective-permute-done | bytes 294944 | tf_op jit(solution)/shard_map/ppermute | solution.py:812
  99.8 5.5 %collective-permute-done.9.refs_3_ = bf16[192,512]{1,0:T(8,128)(2,1)S(1)} collective-permute-done((bf16[192,512]{1,0:T(8,128)(2,1)S(1)}, bf16[192,512]{1,0:T(8,128)(2,1)S(1)}, u32[]{:S(2)}, u32[]{:S(2)}) %collective-permute-start.9) | collective-permute-done | bytes 196640 | tf_op jit(solution)/shard_map/ppermute | solution.py:812
  105.5 2.1 %collective-permute-start.14 = (bf16[64,512]{1,0:T(8,128)(2,1)S(1)}, bf16[64,512]{1,0:T(8,128)(2,1)S(1)}, u32[]{:S(2)}, u32[]{:S(2)}) collective-permute-start(bf16[64,512]{1,0:T(8,128)(2,1)S(1)} %get-tuple-element.177), channel_id=1, source_target_pairs={{0,8},{1,9},{2,10},{3,11},{4,12},{5,13},{6,14},{7,15},{8,0},{9,1},... | collective-permute-start | bytes 196616 | tf_op jit(solution)/shard_map/ppermute | solution.py:812
  108.4 1.6 %collective-permute-done.11.refs_2_ = bf16[96,512]{1,0:T(8,128)(2,1)S(1)} collective-permute-done((bf16[96,512]{1,0:T(8,128)(2,1)S(1)}, bf16[96,512]{1,0:T(8,128)(2,1)S(1)}, u32[]{:S(2)}, u32[]{:S(2)}) %collective-permute-start.11) | collective-permute-done | bytes 98336 | tf_op jit(solution)/shard_map/ppermute | solution.py:812
  110.7 2.4 %collective-permute-start.15 = (bf16[32,512]{1,0:T(8,128)(2,1)S(1)}, bf16[32,512]{1,0:T(8,128)(2,1)S(1)}, u32[]{:S(2)}, u32[]{:S(2)}) collective-permute-start(bf16[32,512]{1,0:T(8,128)(2,1)S(1)} %get-tuple-element.184), channel_id=1, source_target_pairs={{0,16},{1,17},{2,18},{3,19},{4,20},{5,21},{6,22},{7,23},{8,24},{9,... | collective-permute-start | bytes 98312 | tf_op jit(solution)/shard_map/ppermute | solution.py:821
  (75 shorter events, 16.2 us)
Async XLA Ops:
  0.6 9.2 %copy-start.1 = (bf16[3,8,16,512]{3,2,1,0:T(8,128)(2,1)S(1)}, bf16[3,8,16,512]{3,2,1,0:T(8,128)(2,1)}, u32[]{:S(2)}) copy-start(bf16[3,8,16,512]{3,2,1,0:T(8,128)(2,1)} %refs_0_.5) | copy-start | bytes 1179652
  0.6 11.1 %copy-start.5 = (s32[3,4]{1,0:T(4,128)S(1)}, s32[3,4]{1,0:T(4,128)}, u32[]{:S(2)}) copy-start(s32[3,4]{1,0:T(4,128)} %param.17) | copy-start | bytes 148
  0.7 11.1 %copy-start.6 = (s32[3,4]{1,0:T(4,128)S(1)}, s32[3,4]{1,0:T(4,128)}, u32[]{:S(2)}) copy-start(s32[3,4]{1,0:T(4,128)} %param.16) | copy-start | bytes 148
  2.5 22.3 %copy-start = (bf16[512,1024]{1,0:T(8,128)(2,1)S(1)}, bf16[512,1024]{1,0:T(8,128)(2,1)}, u32[]{:S(2)}) copy-start(bf16[512,1024]{1,0:T(8,128)(2,1)} %up_ref.7) | copy-start | bytes 3145732
  2.5 18.2 %all-to-all-start = ((bf16[32,32,128]{2,1,0:T(8,128)(2,1)}), bf16[32,32,128]{2,1,0:T(8,128)(2,1)S(1)}, u32[]{:S(2)}, u32[]{:S(2)}) async-start(bf16[32,32,128]{2,1,0:T(8,128)(2,1)} %shard_map.128), calls=%async_computation | async-start | bytes 524288 | tf_op jit(solution)/shard_map/all_to_all | solution.py:19
  9.9 4.8 %collective-permute-start = (bf16[3,8,1,512]{3,2,1,0:T(2,128)(2,1)S(1)}, bf16[3,8,1,512]{3,2,1,0:T(2,128)(2,1)S(1)}, u32[]{:S(2)}, u32[]{:S(2)}) collective-permute-start(bf16[3,8,1,512]{3,2,1,0:T(2,128)(2,1)S(1)} %broadcast_select_fusion.2), channel_id=1, source_target_pairs={{0,1},{1,0},{2,3},{3,2},{4,5},{5,4},{6,7},{7,6},{8,9},{9,8},{10,11... | collective-permute-start | bytes 73736 | tf_op jit(solution)/shard_map/ppermute | solution.py:132
  15.0 9.8 %collective-permute-start.2 = (bf16[3,1,18,512]{3,2,1,0:T(8,128)(2,1)S(1)}, bf16[3,1,18,512]{3,2,1,0:T(8,128)(2,1)S(1)}, u32[]{:S(2)}, u32[]{:S(2)}) collective-permute-start(bf16[3,1,18,512]{3,2,1,0:T(8,128)(2,1)S(1)} %get-tuple-element.195), channel_id=1, source_target_pairs={{0,2},{2,0},{4,6},{6,4},{8,10},{10,8},{12,14},{14,12},{16,18},{18,... | collective-permute-start | bytes 165896 | tf_op jit(solution)/shard_map/ppermute | solution.py:146
  15.1 9.8 %collective-permute-start.1 = (bf16[3,1,18,512]{3,2,1,0:T(8,128)(2,1)S(1)}, bf16[3,1,18,512]{3,2,1,0:T(8,128)(2,1)S(1)}, u32[]{:S(2)}, u32[]{:S(2)}) collective-permute-start(bf16[3,1,18,512]{3,2,1,0:T(8,128)(2,1)S(1)} %get-tuple-element.196), channel_id=1, source_target_pairs={{0,30},{2,4},{4,2},{6,8},{8,6},{10,12},{12,10},{14,16},{16,14},{18... | collective-permute-start | bytes 165896 | tf_op jit(solution)/shard_map/ppermute | solution.py:148
  22.2 11.2 %all-to-all-start.1 = ((bf16[32,16,128]{2,1,0:T(8,128)(2,1)}), bf16[32,16,128]{2,1,0:T(8,128)(2,1)S(1)}, u32[]{:S(2)}, u32[]{:S(2)}) async-start(bf16[32,16,128]{2,1,0:T(8,128)(2,1)} %bitcast.42), calls=%async_computation.1 | async-start | bytes 262144 | tf_op jit(solution)/shard_map/all_to_all | solution.py:19
  24.8 0.7 copy-start.3
  24.9 0.7 copy-start.4
  25.5 7.9 %copy-start.2 = (bf16[512,1024]{1,0:T(8,128)(2,1)S(1)}, bf16[512,1024]{1,0:T(8,128)(2,1)}, u32[]{:S(2)}) copy-start(bf16[512,1024]{1,0:T(8,128)(2,1)} %down_ref.5) | copy-start | bytes 3145732
  35.0 11.2 %all-to-all-start.2 = ((bf16[32,16,128]{2,1,0:T(8,128)(2,1)}), bf16[32,16,128]{2,1,0:T(8,128)(2,1)S(1)}, u32[]{:S(2)}, u32[]{:S(2)}) async-start(bf16[32,16,128]{2,1,0:T(8,128)(2,1)} %bitcast.37), calls=%async_computation.2 | async-start | bytes 262144 | tf_op jit(solution)/shard_map/all_to_all | solution.py:19
  47.9 11.2 %all-to-all-start.3 = ((bf16[32,16,128]{2,1,0:T(8,128)(2,1)}), bf16[32,16,128]{2,1,0:T(8,128)(2,1)S(1)}, u32[]{:S(2)}, u32[]{:S(2)}) async-start(bf16[32,16,128]{2,1,0:T(8,128)(2,1)} %bitcast.39), calls=%async_computation.3 | async-start | bytes 262144 | tf_op jit(solution)/shard_map/all_to_all | solution.py:19
  60.7 11.2 %all-to-all-start.4 = ((bf16[32,16,128]{2,1,0:T(8,128)(2,1)}), bf16[32,16,128]{2,1,0:T(8,128)(2,1)S(1)}, u32[]{:S(2)}, u32[]{:S(2)}) async-start(bf16[32,16,128]{2,1,0:T(8,128)(2,1)} %bitcast.38), calls=%async_computation.4 | async-start | bytes 262144 | tf_op jit(solution)/shard_map/all_to_all | solution.py:19
  73.7 11.2 %all-to-all-start.5 = ((bf16[32,16,128]{2,1,0:T(8,128)(2,1)}), bf16[32,16,128]{2,1,0:T(8,128)(2,1)S(1)}, u32[]{:S(2)}, u32[]{:S(2)}) async-start(bf16[32,16,128]{2,1,0:T(8,128)(2,1)} %bitcast.40), calls=%async_computation.5 | async-start | bytes 262144 | tf_op jit(solution)/shard_map/all_to_all | solution.py:19
  86.9 2.1 %collective-permute-start.3 = (bf16[544,512]{1,0:T(8,128)(2,1)S(1)}, bf16[544,512]{1,0:T(8,128)(2,1)S(1)}, u32[]{:S(2)}, u32[]{:S(2)}) collective-permute-start(bf16[544,512]{1,0:T(8,128)(2,1)S(1)} %get-tuple-element.153), channel_id=1, source_target_pairs={{0,2},{1,3},{2,0},{3,1},{4,6},{5,7},{6,4},{7,5},{8,10},{9,11},{10,... | collective-permute-start | bytes 1671176 | tf_op jit(solution)/shard_map/ppermute | solution.py:812
  89.2 2.1 %collective-permute-start.5 = (bf16[512,512]{1,0:T(8,128)(2,1)S(1)}, bf16[512,512]{1,0:T(8,128)(2,1)S(1)}, u32[]{:S(2)}, u32[]{:S(2)}) collective-permute-start(bf16[512,512]{1,0:T(8,128)(2,1)S(1)} %get-tuple-element.161), channel_id=1, source_target_pairs={{0,2},{1,3},{2,0},{3,1},{4,6},{5,7},{6,4},{7,5},{8,10},{9,11},{10,... | collective-permute-start | bytes 1572872 | tf_op jit(solution)/shard_map/ppermute | solution.py:812
  89.7 8.7 %collective-permute-start.8 = (bf16[288,512]{1,0:T(8,128)(2,1)S(1)}, bf16[288,512]{1,0:T(8,128)(2,1)S(1)}, u32[]{:S(2)}, u32[]{:S(2)}) collective-permute-start(bf16[288,512]{1,0:T(8,128)(2,1)S(1)} %get-tuple-element.158), channel_id=1, source_target_pairs={{0,4},{1,5},{2,3},{3,2},{4,0},{5,1},{6,7},{7,6},{8,12},{9,13},{10,... | collective-permute-start | bytes 884744 | tf_op jit(solution)/shard_map/ppermute | solution.py:812
  89.8 4.0 %collective-permute-start.4 = (bf16[1,8,1,512]{3,2,1,0:T(2,128)(2,1)S(1)}, bf16[1,8,1,512]{3,2,1,0:T(2,128)(2,1)S(1)}, u32[]{:S(2)}, u32[]{:S(2)}) collective-permute-start(bf16[1,8,1,512]{3,2,1,0:T(2,128)(2,1)S(1)} %broadcast_select_fusion.9), channel_id=1, source_target_pairs={{0,1},{1,0},{2,3},{3,2},{4,5},{5,4},{6,7},{7,6},{8,9},{9,8},{10,11... | collective-permute-start | bytes 24584 | tf_op jit(solution)/shard_map/ppermute | solution.py:132
  91.4 7.5 %collective-permute-start.10 = (bf16[256,512]{1,0:T(8,128)(2,1)S(1)}, bf16[256,512]{1,0:T(8,128)(2,1)S(1)}, u32[]{:S(2)}, u32[]{:S(2)}) collective-permute-start(bf16[256,512]{1,0:T(8,128)(2,1)S(1)} %get-tuple-element.162), channel_id=1, source_target_pairs={{0,1},{1,0},{2,6},{3,7},{4,5},{5,4},{6,2},{7,3},{8,9},{9,8},{10,14... | collective-permute-start | bytes 786440 | tf_op jit(solution)/shard_map/ppermute | solution.py:812
  98.5 6.8 %collective-permute-start.9 = (bf16[192,512]{1,0:T(8,128)(2,1)S(1)}, bf16[192,512]{1,0:T(8,128)(2,1)S(1)}, u32[]{:S(2)}, u32[]{:S(2)}) collective-permute-start(bf16[192,512]{1,0:T(8,128)(2,1)S(1)} %get-tuple-element.169), channel_id=1, source_target_pairs={{0,1},{1,0},{2,6},{3,7},{4,5},{5,4},{6,2},{7,3},{8,9},{9,8},{10,14... | collective-permute-start | bytes 589832 | tf_op jit(solution)/shard_map/ppermute | solution.py:812
  99.0 6.4 %collective-permute-start.12 = (bf16[128,512]{1,0:T(8,128)(2,1)S(1)}, bf16[128,512]{1,0:T(8,128)(2,1)S(1)}, u32[]{:S(2)}, u32[]{:S(2)}) collective-permute-start(bf16[128,512]{1,0:T(8,128)(2,1)S(1)} %get-tuple-element.171), channel_id=1, source_target_pairs={{0,4},{1,5},{2,3},{3,2},{4,0},{5,1},{6,7},{7,6},{8,12},{9,13},{10,... | collective-permute-start | bytes 393224 | tf_op jit(solution)/shard_map/ppermute | solution.py:812
  105.3 4.7 %collective-permute-start.11 = (bf16[96,512]{1,0:T(8,128)(2,1)S(1)}, bf16[96,512]{1,0:T(8,128)(2,1)S(1)}, u32[]{:S(2)}, u32[]{:S(2)}) collective-permute-start(bf16[96,512]{1,0:T(8,128)(2,1)S(1)} %get-tuple-element.175), channel_id=1, source_target_pairs={{0,8},{1,9},{2,10},{3,11},{4,12},{5,13},{6,14},{7,15},{8,0},{9,1},... | collective-permute-start | bytes 294920 | tf_op jit(solution)/shard_map/ppermute | solution.py:812
  105.5 5.2 %collective-permute-start.14 = (bf16[64,512]{1,0:T(8,128)(2,1)S(1)}, bf16[64,512]{1,0:T(8,128)(2,1)S(1)}, u32[]{:S(2)}, u32[]{:S(2)}) collective-permute-start(bf16[64,512]{1,0:T(8,128)(2,1)S(1)} %get-tuple-element.177), channel_id=1, source_target_pairs={{0,8},{1,9},{2,10},{3,11},{4,12},{5,13},{6,14},{7,15},{8,0},{9,1},... | collective-permute-start | bytes 196616 | tf_op jit(solution)/shard_map/ppermute | solution.py:812
  107.6 5.6 %collective-permute-start.7 = (bf16[1,1,18,512]{3,2,1,0:T(8,128)(2,1)S(1)}, bf16[1,1,18,512]{3,2,1,0:T(8,128)(2,1)S(1)}, u32[]{:S(2)}, u32[]{:S(2)}) collective-permute-start(bf16[1,1,18,512]{3,2,1,0:T(8,128)(2,1)S(1)} %get-tuple-element.205), channel_id=1, source_target_pairs={{0,2},{2,0},{4,6},{6,4},{8,10},{10,8},{12,14},{14,12},{16,18},{18,... | collective-permute-start | bytes 55304 | tf_op jit(solution)/shard_map/ppermute | solution.py:146
  107.6 6.1 %collective-permute-start.6 = (bf16[1,1,18,512]{3,2,1,0:T(8,128)(2,1)S(1)}, bf16[1,1,18,512]{3,2,1,0:T(8,128)(2,1)S(1)}, u32[]{:S(2)}, u32[]{:S(2)}) collective-permute-start(bf16[1,1,18,512]{3,2,1,0:T(8,128)(2,1)S(1)} %get-tuple-element.206), channel_id=1, source_target_pairs={{0,30},{2,4},{4,2},{6,8},{8,6},{10,12},{12,10},{14,16},{16,14},{18... | collective-permute-start | bytes 55304 | tf_op jit(solution)/shard_map/ppermute | solution.py:148
  110.1 5.4 %collective-permute-start.13 = (bf16[64,512]{1,0:T(8,128)(2,1)S(1)}, bf16[64,512]{1,0:T(8,128)(2,1)S(1)}, u32[]{:S(2)}, u32[]{:S(2)}) collective-permute-start(bf16[64,512]{1,0:T(8,128)(2,1)S(1)} %get-tuple-element.181), channel_id=1, source_target_pairs={{0,16},{1,17},{2,18},{3,19},{4,20},{5,21},{6,22},{7,23},{8,24},{9,... | collective-permute-start | bytes 196616 | tf_op jit(solution)/shard_map/ppermute | solution.py:821
  110.7 5.0 %collective-permute-start.15 = (bf16[32,512]{1,0:T(8,128)(2,1)S(1)}, bf16[32,512]{1,0:T(8,128)(2,1)S(1)}, u32[]{:S(2)}, u32[]{:S(2)}) collective-permute-start(bf16[32,512]{1,0:T(8,128)(2,1)S(1)} %get-tuple-element.184), channel_id=1, source_target_pairs={{0,16},{1,17},{2,18},{3,19},{4,20},{5,21},{6,22},{7,23},{8,24},{9,... | collective-permute-start | bytes 98312 | tf_op jit(solution)/shard_map/ppermute | solution.py:821

commit v12 on v11

--- a/solution.py
+++ b/solution.py
@@ -431,11 +431,12 @@
 
 def last_kernel(steps, tile, moved_ref, down_ref, up_ref, gain_ref, sums_ref, *refs):
     slope_ref, n_ref, inv_ref, pad_ref, *refs = refs
-    inputs, refs = refs[: 2 * steps - 1], refs[2 * steps - 1 :]
-    field_ref, total_ref, send_ref, keep_ref, left_ref, right_ref, sems = refs
+    inputs, hidden, refs = refs[: 2 * steps - 1], refs[2 * steps - 1 : 3 * steps - 1], refs[3 * steps - 1 :]
+    field_ref, total_ref, send_ref, keep_ref, hidden_ref, left_ref, right_ref, sems = refs
     count = slope_ref.shape[0]
     pairs = side_by_side(inputs[:steps], left_ref, 1) + side_by_side(inputs[steps:], right_ref, 0)
     later = copies(sems, 0, pairs)
+    last = copies(sems, len(pairs), side_by_side(hidden, hidden_ref, 0))
     moved = moved_ref[...].astype(jnp.float32).T
     grad_hidden = jnp.dot(moved.astype(jnp.bfloat16), down_ref[...], preferred_element_type=jnp.float32)
     grad_pre = (grad_hidden * slope_ref[...].astype(jnp.float32)).astype(jnp.bfloat16)
@@ -453,15 +454,16 @@
     gradient_quadrants(left_ref, right_ref, send_ref, keep_ref)
     if keep_ref.ndim > 2:
         send_ref[left_ref.shape[0] :] = pieces_of(total)
-
-
-def last_step(tile, moved, w_down, w_up, norm_gain, sums, near, turned, grads):
+    finish(last)
+
+
+def last_step(tile, moved, w_down, w_up, norm_gain, sums, near, turned, grads, hidden):
     steps = len(turned)
     channels, count = moved.shape
     hid = w_down.shape[1]
     send, keep = quadrant_shapes(channels, hid, 1)
     sds = jax.ShapeDtypeStruct
-    inputs = turned + grads
+    inputs = turned + grads + hidden
     return call(
         functools.partial(last_kernel, steps, tile),
         [
@@ -469,10 +471,11 @@
             sds((ROWS, channels), jnp.float32),
             sds(send, jnp.bfloat16),
             sds(keep, jnp.bfloat16),
+            sds((steps * count, hid), jnp.bfloat16),
         ],
         [moved, w_down, w_up, norm_gain, sums, *near, *inputs],
         "v" * 9 + "h" * len(inputs),
-        "vppp",
+        "vpppv",
         scratch=[pltpu.VMEM((channels, steps * count), jnp.bfloat16), pltpu.VMEM((steps * count, hid), jnp.bfloat16)]
         + [pltpu.SemaphoreType.DMA((len(inputs),))],
         flops=2**30,
@@ -481,29 +484,26 @@
     )
 
 
-def down_kernel(steps, moved_ref, *refs):
-    inputs, (send_ref, keep_ref, left_ref, right_ref, sems) = refs[: 2 * steps - 1], refs[2 * steps - 1 :]
+def down_kernel(steps, moved_ref, right_ref, *refs):
+    inputs, (send_ref, keep_ref, left_ref, sems) = refs[: steps - 1], refs[steps - 1 :]
     count = moved_ref.shape[1]
-    pairs = side_by_side(inputs[: steps - 1], left_ref, 1) + side_by_side(inputs[steps - 1 :], right_ref, 0)
-    arriving = copies(sems, 0, pairs)
+    arriving = copies(sems, 0, side_by_side(inputs, left_ref, 1))
     left_ref[:, (steps - 1) * count :] = moved_ref[...]
     finish(arriving)
     gradient_quadrants(left_ref, right_ref, send_ref, keep_ref)
 
 
 def down_gradients(moved, moveds, hidden):
-    steps = len(hidden)
+    steps = 1 + len(moveds)
     channels, count = moved.shape
-    hid = hidden[0].shape[1]
-    inputs = moveds + hidden
+    hid = hidden.shape[1]
     return call(
         functools.partial(down_kernel, steps),
         [jax.ShapeDtypeStruct(shape, jnp.bfloat16) for shape in quadrant_shapes(channels, hid, 0)],
-        [moved, *inputs],
-        "v" + "h" * len(inputs),
+        [moved, hidden, *moveds],
+        "vv" + "h" * len(moveds),
         "pp",
-        scratch=[pltpu.VMEM((channels, steps * count), jnp.bfloat16), pltpu.VMEM((steps * count, hid), jnp.bfloat16)]
-        + [pltpu.SemaphoreType.DMA((len(inputs),))],
+        scratch=[pltpu.VMEM((channels, steps * count), jnp.bfloat16), pltpu.SemaphoreType.DMA((len(moveds),))],
         flops=2**29,
         moved=2**21,
         limit=16,
@@ -926,8 +926,9 @@
     all_of = lambda values: [values[s] for s in order]
     sums = channel_sums(tile, w_up, gain, *map(earlier, (names["pad"], fields, grads, names["n"])))
     here = after(here, (near, sums))
-    field, total, send, keep = last_step(tile, here, w_down, w_up, gain, sums, near, all_of(names["turned"]), earlier(grads))
-    down = down_gradients(here, earlier(moved), all_of(names["hid"]))
+    parts = (all_of(names["turned"]), earlier(grads), all_of(names["hid"]))
+    field, total, send, keep, hidden = last_step(tile, here, w_down, w_up, gain, sums, near, *parts)
+    down = down_gradients(here, earlier(moved), hidden)
     field = field.reshape(cotangent.shape)
     return all_sums((send, keep), down, total, field, kernel)
 

time: 117 us -> 117 us (level)
  transfers between devices with their start and end apart: 22 -> 22, of which waited for: 15 -> 16; matrix products, arithmetic and copies ran while one was open for 1% -> 1% of each run, Pallas kernels for 15% -> 15%
where the time goes in v12:
time: 117 us; the launch traced here: 116 us
  waiting for transfers between devices  47.9 us (41%)
  starting transfers between devices  36.9 us (32%)
  Pallas kernels  28.8 us (25%)
  between operations  1.22 us (1%)
    all_to_all x6, waiting for transfers between devices, exchanged(): return lax.all_to_all(blocks, AXES, split_axis=0, concat_axis=0, tiled=True)  29 us
    pallas_call x27, Pallas kernels, call(): pl.pallas_call(kernel, out_shape=out_shape, in_specs=[pl.BlockSpec(memory...  28.8 us
    all_to_all x6, starting transfers between devices, exchanged(): return lax.all_to_all(blocks, AXES, split_axis=0, concat_axis=0, tiled=True)  20.4 us
    ppermute x8, waiting for transfers between devices, halving(): lax.ppermute(send, AXES, [(flat(i, j), flat(*partner(i, j))) for i, j in...  13 us
    ppermute x2, starting transfers between devices, lon_edges(): with_last = lax.ppermute(jnp.where(even, first, last), 'lon', pairs)  6.48 us
    ppermute x2, waiting for transfers between devices, lat_edges(): lax.ppermute(jnp.where(lat_at == 0, last, first), 'lat', [(0, 1), (1, 0)])  4.4 us
    ppermute x8, starting transfers between devices, halving(): lax.ppermute(send, AXES, [(flat(i, j), flat(*partner(i, j))) for i, j in...  4.33 us
    ppermute x2, starting transfers between devices, lat_edges(): lax.ppermute(jnp.where(lat_at == 0, last, first), 'lat', [(0, 1), (1, 0)])  2.91 us
  transfers between devices with their start and end apart: 22, of which 16 were waited for; matrix products, arithmetic and copies ran while one was open for 1% of the time, Pallas kernels for 15%

profile of v12, /device:TPU:0, one launch (start us, length us, event | category | flops | bytes accessed | tf_op | source)
XLA Modules:
  0.0 116.4 jit_solution(14611224052036395824)
XLA Ops:
  0.7 1.8 %shard_map.128 = bf16[32,32,128]{2,1,0:T(8,128)(2,1)} custom-call(bf16[128,512]{1,0:T(8,128)(2,1)} %bitcast.41, f32[12,8,16]{2,1,0:T(8,128)} %bitcast.43), custom_call_target="tpu_custom_call" | custom-call | bytes 524288 | tf_op jit(solution)/shard_map/pallas_call | solution.py:35
  2.5 7.3 %all-to-all-start = ((bf16[32,32,128]{2,1,0:T(8,128)(2,1)}), bf16[32,32,128]{2,1,0:T(8,128)(2,1)S(1)}, u32[]{:S(2)}, u32[]{:S(2)}) async-start(bf16[32,32,128]{2,1,0:T(8,128)(2,1)} %shard_map.128), calls=%async_computation | async-start | bytes 524288 | tf_op jit(solution)/shard_map/all_to_all | solution.py:19
  9.9 1.8 %collective-permute-start = (bf16[3,8,1,512]{3,2,1,0:T(2,128)(2,1)S(1)}, bf16[3,8,1,512]{3,2,1,0:T(2,128)(2,1)S(1)}, u32[]{:S(2)}, u32[]{:S(2)}) collective-permute-start(bf16[3,8,1,512]{3,2,1,0:T(2,128)(2,1)S(1)} %broadcast_select_fusion.2), channel_id=1, source_target_pairs={{0,1},{1,0},{2,3},{3,2},{4,5},{5,4},{6,7},{7,6},{8,9},{9,8},{10,11... | collective-permute-start | bytes 73736 | tf_op jit(solution)/shard_map/ppermute | solution.py:132
  12.0 2.7 %collective-permute-done = bf16[3,8,1,512]{3,2,1,0:T(2,128)(2,1)S(1)} collective-permute-done((bf16[3,8,1,512]{3,2,1,0:T(2,128)(2,1)S(1)}, bf16[3,8,1,512]{3,2,1,0:T(2,128)(2,1)S(1)}, u32[]{:S(2)}, u32[]{:S(2)}) %collective-permute-start) | collective-permute-done | bytes 24608 | tf_op jit(solution)/shard_map/ppermute | solution.py:132
  15.1 5.7 %collective-permute-start.1 = (bf16[3,1,18,512]{3,2,1,0:T(8,128)(2,1)S(1)}, bf16[3,1,18,512]{3,2,1,0:T(8,128)(2,1)S(1)}, u32[]{:S(2)}, u32[]{:S(2)}) collective-permute-start(bf16[3,1,18,512]{3,2,1,0:T(8,128)(2,1)S(1)} %get-tuple-element.198), channel_id=1, source_target_pairs={{0,30},{2,4},{4,2},{6,8},{8,6},{10,12},{12,10},{14,16},{16,14},{18... | collective-permute-start | bytes 165896 | tf_op jit(solution)/shard_map/ppermute | solution.py:148
  20.8 1.3 %shard_map.129 = (bf16[16,2,16,128]{3,2,1,0:T(8,128)(2,1)}, bf16[16,2,16,128]{3,2,1,0:T(8,128)(2,1)}) custom-call(s32[8,128]{1,0:T(8,128)S(1)} %broadcast_in_dim.20.refs_0_, bf16[16,2,32,128]{3,2,1,0:T(8,128)(2,1)S(1)} %bitcast.20), custom_call_target="tpu_custom_call" | custom-call | flops 4194304 | bytes 1048576 | tf_op jit(solution)/shard_map/pallas_call | solution.py:35
  22.2 2.6 %all-to-all-start.1 = ((bf16[32,16,128]{2,1,0:T(8,128)(2,1)}), bf16[32,16,128]{2,1,0:T(8,128)(2,1)S(1)}, u32[]{:S(2)}, u32[]{:S(2)}) async-start(bf16[32,16,128]{2,1,0:T(8,128)(2,1)} %bitcast.42), calls=%async_computation.1 | async-start | bytes 262144 | tf_op jit(solution)/shard_map/all_to_all | solution.py:19
  25.5 1.7 %shard_map.130 = (bf16[128,512]{1,0:T(8,128)(2,1)}, bf16[512,128]{1,0:T(8,128)(2,1)}, f32[128,128]{1,0:T(8,128)}, bf16[128,1024]{1,0:T(8,128)(2,1)}, bf16[128,10...) custom-call(bf16[3,8,16,512]{3,2,1,0:T(8,128)(2,1)S(1)} %copy-done.2, ...), custom_call_target="tpu_custom_call" | custom-call | flops 134217728 | bytes 4194304 | tf_op jit(solution)/shard_map/pallas_call | solution.py:35
  28.3 5.1 %all-to-all-done.1 = bf16[32,16,128]{2,1,0:T(8,128)(2,1)S(1)} async-done(((bf16[32,16,128]{2,1,0:T(8,128)(2,1)}), bf16[32,16,128]{2,1,0:T(8,128)(2,1)S(1)}, u32[]{:S(2)}, u32[]{:S(2)}) %all-to-all-start.1) | async-done | bytes 131104 | tf_op jit(solution)/shard_map/all_to_all | solution.py:19
  33.4 1.6 %shard_map.132 = (bf16[512,128]{1,0:T(8,128)(2,1)}, bf16[128,1024]{1,0:T(8,128)(2,1)}, bf16[512,128]{1,0:T(8,128)(2,1)}) custom-call(bf16[512,128]{1,0:T(8,128)(2,1)S(1)} %bitcast.23, bf16[512,1024]{1,0:T(8,128)(2,1)S(1)} %copy-done.1, bf16[512,1024]{1,0:T(8,128)(2,1)S(1)} %copy-done, f32[1,512]{1,0:T(1,128)S(1)} %bitcast.31, ...), custom_call_target="tpu_custom_call" | custom-call | flops 268435456 | bytes 4194304 | tf_op jit(solution)/shard_map/pallas_call | solution.py:35
  35.0 2.6 %all-to-all-start.2 = ((bf16[32,16,128]{2,1,0:T(8,128)(2,1)}), bf16[32,16,128]{2,1,0:T(8,128)(2,1)S(1)}, u32[]{:S(2)}, u32[]{:S(2)}) async-start(bf16[32,16,128]{2,1,0:T(8,128)(2,1)} %bitcast.37), calls=%async_computation.2 | async-start | bytes 262144 | tf_op jit(solution)/shard_map/all_to_all | solution.py:19
  38.7 7.5 %all-to-all-done.2 = bf16[32,16,128]{2,1,0:T(8,128)(2,1)S(1)} async-done(((bf16[32,16,128]{2,1,0:T(8,128)(2,1)}), bf16[32,16,128]{2,1,0:T(8,128)(2,1)S(1)}, u32[]{:S(2)}, u32[]{:S(2)}) %all-to-all-start.2) | async-done | bytes 131104 | tf_op jit(solution)/shard_map/all_to_all | solution.py:19
  46.2 1.7 %shard_map.134 = bf16[16,2,16,128]{3,2,1,0:T(8,128)(2,1)} custom-call(s32[8,128]{1,0:T(8,128)S(1)} %broadcast_in_dim.20.refs_0_, bf16[16,2,16,128]{3,2,1,0:T(8,128)(2,1)S(1)} %bitcast.25, f32[16,128]{1,0:T(8,128)S(1)} %pad.9.refs_2_, bf16[16,2,16,128]{3,2,1,0:T(8,128)(2,1)S(1)} %shard_map.133.refs_3_), custom_call_target="tpu_custom_call" | custom-call | flops 4194304 | bytes 1048576 | tf_op jit(solution)/shard_map/pallas_call | solution.py:35
  47.9 2.6 %all-to-all-start.3 = ((bf16[32,16,128]{2,1,0:T(8,128)(2,1)}), bf16[32,16,128]{2,1,0:T(8,128)(2,1)S(1)}, u32[]{:S(2)}, u32[]{:S(2)}) async-start(bf16[32,16,128]{2,1,0:T(8,128)(2,1)} %bitcast.39), calls=%async_computation.3 | async-start | bytes 262144 | tf_op jit(solution)/shard_map/all_to_all | solution.py:19
  50.5 1.7 %shard_map.137 = (bf16[128,512]{1,0:T(8,128)(2,1)}, bf16[512,128]{1,0:T(8,128)(2,1)}, f32[128,128]{1,0:T(8,128)}, bf16[128,1024]{1,0:T(8,128)(2,1)}, bf16[128,10...) custom-call(bf16[3,8,16,512]{3,2,1,0:T(8,128)(2,1)S(1)} %copy-done.2, ...), custom_call_target="tpu_custom_call" | custom-call | flops 134217728 | bytes 4194304 | tf_op jit(solution)/shard_map/pallas_call | solution.py:35
  52.3 1.7 %shard_map.135 = (bf16[128,512]{1,0:T(8,128)(2,1)}, bf16[512,128]{1,0:T(8,128)(2,1)}, f32[128,128]{1,0:T(8,128)}, bf16[128,1024]{1,0:T(8,128)(2,1)}, bf16[128,10...) custom-call(bf16[3,8,16,512]{3,2,1,0:T(8,128)(2,1)S(1)} %copy-done.2, ...), custom_call_target="tpu_custom_call" | custom-call | flops 134217728 | bytes 4194304 | tf_op jit(solution)/shard_map/pallas_call | solution.py:35
  55.0 4.1 %all-to-all-done.3 = bf16[32,16,128]{2,1,0:T(8,128)(2,1)S(1)} async-done(((bf16[32,16,128]{2,1,0:T(8,128)(2,1)}), bf16[32,16,128]{2,1,0:T(8,128)(2,1)S(1)}, u32[]{:S(2)}, u32[]{:S(2)}) %all-to-all-start.3) | async-done | bytes 131104 | tf_op jit(solution)/shard_map/all_to_all | solution.py:19
  59.2 1.6 %shard_map.138 = (bf16[512,128]{1,0:T(8,128)(2,1)}, bf16[128,1024]{1,0:T(8,128)(2,1)}, bf16[512,128]{1,0:T(8,128)(2,1)}) custom-call(bf16[512,128]{1,0:T(8,128)(2,1)S(1)} %bitcast.24, bf16[512,1024]{1,0:T(8,128)(2,1)S(1)} %copy-done.1, bf16[512,1024]{1,0:T(8,128)(2,1)S(1)} %copy-done, f32[1,512]{1,0:T(1,128)S(1)} %bitcast.34, ...), custom_call_target="tpu_custom_call" | custom-call | flops 268435456 | bytes 4194304 | tf_op jit(solution)/shard_map/pallas_call | solution.py:35
  60.7 2.6 %all-to-all-start.4 = ((bf16[32,16,128]{2,1,0:T(8,128)(2,1)}), bf16[32,16,128]{2,1,0:T(8,128)(2,1)S(1)}, u32[]{:S(2)}, u32[]{:S(2)}) async-start(bf16[32,16,128]{2,1,0:T(8,128)(2,1)} %bitcast.38), calls=%async_computation.4 | async-start | bytes 262144 | tf_op jit(solution)/shard_map/all_to_all | solution.py:19
  64.3 7.7 %all-to-all-done.4 = bf16[32,16,128]{2,1,0:T(8,128)(2,1)S(1)} async-done(((bf16[32,16,128]{2,1,0:T(8,128)(2,1)}), bf16[32,16,128]{2,1,0:T(8,128)(2,1)S(1)}, u32[]{:S(2)}, u32[]{:S(2)}) %all-to-all-start.4) | async-done | bytes 131104 | tf_op jit(solution)/shard_map/all_to_all | solution.py:19
  72.0 1.7 %shard_map.140 = bf16[16,2,16,128]{3,2,1,0:T(8,128)(2,1)} custom-call(s32[8,128]{1,0:T(8,128)S(1)} %broadcast_in_dim.20.refs_0_, bf16[16,2,16,128]{3,2,1,0:T(8,128)(2,1)S(1)} %bitcast.26, f32[16,128]{1,0:T(8,128)S(1)} %pad.9.refs_2_, bf16[16,2,16,128]{3,2,1,0:T(8,128)(2,1)S(1)} %shard_map.139.refs_3_), custom_call_target="tpu_custom_call" | custom-call | flops 4194304 | bytes 1048576 | tf_op jit(solution)/shard_map/pallas_call | solution.py:35
  73.7 2.8 %all-to-all-start.5 = ((bf16[32,16,128]{2,1,0:T(8,128)(2,1)}), bf16[32,16,128]{2,1,0:T(8,128)(2,1)S(1)}, u32[]{:S(2)}, u32[]{:S(2)}) async-start(bf16[32,16,128]{2,1,0:T(8,128)(2,1)} %bitcast.40), calls=%async_computation.5 | async-start | bytes 262144 | tf_op jit(solution)/shard_map/all_to_all | solution.py:19
  76.4 2.7 %shard_map.142.sums_ref = f32[16,512]{1,0:T(8,128)S(1)} custom-call(bf16[512,1024]{1,0:T(8,128)(2,1)S(1)} %copy-done, f32[1,512]{1,0:T(1,128)S(1)} %bitcast.35, bf16[10,32,512]{2,1,0:T(8,128)(2,1)} %get-tuple-element.135.refs_0_, bf16[512,128]{1,0:T(8,128)(2,1)} %get-tuple-element.111.refs_1_, bf16[128,1024]{1,0:T(8,128)(2,1)} %get-tuple-element.148.refs_2_.refs_7_, ...), custom_call_target="tpu_custom_call" | custom-call | bytes 2097152 | tf_op jit(solution)/shard_map/pallas_call | solution.py:35
  80.4 4.5 %all-to-all-done.5 = bf16[32,16,128]{2,1,0:T(8,128)(2,1)S(1)} async-done(((bf16[32,16,128]{2,1,0:T(8,128)(2,1)}), bf16[32,16,128]{2,1,0:T(8,128)(2,1)S(1)}, u32[]{:S(2)}, u32[]{:S(2)}) %all-to-all-start.5) | async-done | bytes 131104 | tf_op jit(solution)/shard_map/all_to_all | solution.py:19
  84.9 2.1 %shard_map.143 = (bf16[128,512]{1,0:T(8,128)(2,1)S(1)}, f32[16,512]{1,0:T(8,128)S(1)}, bf16[544,512]{1,0:T(8,128)(2,1)S(1)}, bf16[4,128,512]{2,1,0:T(8,128)(2,1)S(1)}, bf16[384,1024]{1,0:T(8,128)(2,1)S(1)}) custom-call(bf16[512,128]{1,0:T(8,128)(2,1)S(1)} %bitcast.21, bf16[512,1024]{1,0:T(8,128)(2,1)S(1)} %copy-done.1, bf16[512,1024]{1,0:T(8,128)(2,1)S(1)} %copy-done, ...), custom_call_target="tpu_custom_call" | custom-call | flops 1073741824 | bytes 6291456 | tf_op jit(solution)/shard_map/pallas_call | solution.py:35
  87.0 1.7 %shard_map.144 = (bf16[512,512]{1,0:T(8,128)(2,1)S(1)}, bf16[4,128,512]{2,1,0:T(8,128)(2,1)S(1)}) custom-call(bf16[512,128]{1,0:T(8,128)(2,1)S(1)} %bitcast.22, bf16[384,1024]{1,0:T(8,128)(2,1)S(1)} %get-tuple-element.155.right_ref, bf16[512,128]{1,0:T(8,128)(2,1)} %get-tuple-element.156.refs_0_, bf16[512,128]{1,0:T(8,128)(2,1)} %get-tuple-element.157.refs_1_), custom_call_target="tpu_custom_call" | custom-call | flops 536870912 | bytes 2097152 | tf_op jit(solution)/shard_map/pallas_call | solution.py:35
  91.8 1.7 %collective-permute-done.4 = bf16[1,8,1,512]{3,2,1,0:T(2,128)(2,1)S(1)} collective-permute-done((bf16[1,8,1,512]{3,2,1,0:T(2,128)(2,1)S(1)}, bf16[1,8,1,512]{3,2,1,0:T(2,128)(2,1)S(1)}, u32[]{:S(2)}, u32[]{:S(2)}) %collective-permute-start.4) | collective-permute-done | bytes 8224 | tf_op jit(solution)/shard_map/ppermute | solution.py:132
  93.5 4.7 %collective-permute-done.8.refs_2_ = bf16[288,512]{1,0:T(8,128)(2,1)S(1)} collective-permute-done((bf16[288,512]{1,0:T(8,128)(2,1)S(1)}, bf16[288,512]{1,0:T(8,128)(2,1)S(1)}, u32[]{:S(2)}, u32[]{:S(2)}) %collective-permute-start.8) | collective-permute-done | bytes 294944 | tf_op jit(solution)/shard_map/ppermute | solution.py:812
  99.5 5.5 %collective-permute-done.9.refs_3_ = bf16[192,512]{1,0:T(8,128)(2,1)S(1)} collective-permute-done((bf16[192,512]{1,0:T(8,128)(2,1)S(1)}, bf16[192,512]{1,0:T(8,128)(2,1)S(1)}, u32[]{:S(2)}, u32[]{:S(2)}) %collective-permute-start.9) | collective-permute-done | bytes 196640 | tf_op jit(solution)/shard_map/ppermute | solution.py:812
  105.2 2.1 %collective-permute-start.14 = (bf16[64,512]{1,0:T(8,128)(2,1)S(1)}, bf16[64,512]{1,0:T(8,128)(2,1)S(1)}, u32[]{:S(2)}, u32[]{:S(2)}) collective-permute-start(bf16[64,512]{1,0:T(8,128)(2,1)S(1)} %get-tuple-element.179), channel_id=1, source_target_pairs={{0,8},{1,9},{2,10},{3,11},{4,12},{5,13},{6,14},{7,15},{8,0},{9,1},... | collective-permute-start | bytes 196616 | tf_op jit(solution)/shard_map/ppermute | solution.py:812
  108.2 1.6 %collective-permute-done.11.refs_2_ = bf16[96,512]{1,0:T(8,128)(2,1)S(1)} collective-permute-done((bf16[96,512]{1,0:T(8,128)(2,1)S(1)}, bf16[96,512]{1,0:T(8,128)(2,1)S(1)}, u32[]{:S(2)}, u32[]{:S(2)}) %collective-permute-start.11) | collective-permute-done | bytes 98336 | tf_op jit(solution)/shard_map/ppermute | solution.py:812
  110.5 2.4 %collective-permute-start.15 = (bf16[32,512]{1,0:T(8,128)(2,1)S(1)}, bf16[32,512]{1,0:T(8,128)(2,1)S(1)}, u32[]{:S(2)}, u32[]{:S(2)}) collective-permute-start(bf16[32,512]{1,0:T(8,128)(2,1)S(1)} %get-tuple-element.186), channel_id=1, source_target_pairs={{0,16},{1,17},{2,18},{3,19},{4,20},{5,21},{6,22},{7,23},{8,24},{9,... | collective-permute-start | bytes 98312 | tf_op jit(solution)/shard_map/ppermute | solution.py:821
  (75 shorter events, 16.1 us)
Async XLA Ops:
  0.6 9.2 %copy-start.2 = (bf16[3,8,16,512]{3,2,1,0:T(8,128)(2,1)S(1)}, bf16[3,8,16,512]{3,2,1,0:T(8,128)(2,1)}, u32[]{:S(2)}) copy-start(bf16[3,8,16,512]{3,2,1,0:T(8,128)(2,1)} %refs_0_.5) | copy-start | bytes 1179652
  0.6 11.1 %copy-start.5 = (s32[3,4]{1,0:T(4,128)S(1)}, s32[3,4]{1,0:T(4,128)}, u32[]{:S(2)}) copy-start(s32[3,4]{1,0:T(4,128)} %param.17) | copy-start | bytes 148
  0.7 11.1 %copy-start.6 = (s32[3,4]{1,0:T(4,128)S(1)}, s32[3,4]{1,0:T(4,128)}, u32[]{:S(2)}) copy-start(s32[3,4]{1,0:T(4,128)} %param.16) | copy-start | bytes 148
  2.5 22.3 %copy-start = (bf16[512,1024]{1,0:T(8,128)(2,1)S(1)}, bf16[512,1024]{1,0:T(8,128)(2,1)}, u32[]{:S(2)}) copy-start(bf16[512,1024]{1,0:T(8,128)(2,1)} %up_ref.7) | copy-start | bytes 3145732
  2.5 18.2 %all-to-all-start = ((bf16[32,32,128]{2,1,0:T(8,128)(2,1)}), bf16[32,32,128]{2,1,0:T(8,128)(2,1)S(1)}, u32[]{:S(2)}, u32[]{:S(2)}) async-start(bf16[32,32,128]{2,1,0:T(8,128)(2,1)} %shard_map.128), calls=%async_computation | async-start | bytes 524288 | tf_op jit(solution)/shard_map/all_to_all | solution.py:19
  9.9 4.8 %collective-permute-start = (bf16[3,8,1,512]{3,2,1,0:T(2,128)(2,1)S(1)}, bf16[3,8,1,512]{3,2,1,0:T(2,128)(2,1)S(1)}, u32[]{:S(2)}, u32[]{:S(2)}) collective-permute-start(bf16[3,8,1,512]{3,2,1,0:T(2,128)(2,1)S(1)} %broadcast_select_fusion.2), channel_id=1, source_target_pairs={{0,1},{1,0},{2,3},{3,2},{4,5},{5,4},{6,7},{7,6},{8,9},{9,8},{10,11... | collective-permute-start | bytes 73736 | tf_op jit(solution)/shard_map/ppermute | solution.py:132
  15.0 9.8 %collective-permute-start.2 = (bf16[3,1,18,512]{3,2,1,0:T(8,128)(2,1)S(1)}, bf16[3,1,18,512]{3,2,1,0:T(8,128)(2,1)S(1)}, u32[]{:S(2)}, u32[]{:S(2)}) collective-permute-start(bf16[3,1,18,512]{3,2,1,0:T(8,128)(2,1)S(1)} %get-tuple-element.197), channel_id=1, source_target_pairs={{0,2},{2,0},{4,6},{6,4},{8,10},{10,8},{12,14},{14,12},{16,18},{18,... | collective-permute-start | bytes 165896 | tf_op jit(solution)/shard_map/ppermute | solution.py:146
  15.1 9.8 %collective-permute-start.1 = (bf16[3,1,18,512]{3,2,1,0:T(8,128)(2,1)S(1)}, bf16[3,1,18,512]{3,2,1,0:T(8,128)(2,1)S(1)}, u32[]{:S(2)}, u32[]{:S(2)}) collective-permute-start(bf16[3,1,18,512]{3,2,1,0:T(8,128)(2,1)S(1)} %get-tuple-element.198), channel_id=1, source_target_pairs={{0,30},{2,4},{4,2},{6,8},{8,6},{10,12},{12,10},{14,16},{16,14},{18... | collective-permute-start | bytes 165896 | tf_op jit(solution)/shard_map/ppermute | solution.py:148
  22.2 11.2 %all-to-all-start.1 = ((bf16[32,16,128]{2,1,0:T(8,128)(2,1)}), bf16[32,16,128]{2,1,0:T(8,128)(2,1)S(1)}, u32[]{:S(2)}, u32[]{:S(2)}) async-start(bf16[32,16,128]{2,1,0:T(8,128)(2,1)} %bitcast.42), calls=%async_computation.1 | async-start | bytes 262144 | tf_op jit(solution)/shard_map/all_to_all | solution.py:19
  24.8 0.7 copy-start.3
  24.9 0.7 copy-start.4
  25.5 7.9 %copy-start.1 = (bf16[512,1024]{1,0:T(8,128)(2,1)S(1)}, bf16[512,1024]{1,0:T(8,128)(2,1)}, u32[]{:S(2)}) copy-start(bf16[512,1024]{1,0:T(8,128)(2,1)} %down_ref.5) | copy-start | bytes 3145732
  35.0 11.2 %all-to-all-start.2 = ((bf16[32,16,128]{2,1,0:T(8,128)(2,1)}), bf16[32,16,128]{2,1,0:T(8,128)(2,1)S(1)}, u32[]{:S(2)}, u32[]{:S(2)}) async-start(bf16[32,16,128]{2,1,0:T(8,128)(2,1)} %bitcast.37), calls=%async_computation.2 | async-start | bytes 262144 | tf_op jit(solution)/shard_map/all_to_all | solution.py:19
  47.9 11.2 %all-to-all-start.3 = ((bf16[32,16,128]{2,1,0:T(8,128)(2,1)}), bf16[32,16,128]{2,1,0:T(8,128)(2,1)S(1)}, u32[]{:S(2)}, u32[]{:S(2)}) async-start(bf16[32,16,128]{2,1,0:T(8,128)(2,1)} %bitcast.39), calls=%async_computation.3 | async-start | bytes 262144 | tf_op jit(solution)/shard_map/all_to_all | solution.py:19
  60.7 11.2 %all-to-all-start.4 = ((bf16[32,16,128]{2,1,0:T(8,128)(2,1)}), bf16[32,16,128]{2,1,0:T(8,128)(2,1)S(1)}, u32[]{:S(2)}, u32[]{:S(2)}) async-start(bf16[32,16,128]{2,1,0:T(8,128)(2,1)} %bitcast.38), calls=%async_computation.4 | async-start | bytes 262144 | tf_op jit(solution)/shard_map/all_to_all | solution.py:19
  73.7 11.2 %all-to-all-start.5 = ((bf16[32,16,128]{2,1,0:T(8,128)(2,1)}), bf16[32,16,128]{2,1,0:T(8,128)(2,1)S(1)}, u32[]{:S(2)}, u32[]{:S(2)}) async-start(bf16[32,16,128]{2,1,0:T(8,128)(2,1)} %bitcast.40), calls=%async_computation.5 | async-start | bytes 262144 | tf_op jit(solution)/shard_map/all_to_all | solution.py:19
  87.0 2.0 %collective-permute-start.3 = (bf16[544,512]{1,0:T(8,128)(2,1)S(1)}, bf16[544,512]{1,0:T(8,128)(2,1)S(1)}, u32[]{:S(2)}, u32[]{:S(2)}) collective-permute-start(bf16[544,512]{1,0:T(8,128)(2,1)S(1)} %get-tuple-element.154), channel_id=1, source_target_pairs={{0,2},{1,3},{2,0},{3,1},{4,6},{5,7},{6,4},{7,5},{8,10},{9,11},{10,... | collective-permute-start | bytes 1671176 | tf_op jit(solution)/shard_map/ppermute | solution.py:812
  89.1 2.0 %collective-permute-start.5 = (bf16[512,512]{1,0:T(8,128)(2,1)S(1)}, bf16[512,512]{1,0:T(8,128)(2,1)S(1)}, u32[]{:S(2)}, u32[]{:S(2)}) collective-permute-start(bf16[512,512]{1,0:T(8,128)(2,1)S(1)} %get-tuple-element.163), channel_id=1, source_target_pairs={{0,2},{1,3},{2,0},{3,1},{4,6},{5,7},{6,4},{7,5},{8,10},{9,11},{10,... | collective-permute-start | bytes 1572872 | tf_op jit(solution)/shard_map/ppermute | solution.py:812
  89.5 8.7 %collective-permute-start.8 = (bf16[288,512]{1,0:T(8,128)(2,1)S(1)}, bf16[288,512]{1,0:T(8,128)(2,1)S(1)}, u32[]{:S(2)}, u32[]{:S(2)}) collective-permute-start(bf16[288,512]{1,0:T(8,128)(2,1)S(1)} %get-tuple-element.160), channel_id=1, source_target_pairs={{0,4},{1,5},{2,3},{3,2},{4,0},{5,1},{6,7},{7,6},{8,12},{9,13},{10,... | collective-permute-start | bytes 884744 | tf_op jit(solution)/shard_map/ppermute | solution.py:812
  89.5 4.0 %collective-permute-start.4 = (bf16[1,8,1,512]{3,2,1,0:T(2,128)(2,1)S(1)}, bf16[1,8,1,512]{3,2,1,0:T(2,128)(2,1)S(1)}, u32[]{:S(2)}, u32[]{:S(2)}) collective-permute-start(bf16[1,8,1,512]{3,2,1,0:T(2,128)(2,1)S(1)} %broadcast_select_fusion.9), channel_id=1, source_target_pairs={{0,1},{1,0},{2,3},{3,2},{4,5},{5,4},{6,7},{7,6},{8,9},{9,8},{10,11... | collective-permute-start | bytes 24584 | tf_op jit(solution)/shard_map/ppermute | solution.py:132
  91.2 7.4 %collective-permute-start.10 = (bf16[256,512]{1,0:T(8,128)(2,1)S(1)}, bf16[256,512]{1,0:T(8,128)(2,1)S(1)}, u32[]{:S(2)}, u32[]{:S(2)}) collective-permute-start(bf16[256,512]{1,0:T(8,128)(2,1)S(1)} %get-tuple-element.164), channel_id=1, source_target_pairs={{0,1},{1,0},{2,6},{3,7},{4,5},{5,4},{6,2},{7,3},{8,9},{9,8},{10,14... | collective-permute-start | bytes 786440 | tf_op jit(solution)/shard_map/ppermute | solution.py:812
  98.3 6.8 %collective-permute-start.9 = (bf16[192,512]{1,0:T(8,128)(2,1)S(1)}, bf16[192,512]{1,0:T(8,128)(2,1)S(1)}, u32[]{:S(2)}, u32[]{:S(2)}) collective-permute-start(bf16[192,512]{1,0:T(8,128)(2,1)S(1)} %get-tuple-element.171), channel_id=1, source_target_pairs={{0,1},{1,0},{2,6},{3,7},{4,5},{5,4},{6,2},{7,3},{8,9},{9,8},{10,14... | collective-permute-start | bytes 589832 | tf_op jit(solution)/shard_map/ppermute | solution.py:812
  98.7 6.4 %collective-permute-start.12 = (bf16[128,512]{1,0:T(8,128)(2,1)S(1)}, bf16[128,512]{1,0:T(8,128)(2,1)S(1)}, u32[]{:S(2)}, u32[]{:S(2)}) collective-permute-start(bf16[128,512]{1,0:T(8,128)(2,1)S(1)} %get-tuple-element.173), channel_id=1, source_target_pairs={{0,4},{1,5},{2,3},{3,2},{4,0},{5,1},{6,7},{7,6},{8,12},{9,13},{10,... | collective-permute-start | bytes 393224 | tf_op jit(solution)/shard_map/ppermute | solution.py:812
  105.1 4.7 %collective-permute-start.11 = (bf16[96,512]{1,0:T(8,128)(2,1)S(1)}, bf16[96,512]{1,0:T(8,128)(2,1)S(1)}, u32[]{:S(2)}, u32[]{:S(2)}) collective-permute-start(bf16[96,512]{1,0:T(8,128)(2,1)S(1)} %get-tuple-element.177), channel_id=1, source_target_pairs={{0,8},{1,9},{2,10},{3,11},{4,12},{5,13},{6,14},{7,15},{8,0},{9,1},... | collective-permute-start | bytes 294920 | tf_op jit(solution)/shard_map/ppermute | solution.py:812
  105.2 5.2 %collective-permute-start.14 = (bf16[64,512]{1,0:T(8,128)(2,1)S(1)}, bf16[64,512]{1,0:T(8,128)(2,1)S(1)}, u32[]{:S(2)}, u32[]{:S(2)}) collective-permute-start(bf16[64,512]{1,0:T(8,128)(2,1)S(1)} %get-tuple-element.179), channel_id=1, source_target_pairs={{0,8},{1,9},{2,10},{3,11},{4,12},{5,13},{6,14},{7,15},{8,0},{9,1},... | collective-permute-start | bytes 196616 | tf_op jit(solution)/shard_map/ppermute | solution.py:812
  107.3 5.6 %collective-permute-start.7 = (bf16[1,1,18,512]{3,2,1,0:T(8,128)(2,1)S(1)}, bf16[1,1,18,512]{3,2,1,0:T(8,128)(2,1)S(1)}, u32[]{:S(2)}, u32[]{:S(2)}) collective-permute-start(bf16[1,1,18,512]{3,2,1,0:T(8,128)(2,1)S(1)} %get-tuple-element.207), channel_id=1, source_target_pairs={{0,2},{2,0},{4,6},{6,4},{8,10},{10,8},{12,14},{14,12},{16,18},{18,... | collective-permute-start | bytes 55304 | tf_op jit(solution)/shard_map/ppermute | solution.py:146
  107.4 6.1 %collective-permute-start.6 = (bf16[1,1,18,512]{3,2,1,0:T(8,128)(2,1)S(1)}, bf16[1,1,18,512]{3,2,1,0:T(8,128)(2,1)S(1)}, u32[]{:S(2)}, u32[]{:S(2)}) collective-permute-start(bf16[1,1,18,512]{3,2,1,0:T(8,128)(2,1)S(1)} %get-tuple-element.208), channel_id=1, source_target_pairs={{0,30},{2,4},{4,2},{6,8},{8,6},{10,12},{12,10},{14,16},{16,14},{18... | collective-permute-start | bytes 55304 | tf_op jit(solution)/shard_map/ppermute | solution.py:148
  109.8 5.4 %collective-permute-start.13 = (bf16[64,512]{1,0:T(8,128)(2,1)S(1)}, bf16[64,512]{1,0:T(8,128)(2,1)S(1)}, u32[]{:S(2)}, u32[]{:S(2)}) collective-permute-start(bf16[64,512]{1,0:T(8,128)(2,1)S(1)} %get-tuple-element.183), channel_id=1, source_target_pairs={{0,16},{1,17},{2,18},{3,19},{4,20},{5,21},{6,22},{7,23},{8,24},{9,... | collective-permute-start | bytes 196616 | tf_op jit(solution)/shard_map/ppermute | solution.py:821
  110.5 5.0 %collective-permute-start.15 = (bf16[32,512]{1,0:T(8,128)(2,1)S(1)}, bf16[32,512]{1,0:T(8,128)(2,1)S(1)}, u32[]{:S(2)}, u32[]{:S(2)}) collective-permute-start(bf16[32,512]{1,0:T(8,128)(2,1)S(1)} %get-tuple-element.186), channel_id=1, source_target_pairs={{0,16},{1,17},{2,18},{3,19},{4,20},{5,21},{6,22},{7,23},{8,24},{9,... | collective-permute-start | bytes 98312 | tf_op jit(solution)/shard_map/ppermute | solution.py:821

commit v13 on v12

--- a/solution.py
+++ b/solution.py
@@ -838,13 +838,14 @@
     field = after(field, send)
     arrived_later = behind.send(after(later, send))
     later = behind.send(arrived_later)
-    around = lat_edges(field, lambda value: after(value, later))
-    state = final_parts(field[0], (*around, *lon_edges(field, *around)), kernel)
     for at in range(1, 4):
         arrived = ahead.send(send)
         arrived_later = behind.send(later)
         send = ahead.send(after(arrived, later))
         later = behind.send(arrived_later)
+        if at == 1:
+            around = lat_edges(field, lambda value: after(value, send))
+            state = final_parts(field[0], (*around, *lon_edges(field, *around)), kernel)
     final_ahead = ahead.send(send)
     final_behind = behind.send(later)
     sds = jax.ShapeDtypeStruct

time: 117 us -> 117 us (level)
    ppermute x2, waiting for transfers between devices: 4.4 us -> 2.73 us  [lat_edges(): lax.ppermute(jnp.where(lat_at == 0, last, first), 'lat', [(0, 1), (1, 0)])]
    ppermute x8, waiting for transfers between devices: 13 us -> 14.6 us  [halving(): lax.ppermute(send, AXES, [(flat(i, j), flat(*partner(i, j))) for i, j in...]
  transfers between devices with their start and end apart: 22 -> 22, of which waited for: 16 -> 15; matrix products, arithmetic and copies ran while one was open for 1% -> 1% of each run, Pallas kernels for 15% -> 15%
where the time goes in v13:
time: 117 us; the launch traced here: 116 us
  waiting for transfers between devices  47.9 us (41%)
  starting transfers between devices  36.9 us (32%)
  Pallas kernels  28.8 us (25%)
  between operations  1.24 us (1%)
    all_to_all x6, waiting for transfers between devices, exchanged(): return lax.all_to_all(blocks, AXES, split_axis=0, concat_axis=0, tiled=True)  29 us
    pallas_call x27, Pallas kernels, call(): pl.pallas_call(kernel, out_shape=out_shape, in_specs=[pl.BlockSpec(memory...  28.8 us
    all_to_all x6, starting transfers between devices, exchanged(): return lax.all_to_all(blocks, AXES, split_axis=0, concat_axis=0, tiled=True)  20.4 us
    ppermute x8, waiting for transfers between devices, halving(): lax.ppermute(send, AXES, [(flat(i, j), flat(*partner(i, j))) for i, j in...  14.6 us
    ppermute x2, starting transfers between devices, lon_edges(): with_last = lax.ppermute(jnp.where(even, first, last), 'lon', pairs)  6.48 us
    ppermute x8, starting transfers between devices, halving(): lax.ppermute(send, AXES, [(flat(i, j), flat(*partner(i, j))) for i, j in...  4.33 us
    ppermute x2, starting transfers between devices, lat_edges(): lax.ppermute(jnp.where(lat_at == 0, last, first), 'lat', [(0, 1), (1, 0)])  2.91 us
    ppermute x2, waiting for transfers between devices, lat_edges(): lax.ppermute(jnp.where(lat_at == 0, last, first), 'lat', [(0, 1), (1, 0)])  2.73 us
  transfers between devices with their start and end apart: 22, of which 15 were waited for; matrix products, arithmetic and copies ran while one was open for 1% of the time, Pallas kernels for 15%

profile of v13, /device:TPU:0, one launch (start us, length us, event | category | flops | bytes accessed | tf_op | source)
XLA Modules:
  0.0 116.4 jit_solution(14472377556634289826)
XLA Ops:
  0.7 1.8 %shard_map.128 = bf16[32,32,128]{2,1,0:T(8,128)(2,1)} custom-call(bf16[128,512]{1,0:T(8,128)(2,1)} %bitcast.41, f32[12,8,16]{2,1,0:T(8,128)} %bitcast.43), custom_call_target="tpu_custom_call" | custom-call | bytes 524288 | tf_op jit(solution)/shard_map/pallas_call | solution.py:35
  2.5 7.3 %all-to-all-start = ((bf16[32,32,128]{2,1,0:T(8,128)(2,1)}), bf16[32,32,128]{2,1,0:T(8,128)(2,1)S(1)}, u32[]{:S(2)}, u32[]{:S(2)}) async-start(bf16[32,32,128]{2,1,0:T(8,128)(2,1)} %shard_map.128), calls=%async_computation | async-start | bytes 524288 | tf_op jit(solution)/shard_map/all_to_all | solution.py:19
  9.9 1.8 %collective-permute-start = (bf16[3,8,1,512]{3,2,1,0:T(2,128)(2,1)S(1)}, bf16[3,8,1,512]{3,2,1,0:T(2,128)(2,1)S(1)}, u32[]{:S(2)}, u32[]{:S(2)}) collective-permute-start(bf16[3,8,1,512]{3,2,1,0:T(2,128)(2,1)S(1)} %broadcast_select_fusion.2), channel_id=1, source_target_pairs={{0,1},{1,0},{2,3},{3,2},{4,5},{5,4},{6,7},{7,6},{8,9},{9,8},{10,11... | collective-permute-start | bytes 73736 | tf_op jit(solution)/shard_map/ppermute | solution.py:132
  12.0 2.7 %collective-permute-done = bf16[3,8,1,512]{3,2,1,0:T(2,128)(2,1)S(1)} collective-permute-done((bf16[3,8,1,512]{3,2,1,0:T(2,128)(2,1)S(1)}, bf16[3,8,1,512]{3,2,1,0:T(2,128)(2,1)S(1)}, u32[]{:S(2)}, u32[]{:S(2)}) %collective-permute-start) | collective-permute-done | bytes 24608 | tf_op jit(solution)/shard_map/ppermute | solution.py:132
  15.1 5.7 %collective-permute-start.1 = (bf16[3,1,18,512]{3,2,1,0:T(8,128)(2,1)S(1)}, bf16[3,1,18,512]{3,2,1,0:T(8,128)(2,1)S(1)}, u32[]{:S(2)}, u32[]{:S(2)}) collective-permute-start(bf16[3,1,18,512]{3,2,1,0:T(8,128)(2,1)S(1)} %get-tuple-element.198), channel_id=1, source_target_pairs={{0,30},{2,4},{4,2},{6,8},{8,6},{10,12},{12,10},{14,16},{16,14},{18... | collective-permute-start | bytes 165896 | tf_op jit(solution)/shard_map/ppermute | solution.py:148
  20.8 1.3 %shard_map.129 = (bf16[16,2,16,128]{3,2,1,0:T(8,128)(2,1)}, bf16[16,2,16,128]{3,2,1,0:T(8,128)(2,1)}) custom-call(s32[8,128]{1,0:T(8,128)S(1)} %broadcast_in_dim.20.refs_0_, bf16[16,2,32,128]{3,2,1,0:T(8,128)(2,1)S(1)} %bitcast.20), custom_call_target="tpu_custom_call" | custom-call | flops 4194304 | bytes 1048576 | tf_op jit(solution)/shard_map/pallas_call | solution.py:35
  22.2 2.6 %all-to-all-start.1 = ((bf16[32,16,128]{2,1,0:T(8,128)(2,1)}), bf16[32,16,128]{2,1,0:T(8,128)(2,1)S(1)}, u32[]{:S(2)}, u32[]{:S(2)}) async-start(bf16[32,16,128]{2,1,0:T(8,128)(2,1)} %bitcast.42), calls=%async_computation.1 | async-start | bytes 262144 | tf_op jit(solution)/shard_map/all_to_all | solution.py:19
  25.5 1.7 %shard_map.130 = (bf16[128,512]{1,0:T(8,128)(2,1)}, bf16[512,128]{1,0:T(8,128)(2,1)}, f32[128,128]{1,0:T(8,128)}, bf16[128,1024]{1,0:T(8,128)(2,1)}, bf16[128,10...) custom-call(bf16[3,8,16,512]{3,2,1,0:T(8,128)(2,1)S(1)} %copy-done.2, ...), custom_call_target="tpu_custom_call" | custom-call | flops 134217728 | bytes 4194304 | tf_op jit(solution)/shard_map/pallas_call | solution.py:35
  28.3 5.1 %all-to-all-done.1 = bf16[32,16,128]{2,1,0:T(8,128)(2,1)S(1)} async-done(((bf16[32,16,128]{2,1,0:T(8,128)(2,1)}), bf16[32,16,128]{2,1,0:T(8,128)(2,1)S(1)}, u32[]{:S(2)}, u32[]{:S(2)}) %all-to-all-start.1) | async-done | bytes 131104 | tf_op jit(solution)/shard_map/all_to_all | solution.py:19
  33.4 1.6 %shard_map.132 = (bf16[512,128]{1,0:T(8,128)(2,1)}, bf16[128,1024]{1,0:T(8,128)(2,1)}, bf16[512,128]{1,0:T(8,128)(2,1)}) custom-call(bf16[512,128]{1,0:T(8,128)(2,1)S(1)} %bitcast.23, bf16[512,1024]{1,0:T(8,128)(2,1)S(1)} %copy-done.1, bf16[512,1024]{1,0:T(8,128)(2,1)S(1)} %copy-done, f32[1,512]{1,0:T(1,128)S(1)} %bitcast.31, ...), custom_call_target="tpu_custom_call" | custom-call | flops 268435456 | bytes 4194304 | tf_op jit(solution)/shard_map/pallas_call | solution.py:35
  35.0 2.6 %all-to-all-start.2 = ((bf16[32,16,128]{2,1,0:T(8,128)(2,1)}), bf16[32,16,128]{2,1,0:T(8,128)(2,1)S(1)}, u32[]{:S(2)}, u32[]{:S(2)}) async-start(bf16[32,16,128]{2,1,0:T(8,128)(2,1)} %bitcast.37), calls=%async_computation.2 | async-start | bytes 262144 | tf_op jit(solution)/shard_map/all_to_all | solution.py:19
  38.7 7.5 %all-to-all-done.2 = bf16[32,16,128]{2,1,0:T(8,128)(2,1)S(1)} async-done(((bf16[32,16,128]{2,1,0:T(8,128)(2,1)}), bf16[32,16,128]{2,1,0:T(8,128)(2,1)S(1)}, u32[]{:S(2)}, u32[]{:S(2)}) %all-to-all-start.2) | async-done | bytes 131104 | tf_op jit(solution)/shard_map/all_to_all | solution.py:19
  46.2 1.7 %shard_map.134 = bf16[16,2,16,128]{3,2,1,0:T(8,128)(2,1)} custom-call(s32[8,128]{1,0:T(8,128)S(1)} %broadcast_in_dim.20.refs_0_, bf16[16,2,16,128]{3,2,1,0:T(8,128)(2,1)S(1)} %bitcast.25, f32[16,128]{1,0:T(8,128)S(1)} %pad.9.refs_2_, bf16[16,2,16,128]{3,2,1,0:T(8,128)(2,1)S(1)} %shard_map.133.refs_3_), custom_call_target="tpu_custom_call" | custom-call | flops 4194304 | bytes 1048576 | tf_op jit(solution)/shard_map/pallas_call | solution.py:35
  47.9 2.6 %all-to-all-start.3 = ((bf16[32,16,128]{2,1,0:T(8,128)(2,1)}), bf16[32,16,128]{2,1,0:T(8,128)(2,1)S(1)}, u32[]{:S(2)}, u32[]{:S(2)}) async-start(bf16[32,16,128]{2,1,0:T(8,128)(2,1)} %bitcast.39), calls=%async_computation.3 | async-start | bytes 262144 | tf_op jit(solution)/shard_map/all_to_all | solution.py:19
  50.5 1.7 %shard_map.137 = (bf16[128,512]{1,0:T(8,128)(2,1)}, bf16[512,128]{1,0:T(8,128)(2,1)}, f32[128,128]{1,0:T(8,128)}, bf16[128,1024]{1,0:T(8,128)(2,1)}, bf16[128,10...) custom-call(bf16[3,8,16,512]{3,2,1,0:T(8,128)(2,1)S(1)} %copy-done.2, ...), custom_call_target="tpu_custom_call" | custom-call | flops 134217728 | bytes 4194304 | tf_op jit(solution)/shard_map/pallas_call | solution.py:35
  52.3 1.7 %shard_map.135 = (bf16[128,512]{1,0:T(8,128)(2,1)}, bf16[512,128]{1,0:T(8,128)(2,1)}, f32[128,128]{1,0:T(8,128)}, bf16[128,1024]{1,0:T(8,128)(2,1)}, bf16[128,10...) custom-call(bf16[3,8,16,512]{3,2,1,0:T(8,128)(2,1)S(1)} %copy-done.2, ...), custom_call_target="tpu_custom_call" | custom-call | flops 134217728 | bytes 4194304 | tf_op jit(solution)/shard_map/pallas_call | solution.py:35
  55.0 4.1 %all-to-all-done.3 = bf16[32,16,128]{2,1,0:T(8,128)(2,1)S(1)} async-done(((bf16[32,16,128]{2,1,0:T(8,128)(2,1)}), bf16[32,16,128]{2,1,0:T(8,128)(2,1)S(1)}, u32[]{:S(2)}, u32[]{:S(2)}) %all-to-all-start.3) | async-done | bytes 131104 | tf_op jit(solution)/shard_map/all_to_all | solution.py:19
  59.2 1.6 %shard_map.138 = (bf16[512,128]{1,0:T(8,128)(2,1)}, bf16[128,1024]{1,0:T(8,128)(2,1)}, bf16[512,128]{1,0:T(8,128)(2,1)}) custom-call(bf16[512,128]{1,0:T(8,128)(2,1)S(1)} %bitcast.24, bf16[512,1024]{1,0:T(8,128)(2,1)S(1)} %copy-done.1, bf16[512,1024]{1,0:T(8,128)(2,1)S(1)} %copy-done, f32[1,512]{1,0:T(1,128)S(1)} %bitcast.34, ...), custom_call_target="tpu_custom_call" | custom-call | flops 268435456 | bytes 4194304 | tf_op jit(solution)/shard_map/pallas_call | solution.py:35
  60.7 2.6 %all-to-all-start.4 = ((bf16[32,16,128]{2,1,0:T(8,128)(2,1)}), bf16[32,16,128]{2,1,0:T(8,128)(2,1)S(1)}, u32[]{:S(2)}, u32[]{:S(2)}) async-start(bf16[32,16,128]{2,1,0:T(8,128)(2,1)} %bitcast.38), calls=%async_computation.4 | async-start | bytes 262144 | tf_op jit(solution)/shard_map/all_to_all | solution.py:19
  64.3 7.7 %all-to-all-done.4 = bf16[32,16,128]{2,1,0:T(8,128)(2,1)S(1)} async-done(((bf16[32,16,128]{2,1,0:T(8,128)(2,1)}), bf16[32,16,128]{2,1,0:T(8,128)(2,1)S(1)}, u32[]{:S(2)}, u32[]{:S(2)}) %all-to-all-start.4) | async-done | bytes 131104 | tf_op jit(solution)/shard_map/all_to_all | solution.py:19
  72.0 1.7 %shard_map.140 = bf16[16,2,16,128]{3,2,1,0:T(8,128)(2,1)} custom-call(s32[8,128]{1,0:T(8,128)S(1)} %broadcast_in_dim.20.refs_0_, bf16[16,2,16,128]{3,2,1,0:T(8,128)(2,1)S(1)} %bitcast.26, f32[16,128]{1,0:T(8,128)S(1)} %pad.9.refs_2_, bf16[16,2,16,128]{3,2,1,0:T(8,128)(2,1)S(1)} %shard_map.139.refs_3_), custom_call_target="tpu_custom_call" | custom-call | flops 4194304 | bytes 1048576 | tf_op jit(solution)/shard_map/pallas_call | solution.py:35
  73.7 2.8 %all-to-all-start.5 = ((bf16[32,16,128]{2,1,0:T(8,128)(2,1)}), bf16[32,16,128]{2,1,0:T(8,128)(2,1)S(1)}, u32[]{:S(2)}, u32[]{:S(2)}) async-start(bf16[32,16,128]{2,1,0:T(8,128)(2,1)} %bitcast.40), calls=%async_computation.5 | async-start | bytes 262144 | tf_op jit(solution)/shard_map/all_to_all | solution.py:19
  76.4 2.7 %shard_map.142.sums_ref = f32[16,512]{1,0:T(8,128)S(1)} custom-call(bf16[512,1024]{1,0:T(8,128)(2,1)S(1)} %copy-done, f32[1,512]{1,0:T(1,128)S(1)} %bitcast.35, bf16[10,32,512]{2,1,0:T(8,128)(2,1)} %get-tuple-element.135.refs_0_, bf16[512,128]{1,0:T(8,128)(2,1)} %get-tuple-element.111.refs_1_, bf16[128,1024]{1,0:T(8,128)(2,1)} %get-tuple-element.148.refs_2_.refs_7_, ...), custom_call_target="tpu_custom_call" | custom-call | bytes 2097152 | tf_op jit(solution)/shard_map/pallas_call | solution.py:35
  79.2 1.2 %shard_map.141 = (bf16[128,1024]{1,0:T(8,128)(2,1)S(1)}, bf16[128,512]{1,0:T(8,128)(2,1)S(1)}, f32[128,128]{1,0:T(8,128)S(1)}, bf16[10,32,512]{2,1,0:T(8,128)(2,1)S(1)}) custom-call(bf16[128,1024]{1,0:T(8,128)(2,1)} %get-tuple-element.140.refs_0_, bf16[128,512]{1,0:T(8,128)(2,1)} %get-tuple-element.141.refs_1_, f32[128,128]{1,0:T(8,128)} %get-tuple-element.142.refs_2_, ...), custom_call_target="tpu_custom_call" | custom-call | bytes 524288 | tf_op jit(solution)/shard_map/pallas_call | solution.py:35
  80.4 4.5 %all-to-all-done.5 = bf16[32,16,128]{2,1,0:T(8,128)(2,1)S(1)} async-done(((bf16[32,16,128]{2,1,0:T(8,128)(2,1)}), bf16[32,16,128]{2,1,0:T(8,128)(2,1)S(1)}, u32[]{:S(2)}, u32[]{:S(2)}) %all-to-all-start.5) | async-done | bytes 131104 | tf_op jit(solution)/shard_map/all_to_all | solution.py:19
  84.9 2.1 %shard_map.143 = (bf16[128,512]{1,0:T(8,128)(2,1)S(1)}, f32[16,512]{1,0:T(8,128)S(1)}, bf16[544,512]{1,0:T(8,128)(2,1)S(1)}, bf16[4,128,512]{2,1,0:T(8,128)(2,1)S(1)}, bf16[384,1024]{1,0:T(8,128)(2,1)S(1)}) custom-call(bf16[512,128]{1,0:T(8,128)(2,1)S(1)} %bitcast.21, bf16[512,1024]{1,0:T(8,128)(2,1)S(1)} %copy-done.1, bf16[512,1024]{1,0:T(8,128)(2,1)S(1)} %copy-done, ...), custom_call_target="tpu_custom_call" | custom-call | flops 1073741824 | bytes 6291456 | tf_op jit(solution)/shard_map/pallas_call | solution.py:35
  87.0 1.7 %shard_map.144 = (bf16[512,512]{1,0:T(8,128)(2,1)S(1)}, bf16[4,128,512]{2,1,0:T(8,128)(2,1)S(1)}) custom-call(bf16[512,128]{1,0:T(8,128)(2,1)S(1)} %bitcast.22, bf16[384,1024]{1,0:T(8,128)(2,1)S(1)} %get-tuple-element.155.right_ref, bf16[512,128]{1,0:T(8,128)(2,1)} %get-tuple-element.156.refs_0_, bf16[512,128]{1,0:T(8,128)(2,1)} %get-tuple-element.157.refs_1_), custom_call_target="tpu_custom_call" | custom-call | flops 536870912 | bytes 2097152 | tf_op jit(solution)/shard_map/pallas_call | solution.py:35
  91.8 6.4 %collective-permute-done.5.refs_2_ = bf16[288,512]{1,0:T(8,128)(2,1)S(1)} collective-permute-done((bf16[288,512]{1,0:T(8,128)(2,1)S(1)}, bf16[288,512]{1,0:T(8,128)(2,1)S(1)}, u32[]{:S(2)}, u32[]{:S(2)}) %collective-permute-start.5) | collective-permute-done | bytes 294944 | tf_op jit(solution)/shard_map/ppermute | solution.py:812
  99.6 5.5 %collective-permute-done.9.refs_3_ = bf16[192,512]{1,0:T(8,128)(2,1)S(1)} collective-permute-done((bf16[192,512]{1,0:T(8,128)(2,1)S(1)}, bf16[192,512]{1,0:T(8,128)(2,1)S(1)}, u32[]{:S(2)}, u32[]{:S(2)}) %collective-permute-start.9) | collective-permute-done | bytes 196640 | tf_op jit(solution)/shard_map/ppermute | solution.py:812
  105.2 2.1 %collective-permute-start.14 = (bf16[64,512]{1,0:T(8,128)(2,1)S(1)}, bf16[64,512]{1,0:T(8,128)(2,1)S(1)}, u32[]{:S(2)}, u32[]{:S(2)}) collective-permute-start(bf16[64,512]{1,0:T(8,128)(2,1)S(1)} %get-tuple-element.179), channel_id=1, source_target_pairs={{0,8},{1,9},{2,10},{3,11},{4,12},{5,13},{6,14},{7,15},{8,0},{9,1},... | collective-permute-start | bytes 196616 | tf_op jit(solution)/shard_map/ppermute | solution.py:812
  108.2 1.6 %collective-permute-done.11.refs_2_ = bf16[96,512]{1,0:T(8,128)(2,1)S(1)} collective-permute-done((bf16[96,512]{1,0:T(8,128)(2,1)S(1)}, bf16[96,512]{1,0:T(8,128)(2,1)S(1)}, u32[]{:S(2)}, u32[]{:S(2)}) %collective-permute-start.11) | collective-permute-done | bytes 98336 | tf_op jit(solution)/shard_map/ppermute | solution.py:812
  110.5 2.4 %collective-permute-start.15 = (bf16[32,512]{1,0:T(8,128)(2,1)S(1)}, bf16[32,512]{1,0:T(8,128)(2,1)S(1)}, u32[]{:S(2)}, u32[]{:S(2)}) collective-permute-start(bf16[32,512]{1,0:T(8,128)(2,1)S(1)} %get-tuple-element.186), channel_id=1, source_target_pairs={{0,16},{1,17},{2,18},{3,19},{4,20},{5,21},{6,22},{7,23},{8,24},{9,... | collective-permute-start | bytes 98312 | tf_op jit(solution)/shard_map/ppermute | solution.py:821
  (75 shorter events, 15.0 us)
Async XLA Ops:
  0.6 9.2 %copy-start.2 = (bf16[3,8,16,512]{3,2,1,0:T(8,128)(2,1)S(1)}, bf16[3,8,16,512]{3,2,1,0:T(8,128)(2,1)}, u32[]{:S(2)}) copy-start(bf16[3,8,16,512]{3,2,1,0:T(8,128)(2,1)} %refs_0_.5) | copy-start | bytes 1179652
  0.6 11.1 %copy-start.5 = (s32[3,4]{1,0:T(4,128)S(1)}, s32[3,4]{1,0:T(4,128)}, u32[]{:S(2)}) copy-start(s32[3,4]{1,0:T(4,128)} %param.17) | copy-start | bytes 148
  0.7 11.1 %copy-start.6 = (s32[3,4]{1,0:T(4,128)S(1)}, s32[3,4]{1,0:T(4,128)}, u32[]{:S(2)}) copy-start(s32[3,4]{1,0:T(4,128)} %param.16) | copy-start | bytes 148
  2.5 22.3 %copy-start = (bf16[512,1024]{1,0:T(8,128)(2,1)S(1)}, bf16[512,1024]{1,0:T(8,128)(2,1)}, u32[]{:S(2)}) copy-start(bf16[512,1024]{1,0:T(8,128)(2,1)} %up_ref.7) | copy-start | bytes 3145732
  2.5 18.2 %all-to-all-start = ((bf16[32,32,128]{2,1,0:T(8,128)(2,1)}), bf16[32,32,128]{2,1,0:T(8,128)(2,1)S(1)}, u32[]{:S(2)}, u32[]{:S(2)}) async-start(bf16[32,32,128]{2,1,0:T(8,128)(2,1)} %shard_map.128), calls=%async_computation | async-start | bytes 524288 | tf_op jit(solution)/shard_map/all_to_all | solution.py:19
  9.9 4.8 %collective-permute-start = (bf16[3,8,1,512]{3,2,1,0:T(2,128)(2,1)S(1)}, bf16[3,8,1,512]{3,2,1,0:T(2,128)(2,1)S(1)}, u32[]{:S(2)}, u32[]{:S(2)}) collective-permute-start(bf16[3,8,1,512]{3,2,1,0:T(2,128)(2,1)S(1)} %broadcast_select_fusion.2), channel_id=1, source_target_pairs={{0,1},{1,0},{2,3},{3,2},{4,5},{5,4},{6,7},{7,6},{8,9},{9,8},{10,11... | collective-permute-start | bytes 73736 | tf_op jit(solution)/shard_map/ppermute | solution.py:132
  15.0 9.8 %collective-permute-start.2 = (bf16[3,1,18,512]{3,2,1,0:T(8,128)(2,1)S(1)}, bf16[3,1,18,512]{3,2,1,0:T(8,128)(2,1)S(1)}, u32[]{:S(2)}, u32[]{:S(2)}) collective-permute-start(bf16[3,1,18,512]{3,2,1,0:T(8,128)(2,1)S(1)} %get-tuple-element.197), channel_id=1, source_target_pairs={{0,2},{2,0},{4,6},{6,4},{8,10},{10,8},{12,14},{14,12},{16,18},{18,... | collective-permute-start | bytes 165896 | tf_op jit(solution)/shard_map/ppermute | solution.py:146
  15.1 9.8 %collective-permute-start.1 = (bf16[3,1,18,512]{3,2,1,0:T(8,128)(2,1)S(1)}, bf16[3,1,18,512]{3,2,1,0:T(8,128)(2,1)S(1)}, u32[]{:S(2)}, u32[]{:S(2)}) collective-permute-start(bf16[3,1,18,512]{3,2,1,0:T(8,128)(2,1)S(1)} %get-tuple-element.198), channel_id=1, source_target_pairs={{0,30},{2,4},{4,2},{6,8},{8,6},{10,12},{12,10},{14,16},{16,14},{18... | collective-permute-start | bytes 165896 | tf_op jit(solution)/shard_map/ppermute | solution.py:148
  22.2 11.2 %all-to-all-start.1 = ((bf16[32,16,128]{2,1,0:T(8,128)(2,1)}), bf16[32,16,128]{2,1,0:T(8,128)(2,1)S(1)}, u32[]{:S(2)}, u32[]{:S(2)}) async-start(bf16[32,16,128]{2,1,0:T(8,128)(2,1)} %bitcast.42), calls=%async_computation.1 | async-start | bytes 262144 | tf_op jit(solution)/shard_map/all_to_all | solution.py:19
  24.8 0.7 copy-start.3
  24.9 0.7 copy-start.4
  25.5 7.9 %copy-start.1 = (bf16[512,1024]{1,0:T(8,128)(2,1)S(1)}, bf16[512,1024]{1,0:T(8,128)(2,1)}, u32[]{:S(2)}) copy-start(bf16[512,1024]{1,0:T(8,128)(2,1)} %down_ref.5) | copy-start | bytes 3145732
  35.0 11.2 %all-to-all-start.2 = ((bf16[32,16,128]{2,1,0:T(8,128)(2,1)}), bf16[32,16,128]{2,1,0:T(8,128)(2,1)S(1)}, u32[]{:S(2)}, u32[]{:S(2)}) async-start(bf16[32,16,128]{2,1,0:T(8,128)(2,1)} %bitcast.37), calls=%async_computation.2 | async-start | bytes 262144 | tf_op jit(solution)/shard_map/all_to_all | solution.py:19
  47.9 11.2 %all-to-all-start.3 = ((bf16[32,16,128]{2,1,0:T(8,128)(2,1)}), bf16[32,16,128]{2,1,0:T(8,128)(2,1)S(1)}, u32[]{:S(2)}, u32[]{:S(2)}) async-start(bf16[32,16,128]{2,1,0:T(8,128)(2,1)} %bitcast.39), calls=%async_computation.3 | async-start | bytes 262144 | tf_op jit(solution)/shard_map/all_to_all | solution.py:19
  60.7 11.2 %all-to-all-start.4 = ((bf16[32,16,128]{2,1,0:T(8,128)(2,1)}), bf16[32,16,128]{2,1,0:T(8,128)(2,1)S(1)}, u32[]{:S(2)}, u32[]{:S(2)}) async-start(bf16[32,16,128]{2,1,0:T(8,128)(2,1)} %bitcast.38), calls=%async_computation.4 | async-start | bytes 262144 | tf_op jit(solution)/shard_map/all_to_all | solution.py:19
  73.7 11.2 %all-to-all-start.5 = ((bf16[32,16,128]{2,1,0:T(8,128)(2,1)}), bf16[32,16,128]{2,1,0:T(8,128)(2,1)S(1)}, u32[]{:S(2)}, u32[]{:S(2)}) async-start(bf16[32,16,128]{2,1,0:T(8,128)(2,1)} %bitcast.40), calls=%async_computation.5 | async-start | bytes 262144 | tf_op jit(solution)/shard_map/all_to_all | solution.py:19
  87.0 2.0 %collective-permute-start.3 = (bf16[544,512]{1,0:T(8,128)(2,1)S(1)}, bf16[544,512]{1,0:T(8,128)(2,1)S(1)}, u32[]{:S(2)}, u32[]{:S(2)}) collective-permute-start(bf16[544,512]{1,0:T(8,128)(2,1)S(1)} %get-tuple-element.154), channel_id=1, source_target_pairs={{0,2},{1,3},{2,0},{3,1},{4,6},{5,7},{6,4},{7,5},{8,10},{9,11},{10,... | collective-permute-start | bytes 1671176 | tf_op jit(solution)/shard_map/ppermute | solution.py:812
  89.1 2.0 %collective-permute-start.6 = (bf16[512,512]{1,0:T(8,128)(2,1)S(1)}, bf16[512,512]{1,0:T(8,128)(2,1)S(1)}, u32[]{:S(2)}, u32[]{:S(2)}) collective-permute-start(bf16[512,512]{1,0:T(8,128)(2,1)S(1)} %get-tuple-element.165), channel_id=1, source_target_pairs={{0,2},{1,3},{2,0},{3,1},{4,6},{5,7},{6,4},{7,5},{8,10},{9,11},{10,... | collective-permute-start | bytes 1572872 | tf_op jit(solution)/shard_map/ppermute | solution.py:812
  89.5 8.7 %collective-permute-start.5 = (bf16[288,512]{1,0:T(8,128)(2,1)S(1)}, bf16[288,512]{1,0:T(8,128)(2,1)S(1)}, u32[]{:S(2)}, u32[]{:S(2)}) collective-permute-start(bf16[288,512]{1,0:T(8,128)(2,1)S(1)} %get-tuple-element.160), channel_id=1, source_target_pairs={{0,4},{1,5},{2,3},{3,2},{4,0},{5,1},{6,7},{7,6},{8,12},{9,13},{10,... | collective-permute-start | bytes 884744 | tf_op jit(solution)/shard_map/ppermute | solution.py:812
  89.5 9.1 %collective-permute-start.4 = (bf16[1,8,1,512]{3,2,1,0:T(2,128)(2,1)S(1)}, bf16[1,8,1,512]{3,2,1,0:T(2,128)(2,1)S(1)}, u32[]{:S(2)}, u32[]{:S(2)}) collective-permute-start(bf16[1,8,1,512]{3,2,1,0:T(2,128)(2,1)S(1)} %broadcast_select_fusion.9), channel_id=1, source_target_pairs={{0,1},{1,0},{2,3},{3,2},{4,5},{5,4},{6,7},{7,6},{8,9},{9,8},{10,11... | collective-permute-start | bytes 24584 | tf_op jit(solution)/shard_map/ppermute | solution.py:132
  91.2 7.5 %collective-permute-start.10 = (bf16[256,512]{1,0:T(8,128)(2,1)S(1)}, bf16[256,512]{1,0:T(8,128)(2,1)S(1)}, u32[]{:S(2)}, u32[]{:S(2)}) collective-permute-start(bf16[256,512]{1,0:T(8,128)(2,1)S(1)} %get-tuple-element.166), channel_id=1, source_target_pairs={{0,1},{1,0},{2,6},{3,7},{4,5},{5,4},{6,2},{7,3},{8,9},{9,8},{10,14... | collective-permute-start | bytes 786440 | tf_op jit(solution)/shard_map/ppermute | solution.py:812
  98.3 6.8 %collective-permute-start.9 = (bf16[192,512]{1,0:T(8,128)(2,1)S(1)}, bf16[192,512]{1,0:T(8,128)(2,1)S(1)}, u32[]{:S(2)}, u32[]{:S(2)}) collective-permute-start(bf16[192,512]{1,0:T(8,128)(2,1)S(1)} %get-tuple-element.168), channel_id=1, source_target_pairs={{0,1},{1,0},{2,6},{3,7},{4,5},{5,4},{6,2},{7,3},{8,9},{9,8},{10,14... | collective-permute-start | bytes 589832 | tf_op jit(solution)/shard_map/ppermute | solution.py:812
  98.8 6.4 %collective-permute-start.12 = (bf16[128,512]{1,0:T(8,128)(2,1)S(1)}, bf16[128,512]{1,0:T(8,128)(2,1)S(1)}, u32[]{:S(2)}, u32[]{:S(2)}) collective-permute-start(bf16[128,512]{1,0:T(8,128)(2,1)S(1)} %get-tuple-element.173), channel_id=1, source_target_pairs={{0,4},{1,5},{2,3},{3,2},{4,0},{5,1},{6,7},{7,6},{8,12},{9,13},{10,... | collective-permute-start | bytes 393224 | tf_op jit(solution)/shard_map/ppermute | solution.py:812
  105.1 4.7 %collective-permute-start.11 = (bf16[96,512]{1,0:T(8,128)(2,1)S(1)}, bf16[96,512]{1,0:T(8,128)(2,1)S(1)}, u32[]{:S(2)}, u32[]{:S(2)}) collective-permute-start(bf16[96,512]{1,0:T(8,128)(2,1)S(1)} %get-tuple-element.177), channel_id=1, source_target_pairs={{0,8},{1,9},{2,10},{3,11},{4,12},{5,13},{6,14},{7,15},{8,0},{9,1},... | collective-permute-start | bytes 294920 | tf_op jit(solution)/shard_map/ppermute | solution.py:812
  105.2 5.2 %collective-permute-start.14 = (bf16[64,512]{1,0:T(8,128)(2,1)S(1)}, bf16[64,512]{1,0:T(8,128)(2,1)S(1)}, u32[]{:S(2)}, u32[]{:S(2)}) collective-permute-start(bf16[64,512]{1,0:T(8,128)(2,1)S(1)} %get-tuple-element.179), channel_id=1, source_target_pairs={{0,8},{1,9},{2,10},{3,11},{4,12},{5,13},{6,14},{7,15},{8,0},{9,1},... | collective-permute-start | bytes 196616 | tf_op jit(solution)/shard_map/ppermute | solution.py:812
  107.3 5.6 %collective-permute-start.8 = (bf16[1,1,18,512]{3,2,1,0:T(8,128)(2,1)S(1)}, bf16[1,1,18,512]{3,2,1,0:T(8,128)(2,1)S(1)}, u32[]{:S(2)}, u32[]{:S(2)}) collective-permute-start(bf16[1,1,18,512]{3,2,1,0:T(8,128)(2,1)S(1)} %get-tuple-element.207), channel_id=1, source_target_pairs={{0,2},{2,0},{4,6},{6,4},{8,10},{10,8},{12,14},{14,12},{16,18},{18,... | collective-permute-start | bytes 55304 | tf_op jit(solution)/shard_map/ppermute | solution.py:146
  107.4 6.1 %collective-permute-start.7 = (bf16[1,1,18,512]{3,2,1,0:T(8,128)(2,1)S(1)}, bf16[1,1,18,512]{3,2,1,0:T(8,128)(2,1)S(1)}, u32[]{:S(2)}, u32[]{:S(2)}) collective-permute-start(bf16[1,1,18,512]{3,2,1,0:T(8,128)(2,1)S(1)} %get-tuple-element.208), channel_id=1, source_target_pairs={{0,30},{2,4},{4,2},{6,8},{8,6},{10,12},{12,10},{14,16},{16,14},{18... | collective-permute-start | bytes 55304 | tf_op jit(solution)/shard_map/ppermute | solution.py:148
  109.8 5.4 %collective-permute-start.13 = (bf16[64,512]{1,0:T(8,128)(2,1)S(1)}, bf16[64,512]{1,0:T(8,128)(2,1)S(1)}, u32[]{:S(2)}, u32[]{:S(2)}) collective-permute-start(bf16[64,512]{1,0:T(8,128)(2,1)S(1)} %get-tuple-element.183), channel_id=1, source_target_pairs={{0,16},{1,17},{2,18},{3,19},{4,20},{5,21},{6,22},{7,23},{8,24},{9,... | collective-permute-start | bytes 196616 | tf_op jit(solution)/shard_map/ppermute | solution.py:821
  110.5 5.0 %collective-permute-start.15 = (bf16[32,512]{1,0:T(8,128)(2,1)S(1)}, bf16[32,512]{1,0:T(8,128)(2,1)S(1)}, u32[]{:S(2)}, u32[]{:S(2)}) collective-permute-start(bf16[32,512]{1,0:T(8,128)(2,1)S(1)} %get-tuple-element.186), channel_id=1, source_target_pairs={{0,16},{1,17},{2,18},{3,19},{4,20},{5,21},{6,22},{7,23},{8,24},{9,... | collective-permute-start | bytes 98312 | tf_op jit(solution)/shard_map/ppermute | solution.py:821
